TPU v7x, 32 devices: a whole 2x2x4 slice. The times are simulated.
32 devices in a mesh: section: 2 (over core), ctx: 8 (over z, x), shard: 2 (over y).
Axes of the slice: x: 2, y: 2, z: 4, core: 2. Of those that a mesh axis runs over, the one named last changes fastest.
Arguments:
- ends_in: bfloat16 [2, 2, 2, 512, 1536], P('section', None, 'shard', 'ctx'), may hold values from -6 to 6
- pair_table: int32 [8], replicated, may hold values from 0 to 7, each once
- norm_attn: bfloat16 [2, 1536], P('section', ('ctx', 'shard')), may hold values from 0.5 to 1.5
- w_query: bfloat16 [2, 1536, 1536], P('section', ('ctx', 'shard')), may hold values from -0.15625 to 0.15625
- w_key: bfloat16 [2, 1536, 768], P('section', ('ctx', 'shard')), may hold values from -0.15625 to 0.15625
- w_value: bfloat16 [2, 1536, 768], P('section', ('ctx', 'shard')), may hold values from -0.15625 to 0.15625
- w_out: bfloat16 [2, 1536, 1536], P('section', ('ctx', 'shard')), may hold values from -1.5 to 1.5
- norm_mlp: bfloat16 [2, 1536], P('section', ('ctx', 'shard')), may hold values from 0.5 to 1.5
- w_gate: bfloat16 [2, 1536, 4096], P('section', ('ctx', 'shard')), may hold values from -0.15625 to 0.15625
- w_up: bfloat16 [2, 1536, 4096], P('section', ('ctx', 'shard')), may hold values from -0.15625 to 0.15625
- w_down: bfloat16 [2, 4096, 1536], P('section', ('ctx', 'shard')), may hold values from -0.09375 to 0.09375
Outputs:
- ends_out: bfloat16 [2, 2, 2, 512, 1536], P('section', None, 'shard', 'ctx')
- norm_attn_grad: float32 [2, 1536], P('section', ('ctx', 'shard'))
- w_query_grad: float32 [2, 1536, 1536], P('section', ('ctx', 'shard'))
- w_key_grad: float32 [2, 1536, 768], P('section', ('ctx', 'shard'))
- w_value_grad: float32 [2, 1536, 768], P('section', ('ctx', 'shard'))
- w_out_grad: float32 [2, 1536, 1536], P('section', ('ctx', 'shard'))
- norm_mlp_grad: float32 [2, 1536], P('section', ('ctx', 'shard'))
- w_gate_grad: float32 [2, 1536, 4096], P('section', ('ctx', 'shard'))
- w_up_grad: float32 [2, 1536, 4096], P('section', ('ctx', 'shard'))
- w_down_grad: float32 [2, 4096, 1536], P('section', ('ctx', 'shard'))
Inputs may be any that keep to these rules, and one draw needn't show every extreme that they name: `pair_table`: each value once.
All inputs are finite; a program needn't handle non-finite values.
Results may differ from a plain program's by a relative error of at most 0.024.
Values may be sent and summed in bfloat16 or wider, within the bound.
No kernel may reach another device: no remote copies, remote signals or barrier semaphores. Data moves between devices by JAX's collectives and lax.ppermute only.
A program may use at most 320 MiB of HBM per device.

v0:
```python
import jax
import jax.numpy as jnp
from jax import lax
from jax.sharding import PartitionSpec as P

HEADS = 16
KV_HEADS = 8
HEAD_DIM = 96


NORM_EPS = 1e-05
ROPE_BASE = 100000.0
MASK_FILL = -1e30


def from_behind(block, axis, distance):
    devices = range(lax.axis_size(axis))
    route = [(i - distance, i) for i in devices if i - distance in devices]
    return lax.ppermute(block, axis, route)


def layout_positions(pair_table, block_rows, ctx_count):
    row_ids = jnp.arange(2 * block_rows * ctx_count, dtype=jnp.int32)
    device_ids = row_ids // (2 * block_rows)
    upper_half = row_ids // block_rows % 2
    offset_in = row_ids % block_rows
    matches = device_ids[:, None] == jnp.arange(ctx_count, dtype=jnp.int32)[None, :]
    owned_pair = jnp.sum(jnp.where(matches, pair_table[None, :], 0), 1)
    block_ids = jnp.where(upper_half == 0, owned_pair, 2 * ctx_count - 1 - owned_pair)
    return block_ids * block_rows + offset_in


def rope_tables(positions):
    half_dim = HEAD_DIM // 2
    freq_idx = jnp.arange(half_dim, dtype=jnp.float32)
    inverse = ROPE_BASE ** (-2.0 * freq_idx / HEAD_DIM)
    angles = positions.astype(jnp.float32)[:, None] * inverse[None, :]
    return (jnp.cos(angles), jnp.sin(angles))


def rotate(vectors, cosine_table, sine_table):
    half_dim = vectors.shape[-1] // 2
    first_half = vectors[..., :half_dim]
    second_half = vectors[..., half_dim:]
    cosine = cosine_table[:, None, :]
    sine_part = sine_table[:, None, :]
    return jnp.concatenate(
        [
            first_half * cosine - second_half * sine_part,
            second_half * cosine + first_half * sine_part,
        ],
        -1,
    )


def unrotate(grads_in, cosine_table, sine_table):
    half_dim = grads_in.shape[-1] // 2
    first_half = grads_in[..., :half_dim]
    second_half = grads_in[..., half_dim:]
    cosine = cosine_table[:, None, :]
    sine_part = sine_table[:, None, :]
    return jnp.concatenate(
        [
            first_half * cosine + second_half * sine_part,
            second_half * cosine - first_half * sine_part,
        ],
        -1,
    )


def norm_forward(inputs, gain_vec):
    inverse_rms = lax.rsqrt(jnp.mean(inputs * inputs, -1, keepdims=True) + NORM_EPS)
    return (inputs * inverse_rms * gain_vec, inverse_rms)


def norm_backward(inputs, inverse_rms, gain_vec, upstream):
    scaled = upstream * gain_vec
    input_grad = inverse_rms * scaled - inputs * inverse_rms**3 * jnp.mean(
        scaled * inputs, -1, keepdims=True
    )
    gain_grad = jnp.sum(upstream * inputs * inverse_rms, 0)
    return (input_grad, gain_grad)


def attend(queries, key_all, val_all, query_pos, key_pos):
    row_count = queries.shape[0]
    key_count = key_all.shape[0]
    group_size = HEADS // KV_HEADS
    score_scale = HEAD_DIM ** (-0.5)
    grouped = queries.reshape(row_count, KV_HEADS, group_size, HEAD_DIM)
    key_heads = key_all.reshape(key_count, KV_HEADS, HEAD_DIM)
    val_heads = val_all.reshape(key_count, KV_HEADS, HEAD_DIM)
    causal_mask = query_pos[:, None] >= key_pos[None, :]
    pieces_out = []
    pieces_lse = []
    step_heads = min(2, KV_HEADS)
    for head_first in range(0, KV_HEADS, step_heads):
        query_part = grouped[:, head_first : head_first + step_heads]
        key_part = key_heads[:, head_first : head_first + step_heads]
        value_part = val_heads[:, head_first : head_first + step_heads]
        scores = (
            jnp.einsum("qkgd,tkd->kgqt", query_part, key_part, preferred_element_type=jnp.float32)
            * score_scale
        )
        scores = jnp.where(causal_mask, scores, MASK_FILL)
        row_max = jnp.max(scores, -1, keepdims=True)
        exp_scores = jnp.exp(scores - row_max)
        row_total = jnp.sum(exp_scores, -1, keepdims=True)
        attn_probs = (exp_scores / row_total).astype(jnp.bfloat16)
        pieces_out.append(
            jnp.einsum("kgqt,tkd->qkgd", attn_probs, value_part, preferred_element_type=jnp.float32)
        )
        pieces_lse.append(row_max + jnp.log(row_total))
    return (
        jnp.concatenate(pieces_out, 1).reshape(row_count, HEADS * HEAD_DIM),
        jnp.concatenate(pieces_lse, 0),
    )


def attend_back(queries, key_all, val_all, query_pos, key_pos, log_totals, out_grad):
    row_count = queries.shape[0]
    key_count = key_all.shape[0]
    group_size = HEADS // KV_HEADS
    score_scale = HEAD_DIM ** (-0.5)
    grouped = queries.reshape(row_count, KV_HEADS, group_size, HEAD_DIM)
    out_heads = out_grad.reshape(row_count, KV_HEADS, group_size, HEAD_DIM)
    key_heads = key_all.reshape(key_count, KV_HEADS, HEAD_DIM)
    val_heads = val_all.reshape(key_count, KV_HEADS, HEAD_DIM)
    causal_mask = query_pos[:, None] >= key_pos[None, :]
    query_grads = []
    key_grads = []
    value_grads = []
    step_heads = min(2, KV_HEADS)
    for head_first in range(0, KV_HEADS, step_heads):
        query_part = grouped[:, head_first : head_first + step_heads]
        out_part = out_heads[:, head_first : head_first + step_heads]
        key_part = key_heads[:, head_first : head_first + step_heads]
        value_part = val_heads[:, head_first : head_first + step_heads]
        lse_part = log_totals[head_first : head_first + step_heads]
        scores = (
            jnp.einsum("qkgd,tkd->kgqt", query_part, key_part, preferred_element_type=jnp.float32)
            * score_scale
        )
        scores = jnp.where(causal_mask, scores, MASK_FILL)
        attn_float = jnp.exp(scores - lse_part)
        attn_probs = attn_float.astype(jnp.bfloat16)
        prob_grad = jnp.einsum(
            "qkgd,tkd->kgqt", out_part, value_part, preferred_element_type=jnp.float32
        )
        row_delta = jnp.sum(attn_float * prob_grad, -1, keepdims=True)
        score_grad = (attn_float * (prob_grad - row_delta)).astype(jnp.bfloat16)
        query_grads.append(
            jnp.einsum("kgqt,tkd->qkgd", score_grad, key_part, preferred_element_type=jnp.float32)
            * score_scale
        )
        key_grads.append(
            jnp.einsum("kgqt,qkgd->tkd", score_grad, query_part, preferred_element_type=jnp.float32)
            * score_scale
        )
        value_grads.append(
            jnp.einsum("kgqt,qkgd->tkd", attn_probs, out_part, preferred_element_type=jnp.float32)
        )
    query_grad = jnp.concatenate(query_grads, 1).reshape(row_count, HEADS, HEAD_DIM)
    key_grad = jnp.concatenate(key_grads, 1).reshape(key_count, KV_HEADS * HEAD_DIM)
    value_grad = jnp.concatenate(value_grads, 1).reshape(key_count, KV_HEADS * HEAD_DIM)
    return (query_grad, key_grad, value_grad)


def layer_forward(inputs, attn_weights, mlp_weights, cosine_table, sine_table, query_pos, key_pos):
    norm_gain, query_w, key_w, value_w, out_w = attn_weights
    gain_two, gate_w, up_w, down_w = mlp_weights
    row_count = inputs.shape[0]
    normed, inverse_first = norm_forward(inputs, norm_gain.astype(jnp.float32))
    normed = normed.astype(jnp.bfloat16)
    query_raw = jnp.dot(normed, query_w, preferred_element_type=jnp.float32).reshape(
        row_count, HEADS, HEAD_DIM
    )
    queries = (
        rotate(query_raw, cosine_table, sine_table)
        .astype(jnp.bfloat16)
        .reshape(row_count, HEADS * HEAD_DIM)
    )
    key_raw = jnp.dot(normed, key_w, preferred_element_type=jnp.float32).reshape(
        row_count, KV_HEADS, HEAD_DIM
    )
    key_local = (
        rotate(key_raw, cosine_table, sine_table)
        .astype(jnp.bfloat16)
        .reshape(row_count, KV_HEADS * HEAD_DIM)
    )
    val_local = jnp.dot(normed, value_w, preferred_element_type=jnp.float32).astype(jnp.bfloat16)
    key_all, val_all = (
        lax.all_gather(key_local, "ctx", axis=0, tiled=True),
        lax.all_gather(val_local, "ctx", axis=0, tiled=True),
    )
    attn_out, log_totals = attend(queries, key_all, val_all, query_pos, key_pos)
    attn_out = attn_out.astype(jnp.bfloat16)
    mid_stream = inputs + jnp.dot(attn_out, out_w, preferred_element_type=jnp.float32)
    normed_mid, inverse_second = norm_forward(mid_stream, gain_two.astype(jnp.float32))
    normed_mid = normed_mid.astype(jnp.bfloat16)
    gate_pre = jnp.dot(normed_mid, gate_w, preferred_element_type=jnp.float32)
    up_pre = jnp.dot(normed_mid, up_w, preferred_element_type=jnp.float32)
    hidden = (jax.nn.silu(gate_pre) * up_pre).astype(jnp.bfloat16)
    outputs = mid_stream + jnp.dot(hidden, down_w, preferred_element_type=jnp.float32)
    key_store = (key_all, val_all)
    kept_state = (
        inputs,
        inverse_first,
        normed,
        queries,
        key_local,
        val_local,
        key_store,
        attn_out,
        log_totals,
        mid_stream,
        inverse_second,
        normed_mid,
        gate_pre,
        up_pre,
        hidden,
    )
    return (outputs, kept_state)


def layer_backward(
    out_grad, kept_state, attn_weights, mlp_weights, cosine_table, sine_table, query_pos, key_pos
):
    (
        inputs,
        inverse_first,
        normed,
        queries,
        key_local,
        val_local,
        key_store,
        attn_out,
        log_totals,
        mid_stream,
        inverse_second,
        normed_mid,
        gate_pre,
        up_pre,
        hidden,
    ) = kept_state
    norm_gain, query_w, key_w, value_w, out_w = attn_weights
    gain_two, gate_w, up_w, down_w = mlp_weights
    row_count = inputs.shape[0]
    down_in = out_grad.astype(jnp.bfloat16)
    hidden_grad = jnp.einsum("rd,fd->rf", down_in, down_w, preferred_element_type=jnp.float32)
    sigmoid_gate = jax.nn.sigmoid(gate_pre)
    gate_grad_in = (
        hidden_grad * up_pre * sigmoid_gate * (1.0 + gate_pre * (1.0 - sigmoid_gate))
    ).astype(jnp.bfloat16)
    up_grad_in = (hidden_grad * gate_pre * sigmoid_gate).astype(jnp.bfloat16)
    normed_mid_grad = jnp.einsum(
        "rf,df->rd", gate_grad_in, gate_w, preferred_element_type=jnp.float32
    )
    normed_mid_grad = normed_mid_grad + jnp.einsum(
        "rf,df->rd", up_grad_in, up_w, preferred_element_type=jnp.float32
    )
    mid_part, gain_two_grad = norm_backward(
        mid_stream, inverse_second, gain_two.astype(jnp.float32), normed_mid_grad
    )
    mid_grad = out_grad + mid_part
    mid_low = mid_grad.astype(jnp.bfloat16)
    attn_grad = jnp.einsum("rd,ed->re", mid_low, out_w, preferred_element_type=jnp.float32).astype(
        jnp.bfloat16
    )
    key_all, val_all = key_store
    query_grad, key_grad_all, value_grad_all = attend_back(
        queries, key_all, val_all, query_pos, key_pos, log_totals, attn_grad
    )
    key_grad, value_grad = (
        lax.psum_scatter(
            key_grad_all.astype(jnp.bfloat16), "ctx", scatter_dimension=0, tiled=True
        ).astype(jnp.float32),
        lax.psum_scatter(
            value_grad_all.astype(jnp.bfloat16), "ctx", scatter_dimension=0, tiled=True
        ).astype(jnp.float32),
    )
    query_low = (
        unrotate(query_grad, cosine_table, sine_table)
        .reshape(row_count, HEADS * HEAD_DIM)
        .astype(jnp.bfloat16)
    )
    key_low = (
        unrotate(key_grad.reshape(row_count, KV_HEADS, HEAD_DIM), cosine_table, sine_table)
        .reshape(row_count, KV_HEADS * HEAD_DIM)
        .astype(jnp.bfloat16)
    )
    value_low = value_grad.astype(jnp.bfloat16)
    normed_grad = jnp.einsum("re,de->rd", query_low, query_w, preferred_element_type=jnp.float32)
    normed_grad = normed_grad + jnp.einsum(
        "re,de->rd", key_low, key_w, preferred_element_type=jnp.float32
    )
    normed_grad = normed_grad + jnp.einsum(
        "re,de->rd", value_low, value_w, preferred_element_type=jnp.float32
    )
    input_part, gain_one_grad = norm_backward(
        inputs, inverse_first, norm_gain.astype(jnp.float32), normed_grad
    )
    input_grad = mid_grad + input_part
    operands = (
        hidden,
        down_in,
        normed_mid,
        gate_grad_in,
        up_grad_in,
        attn_out,
        mid_low,
        normed,
        query_low,
        key_low,
        value_low,
    )
    return (input_grad, (gain_one_grad, gain_two_grad), operands)


def weight_grads(operands, gains):
    (
        hidden,
        down_in,
        normed_mid,
        gate_grad_in,
        up_grad_in,
        attn_out,
        mid_low,
        normed,
        query_low,
        key_low,
        value_low,
    ) = operands
    down_w_grad = jnp.einsum("rf,rd->fd", hidden, down_in, preferred_element_type=jnp.float32)
    gate_w_grad = jnp.einsum(
        "rd,rf->df", normed_mid, gate_grad_in, preferred_element_type=jnp.float32
    )
    up_w_grad = jnp.einsum("rd,rf->df", normed_mid, up_grad_in, preferred_element_type=jnp.float32)
    out_w_grad = jnp.einsum("re,rd->ed", attn_out, mid_low, preferred_element_type=jnp.float32)
    query_w_grad = jnp.einsum("rd,re->de", normed, query_low, preferred_element_type=jnp.float32)
    key_w_grad = jnp.einsum("rd,re->de", normed, key_low, preferred_element_type=jnp.float32)
    value_w_grad = jnp.einsum("rd,re->de", normed, value_low, preferred_element_type=jnp.float32)
    attn_grads = (
        gains[0][None],
        query_w_grad[None],
        key_w_grad[None],
        value_w_grad[None],
        out_w_grad[None],
    )
    mlp_grads = (gains[1][None], gate_w_grad[None], up_w_grad[None], down_w_grad[None])
    return (attn_grads, mlp_grads)


def body(
    ends_in, pair_table, norm_attn, w_query, w_key, w_value, w_out, norm_mlp, w_gate, w_up, w_down
):
    section_index = lax.axis_index("section")
    ctx_index = lax.axis_index("ctx")
    ctx_count = lax.axis_size("ctx")
    row_count = ends_in.shape[3]
    block_rows = row_count // 2
    key_pos = layout_positions(pair_table, block_rows, ctx_count)
    query_pos = lax.dynamic_slice_in_dim(key_pos, ctx_index * row_count, row_count)
    cosine_table, sine_table = rope_tables(query_pos)
    attn_full = (
        lax.all_gather(norm_attn, ("ctx", "shard"), axis=1, tiled=True),
        lax.all_gather(w_query, ("ctx", "shard"), axis=1, tiled=True),
        lax.all_gather(w_key, ("ctx", "shard"), axis=1, tiled=True),
        lax.all_gather(w_value, ("ctx", "shard"), axis=1, tiled=True),
        lax.all_gather(w_out, ("ctx", "shard"), axis=1, tiled=True),
    )
    mlp_full = (
        lax.all_gather(norm_mlp, ("ctx", "shard"), axis=1, tiled=True),
        lax.all_gather(w_gate, ("ctx", "shard"), axis=1, tiled=True),
        lax.all_gather(w_up, ("ctx", "shard"), axis=1, tiled=True),
        lax.all_gather(w_down, ("ctx", "shard"), axis=1, tiled=True),
    )
    attn_weights = tuple((part_full[0] for part_full in attn_full))
    mlp_weights = tuple((part_full[0] for part_full in mlp_full))
    local_data = ends_in[0, :, 0].astype(jnp.float32)
    batch_count = local_data.shape[0]
    is_first = section_index == 0
    received = jnp.zeros((row_count, ends_in.shape[4]), jnp.float32)
    section_outputs = []
    kept_store = None
    for tick_index in range(batch_count + 1):
        own_input = local_data[min(tick_index, batch_count - 1)]
        layer_in = jnp.where(is_first, own_input, received)
        layer_out, kept_state = layer_forward(
            layer_in, attn_weights, mlp_weights, cosine_table, sine_table, query_pos, key_pos
        )
        slot_index = jnp.clip(tick_index - section_index, 0, batch_count - 1)
        if tick_index == 0:
            kept_store = jax.tree.map(
                lambda array_in: jnp.zeros((batch_count,) + array_in.shape, array_in.dtype),
                kept_state,
            )
        kept_store = jax.tree.map(
            lambda stored, array_in: lax.dynamic_update_index_in_dim(
                stored, array_in, slot_index, 0
            ),
            kept_store,
            kept_state,
        )
        sent_rows = layer_out.astype(jnp.bfloat16)
        if tick_index >= 1:
            section_outputs.append(sent_rows)
        if tick_index < batch_count:
            received = from_behind(sent_rows, "section", 1).astype(jnp.float32)
    back_received = jnp.zeros((row_count, ends_in.shape[4]), jnp.float32)
    input_grads = []
    attn_total = None
    mlp_total = None
    gain_total = None
    operand_list = []
    for tick_index in range(batch_count + 1):
        if tick_index < batch_count:
            own_grad = local_data[tick_index]
        else:
            own_grad = jnp.zeros_like(back_received)
        grad_in = jnp.where(is_first, back_received, own_grad)
        slot_index = jnp.clip(tick_index - 1 + section_index, 0, batch_count - 1)
        kept_state = jax.tree.map(
            lambda stored: lax.dynamic_index_in_dim(stored, slot_index, 0, False), kept_store
        )
        input_grad, gain_grads, operands = layer_backward(
            grad_in,
            kept_state,
            attn_weights,
            mlp_weights,
            cosine_table,
            sine_table,
            query_pos,
            key_pos,
        )
        operand_list.append(operands)
        if gain_total is None:
            gain_total = gain_grads
        else:
            gain_total = (gain_total[0] + gain_grads[0], gain_total[1] + gain_grads[1])
        grad_sent = input_grad.astype(jnp.bfloat16)
        if tick_index >= 1:
            input_grads.append(grad_sent)
        if tick_index < batch_count:
            back_received = from_behind(grad_sent, "section", -1).astype(jnp.float32)
    joined = jax.tree.map(lambda *pieces: jnp.concatenate(pieces, 0), *operand_list)
    attn_total, mlp_total = weight_grads(joined, gain_total)
    attn_total = (
        lax.psum_scatter(attn_total[0], ("ctx", "shard"), scatter_dimension=1, tiled=True),
        lax.psum_scatter(attn_total[1], ("ctx", "shard"), scatter_dimension=1, tiled=True),
        lax.psum_scatter(attn_total[2], ("ctx", "shard"), scatter_dimension=1, tiled=True),
        lax.psum_scatter(attn_total[3], ("ctx", "shard"), scatter_dimension=1, tiled=True),
        lax.psum_scatter(attn_total[4], ("ctx", "shard"), scatter_dimension=1, tiled=True),
    )
    mlp_total = (
        lax.psum_scatter(mlp_total[0], ("ctx", "shard"), scatter_dimension=1, tiled=True),
        lax.psum_scatter(mlp_total[1], ("ctx", "shard"), scatter_dimension=1, tiled=True),
        lax.psum_scatter(mlp_total[2], ("ctx", "shard"), scatter_dimension=1, tiled=True),
        lax.psum_scatter(mlp_total[3], ("ctx", "shard"), scatter_dimension=1, tiled=True),
    )
    first_rows = jnp.stack(input_grads)
    last_rows = jnp.stack(section_outputs)
    ends_out = jnp.where(is_first, first_rows, last_rows)[None, :, None]
    return (
        ends_out,
        attn_total[0],
        attn_total[1],
        attn_total[2],
        attn_total[3],
        attn_total[4],
        mlp_total[0],
        mlp_total[1],
        mlp_total[2],
        mlp_total[3],
    )


def solution(mesh):
    return jax.shard_map(
        body,
        mesh=mesh,
        in_specs=(
            P("section", None, "shard", "ctx", None),
            P(),
            P("section", ("ctx", "shard")),
            P("section", ("ctx", "shard"), None),
            P("section", ("ctx", "shard"), None),
            P("section", ("ctx", "shard"), None),
            P("section", ("ctx", "shard"), None),
            P("section", ("ctx", "shard")),
            P("section", ("ctx", "shard"), None),
            P("section", ("ctx", "shard"), None),
            P("section", ("ctx", "shard"), None),
        ),
        out_specs=(
            P("section", None, "shard", "ctx", None),
            P("section", ("ctx", "shard")),
            P("section", ("ctx", "shard"), None),
            P("section", ("ctx", "shard"), None),
            P("section", ("ctx", "shard"), None),
            P("section", ("ctx", "shard"), None),
            P("section", ("ctx", "shard")),
            P("section", ("ctx", "shard"), None),
            P("section", ("ctx", "shard"), None),
            P("section", ("ctx", "shard"), None),
        ),
        check_vma=False,
    )
```

profile of v0, /device:TPU:0, one launch (start us, length us, event | category | flops | bytes accessed | tf_op | source)
XLA Modules:
  0.0 3568.6 jit_solution(1314229214990664924)
XLA Ops:
  13.8 44.3 %all-reduce.2 = (bf16[1536]{0:T(1024)(128)(2,1)S(1)}, bf16[1536]{0:T(1024)(128)(2,1)S(1)}) all-reduce(bf16[1536]{0:T(1024)(128)(2,1)S(1)} %dynamic-update-slice, bf16[1536]{0:T(1024)(128)(2,1)S(1)} %dynamic-update-slice.1), channel_id=1, replica_groups=mesh['section'=2,'ctx'=8,'shard'=2] {'ctx','shard'}, use_global_device_ids=true, to_apply=%add | all-reduce | flops 3072 | bytes 12288
  62.2 13.9 all-gather.10.cloned.1.call-done
  82.7 34.7 all_gather.49
  119.7 23.7 all-gather.8.cloned.1.call-done
  145.6 34.7 all_gather.47
  188.1 40.0 %all-gather.12.cloned.1.call-done = bf16[1,1536,1536]{2,1,0:T(8,128)(2,1)} async-done(((bf16[1,96,1536]{2,1,0:T(8,128)(2,1)}), bf16[1,1536,1536]{2,1,0:T(8,128)(2,1)}) %all-gather.12.cloned.1.call-update) | async-done | bytes 4718608 | tf_op jit(solution)/shard_map/all_gather | solution.py:367
  250.5 59.3 %all-gather.14.cloned.1.call-done = bf16[1,1536,1536]{2,1,0:T(8,128)(2,1)} async-done(((bf16[1,96,1536]{2,1,0:T(8,128)(2,1)}), bf16[1,1536,1536]{2,1,0:T(8,128)(2,1)}) %all-gather.14.cloned.1.call-update) | async-done | bytes 4718608 | tf_op jit(solution)/shard_map/all_gather | solution.py:370
  317.6 145.5 %all-gather.18.cloned.1.call-done = bf16[1,1536,4096]{2,1,0:T(8,128)(2,1)} async-done(((bf16[1,96,4096]{2,1,0:T(8,128)(2,1)}), bf16[1,1536,4096]{2,1,0:T(8,128)(2,1)}) %all-gather.18.cloned.1.call-update) | async-done | bytes 12582928 | tf_op jit(solution)/shard_map/all_gather | solution.py:375
  472.9 143.2 %all-gather.16.cloned.1.call-done = bf16[1,1536,4096]{2,1,0:T(8,128)(2,1)} async-done(((bf16[1,96,4096]{2,1,0:T(8,128)(2,1)}), bf16[1,1536,4096]{2,1,0:T(8,128)(2,1)}) %all-gather.16.cloned.1.call-update) | async-done | bytes 12582928 | tf_op jit(solution)/shard_map/all_gather | solution.py:374
  628.0 141.3 %all-gather.20.cloned.1.call-done = bf16[1,4096,1536]{2,1,0:T(8,128)(2,1)} async-done(((bf16[1,256,1536]{2,1,0:T(8,128)(2,1)}), bf16[1,4096,1536]{2,1,0:T(8,128)(2,1)}) %all-gather.20.cloned.1.call-update) | async-done | bytes 12582928 | tf_op jit(solution)/shard_map/all_gather | solution.py:376
  784.0 32.0 all_gather.57
  825.0 34.0 all_gather.56
  917.6 34.3 all_gather.59
  961.1 32.0 all_gather.58
  1097.6 39.0 %reduce-scatter.26.cloned.1.call-done = bf16[64,768]{1,0:T(8,128)(2,1)} async-done(((bf16[512,768]{1,0:T(8,128)(2,1)}), bf16[64,768]{1,0:T(8,128)(2,1)}) %reduce-scatter.26.cloned.1.call-update) | async-done | bytes 98320 | tf_op jit(solution)/shard_map/reduce_scatter | solution.py:275
  1141.8 60.6 %reduce-scatter.46.cloned.1.call-done = bf16[64,768]{1,0:T(8,128)(2,1)} async-done(((bf16[512,768]{1,0:T(8,128)(2,1)}), bf16[64,768]{1,0:T(8,128)(2,1)}) %reduce-scatter.46.cloned.1.call-update) | async-done | bytes 98320
  1280.9 39.2 %reduce-scatter.28.cloned.1.call-done = bf16[64,768]{1,0:T(8,128)(2,1)} async-done(((bf16[512,768]{1,0:T(8,128)(2,1)}), bf16[64,768]{1,0:T(8,128)(2,1)}) %reduce-scatter.28.cloned.1.call-update) | async-done | bytes 98320 | tf_op jit(solution)/shard_map/reduce_scatter | solution.py:275
  1325.1 60.1 %reduce-scatter.48.cloned.1.call-done = bf16[64,768]{1,0:T(8,128)(2,1)} async-done(((bf16[512,768]{1,0:T(8,128)(2,1)}), bf16[64,768]{1,0:T(8,128)(2,1)}) %reduce-scatter.48.cloned.1.call-update) | async-done | bytes 98320
  1466.3 37.2 %reduce-scatter.30.cloned.1.call-done = bf16[64,768]{1,0:T(8,128)(2,1)} async-done(((bf16[512,768]{1,0:T(8,128)(2,1)}), bf16[64,768]{1,0:T(8,128)(2,1)}) %reduce-scatter.30.cloned.1.call-update) | async-done | bytes 98320 | tf_op jit(solution)/shard_map/reduce_scatter | solution.py:275
  1508.4 60.1 %reduce-scatter.50.cloned.1.call-done = bf16[64,768]{1,0:T(8,128)(2,1)} async-done(((bf16[512,768]{1,0:T(8,128)(2,1)}), bf16[64,768]{1,0:T(8,128)(2,1)}) %reduce-scatter.50.cloned.1.call-update) | async-done | bytes 98320
  1596.1 10.3 convolution_bitcast_fusion.2
  1607.8 10.3 convolution_bitcast_fusion.1
  1622.2 10.3 convolution_bitcast_fusion
  1640.4 54.2 %reduce-scatter.54.cloned.1.call-done = f32[96,1]{1,0:T(8,128)} async-done(((f32[1536,1]{1,0:T(8,128)}), f32[96,1]{1,0:T(8,128)}) %reduce-scatter.54.cloned.1.call-update) | async-done | bytes 400
  1699.0 121.8 %reduce-scatter.52.cloned.1.call-done = f32[96,1]{1,0:T(8,128)} async-done(((f32[1536,1]{1,0:T(8,128)}), f32[96,1]{1,0:T(8,128)}) %reduce-scatter.52.cloned.1.call-update) | async-done | bytes 400
  1822.1 141.1 %reduce-scatter.34.cloned.1.call-done = f32[1,96,768]{2,1,0:T(8,128)} async-done(((f32[1,1536,768]{2,1,0:T(8,128)}), f32[1,96,768]{2,1,0:T(8,128)}) %reduce-scatter.34.cloned.1.call-update) | async-done | bytes 294928 | tf_op jit(solution)/shard_map/reduce_scatter | solution.py:451
  1963.2 143.5 %reduce-scatter.36.cloned.1.call-done = f32[1,96,768]{2,1,0:T(8,128)} async-done(((f32[1,1536,768]{2,1,0:T(8,128)}), f32[1,96,768]{2,1,0:T(8,128)}) %reduce-scatter.36.cloned.1.call-update) | async-done | bytes 294928 | tf_op jit(solution)/shard_map/reduce_scatter | solution.py:452
  2106.7 176.5 %reduce-scatter.32.cloned.1.call-done = f32[1,96,1536]{2,1,0:T(8,128)} async-done(((f32[1,1536,1536]{2,1,0:T(8,128)}), f32[1,96,1536]{2,1,0:T(8,128)}) %reduce-scatter.32.cloned.1.call-update) | async-done | bytes 589840 | tf_op jit(solution)/shard_map/reduce_scatter | solution.py:450
  2283.2 177.5 %reduce-scatter.38.cloned.1.call-done = f32[1,96,1536]{2,1,0:T(8,128)} async-done(((f32[1,1536,1536]{2,1,0:T(8,128)}), f32[1,96,1536]{2,1,0:T(8,128)}) %reduce-scatter.38.cloned.1.call-update) | async-done | bytes 589840 | tf_op jit(solution)/shard_map/reduce_scatter | solution.py:453
  2460.7 366.8 %reduce-scatter.40.cloned.1.call-done = f32[1,96,4096]{2,1,0:T(8,128)} async-done(((f32[1,1536,4096]{2,1,0:T(8,128)}), f32[1,96,4096]{2,1,0:T(8,128)}) %reduce-scatter.40.cloned.1.call-update) | async-done | bytes 1572880 | tf_op jit(solution)/shard_map/reduce_scatter | solution.py:457
  2827.5 367.0 %reduce-scatter.42.cloned.1.call-done = f32[1,96,4096]{2,1,0:T(8,128)} async-done(((f32[1,1536,4096]{2,1,0:T(8,128)}), f32[1,96,4096]{2,1,0:T(8,128)}) %reduce-scatter.42.cloned.1.call-update) | async-done | bytes 1572880 | tf_op jit(solution)/shard_map/reduce_scatter | solution.py:458
  3194.6 367.0 %reduce-scatter.44.cloned.1.call-done = f32[1,256,1536]{2,1,0:T(8,128)} async-done(((f32[1,4096,1536]{2,1,0:T(8,128)}), f32[1,256,1536]{2,1,0:T(8,128)}) %reduce-scatter.44.cloned.1.call-update) | async-done | bytes 1572880 | tf_op jit(solution)/shard_map/reduce_scatter | solution.py:459
  (838 shorter events, 494.4 us)
Async XLA Ops:
  7.2 68.9 %all-gather.10.cloned.1.call-start = ((), (), s32[]{:S(2)}) async-start(), calls=%async_computation.16 | async-start | bytes 2506752 | tf_op jit(solution)/shard_map/all_gather | solution.py:368
  8.0 135.4 %all-gather.8.cloned.1.call-start = ((), (), s32[]{:S(2)}) async-start(), calls=%async_computation.15 | async-start | bytes 2506752 | tf_op jit(solution)/shard_map/all_gather | solution.py:369
  8.7 219.4 %all-gather.12.cloned.1.call-start = ((), (), s32[]{:S(2)}) async-start(), calls=%async_computation.17 | async-start | bytes 5013504 | tf_op jit(solution)/shard_map/all_gather | solution.py:367
  9.4 300.3 %all-gather.14.cloned.1.call-start = ((), (), s32[]{:S(2)}) async-start(), calls=%async_computation.18 | async-start | bytes 5013504 | tf_op jit(solution)/shard_map/all_gather | solution.py:370
  10.0 453.1 %all-gather.18.cloned.1.call-start = ((), (), s32[]{:S(2)}) async-start(), calls=%async_computation.20 | async-start | bytes 13369344 | tf_op jit(solution)/shard_map/all_gather | solution.py:375
  10.6 605.5 %all-gather.16.cloned.1.call-start = ((), (), s32[]{:S(2)}) async-start(), calls=%async_computation.19 | async-start | bytes 13369344 | tf_op jit(solution)/shard_map/all_gather | solution.py:374
  11.2 758.1 %all-gather.20.cloned.1.call-start = ((), (), s32[]{:S(2)}) async-start(), calls=%async_computation.21 | async-start | bytes 13369344 | tf_op jit(solution)/shard_map/all_gather | solution.py:376
  11.9 1124.6 %reduce-scatter.26.cloned.1.call-start = ((), (), s32[]{:S(2)}) async-start(), calls=%async_computation.22 | async-start | bytes 884736 | tf_op jit(solution)/shard_map/reduce_scatter | solution.py:275
  79.0 702.6 %copy-start.2 = (bf16[768,1536]{1,0:T(8,128)(2,1)}, bf16[768,1536]{1,0:T(8,128)(2,1)S(1)}, u32[]{:S(2)}) copy-start(bf16[768,1536]{1,0:T(8,128)(2,1)S(1)} %copy.187) | copy-start | bytes 7077892
  776.4 2.4 collective-permute-start
  896.9 10.7 collective-permute-start.1
  1075.1 127.3 %reduce-scatter.46.cloned.1.call-start = ((), (), s32[]{:S(2)}) async-start(), calls=%async_computation.32 | async-start | bytes 884736
  1082.8 237.3 %reduce-scatter.28.cloned.1.call-start = ((), (), s32[]{:S(2)}) async-start(), calls=%async_computation.23 | async-start | bytes 884736 | tf_op jit(solution)/shard_map/reduce_scatter | solution.py:275
  1137.7 64.6 %copy-start.1 = (bf16[1,1536,768]{2,1,0:T(8,128)(2,1)S(1)}, bf16[1,1536,768]{2,1,0:T(8,128)(2,1)}, u32[]{:S(2)}) copy-start(bf16[1,1536,768]{2,1,0:T(8,128)(2,1)} %all-gather.8.cloned.1.call-done) | copy-start | bytes 7077892
  1138.2 64.1 %copy-start.138 = (bf16[64,768]{1,0:T(8,128)(2,1)}, bf16[64,768]{1,0:T(8,128)(2,1)S(1)}, u32[]{:S(2)}) copy-start(bf16[64,768]{1,0:T(8,128)(2,1)S(1)} %convert_element_type.536) | copy-start | bytes 294916
  1205.7 3.3 collective-permute-start.2
  1258.5 126.7 %reduce-scatter.48.cloned.1.call-start = ((), (), s32[]{:S(2)}) async-start(), calls=%async_computation.33 | async-start | bytes 884736
  1272.5 230.9 %reduce-scatter.30.cloned.1.call-start = ((), (), s32[]{:S(2)}) async-start(), calls=%async_computation.24 | async-start | bytes 884736 | tf_op jit(solution)/shard_map/reduce_scatter | solution.py:275
  1321.3 64.0 %copy-start.163 = (f32[64]{0:T(128)S(1)}, f32[64]{0:T(128)}, u32[]{:S(2)}) copy-start(f32[64]{0:T(128)} %get-tuple-element.156) | copy-start | bytes 772
  1389.1 3.3 collective-permute-start.3
  1441.8 126.8 %reduce-scatter.50.cloned.1.call-start = ((), (), s32[]{:S(2)}) async-start(), calls=%async_computation.34 | async-start | bytes 884736
  1453.9 240.7 %reduce-scatter.54.cloned.1.call-start = ((), (), s32[]{:S(2)}) async-start(), calls=%async_computation.36 | async-start | bytes 835584
  1461.6 359.2 %reduce-scatter.52.cloned.1.call-start = ((), (), s32[]{:S(2)}) async-start(), calls=%async_computation.35 | async-start | bytes 835584
  1505.1 63.5 %copy-start.140 = (bf16[64,768]{1,0:T(8,128)(2,1)}, bf16[64,768]{1,0:T(8,128)(2,1)S(1)}, u32[]{:S(2)}) copy-start(bf16[64,768]{1,0:T(8,128)(2,1)S(1)} %convert_element_type.578) | copy-start | bytes 294916
  1573.2 390.0 %reduce-scatter.34.cloned.1.call-start = ((), (), s32[]{:S(2)}) async-start(), calls=%async_computation.26 | async-start | bytes 5013504 | tf_op jit(solution)/shard_map/reduce_scatter | solution.py:451
  1577.4 529.3 %reduce-scatter.36.cloned.1.call-start = ((), (), s32[]{:S(2)}) async-start(), calls=%async_computation.27 | async-start | bytes 5013504 | tf_op jit(solution)/shard_map/reduce_scatter | solution.py:452
  1581.9 701.3 %reduce-scatter.32.cloned.1.call-start = ((), (), s32[]{:S(2)}) async-start(), calls=%async_computation.25 | async-start | bytes 10027008 | tf_op jit(solution)/shard_map/reduce_scatter | solution.py:450
  1588.1 872.6 %reduce-scatter.38.cloned.1.call-start = ((), (), s32[]{:S(2)}) async-start(), calls=%async_computation.28 | async-start | bytes 10027008 | tf_op jit(solution)/shard_map/reduce_scatter | solution.py:453
  1594.5 1233.0 %reduce-scatter.40.cloned.1.call-start = ((), (), s32[]{:S(2)}) async-start(), calls=%async_computation.29 | async-start | bytes 26738688 | tf_op jit(solution)/shard_map/reduce_scatter | solution.py:457
  1606.4 1588.1 %reduce-scatter.42.cloned.1.call-start = ((), (), s32[]{:S(2)}) async-start(), calls=%async_computation.30 | async-start | bytes 26738688 | tf_op jit(solution)/shard_map/reduce_scatter | solution.py:458
  1618.1 1943.5 %reduce-scatter.44.cloned.1.call-start = ((), (), s32[]{:S(2)}) async-start(), calls=%async_computation.31 | async-start | bytes 26738688 | tf_op jit(solution)/shard_map/reduce_scatter | solution.py:459
  1633.5 63.7 %copy-start.111 = (bf16[64,1536]{1,0:T(8,128)(2,1)S(1)}, bf16[64,1536]{1,0:T(8,128)(2,1)}, u32[]{:S(2)}) copy-start(bf16[64,1536]{1,0:T(8,128)(2,1)} %copy-done.110) | copy-start | bytes 589828
  (196 other events, 1454.8 us)
Sparse Core Ops, SparseCore 0:
  10.9 65.2 all-gather.9
  78.9 64.4 all-gather.7
  146.2 81.9 all-gather.11
  230.8 78.9 all-gather.13
  312.5 150.6 all-gather.17
  465.9 150.1 all-gather.15
  619.0 150.1 all-gather.19
  1075.2 61.3 reduce-scatter.25
  1140.8 61.5 reduce-scatter.45
  1258.7 61.4 reduce-scatter.27
  1323.8 61.4 reduce-scatter.47
  1441.9 61.4 reduce-scatter.29
  1507.1 61.4 reduce-scatter.49
  1573.1 121.4 reduce-scatter.53
  1699.2 121.5 reduce-scatter.51
  1826.3 136.8 reduce-scatter.33
  1969.6 137.0 reduce-scatter.35
  2112.8 170.3 reduce-scatter.31
  2290.4 170.2 reduce-scatter.37
  2466.8 360.6 reduce-scatter.39
  2833.8 360.6 reduce-scatter.41
  3200.9 360.6 reduce-scatter.43
where the time goes:
time: 3580 us; the launch traced here: 3570 us
  waiting for transfers between devices  2790 us (78%)
  matrix products  325 us (9%)
  blocking collectives  246 us (7%)
  local copies, waits for them, and re-layouts  137 us (4%)
  other arithmetic  48.6 us (1%)
    reduce_scatter x1, waiting for transfers between devices, body(): lax.psum_scatter(mlp_total[2], ('ctx', 'shard'), scatter_dimension=1, til...  367 us
    reduce_scatter x1, waiting for transfers between devices, body(): lax.psum_scatter(mlp_total[3], ('ctx', 'shard'), scatter_dimension=1, til...  367 us
    reduce_scatter x1, waiting for transfers between devices, body(): lax.psum_scatter(mlp_total[1], ('ctx', 'shard'), scatter_dimension=1, til...  367 us
    unnamed x27, waiting for transfers between devices  361 us
    reduce_scatter x1, waiting for transfers between devices, body(): lax.psum_scatter(attn_total[4], ('ctx', 'shard'), scatter_dimension=1, ti...  177 us
    reduce_scatter x1, waiting for transfers between devices, body(): lax.psum_scatter(attn_total[1], ('ctx', 'shard'), scatter_dimension=1, ti...  176 us
    all_gather x1, waiting for transfers between devices, body(): lax.all_gather(w_up, ('ctx', 'shard'), axis=1, tiled=True)  146 us
    reduce_scatter x1, waiting for transfers between devices, body(): lax.psum_scatter(attn_total[3], ('ctx', 'shard'), scatter_dimension=1, ti...  144 us
  transfers between devices with their start and end apart: 26, of which 25 were waited for; matrix products, arithmetic and copies ran while one was open for 7% of the time, Pallas kernels for 0%

commit v1 on v0

v1 whole, which is shorter than its diff:
```python
import jax
import jax.numpy as jnp
from jax import lax
from jax.experimental import pallas as pl
from jax.experimental.pallas import tpu as pltpu
from jax.sharding import PartitionSpec as P

HEADS = 16
KV_HEADS = 8
HEAD_DIM = 96
HALF = HEAD_DIM // 2
LANES = 128
HALF_LANES = LANES // 2

NORM_EPS = 1e-05
ROPE_BASE = 100000.0
MASK_FILL = -1e30

MESH_AXES = ("section", "ctx", "shard")
F32 = jnp.float32
BF16 = jnp.bfloat16


class Layout:
    def __init__(self):
        self.sections = lax.axis_size("section")
        self.ctx = lax.axis_size("ctx")
        self.shards = lax.axis_size("shard")
        self.halves = 2
        self.group = self.ctx // self.halves
        ctx_index = lax.axis_index("ctx")
        self.section_index = lax.axis_index("section")
        self.ctx_index = ctx_index
        self.half = ctx_index // self.group
        self.member = ctx_index % self.group
        self.shard = lax.axis_index("shard")

    def move(self, block, sections, target):
        pairs = []
        for sec in sections:
            for c in range(self.ctx):
                for s in range(self.shards):
                    new_sec, new_c, new_s = target(sec, c, s)
                    pairs.append((self.flat(sec, c, s), self.flat(new_sec, new_c, new_s)))
        return lax.ppermute(block, MESH_AXES, pairs)

    def flat(self, sec, c, s):
        return (sec * self.ctx + c) * self.shards + s

    def to_member(self, block, sections, step):
        return self.move(block, sections, lambda sec, c, s: (sec, c ^ step, s))

    def to_half(self, block, sections):
        return self.move(block, sections, lambda sec, c, s: (sec, c ^ self.group, s))

    def to_shard(self, block, sections):
        return self.move(block, sections, lambda sec, c, s: (sec, c, s ^ 1))

    def to_section(self, block, source):
        pairs = []
        for c in range(self.ctx):
            for s in range(self.shards):
                pairs.append((self.flat(source, c, s), self.flat(1 - source, c, s)))
        return lax.ppermute(block, MESH_AXES, pairs)


def pick(parts, index):
    return lax.dynamic_index_in_dim(parts, index, 0, False)


def split_blocks(weight, lay, unit):
    rows = weight.shape[0]
    parts = weight.reshape(rows, lay.halves, lay.group, unit)
    return parts.transpose(2, 0, 1, 3).reshape(lay.group, rows, lay.halves * unit)


def merge_blocks(parts, lay, unit):
    rows = parts.shape[1]
    parts = parts.reshape(lay.group, rows, lay.halves, unit)
    return parts.transpose(1, 2, 0, 3).reshape(rows, lay.halves * lay.group * unit)


def aligned(lay, block_rows):
    return block_rows == HEAD_DIM and KV_HEADS % lay.group == 0


def split_query(weight, lay):
    if aligned(lay, weight.shape[0]):
        return split_blocks(weight, lay, lay.shards * HEAD_DIM)
    rows = weight.shape[0]
    return weight.reshape(rows, lay.group, -1).transpose(1, 0, 2)


def merge_query(parts, lay):
    rows = parts.shape[1]
    if aligned(lay, rows):
        return merge_blocks(parts, lay, lay.shards * HEAD_DIM)
    return parts.transpose(1, 0, 2).reshape(rows, -1)


def split_key(weight, lay):
    rows = weight.shape[0]
    if aligned(lay, rows):
        return split_blocks(weight, lay, HEAD_DIM)
    copies = max(1, lay.group // KV_HEADS)
    parts = weight.reshape(rows, lay.group // copies, -1).transpose(1, 0, 2)
    return jnp.repeat(parts, copies, axis=0)


def merge_key(parts, lay):
    rows = parts.shape[1]
    if aligned(lay, rows):
        return merge_blocks(parts, lay, HEAD_DIM)
    copies = max(1, lay.group // KV_HEADS)
    parts = jnp.sum(parts.reshape(lay.group // copies, copies, rows, -1), 1)
    return parts.transpose(1, 0, 2).reshape(rows, -1)


def place(own, others, member):
    group = 1 + len(others)
    stacked = jnp.zeros((group,) + own.shape, own.dtype)
    for step, block in enumerate((own,) + tuple(others)):
        stacked = lax.dynamic_update_index_in_dim(stacked, block, member ^ step, 0)
    return stacked


def swap_columns(parts, lay, secs):
    others = [
        lay.to_member(pick(parts, lay.member ^ step), secs, step) for step in range(1, lay.group)
    ]
    return place(pick(parts, lay.member), others, lay.member)


def join_two(own, other, index, axis):
    first = jnp.where(index == 0, own, other)
    second = jnp.where(index == 0, other, own)
    return jnp.stack([first, second], axis)


def spread(block, lay, secs):
    over_half = join_two(block, lay.to_half(block, secs), lay.half, 0)
    return join_two(over_half, lay.to_shard(over_half, secs), lay.shard, 2)


def collect(sums, lay, secs, wire):
    own = lax.dynamic_index_in_dim(sums, lay.shard, 2, False)
    sent = lax.dynamic_index_in_dim(sums, 1 - lay.shard, 2, False).astype(wire)
    own = own + lay.to_shard(sent, secs).astype(F32)
    kept = pick(own, lay.half)
    sent = pick(own, 1 - lay.half).astype(wire)
    return kept + lay.to_half(sent, secs).astype(F32)


def return_columns(parts, lay, secs, wire):
    others = [
        lay.to_member(pick(parts, lay.member ^ step).astype(wire), secs, step).astype(F32)
        for step in range(1, lay.group)
    ]
    return place(pick(parts, lay.member), others, lay.member)


def lane_matrix(heads):
    source = jnp.arange(heads * HEAD_DIM)
    head, offset = source // HEAD_DIM, source % HEAD_DIM
    target = head * LANES + (offset // HALF) * HALF_LANES + offset % HALF
    return (target[:, None] == jnp.arange(heads * LANES)[None, :]).astype(BF16)


def rot(vec, cos_t, sin_t):
    return vec * cos_t + pltpu.roll(vec, HALF_LANES, 1) * sin_t


def rot_back(vec, cos_t, sin_t):
    return vec * cos_t - pltpu.roll(vec, HALF_LANES, 1) * sin_t


def mm(a, b):
    return lax.dot_general(a, b, (((1,), (0,)), ((), ())), preferred_element_type=F32)


def mm_nt(a, b):
    return lax.dot_general(a, b, (((1,), (1,)), ((), ())), preferred_element_type=F32)


def mm_tn(a, b):
    return lax.dot_general(a, b, (((0,), (0,)), ((), ())), preferred_element_type=F32)


def attend_kernel(per_key, q_raw, k_raw, v_raw, cos_t, sin_t, pos_q, pos_k, q_out, k_out, v_out, o_out, lse_out):
    scale = HEAD_DIM ** (-0.5)
    cos_v, sin_v = cos_t[...], sin_t[...]
    key = rot(k_raw[...], cos_v, sin_v).astype(BF16)
    value = v_raw[...].astype(BF16)
    k_out[...] = key
    v_out[...] = value
    mask = pos_q[...] >= pos_k[...]
    for head in range(per_key):
        lanes = slice(head * LANES, (head + 1) * LANES)
        query = rot(q_raw[:, lanes], cos_v, sin_v).astype(BF16)
        q_out[:, lanes] = query
        scores = jnp.where(mask, mm_nt(query, key) * scale, MASK_FILL)
        row_max = jnp.max(scores, -1, keepdims=True)
        weights = jnp.exp(scores - row_max)
        total = jnp.sum(weights, -1, keepdims=True)
        probs = (weights * (1.0 / total)).astype(BF16)
        o_out[:, lanes] = mm(probs, value).astype(BF16)
        lse_out[head] = row_max + jnp.log(total)


def attend(raw, tables, n_query, n_key):
    rows = raw.shape[0]
    per_key = n_query // n_key
    cos_t, sin_t, pos_q, pos_k = tables
    full = lambda g: (0, 0)
    wide = pl.BlockSpec((rows, per_key * LANES), lambda g: (0, g))
    slim = pl.BlockSpec((rows, LANES), lambda g: (0, g))
    return pl.pallas_call(
        lambda *refs: attend_kernel(per_key, *refs),
        grid=(n_key,),
        in_specs=[
            wide,
            pl.BlockSpec((rows, LANES), lambda g: (0, n_query + g)),
            pl.BlockSpec((rows, LANES), lambda g: (0, n_query + n_key + g)),
            pl.BlockSpec((rows, LANES), full),
            pl.BlockSpec((rows, LANES), full),
            pl.BlockSpec((rows, 1), full),
            pl.BlockSpec((1, rows), full),
        ],
        out_specs=[
            wide,
            slim,
            slim,
            wide,
            pl.BlockSpec((per_key, rows, 1), lambda g: (g, 0, 0)),
        ],
        out_shape=[
            jax.ShapeDtypeStruct((rows, n_query * LANES), BF16),
            jax.ShapeDtypeStruct((rows, n_key * LANES), BF16),
            jax.ShapeDtypeStruct((rows, n_key * LANES), BF16),
            jax.ShapeDtypeStruct((rows, n_query * LANES), BF16),
            jax.ShapeDtypeStruct((n_query, rows, 1), F32),
        ],
        compiler_params=pltpu.CompilerParams(vmem_limit_bytes=56 * 1024 * 1024),
        cost_estimate=pl.CostEstimate(
            flops=4 * n_query * rows * rows * LANES,
            bytes_accessed=rows * (n_query + 2 * n_key) * LANES * 8,
            transcendentals=n_query * rows * rows,
        ),
        name="attend",
    )(raw, raw, raw, cos_t, sin_t, pos_q, pos_k)


def attend_back_kernel(per_key, q, k, v, do, lse, cos_t, sin_t, pos_q, pos_k, dq_out, dk_out, dv_out):
    scale = HEAD_DIM ** (-0.5)
    cos_v, sin_v = cos_t[...], sin_t[...]
    key, value = k[...], v[...]
    mask = pos_q[...] >= pos_k[...]
    key_grad = None
    value_grad = None
    for head in range(per_key):
        lanes = slice(head * LANES, (head + 1) * LANES)
        query = q[:, lanes]
        grad = do[:, lanes]
        scores = jnp.where(mask, mm_nt(query, key) * scale, MASK_FILL)
        probs = jnp.exp(scores - lse[head])
        prob_grad = mm_nt(grad, value)
        delta = jnp.sum(probs * prob_grad, -1, keepdims=True)
        score_grad = (probs * (prob_grad - delta)).astype(BF16)
        dq_out[:, lanes] = rot_back(mm(score_grad, key) * scale, cos_v, sin_v).astype(BF16)
        dk = mm_tn(score_grad, query)
        dv = mm_tn(probs.astype(BF16), grad)
        key_grad = dk if key_grad is None else key_grad + dk
        value_grad = dv if value_grad is None else value_grad + dv
    dk_out[...] = rot_back(key_grad * scale, cos_v, sin_v).astype(BF16)
    dv_out[...] = value_grad.astype(BF16)


def attend_back(kept, out_grad, tables, n_query, n_key):
    queries, keys, values, lse = kept
    rows = queries.shape[0]
    per_key = n_query // n_key
    cos_t, sin_t, pos_q, pos_k = tables
    full = lambda g: (0, 0)
    wide = pl.BlockSpec((rows, per_key * LANES), lambda g: (0, g))
    slim = pl.BlockSpec((rows, LANES), lambda g: (0, g))
    return pl.pallas_call(
        lambda *refs: attend_back_kernel(per_key, *refs),
        grid=(n_key,),
        in_specs=[
            wide,
            slim,
            slim,
            wide,
            pl.BlockSpec((per_key, rows, 1), lambda g: (g, 0, 0)),
            pl.BlockSpec((rows, LANES), full),
            pl.BlockSpec((rows, LANES), full),
            pl.BlockSpec((rows, 1), full),
            pl.BlockSpec((1, rows), full),
        ],
        out_specs=[wide, slim, slim],
        out_shape=[
            jax.ShapeDtypeStruct((rows, n_query * LANES), BF16),
            jax.ShapeDtypeStruct((rows, n_key * LANES), BF16),
            jax.ShapeDtypeStruct((rows, n_key * LANES), BF16),
        ],
        compiler_params=pltpu.CompilerParams(vmem_limit_bytes=56 * 1024 * 1024),
        cost_estimate=pl.CostEstimate(
            flops=10 * n_query * rows * rows * LANES,
            bytes_accessed=rows * (n_query + n_key) * LANES * 8,
            transcendentals=n_query * rows * rows,
        ),
        name="attend_back",
    )(queries, keys, values, out_grad, lse, cos_t, sin_t, pos_q, pos_k)


def gather_rows(block, lay, secs):
    others = [lay.to_member(block, secs, step) for step in range(1, lay.group)]
    return jnp.concatenate([block] + others, 0)


def scatter_rows(partial, lay, secs):
    rows = partial.shape[0] // lay.group
    parts = partial.reshape(lay.group, rows, -1)
    total = parts[0]
    for step in range(1, lay.group):
        total = total + lay.to_member(parts[step].astype(BF16), secs, step).astype(F32)
    return total


def norm_forward(inputs, gain_vec):
    inverse_rms = lax.rsqrt(jnp.mean(inputs * inputs, -1, keepdims=True) + NORM_EPS)
    return (inputs * inverse_rms * gain_vec).astype(BF16), inverse_rms


def norm_backward(inputs, inverse_rms, gain_vec, upstream):
    scaled = upstream * gain_vec
    input_grad = inverse_rms * scaled - inputs * inverse_rms**3 * jnp.mean(
        scaled * inputs, -1, keepdims=True
    )
    gain_grad = jnp.sum(upstream * inputs * inverse_rms, 0)
    return input_grad, gain_grad


def layer_forward(inputs, weights, tables, lay, secs):
    gain_one, gain_two, qkv_w, out_w, gate_up_w, down_w, n_query, n_key = weights
    normed_own, inverse_first = norm_forward(inputs, gain_one)
    normed = gather_rows(normed_own, lay, secs)
    raw = jnp.dot(normed, qkv_w, preferred_element_type=F32)
    queries, keys, values, attn_out, lse = attend(raw, tables, n_query, n_key)
    mid_stream = inputs + scatter_rows(
        jnp.dot(attn_out, out_w, preferred_element_type=F32), lay, secs
    )
    mid_own, inverse_second = norm_forward(mid_stream, gain_two)
    normed_mid = gather_rows(mid_own, lay, secs)
    gate_up = jnp.dot(normed_mid, gate_up_w, preferred_element_type=F32)
    ff = gate_up.shape[1] // 2
    gate_pre, up_pre = gate_up[:, :ff], gate_up[:, ff:]
    hidden = (jax.nn.silu(gate_pre) * up_pre).astype(BF16)
    outputs = mid_stream + scatter_rows(
        jnp.dot(hidden, down_w, preferred_element_type=F32), lay, secs
    )
    kept = (
        inputs,
        inverse_first,
        normed,
        (queries, keys, values, lse),
        attn_out,
        mid_stream,
        inverse_second,
        normed_mid,
        gate_pre,
        up_pre,
        hidden,
    )
    return outputs, kept


def layer_backward(out_grad, kept, weights, tables, lay, secs):
    gain_one, gain_two, qkv_w, out_w, gate_up_w, down_w, n_query, n_key = weights
    (
        inputs,
        inverse_first,
        normed,
        attn_kept,
        attn_out,
        mid_stream,
        inverse_second,
        normed_mid,
        gate_pre,
        up_pre,
        hidden,
    ) = kept
    down_in = gather_rows(out_grad.astype(BF16), lay, secs)
    hidden_grad = jnp.einsum("rd,fd->rf", down_in, down_w, preferred_element_type=F32)
    sigmoid_gate = jax.nn.sigmoid(gate_pre)
    gate_grad_in = (
        hidden_grad * up_pre * sigmoid_gate * (1.0 + gate_pre * (1.0 - sigmoid_gate))
    ).astype(BF16)
    up_grad_in = (hidden_grad * gate_pre * sigmoid_gate).astype(BF16)
    gate_up_grad = jnp.concatenate([gate_grad_in, up_grad_in], 1)
    normed_mid_grad = scatter_rows(
        jnp.einsum("rf,df->rd", gate_up_grad, gate_up_w, preferred_element_type=F32), lay, secs
    )
    mid_part, gain_two_grad = norm_backward(mid_stream, inverse_second, gain_two, normed_mid_grad)
    mid_grad = out_grad + mid_part
    mid_low = gather_rows(mid_grad.astype(BF16), lay, secs)
    attn_grad = jnp.einsum("rd,ed->re", mid_low, out_w, preferred_element_type=F32).astype(BF16)
    lows = jnp.concatenate(attend_back(attn_kept, attn_grad, tables, n_query, n_key), 1)
    normed_grad = scatter_rows(
        jnp.einsum("re,de->rd", lows, qkv_w, preferred_element_type=F32), lay, secs
    )
    input_part, gain_one_grad = norm_backward(inputs, inverse_first, gain_one, normed_grad)
    input_grad = mid_grad + input_part
    operands = (hidden, down_in, normed_mid, gate_up_grad, attn_out, mid_low, normed, lows)
    return input_grad, jnp.stack([gain_one_grad, gain_two_grad]), operands


def weight_grads(operands, lay, secs, spread_out, spread_lanes, n_query, n_key):
    hidden, down_in, normed_mid, gate_up_grad, attn_out, mid_low, normed, lows = operands
    halves, group, shards = lay.halves, lay.group, lay.shards
    wire = BF16
    width = normed.shape[1]
    row_block = width // (halves * group * shards)
    down_grad = mm_tn(hidden, down_in)
    down_grad = down_grad.reshape(halves, 1, shards, -1, width)
    down_grad = collect(down_grad, lay, secs, wire)[0]
    gate_up = mm_tn(normed_mid, gate_up_grad).reshape(halves, group, shards, row_block, -1)
    gate_up = return_columns(collect(gate_up, lay, secs, wire), lay, secs, wire)
    ff = gate_up.shape[2] // 2
    unit = ff // halves
    gate_grad = merge_blocks(gate_up[:, :, :ff], lay, unit)
    up_grad = merge_blocks(gate_up[:, :, ff:], lay, unit)
    attn_low = mm_nt(attn_out, spread_out).astype(BF16)
    out_grad = mm_tn(attn_low, mid_low)
    if aligned(lay, row_block):
        out_grad = out_grad.reshape(halves, 1, shards, row_block, width)
        out_grad = collect(out_grad, lay, secs, wire)[0]
    else:
        all_rows = jnp.zeros((lay.group,) + out_grad.shape, F32)
        all_rows = lax.dynamic_update_index_in_dim(all_rows, out_grad, lay.member, 0)
        out_grad = lax.psum_scatter(
            all_rows.reshape(width, width), ("ctx", "shard"), scatter_dimension=0, tiled=True
        )
    low = mm_nt(lows, spread_lanes).astype(BF16)
    qkv = mm_tn(normed, low).reshape(halves, group, shards, row_block, -1)
    qkv = return_columns(collect(qkv, lay, secs, wire), lay, secs, wire)
    q_cols, k_cols = n_query * HEAD_DIM, n_key * HEAD_DIM
    query_grad = merge_query(qkv[:, :, :q_cols], lay)
    key_grad = merge_key(qkv[:, :, q_cols : q_cols + k_cols], lay)
    value_grad = merge_key(qkv[:, :, q_cols + k_cols :], lay)
    return query_grad, key_grad, value_grad, out_grad, gate_grad, up_grad, down_grad


def gain_sums(gains, lay, secs):
    parts = gains.reshape(2, lay.halves, lay.group, lay.shards, -1).transpose(1, 2, 3, 0, 4)
    parts = collect(parts, lay, secs, F32)
    total = pick(parts, lay.member)
    for step in range(1, lay.group):
        total = total + lay.to_member(pick(parts, lay.member ^ step), secs, step)
    return total


def group_tables(pair_table, block_rows, lay, head_dim):
    ctx_ids = []
    for step in range(lay.group):
        for half in range(lay.halves):
            ctx_ids.append((lay.half ^ half) * lay.group + (lay.member ^ step))
    ctx_ids = jnp.stack(ctx_ids)
    owned = jnp.sum(
        jnp.where(ctx_ids[:, None] == jnp.arange(lay.ctx)[None, :], pair_table[None, :], 0), 1
    )
    blocks = jnp.stack([owned, 2 * lay.ctx - 1 - owned], 1)
    positions = (blocks[:, :, None] * block_rows + jnp.arange(block_rows)[None, None, :]).reshape(-1)
    freq_idx = jnp.arange(HALF, dtype=F32)
    inverse = ROPE_BASE ** (-2.0 * freq_idx / head_dim)
    angles = positions.astype(F32)[:, None] * inverse[None, :]
    pad = ((0, 0), (0, HALF_LANES - HALF))
    cos_h, sin_h = jnp.pad(jnp.cos(angles), pad), jnp.pad(jnp.sin(angles), pad)
    cos_t = jnp.concatenate([cos_h, cos_h], 1)
    sin_t = jnp.concatenate([-sin_h, sin_h], 1)
    return cos_t, sin_t, positions[:, None], positions[None, :]


def body(
    ends_in, pair_table, norm_attn, w_query, w_key, w_value, w_out, norm_mlp, w_gate, w_up, w_down
):
    lay = Layout()
    both = tuple(range(lay.sections))
    is_first = lay.section_index == 0
    rows = ends_in.shape[3]
    width = ends_in.shape[4]
    row_block = w_query.shape[1]
    n_query = HEADS // lay.group
    n_key = max(1, KV_HEADS // lay.group)
    tables = group_tables(pair_table, rows // 2, lay, HEAD_DIM)

    local = ends_in[0, :, 0]
    local = jnp.concatenate(
        [pick(local, lay.half), lay.to_half(pick(local, 1 - lay.half), both)], 0
    )

    gains = jnp.stack([norm_attn[0], norm_mlp[0]])
    gains = place(
        gains, [lay.to_member(gains, both, step) for step in range(1, lay.group)], lay.member
    )
    gains = spread(gains, lay, both)
    gains = gains.transpose(3, 0, 1, 2, 4).reshape(2, width).astype(F32)

    qkv_parts = jnp.concatenate(
        [split_query(w_query[0], lay), split_key(w_key[0], lay), split_key(w_value[0], lay)], 2
    )
    ff_unit = lay.shards * w_down.shape[1]
    gate_up_parts = jnp.concatenate(
        [split_blocks(w_gate[0], lay, ff_unit), split_blocks(w_up[0], lay, ff_unit)], 2
    )
    spread_lanes = lane_matrix(n_query + 2 * n_key)
    spread_out = lane_matrix(n_query)

    def fetch(secs):
        qkv = spread(swap_columns(qkv_parts, lay, secs), lay, secs)
        if aligned(lay, row_block):
            out_w = spread(w_out, lay, secs).reshape(-1, width)
        else:
            out_w = lax.all_gather(w_out[0], ("ctx", "shard"), axis=0, tiled=True)
            out_w = pick(out_w.reshape(lay.group, -1, width), lay.member)
        gate_up = spread(swap_columns(gate_up_parts, lay, secs), lay, secs)
        down_w = spread(w_down, lay, secs)
        return qkv, out_w, gate_up, down_w

    fetched = [fetch((sec,)) for sec in both]
    qkv_w, out_w, gate_up_w, down_w = jax.tree.map(
        lambda a, b: jnp.where(is_first, a, b), fetched[0], fetched[1]
    )
    qkv_w = mm(qkv_w.reshape(width, -1), spread_lanes).astype(BF16)
    out_w = mm_tn(spread_out, out_w).astype(BF16)
    gate_up_w = gate_up_w.reshape(width, -1)
    down_w = down_w.reshape(-1, width)
    weights = (gains[0], gains[1], qkv_w, out_w, gate_up_w, down_w, n_query, n_key)

    first_out, first_kept = layer_forward(local.astype(F32), weights, tables, lay, (0,))
    second_in = lay.to_section(first_out.astype(BF16), 0).astype(F32)
    second_out, second_kept = layer_forward(second_in, weights, tables, lay, (1,))
    second_grad, second_gains, second_ops = layer_backward(
        local.astype(F32), second_kept, weights, tables, lay, (1,)
    )
    second_w = weight_grads(second_ops, lay, (1,), spread_out, spread_lanes, n_query, n_key)
    second_g = gain_sums(second_gains, lay, (1,))
    first_in = lay.to_section(second_grad.astype(BF16), 1).astype(F32)
    first_grad, first_gains, first_ops = layer_backward(
        first_in, first_kept, weights, tables, lay, (0,)
    )
    first_w = weight_grads(first_ops, lay, (0,), spread_out, spread_lanes, n_query, n_key)
    first_g = gain_sums(first_gains, lay, (0,))

    ends = jnp.where(is_first, first_grad.astype(BF16), second_out.astype(BF16))
    ends = ends.reshape(2, rows, width)
    other = lay.to_half(ends[1], both)
    ends = join_two(ends[0], other, lay.half, 0)[None, :, None]
    query_g, key_g, value_g, out_g, gate_g, up_g, down_g = (
        jnp.where(is_first, a, b)[None] for a, b in zip(first_w, second_w)
    )
    gain_g = jnp.where(is_first, first_g, second_g)
    return (
        ends,
        gain_g[0][None],
        query_g,
        key_g,
        value_g,
        out_g,
        gain_g[1][None],
        gate_g,
        up_g,
        down_g,
    )


def solution(mesh):
    rows = P("section", None, "shard", "ctx", None)
    vector = P("section", ("ctx", "shard"))
    matrix = P("section", ("ctx", "shard"), None)
    return jax.shard_map(
        body,
        mesh=mesh,
        in_specs=(rows, P(), vector, matrix, matrix, matrix, matrix, vector, matrix, matrix, matrix),
        out_specs=(rows, vector, matrix, matrix, matrix, matrix, vector, matrix, matrix, matrix),
        check_vma=False,
    )
```

time: 3580 us -> 966 us (0.27)
  waiting for transfers between devices: 2790 us -> 384 us
  blocking collectives: 246 us -> 0 us
  starting transfers between devices: 7.09 us -> 251 us
  matrix products: 325 us -> 86.1 us
    reduce_scatter x10 -> x0, waiting for transfers between devices: 1850 us -> none  [the longest x1 367 us: body(): lax.psum_scatter(mlp_total[2], ('ctx', 'shard'), scatter_dimension=1, til...]
    all_gather x7 -> x0, waiting for transfers between devices: 567 us -> none  [the longest x1 146 us: body(): lax.all_gather(w_up, ('ctx', 'shard'), axis=1, tiled=True)]
    ppermute x4 -> x123, waiting for transfers between devices: 2.71 us -> 384 us  [the longest x121 313 us: move(): return lax.ppermute(block, MESH_AXES, pairs)]
    unnamed x27 -> x0, waiting for transfers between devices: 361 us -> none
    ppermute x4 -> x123, starting transfers between devices: 5.99 us -> 251 us  [the longest x121 249 us: move(): return lax.ppermute(block, MESH_AXES, pairs)]
    dot_general x133 -> x26, matrix products: 325 us -> 86.1 us  [the longest x9 32.7 us: mm_tn(): lax.dot_general(a, b, (((0,), (0,)), ((), ())), preferred_element_type=F32)]
    all_gather x6 -> x0, blocking collectives: 202 us -> none  [the longest x3 101 us: layer_forward(): lax.all_gather(key_local, 'ctx', axis=0, tiled=True)]
    unnamed x1 -> x0, blocking collectives: 44.3 us -> none
  transfers between devices with their start and end apart: 26 -> 123, of which waited for: 25 -> 30; matrix products, arithmetic and copies ran while one was open for 7% -> 23% of each run, Pallas kernels for 0% -> 3%
where the time goes in v1:
time: 966 us; the launch traced here: 954 us
  waiting for transfers between devices  384 us (40%)
  starting transfers between devices  251 us (26%)
  local copies, waits for them, and re-layouts  122 us (13%)
  matrix products  86.1 us (9%)
  other arithmetic  76.2 us (8%)
  Pallas kernels  29.7 us (3%)
    ppermute x121, waiting for transfers between devices, move(): return lax.ppermute(block, MESH_AXES, pairs)  313 us
    ppermute x121, starting transfers between devices, move(): return lax.ppermute(block, MESH_AXES, pairs)  249 us
    ppermute x2, waiting for transfers between devices, to_section(): return lax.ppermute(block, MESH_AXES, pairs)  71.1 us
    dot_general x9, matrix products, mm_tn(): lax.dot_general(a, b, (((0,), (0,)), ((), ())), preferred_element_type=F32)  32.7 us
    unnamed x212, local copies, waits for them, and re-layouts  24.3 us
    select_n x13, local copies, waits for them, and re-layouts, body(): jnp.where(is_first, a, b)[None]  21 us
  transfers between devices with their start and end apart: 123, of which 30 were waited for; matrix products, arithmetic and copies ran while one was open for 23% of the time, Pallas kernels for 3%

profile of v1, /device:TPU:0, one launch (start us, length us, event | category | flops | bytes accessed | tf_op | source)
XLA Modules:
  0.0 953.6 jit_solution(10124822399405907853)
XLA Ops:
  7.0 4.8 collective-permute-start.9
  55.6 4.5 collective-permute-start.19
  71.3 7.9 collective-permute-done
  93.7 7.2 collective-permute-done.30
  102.9 5.2 collective-permute-done.31
  114.2 37.6 %collective-permute-done.12 = bf16[4,96,768]{2,1,0:T(8,128)(2,1)S(1)} collective-permute-done((bf16[4,96,768]{2,1,0:T(8,128)(2,1)S(1)}, bf16[4,96,768]{2,1,0:T(8,128)(2,1)S(1)}, u32[]{:S(2)}, u32[]{:S(2)}) %collective-permute-start.12) | collective-permute-done | bytes 589856 | tf_op jit(solution)/shard_map/ppermute | solution.py:45
  161.2 7.5 collective-permute-done.20
  175.0 18.7 %collective-permute-done.13 = bf16[2,4,96,768]{3,2,1,0:T(8,128)(2,1)S(1)} collective-permute-done((bf16[2,4,96,768]{3,2,1,0:T(8,128)(2,1)S(1)}, bf16[2,4,96,768]{3,2,1,0:T(8,128)(2,1)S(1)}, u32[]{:S(2)}, u32[]{:S(2)}) %collective-permute-start.13) | collective-permute-done | bytes 1179680 | tf_op jit(solution)/shard_map/ppermute | solution.py:45
  206.5 7.5 attend.2
  216.1 7.0 collective-permute-start.25
  231.2 29.8 %collective-permute-done.32 = bf16[4,96,2048]{2,1,0:T(8,128)(2,1)} collective-permute-done((bf16[4,96,2048]{2,1,0:T(8,128)(2,1)S(1)}, bf16[4,96,2048]{2,1,0:T(8,128)(2,1)}, u32[]{:S(2)}, u32[]{:S(2)}) %collective-permute-start.32) | collective-permute-done | bytes 1572896 | tf_op jit(solution)/shard_map/ppermute | solution.py:45
  278.5 25.6 %collective-permute-done.40 = bf16[2,1,256,1536]{3,2,0,1:T(8,128)(2,1)S(1)} collective-permute-done((bf16[2,1,256,1536]{3,2,0,1:T(8,128)(2,1)S(1)}, bf16[2,1,256,1536]{3,2,0,1:T(8,128)(2,1)S(1)}, u32[]{:S(2)}, u32[]{:S(2)}) %collective-permute-start.40) | collective-permute-done | bytes 1572896 | tf_op jit(solution)/shard_map/ppermute | solution.py:45
  307.6 41.0 %collective-permute-done.33 = bf16[2,4,96,2048]{3,2,1,0:T(8,128)(2,1)S(1)} collective-permute-done((bf16[2,4,96,2048]{3,2,1,0:T(8,128)(2,1)S(1)}, bf16[2,4,96,2048]{3,2,1,0:T(8,128)(2,1)S(1)}, u32[]{:S(2)}, u32[]{:S(2)}) %collective-permute-start.33) | collective-permute-done | bytes 3145760 | tf_op jit(solution)/shard_map/ppermute | solution.py:45
  382.8 5.4 fusion.86.refs_0_.refs_1_.refs_2_
  388.2 7.6 attend.3
  436.9 4.5 copy-done.9
  448.4 7.3 attend_back.2
  467.8 6.4 fusion.22
  501.1 69.8 %collective-permute-done.68 = bf16[128,1536]{1,0:T(8,128)(2,1)S(1)} collective-permute-done((bf16[128,1536]{1,0:T(8,128)(2,1)S(1)}, bf16[128,1536]{1,0:T(8,128)(2,1)S(1)}, u32[]{:S(2)}, u32[]{:S(2)}) %collective-permute-start.68) | collective-permute-done | bytes 393248 | tf_op jit(solution)/shard_map/ppermute | solution.py:64
  635.2 7.3 attend_back.3
  659.9 6.4 fusion.23
  686.3 4.8 bitcast_add_fusion
  691.2 5.0 collective-permute-start.86
  697.7 11.1 %collective-permute-done.86 = f32[4,2,96]{2,0,1:T(4,128)S(1)} collective-permute-done((f32[4,2,96]{2,0,1:T(4,128)S(1)}, f32[4,2,96]{2,0,1:T(4,128)S(1)}, u32[]{:S(2)}, u32[]{:S(2)}) %collective-permute-start.86) | collective-permute-done | bytes 3104 | tf_op jit(solution)/shard_map/ppermute | solution.py:45
  734.1 7.5 collective-permute-done.84
  745.9 37.4 %collective-permute-done.119 = bf16[2,1,256,1536]{3,2,1,0:T(8,128)(2,1)S(1)} collective-permute-done((bf16[2,1,256,1536]{3,2,1,0:T(8,128)(2,1)S(1)}, bf16[2,1,256,1536]{3,2,1,0:T(8,128)(2,1)S(1)}, u32[]{:S(2)}, u32[]{:S(2)}) %collective-permute-start.119) | collective-permute-done | bytes 1572896 | tf_op jit(solution)/shard_map/ppermute | solution.py:45
  787.2 4.4 collective-permute-start.120
  791.6 15.6 %collective-permute-done.106 = bf16[1,96,1536]{2,1,0:T(8,128)(2,1)S(1)} collective-permute-done((bf16[1,96,1536]{2,1,0:T(8,128)(2,1)S(1)}, bf16[1,96,1536]{2,1,0:T(8,128)(2,1)S(1)}, u32[]{:S(2)}, u32[]{:S(2)}) %collective-permute-start.106) | collective-permute-done | bytes 294944 | tf_op jit(solution)/shard_map/ppermute | solution.py:45
  834.9 9.4 collective-permute-done.96
  855.9 5.0 collective-permute-start.99
  872.3 4.7 bitcast_add_fusion.1
  899.8 21.7 %collective-permute-done.110 = bf16[4,96,2048]{2,1,0:T(8,128)(2,1)} collective-permute-done((bf16[4,96,2048]{2,1,0:T(8,128)(2,1)}, bf16[4,96,2048]{2,1,0:T(8,128)(2,1)}, u32[]{:S(2)}, u32[]{:S(2)}) %collective-permute-start.110) | collective-permute-done | bytes 1572896 | tf_op jit(solution)/shard_map/ppermute | solution.py:45
  (686 shorter events, 503.6 us)
Async XLA Ops:
  5.7 44.9 %collective-permute-start.14 = (bf16[96,768]{1,0:T(8,128)(2,1)}, bf16[96,768]{1,0:T(8,128)(2,1)}, u32[]{:S(2)}, u32[]{:S(2)}) collective-permute-start(bf16[96,768]{1,0:T(8,128)(2,1)} %get-tuple-element.203), channel_id=1, source_target_pairs={{16,18},{17,19},{18,16},{19,17},{20,22},{21,23},{22,20},{23,21},{2... | collective-permute-start | bytes 442376 | tf_op jit(solution)/shard_map/ppermute | solution.py:45
  7.0 48.6 %collective-permute-start.9 = (bf16[96,768]{1,0:T(8,128)(2,1)}, bf16[96,768]{1,0:T(8,128)(2,1)}, u32[]{:S(2)}, u32[]{:S(2)}) collective-permute-start(bf16[96,768]{1,0:T(8,128)(2,1)} %get-tuple-element.203), channel_id=1, source_target_pairs={{0,2},{1,3},{2,0},{3,1},{4,6},{5,7},{6,4},{7,5},{8,10},{9,11},{10,... | collective-permute-start | bytes 442376 | tf_op jit(solution)/shard_map/ppermute | solution.py:45
  11.8 49.9 %collective-permute-start.15 = (bf16[96,768]{1,0:T(8,128)(2,1)}, bf16[96,768]{1,0:T(8,128)(2,1)}, u32[]{:S(2)}, u32[]{:S(2)}) collective-permute-start(bf16[96,768]{1,0:T(8,128)(2,1)} %get-tuple-element.202), channel_id=1, source_target_pairs={{16,20},{17,21},{18,22},{19,23},{20,16},{21,17},{22,18},{23,19},{2... | collective-permute-start | bytes 442376 | tf_op jit(solution)/shard_map/ppermute | solution.py:45
  13.2 53.1 %collective-permute-start.10 = (bf16[96,768]{1,0:T(8,128)(2,1)}, bf16[96,768]{1,0:T(8,128)(2,1)}, u32[]{:S(2)}, u32[]{:S(2)}) collective-permute-start(bf16[96,768]{1,0:T(8,128)(2,1)} %get-tuple-element.202), channel_id=1, source_target_pairs={{0,4},{1,5},{2,6},{3,7},{4,0},{5,1},{6,2},{7,3},{8,12},{9,13},{10,... | collective-permute-start | bytes 442376 | tf_op jit(solution)/shard_map/ppermute | solution.py:45
  88.9 65.6 %collective-permute-start.39 = (bf16[1,256,1536]{2,1,0:T(8,128)(2,1)S(1)}, bf16[1,256,1536]{2,1,0:T(8,128)(2,1)S(1)}, u32[]{:S(2)}, u32[]{:S(2)}) collective-permute-start(bf16[1,256,1536]{2,1,0:T(8,128)(2,1)S(1)} %copy-done.37), channel_id=1, source_target_pairs={{0,8},{1,9},{2,10},{3,11},{4,12},{5,13},{6,14},{7,15},{8,0},{9,1},... | collective-permute-start | bytes 2359304 | tf_op jit(solution)/shard_map/ppermute | solution.py:45
  91.7 63.5 %collective-permute-start.41 = (bf16[1,256,1536]{2,1,0:T(8,128)(2,1)S(1)}, bf16[1,256,1536]{2,1,0:T(8,128)(2,1)S(1)}, u32[]{:S(2)}, u32[]{:S(2)}) collective-permute-start(bf16[1,256,1536]{2,1,0:T(8,128)(2,1)S(1)} %copy-done.37), channel_id=1, source_target_pairs={{16,24},{17,25},{18,26},{19,27},{20,28},{21,29},{22,30},{23,31},{2... | collective-permute-start | bytes 2359304 | tf_op jit(solution)/shard_map/ppermute | solution.py:45
  101.0 50.8 %collective-permute-start.12 = (bf16[4,96,768]{2,1,0:T(8,128)(2,1)S(1)}, bf16[4,96,768]{2,1,0:T(8,128)(2,1)S(1)}, u32[]{:S(2)}, u32[]{:S(2)}) collective-permute-start(bf16[4,96,768]{2,1,0:T(8,128)(2,1)S(1)} %copy-done.27), channel_id=1, source_target_pairs={{0,8},{1,9},{2,10},{3,11},{4,12},{5,13},{6,14},{7,15},{8,0},{9,1},... | collective-permute-start | bytes 1769480 | tf_op jit(solution)/shard_map/ppermute | solution.py:45
  108.1 91.5 %collective-permute-start.8 = (bf16[128,1536]{1,0:T(8,128)(2,1)S(1)}, bf16[128,1536]{1,0:T(8,128)(2,1)S(1)}, u32[]{:S(2)}, u32[]{:S(2)}) collective-permute-start(bf16[128,1536]{1,0:T(8,128)(2,1)S(1)} %fusion.38), channel_id=1, source_target_pairs={{0,6},{1,7},{2,4},{3,5},{4,2},{5,3},{6,0},{7,1},{8,14},{9,15},{10,... | collective-permute-start | bytes 1179656 | tf_op jit(solution)/shard_map/ppermute | solution.py:45
  110.1 91.8 %collective-permute-start.7 = (bf16[128,1536]{1,0:T(8,128)(2,1)S(1)}, bf16[128,1536]{1,0:T(8,128)(2,1)S(1)}, u32[]{:S(2)}, u32[]{:S(2)}) collective-permute-start(bf16[128,1536]{1,0:T(8,128)(2,1)S(1)} %fusion.38), channel_id=1, source_target_pairs={{0,4},{1,5},{2,6},{3,7},{4,0},{5,1},{6,2},{7,3},{8,12},{9,13},{10,... | collective-permute-start | bytes 1179656 | tf_op jit(solution)/shard_map/ppermute | solution.py:45
  151.8 50.1 %collective-permute-start.6 = (bf16[128,1536]{1,0:T(8,128)(2,1)S(1)}, bf16[128,1536]{1,0:T(8,128)(2,1)S(1)}, u32[]{:S(2)}, u32[]{:S(2)}) collective-permute-start(bf16[128,1536]{1,0:T(8,128)(2,1)S(1)} %fusion.38), channel_id=1, source_target_pairs={{0,2},{1,3},{2,0},{3,1},{4,6},{5,7},{6,4},{7,5},{8,10},{9,11},{10,... | collective-permute-start | bytes 1179656 | tf_op jit(solution)/shard_map/ppermute | solution.py:45
  173.0 52.9 %collective-permute-start.37 = (bf16[4,96,2048]{2,1,0:T(8,128)(2,1)S(1)}, bf16[4,96,2048]{2,1,0:T(8,128)(2,1)}, u32[]{:S(2)}, u32[]{:S(2)}) collective-permute-start(bf16[4,96,2048]{2,1,0:T(8,128)(2,1)S(1)} %bitcast_dynamic-update-slice_fusion), channel_id=1, source_target_pairs={{16,24},{17,25},{18,26},{19,27},{20,28},{21,29},{22,30},{23,31},{2... | collective-permute-start | bytes 4718600 | tf_op jit(solution)/shard_map/ppermute | solution.py:45
  193.7 67.3 %collective-permute-start.32 = (bf16[4,96,2048]{2,1,0:T(8,128)(2,1)S(1)}, bf16[4,96,2048]{2,1,0:T(8,128)(2,1)}, u32[]{:S(2)}, u32[]{:S(2)}) collective-permute-start(bf16[4,96,2048]{2,1,0:T(8,128)(2,1)S(1)} %bitcast_dynamic-update-slice_fusion.3), channel_id=1, source_target_pairs={{0,8},{1,9},{2,10},{3,11},{4,12},{5,13},{6,14},{7,15},{8,0},{9,1},... | collective-permute-start | bytes 4718600 | tf_op jit(solution)/shard_map/ppermute | solution.py:45
  199.6 74.3 %collective-permute-start.42 = (bf16[2,1,256,1536]{3,2,0,1:T(8,128)(2,1)}, bf16[2,1,256,1536]{3,2,0,1:T(8,128)(2,1)}, u32[]{:S(2)}, u32[]{:S(2)}) collective-permute-start(bf16[2,1,256,1536]{3,2,0,1:T(8,128)(2,1)} %pad_maximum_fusion.10), channel_id=1, source_target_pairs={{16,17},{17,16},{18,19},{19,18},{20,21},{21,20},{22,23},{23,22},{2... | collective-permute-start | bytes 4718600 | tf_op jit(solution)/shard_map/ppermute | solution.py:45
  216.1 47.7 %collective-permute-start.25 = (bf16[128,1536]{1,0:T(8,128)(2,1)S(1)}, bf16[128,1536]{1,0:T(8,128)(2,1)S(1)}, u32[]{:S(2)}, u32[]{:S(2)}) collective-permute-start(bf16[128,1536]{1,0:T(8,128)(2,1)S(1)} %get-tuple-element.183), channel_id=1, source_target_pairs={{0,6},{1,7},{2,4},{3,5},{4,2},{5,3},{6,0},{7,1},{8,14},{9,15},{10,... | collective-permute-start | bytes 1179656 | tf_op jit(solution)/shard_map/ppermute | solution.py:45
  223.1 44.2 %collective-permute-start.24 = (bf16[128,1536]{1,0:T(8,128)(2,1)S(1)}, bf16[128,1536]{1,0:T(8,128)(2,1)S(1)}, u32[]{:S(2)}, u32[]{:S(2)}) collective-permute-start(bf16[128,1536]{1,0:T(8,128)(2,1)S(1)} %get-tuple-element.184), channel_id=1, source_target_pairs={{0,4},{1,5},{2,6},{3,7},{4,0},{5,1},{6,2},{7,3},{8,12},{9,13},{10,... | collective-permute-start | bytes 1179656 | tf_op jit(solution)/shard_map/ppermute | solution.py:45
  225.9 45.1 %collective-permute-start.23 = (bf16[128,1536]{1,0:T(8,128)(2,1)S(1)}, bf16[128,1536]{1,0:T(8,128)(2,1)S(1)}, u32[]{:S(2)}, u32[]{:S(2)}) collective-permute-start(bf16[128,1536]{1,0:T(8,128)(2,1)S(1)} %get-tuple-element.182), channel_id=1, source_target_pairs={{0,2},{1,3},{2,0},{3,1},{4,6},{5,7},{6,4},{7,5},{8,10},{9,11},{10,... | collective-permute-start | bytes 1179656 | tf_op jit(solution)/shard_map/ppermute | solution.py:45
  261.0 46.1 %collective-permute-start.38 = (bf16[2,4,96,2048]{3,2,1,0:T(8,128)(2,1)S(1)}, bf16[2,4,96,2048]{3,2,1,0:T(8,128)(2,1)S(1)}, u32[]{:S(2)}, u32[]{:S(2)}) collective-permute-start(bf16[2,4,96,2048]{3,2,1,0:T(8,128)(2,1)S(1)} %pad_maximum_fusion.2), channel_id=1, source_target_pairs={{16,17},{17,16},{18,19},{19,18},{20,21},{21,20},{22,23},{23,22},{2... | collective-permute-start | bytes 9437192 | tf_op jit(solution)/shard_map/ppermute | solution.py:45
  267.3 81.3 %collective-permute-start.33 = (bf16[2,4,96,2048]{3,2,1,0:T(8,128)(2,1)S(1)}, bf16[2,4,96,2048]{3,2,1,0:T(8,128)(2,1)S(1)}, u32[]{:S(2)}, u32[]{:S(2)}) collective-permute-start(bf16[2,4,96,2048]{3,2,1,0:T(8,128)(2,1)S(1)} %pad_maximum_fusion.1), channel_id=1, source_target_pairs={{0,1},{1,0},{2,3},{3,2},{4,5},{5,4},{6,7},{7,6},{8,9},{9,8},{10,11... | collective-permute-start | bytes 9437192 | tf_op jit(solution)/shard_map/ppermute | solution.py:45
  272.0 79.7 %collective-permute-start.28 = (bf16[128,1536]{1,0:T(8,128)(2,1)S(1)}, bf16[128,1536]{1,0:T(8,128)(2,1)S(1)}, u32[]{:S(2)}, u32[]{:S(2)}) collective-permute-start(bf16[128,1536]{1,0:T(8,128)(2,1)S(1)} %multiply_convert_fusion.7), channel_id=1, source_target_pairs={{0,6},{1,7},{2,4},{3,5},{4,2},{5,3},{6,0},{7,1},{8,14},{9,15},{10,... | collective-permute-start | bytes 1179656 | tf_op jit(solution)/shard_map/ppermute | solution.py:45
  273.9 77.7 %collective-permute-start.27 = (bf16[128,1536]{1,0:T(8,128)(2,1)S(1)}, bf16[128,1536]{1,0:T(8,128)(2,1)S(1)}, u32[]{:S(2)}, u32[]{:S(2)}) collective-permute-start(bf16[128,1536]{1,0:T(8,128)(2,1)S(1)} %multiply_convert_fusion.7), channel_id=1, source_target_pairs={{0,4},{1,5},{2,6},{3,7},{4,0},{5,1},{6,2},{7,3},{8,12},{9,13},{10,... | collective-permute-start | bytes 1179656 | tf_op jit(solution)/shard_map/ppermute | solution.py:45
  304.1 47.6 %collective-permute-start.26 = (bf16[128,1536]{1,0:T(8,128)(2,1)S(1)}, bf16[128,1536]{1,0:T(8,128)(2,1)S(1)}, u32[]{:S(2)}, u32[]{:S(2)}) collective-permute-start(bf16[128,1536]{1,0:T(8,128)(2,1)S(1)} %multiply_convert_fusion.7), channel_id=1, source_target_pairs={{0,2},{1,3},{2,0},{3,1},{4,6},{5,7},{6,4},{7,5},{8,10},{9,11},{10,... | collective-permute-start | bytes 1179656 | tf_op jit(solution)/shard_map/ppermute | solution.py:45
  422.3 287.9 %collective-permute-start.83 = (bf16[128,1536]{1,0:T(8,128)(2,1)}, bf16[128,1536]{1,0:T(8,128)(2,1)}, u32[]{:S(2)}, u32[]{:S(2)}) collective-permute-start(bf16[128,1536]{1,0:T(8,128)(2,1)} %get-tuple-element.166), channel_id=1, source_target_pairs={{16,22},{17,23},{18,20},{19,21},{20,18},{21,19},{22,16},{23,17},{2... | collective-permute-start | bytes 1179656 | tf_op jit(solution)/shard_map/ppermute | solution.py:45
  425.6 70.9 %collective-permute-start.121 = (bf16[2,1,256,1536]{3,2,1,0:T(8,128)(2,1)}, bf16[2,1,256,1536]{3,2,1,0:T(8,128)(2,1)}, u32[]{:S(2)}, u32[]{:S(2)}) collective-permute-start(bf16[2,1,256,1536]{3,2,1,0:T(8,128)(2,1)} %fusion.7), channel_id=1, source_target_pairs={{16,17},{17,16},{18,19},{19,18},{20,21},{21,20},{22,23},{23,22},{2... | collective-permute-start | bytes 4718600 | tf_op jit(solution)/shard_map/ppermute | solution.py:45
  483.2 97.0 %collective-permute-start.100 = (bf16[2,4,96,768]{3,2,1,0:T(8,128)(2,1)}, bf16[2,4,96,768]{3,2,1,0:T(8,128)(2,1)}, u32[]{:S(2)}, u32[]{:S(2)}) collective-permute-start(bf16[2,4,96,768]{3,2,1,0:T(8,128)(2,1)} %fusion.21), channel_id=1, source_target_pairs={{16,17},{17,16},{18,19},{19,18},{20,21},{21,20},{22,23},{23,22},{2... | collective-permute-start | bytes 3538952 | tf_op jit(solution)/shard_map/ppermute | solution.py:45
  492.2 78.7 %collective-permute-start.68 = (bf16[128,1536]{1,0:T(8,128)(2,1)S(1)}, bf16[128,1536]{1,0:T(8,128)(2,1)S(1)}, u32[]{:S(2)}, u32[]{:S(2)}) collective-permute-start(bf16[128,1536]{1,0:T(8,128)(2,1)S(1)} %fusion.32), channel_id=1, source_target_pairs={{16,0},{17,1},{18,2},{19,3},{20,4},{21,5},{22,6},{23,7},{24,8},{25... | collective-permute-start | bytes 1179656 | tf_op jit(solution)/shard_map/ppermute | solution.py:64
  627.4 58.9 %collective-permute-start.114 = (bf16[2,4,96,2048]{3,2,1,0:T(8,128)(2,1)}, bf16[2,4,96,2048]{3,2,1,0:T(8,128)(2,1)}, u32[]{:S(2)}, u32[]{:S(2)}) collective-permute-start(bf16[2,4,96,2048]{3,2,1,0:T(8,128)(2,1)} %fusion.1), channel_id=1, source_target_pairs={{16,17},{17,16},{18,19},{19,18},{20,21},{21,20},{22,23},{23,22},{2... | collective-permute-start | bytes 9437192 | tf_op jit(solution)/shard_map/ppermute | solution.py:45
  724.7 62.4 %collective-permute-start.108 = (bf16[1,96,1536]{2,1,0:T(8,128)(2,1)S(1)}, bf16[1,96,1536]{2,1,0:T(8,128)(2,1)S(1)}, u32[]{:S(2)}, u32[]{:S(2)}) collective-permute-start(bf16[1,96,1536]{2,1,0:T(8,128)(2,1)S(1)} %copy-done.48), channel_id=1, source_target_pairs={{16,24},{17,25},{18,26},{19,27},{20,28},{21,29},{22,30},{23,31},{2... | collective-permute-start | bytes 884744 | tf_op jit(solution)/shard_map/ppermute | solution.py:45
  725.6 125.5 %collective-permute-start.122 = (bf16[1,256,1536]{2,1,0:T(8,128)(2,1)}, bf16[1,256,1536]{2,1,0:T(8,128)(2,1)}, u32[]{:S(2)}, u32[]{:S(2)}) collective-permute-start(bf16[1,256,1536]{2,1,0:T(8,128)(2,1)} %fusion.25), channel_id=1, source_target_pairs={{16,24},{17,25},{18,26},{19,27},{20,28},{21,29},{22,30},{23,31},{2... | collective-permute-start | bytes 2359304 | tf_op jit(solution)/shard_map/ppermute | solution.py:45
  727.1 145.2 %collective-permute-start.109 = (bf16[2,4,96,2048]{3,2,1,0:T(8,128)(2,1)}, bf16[2,4,96,2048]{3,2,1,0:T(8,128)(2,1)}, u32[]{:S(2)}, u32[]{:S(2)}) collective-permute-start(bf16[2,4,96,2048]{3,2,1,0:T(8,128)(2,1)} %fusion), channel_id=1, source_target_pairs={{0,1},{1,0},{2,3},{3,2},{4,5},{5,4},{6,7},{7,6},{8,9},{9,8},{10,11... | collective-permute-start | bytes 9437192 | tf_op jit(solution)/shard_map/ppermute | solution.py:45
  730.6 52.8 %collective-permute-start.119 = (bf16[2,1,256,1536]{3,2,1,0:T(8,128)(2,1)S(1)}, bf16[2,1,256,1536]{3,2,1,0:T(8,128)(2,1)S(1)}, u32[]{:S(2)}, u32[]{:S(2)}) collective-permute-start(bf16[2,1,256,1536]{3,2,1,0:T(8,128)(2,1)S(1)} %copy-done.29), channel_id=1, source_target_pairs={{0,1},{1,0},{2,3},{3,2},{4,5},{5,4},{6,7},{7,6},{8,9},{9,8},{10,11... | collective-permute-start | bytes 4718600 | tf_op jit(solution)/shard_map/ppermute | solution.py:45
  741.7 66.5 %collective-permute-start.95 = (bf16[2,4,96,768]{3,2,1,0:T(8,128)(2,1)S(1)}, bf16[2,4,96,768]{3,2,1,0:T(8,128)(2,1)S(1)}, u32[]{:S(2)}, u32[]{:S(2)}) collective-permute-start(bf16[2,4,96,768]{3,2,1,0:T(8,128)(2,1)S(1)} %copy-done.33), channel_id=1, source_target_pairs={{0,1},{1,0},{2,3},{3,2},{4,5},{5,4},{6,7},{7,6},{8,9},{9,8},{10,11... | collective-permute-start | bytes 3538952 | tf_op jit(solution)/shard_map/ppermute | solution.py:45
  787.2 63.9 %collective-permute-start.120 = (bf16[1,256,1536]{2,1,0:T(8,128)(2,1)}, bf16[1,256,1536]{2,1,0:T(8,128)(2,1)}, u32[]{:S(2)}, u32[]{:S(2)}) collective-permute-start(bf16[1,256,1536]{2,1,0:T(8,128)(2,1)} %fusion.24), channel_id=1, source_target_pairs={{0,8},{1,9},{2,10},{3,11},{4,12},{5,13},{6,14},{7,15},{8,0},{9,1},... | collective-permute-start | bytes 2359304 | tf_op jit(solution)/shard_map/ppermute | solution.py:45
  (189 other events, 2964.6 us)

commit v2 on v1

v2 whole, which is shorter than its diff:
```python
import jax
import jax.numpy as jnp
from jax import lax
from jax.experimental import pallas as pl
from jax.experimental.pallas import tpu as pltpu
from jax.sharding import PartitionSpec as P

HEADS = 16
KV_HEADS = 8
HEAD_DIM = 96
HALF = HEAD_DIM // 2
LANES = 128
HALF_LANES = LANES // 2

NORM_EPS = 1e-05
ROPE_BASE = 100000.0
MASK_FILL = -1e30

MESH_AXES = ("section", "ctx", "shard")
F32 = jnp.float32
BF16 = jnp.bfloat16
VMEM_LIMIT = pltpu.CompilerParams(vmem_limit_bytes=56 * 1024 * 1024)


class Layout:
    def __init__(self):
        self.cores = lax.axis_size("section")
        self.ctx = lax.axis_size("ctx")
        self.shards = lax.axis_size("shard")
        self.halves = 2
        self.group = self.ctx // self.halves
        ctx_index = lax.axis_index("ctx")
        self.core = lax.axis_index("section")
        self.half = ctx_index // self.group
        self.member = ctx_index % self.group
        self.shard = lax.axis_index("shard")

    def move(self, block, target):
        pairs = []
        for core in range(self.cores):
            for half in range(self.halves):
                for member in range(self.group):
                    for shard in range(self.shards):
                        to = target(core, half, member, shard)
                        pairs.append((self.flat(core, half, member, shard), self.flat(*to)))
        return lax.ppermute(block, MESH_AXES, pairs)

    def move_some(self, block, sends, target):
        pairs = []
        for core in range(self.cores):
            for half in range(self.halves):
                for member in range(self.group):
                    for shard in range(self.shards):
                        if sends(core, half, member, shard):
                            to = target(core, half, member, shard)
                            pairs.append((self.flat(core, half, member, shard), self.flat(*to)))
        return lax.ppermute(block, MESH_AXES, pairs)

    def flat(self, core, half, member, shard):
        return (core * self.ctx + half * self.group + member) * self.shards + shard

    def to_member(self, block, step):
        return self.move(block, lambda core, half, member, shard: (core, half, member ^ step, shard))

    def to_half(self, block):
        return self.move(block, lambda core, half, member, shard: (core, 1 - half, member, shard))

    def to_shard(self, block):
        return self.move(block, lambda core, half, member, shard: (core, half, member, 1 - shard))

    def to_core(self, block):
        return self.move(block, lambda core, half, member, shard: (1 - core, half, member, shard))


def pick(parts, index):
    return lax.dynamic_index_in_dim(parts, index, 0, False)


def after(block, *earlier):
    return lax.optimization_barrier((block,) + earlier)[0] if earlier else block


class Wire:
    def __init__(self, move):
        self.move = move
        self.last = ()

    def send(self, block, deps=(), move=None, beside=False):
        block = after(block, *(() if beside else self.last), *deps)
        got = (move or self.move)(block)
        self.last = self.last + (got,) if beside else (got,)
        return got, block


def two_way(index, own, other, axis):
    first = jnp.where(index == 0, own, other)
    second = jnp.where(index == 0, other, own)
    return jnp.stack([first, second], axis)


def rearrange_kernel(plans, count, *refs):
    sources, outs = refs[:count], refs[count:]
    for out, plan in zip(outs, plans):
        for index, pieces in plan:
            blocks = [
                sources[source][place + (slice(None), slice(column, column + width))]
                for source, place, column, width in pieces
            ]
            out[index] = jnp.concatenate(blocks, 1) if len(blocks) > 1 else blocks[0]


def rearrange(sources, shapes, plans):
    dtype = sources[0].dtype
    moved = sum(source.size for source in sources) * dtype.itemsize
    return pl.pallas_call(
        lambda *refs: rearrange_kernel(plans, len(sources), *refs),
        out_shape=[jax.ShapeDtypeStruct(shape, dtype) for shape in shapes],
        compiler_params=VMEM_LIMIT,
        cost_estimate=pl.CostEstimate(flops=0, bytes_accessed=2 * moved, transcendentals=0),
        name="rearrange",
    )(*sources)


def kernel_width(width):
    return width % HEAD_DIM == 0 or width % LANES == 0


def to_inner(block, lay, inner=True):
    blocks = lay.shards * lay.halves * lay.group
    width = block.shape[-1] // blocks
    outer_order = [
        ((half * lay.group + member) * lay.shards + shard) * width
        for shard in range(lay.shards)
        for half in range(lay.halves)
        for member in range(lay.group)
    ]
    if kernel_width(width):
        columns = outer_order
        if not inner:
            columns = [outer_order.index(i * width) * width for i in range(blocks)]
        flat = block.reshape(-1, block.shape[-1])
        plan = [((slice(None), slice(None)), [(0, (), column, width) for column in columns])]
        return rearrange([flat], [flat.shape], [plan])[0].reshape(block.shape)
    if inner:
        parts = block.reshape(block.shape[:-1] + (lay.halves, lay.group, lay.shards, -1))
        return jnp.moveaxis(parts, -2, -4).reshape(block.shape)
    parts = block.reshape(block.shape[:-1] + (lay.shards, lay.halves, lay.group, -1))
    return jnp.moveaxis(parts, -4, -2).reshape(block.shape)


def to_outer(block, lay):
    return to_inner(block, lay, False)


def relative(block, lay):
    width = block.shape[-1] // 4
    parts = [block[..., i * width : (i + 1) * width] for i in range(4)]
    parts = [jnp.where(lay.half == 0, parts[i], parts[i ^ 1]) for i in range(4)]
    parts = [jnp.where(lay.shard == 0, parts[i], parts[i ^ 2]) for i in range(4)]
    return jnp.concatenate(parts, -1)


def head_copies(lay):
    return max(1, lay.cores * lay.group // HEADS)


def split_heads(weight, lay, heads):
    rows = weight.shape[0]
    pairs = lay.cores * lay.group
    distinct = min(pairs, heads)
    parts = weight.reshape(rows, distinct, -1).transpose(1, 0, 2)
    parts = jnp.repeat(parts, pairs // distinct, axis=0) if pairs > distinct else parts
    return parts.reshape((lay.cores, lay.group) + parts.shape[1:])


def merge_heads(parts, lay, heads):
    pairs = lay.cores * lay.group
    distinct = min(pairs, heads)
    rows = parts.shape[2]
    parts = parts.reshape(distinct, pairs // distinct, rows, -1)
    parts = jnp.sum(parts, 1) if pairs > distinct else parts[:, 0]
    return parts.transpose(1, 0, 2).reshape(rows, -1)


def split_ff(weight, lay, unit):
    rows = weight.shape[0]
    parts = weight.reshape(rows, lay.halves, lay.group, lay.shards, lay.cores, unit)
    return parts.transpose(4, 2, 0, 3, 1, 5).reshape(lay.cores, lay.group, rows, -1)


def merge_ff(parts, lay, unit):
    rows = parts.shape[2]
    parts = parts.reshape(lay.cores, lay.group, rows, lay.shards, lay.halves, unit)
    return parts.transpose(2, 4, 1, 3, 0, 5).reshape(rows, -1)


def pack_heads(query, key, value, lay):
    pairs = lay.cores * lay.group
    if pairs != KV_HEADS or query.shape[0] % 16:
        sides = [(query, HEADS), (key, KV_HEADS), (value, KV_HEADS)]
        return jnp.concatenate([split_heads(block, lay, heads) for block, heads in sides], -1)
    wide, slim = query.shape[1] // pairs, key.shape[1] // pairs
    plan = []
    for pair in range(pairs):
        pieces = [(0, (), pair * wide, wide), (1, (), pair * slim, slim), (2, (), pair * slim, slim)]
        plan.append(((pair // lay.group, pair % lay.group), pieces))
    shape = (lay.cores, lay.group, query.shape[0], wide + 2 * slim)
    return rearrange([query, key, value], [shape], [plan])[0]


def unpack_heads(parts, lay):
    pairs = lay.cores * lay.group
    q_cols = max(1, HEADS // pairs) * HEAD_DIM
    k_cols = max(1, KV_HEADS // pairs) * HEAD_DIM
    if pairs != KV_HEADS:
        sides = [(0, q_cols, HEADS), (q_cols, k_cols, KV_HEADS), (q_cols + k_cols, k_cols, KV_HEADS)]
        return [merge_heads(parts[..., at : at + cols], lay, heads) for at, cols, heads in sides]
    rows = parts.shape[2]
    plans, shapes = [], []
    for first, cols in ((0, q_cols), (q_cols, k_cols), (q_cols + k_cols, k_cols)):
        pieces = [(0, (pair // lay.group, pair % lay.group), first, cols) for pair in range(pairs)]
        plans.append([((slice(None), slice(None)), pieces)])
        shapes.append((rows, pairs * cols))
    return rearrange([parts], shapes, plans)


def ff_columns(lay, core, member, unit):
    for shard in range(lay.shards):
        for half in range(lay.halves):
            block = (half * lay.group + member) * lay.shards + shard
            yield (block * lay.cores + core) * unit, shard * lay.halves + half


def pack_ff(gate, up, lay, unit):
    if not kernel_width(unit):
        return jnp.concatenate([split_ff(gate, lay, unit), split_ff(up, lay, unit)], -1)
    plan = []
    for core in range(lay.cores):
        for member in range(lay.group):
            columns = [column for column, _ in ff_columns(lay, core, member, unit)]
            pieces = [(side, (), column, unit) for side in (0, 1) for column in columns]
            plan.append(((core, member), pieces))
    shape = (lay.cores, lay.group, gate.shape[0], 8 * unit)
    return rearrange([gate, up], [shape], [plan])[0]


def unpack_ff(parts, lay, unit):
    ff = 4 * unit
    if not kernel_width(unit):
        return [merge_ff(parts[..., :ff], lay, unit), merge_ff(parts[..., ff:], lay, unit)]
    rows = parts.shape[2]
    plans = []
    for side in (0, 1):
        found = {}
        for core in range(lay.cores):
            for member in range(lay.group):
                for column, place in ff_columns(lay, core, member, unit):
                    found[column] = (0, (core, member), side * ff + place * unit, unit)
        pieces = [found[column] for column in sorted(found)]
        plans.append([((slice(None), slice(None)), pieces)])
    return rearrange([parts], [(rows, len(found) * unit)] * 2, plans)


def place(own, others, member):
    group = 1 + len(others)
    stacked = jnp.zeros((group,) + own.shape, own.dtype)
    for step, block in enumerate((own,) + tuple(others)):
        stacked = lax.dynamic_update_index_in_dim(stacked, block, member ^ step, 0)
    return stacked


def split_cores(parts, lay, deps=()):
    kept = pick(parts, lay.core)
    other = lay.to_core(after(pick(parts, 1 - lay.core), *deps))
    return jnp.where(lay.core == 0, kept, other), jnp.where(lay.core == 0, other, kept)


def swap_columns(parts, lay, deps=()):
    sent = [after(pick(parts, lay.member ^ step), *deps) for step in range(1, lay.group)]
    others = [lay.to_member(block, step) for step, block in enumerate(sent, 1)]
    placed = place(pick(parts, lay.member), others, lay.member)
    return placed.reshape(-1, parts.shape[-1]), sent[-1]


class Spread:
    def __init__(self, block):
        self.block = block

    def over_half(self, wire, deps=()):
        self.got, sent = wire.send(self.block, deps)
        return sent

    def over_shard(self, wire, deps=()):
        self.pair = jnp.concatenate([self.block, after(self.got, *deps)], 0)
        self.got, sent = wire.send(self.pair)
        return sent

    def full(self):
        return jnp.concatenate([self.pair, self.got], 0)


class Collect:
    def __init__(self, left, right):
        self.left, self.right = left, right
        self.rows = left.shape[1] // 4

    def over_shard(self, wire, deps=(), **how):
        block = mm_tn(self.left[:, 2 * self.rows :], self.right).astype(BF16)
        self.got, sent = wire.send(block, deps, **how)
        return sent

    def over_half(self, wire, deps=(), **how):
        rows = self.rows
        kept = mm_tn(self.left[:, : 2 * rows], self.right)
        got = after(self.got, *deps).astype(F32)
        self.kept = kept[:rows] + got[:rows]
        self.arrived, sent = wire.send((kept[rows:] + got[rows:]).astype(BF16), **how)
        return sent

    def total(self, deps=()):
        return self.kept + after(self.arrived, *deps).astype(F32)


def return_columns(parts, lay, deps):
    others = [
        lay.to_member(after(pick(parts, lay.member ^ step).astype(BF16), *deps), step)
        for step in range(1, lay.group)
    ]
    placed = place(pick(parts, lay.member), [block.astype(F32) for block in others], lay.member)
    return placed, others


def join_cores(first, second, lay):
    kept = jnp.where(lay.core == 0, first, second)
    sent = jnp.where(lay.core == 0, second, first).astype(BF16)
    return two_way(lay.core, kept, lay.to_core(sent).astype(F32), 0)


def out_aligned(lay, block_rows):
    return block_rows == HEAD_DIM and lay.cores * lay.group == KV_HEADS and lay.cores == lay.halves


class SpreadOut:
    def __init__(self, w_out, lay, deps):
        self.lay, self.width = lay, w_out.shape[-1]
        self.aligned = out_aligned(lay, w_out.shape[0])
        if not self.aligned:
            w_out = lax.all_gather(w_out, ("ctx", "shard"), axis=0, tiled=True)
        w_out = after(w_out, *deps)
        other = lay.to_core(w_out)
        layers = [jnp.where(lay.core == 0, w_out, other), jnp.where(lay.core == 0, other, w_out)]
        self.block = jnp.stack(layers)

    def over_half(self, wire, deps=()):
        lay = self.lay
        if not self.aligned:
            return self.block
        move = lambda block: lay.move_some(
            block,
            lambda core, half, member, shard: half == core,
            lambda core, half, member, shard: (core, 1 - half, member, shard),
        )
        self.got, sent = wire.send(self.block, deps, move)
        return sent

    def over_shard(self, wire, deps=()):
        lay = self.lay
        if not self.aligned:
            return self.block
        self.block = jnp.where(lay.half == lay.core, self.block, after(self.got, *deps))
        self.got, sent = wire.send(self.block)
        return sent

    def full(self):
        if self.aligned:
            return jnp.concatenate([self.block, self.got], 1)
        head = (self.lay.core * self.lay.group + self.lay.member) // head_copies(self.lay)
        count = max(1, HEADS // (self.lay.cores * self.lay.group)) * HEAD_DIM
        return lax.dynamic_slice_in_dim(self.block, head * count, count, 1)


class CollectOut:
    def __init__(self, left, right, lay, block_rows):
        self.left, self.right, self.lay = left, right, lay
        self.aligned = out_aligned(lay, block_rows)
        self.rows = left.shape[1] // 2

    def over_shard(self, wire, deps=(), **how):
        if not self.aligned:
            self.kept = mm_tn(self.left, self.right)
            return self.kept
        block = mm_tn(self.left[:, self.rows :], self.right).astype(BF16)
        self.got, sent = wire.send(block, deps, **how)
        return sent

    def over_half(self, wire, deps=(), **how):
        lay = self.lay
        if not self.aligned:
            return self.kept
        self.kept = mm_tn(self.left[:, : self.rows], self.right) + after(self.got, *deps).astype(F32)
        move = lambda block: lay.move_some(
            block,
            lambda core, half, member, shard: half != core,
            lambda core, half, member, shard: (core, 1 - half, member, shard),
        )
        self.arrived, sent = wire.send(self.kept.astype(BF16), (), move, **how)
        return sent

    def total(self, deps=()):
        return self.kept + after(self.arrived, *deps).astype(F32) if self.aligned else self.kept


def join_out(first, second, lay, block_rows):
    if not out_aligned(lay, block_rows):
        width = first.shape[1]
        head = (lay.core * lay.group + lay.member) // head_copies(lay)
        full = jnp.zeros((2, HEADS * HEAD_DIM, width), F32)
        full = lax.dynamic_update_slice_in_dim(
            full, jnp.stack([first, second]), head * first.shape[0], 1
        )
        full = pick(lax.psum(full, MESH_AXES), lay.core)
        block = (lay.half * lay.group + lay.member) * lay.shards + lay.shard
        return lax.dynamic_slice_in_dim(full, block * block_rows, block_rows, 0)
    kept = jnp.where(lay.core == 0, first, second)
    sent = jnp.where(lay.core == 0, second, first).astype(BF16)
    other = lay.to_core(sent).astype(F32)
    return jnp.where(lay.half == lay.core, kept, other)


def lane_matrix(heads):
    source = jnp.arange(heads * HEAD_DIM)
    head, offset = source // HEAD_DIM, source % HEAD_DIM
    target = head * LANES + (offset // HALF) * HALF_LANES + offset % HALF
    return (target[:, None] == jnp.arange(heads * LANES)[None, :]).astype(BF16)


def rot(vec, cos_t, sin_t):
    return vec * cos_t + pltpu.roll(vec, HALF_LANES, 1) * sin_t


def rot_back(vec, cos_t, sin_t):
    return vec * cos_t - pltpu.roll(vec, HALF_LANES, 1) * sin_t


def mm(a, b):
    return lax.dot_general(a, b, (((1,), (0,)), ((), ())), preferred_element_type=F32)


def mm_nt(a, b):
    return lax.dot_general(a, b, (((1,), (1,)), ((), ())), preferred_element_type=F32)


def mm_tn(a, b):
    return lax.dot_general(a, b, (((0,), (0,)), ((), ())), preferred_element_type=F32)


def heads_of(block, count):
    return jnp.concatenate([block[:, i * LANES : (i + 1) * LANES] for i in range(count)], 0)


def project_kernel(n_query, n_key, x, w, cos_t, sin_t, out):
    cos_v, sin_v = cos_t[...], sin_t[...]
    xv = x[...]
    step = 2 * LANES
    for first in range(0, out.shape[1], step):
        raw = mm(xv, w[:, first : first + step])
        for lane in range(first, first + step, LANES):
            block = raw[:, lane - first : lane - first + LANES]
            if lane < (n_query + n_key) * LANES:
                block = rot(block, cos_v, sin_v)
            out[:, lane : lane + LANES] = block.astype(BF16)


def project(normed, qkv_w, cos_t, sin_t, n_query, n_key):
    rows = normed.shape[0]
    if (n_query + 2 * n_key) % 2:
        qkv_w = jnp.pad(qkv_w, ((0, 0), (0, LANES)))
    out = pl.pallas_call(
        lambda *refs: project_kernel(n_query, n_key, *refs),
        out_shape=jax.ShapeDtypeStruct((rows, qkv_w.shape[1]), BF16),
        compiler_params=VMEM_LIMIT,
        cost_estimate=pl.CostEstimate(
            flops=2 * rows * qkv_w.shape[0] * qkv_w.shape[1],
            bytes_accessed=2 * qkv_w.shape[0] * qkv_w.shape[1],
            transcendentals=0,
        ),
        name="project",
    )(normed, qkv_w, cos_t, sin_t)
    return out[:, : (n_query + 2 * n_key) * LANES]


def lanes_of(index, count=1):
    return slice(index * LANES, (index + count) * LANES)


def attend_kernel(n_query, n_key, own, sib, pos_q, pos_k, out_own, out_sib, lse_out):
    scale = HEAD_DIM ** (-0.5)
    per_key = n_query // n_key
    half = own.shape[0]
    rows = 2 * half
    mask = pos_q[...] >= pos_k[...]
    mask = jnp.concatenate([mask] * per_key, 0)
    for kv_head in range(n_key):
        both = lambda index: jnp.concatenate([own[:, lanes_of(index)], sib[:, lanes_of(index)]], 0)
        key, value = both(n_query + kv_head), both(n_query + n_key + kv_head)
        q_first = kv_head * per_key
        query = jnp.concatenate([both(q_first + i) for i in range(per_key)], 0)
        scores = jnp.where(mask, mm_nt(query, key) * scale, MASK_FILL)
        row_max = jnp.max(scores, -1, keepdims=True)
        weights = jnp.exp(scores - row_max)
        total = jnp.sum(weights, -1, keepdims=True)
        probs = (weights * (1.0 / total)).astype(BF16)
        out = mm(probs, value).astype(BF16)
        for i in range(per_key):
            out_own[:, lanes_of(q_first + i)] = out[i * rows : i * rows + half]
            out_sib[:, lanes_of(q_first + i)] = out[i * rows + half : (i + 1) * rows]
        lse_out[kv_head] = row_max + jnp.log(total)


def attend(own, sib, pos_q, pos_k, n_query, n_key):
    half = own.shape[0]
    return pl.pallas_call(
        lambda *refs: attend_kernel(n_query, n_key, *refs),
        out_shape=[
            jax.ShapeDtypeStruct((half, n_query * LANES), BF16),
            jax.ShapeDtypeStruct((half, n_query * LANES), BF16),
            jax.ShapeDtypeStruct((n_key, n_query // n_key * 2 * half, 1), F32),
        ],
        compiler_params=VMEM_LIMIT,
        cost_estimate=pl.CostEstimate(
            flops=16 * n_query * half * half * LANES,
            bytes_accessed=half * n_query * LANES * 8,
            transcendentals=4 * n_query * half * half,
        ),
        name="attend",
    )(own, sib, pos_q, pos_k)


def attend_back_kernel(
    n_query, n_key, own, sib, do_own, do_sib, lse, cos_t, sin_t, pos_q, pos_k, low_own, low_sib
):
    scale = HEAD_DIM ** (-0.5)
    per_key = n_query // n_key
    half = own.shape[0]
    rows = 2 * half
    cos_v, sin_v = cos_t[...], sin_t[...]
    mask = pos_q[...] >= pos_k[...]
    mask = jnp.concatenate([mask] * per_key, 0)

    def put(index, block):
        low_own[:, lanes_of(index)] = block[:half].astype(BF16)
        low_sib[:, lanes_of(index)] = block[half:].astype(BF16)

    def both(a, b, index):
        return jnp.concatenate([a[:, lanes_of(index)], b[:, lanes_of(index)]], 0)

    for kv_head in range(n_key):
        key, value = both(own, sib, n_query + kv_head), both(own, sib, n_query + n_key + kv_head)
        q_first = kv_head * per_key
        query = jnp.concatenate([both(own, sib, q_first + i) for i in range(per_key)], 0)
        grad = jnp.concatenate([both(do_own, do_sib, q_first + i) for i in range(per_key)], 0)
        scores = jnp.where(mask, mm_nt(query, key) * scale, MASK_FILL)
        probs = jnp.exp(scores - lse[kv_head])
        prob_grad = mm_nt(grad, value)
        delta = jnp.sum(probs * prob_grad, -1, keepdims=True)
        score_grad = (probs * (prob_grad - delta)).astype(BF16)
        dq = mm(score_grad, key) * scale
        for i in range(per_key):
            put(q_first + i, rot_back(dq[i * rows : (i + 1) * rows], cos_v, sin_v))
        put(n_query + kv_head, rot_back(mm_tn(score_grad, query) * scale, cos_v, sin_v))
        put(n_query + n_key + kv_head, mm_tn(probs.astype(BF16), grad))


def attend_back(kept, out_grads, tables, n_query, n_key):
    own, sib, lse = kept
    half, lanes = own.shape
    return pl.pallas_call(
        lambda *refs: attend_back_kernel(n_query, n_key, *refs),
        out_shape=[
            jax.ShapeDtypeStruct((half, lanes), BF16),
            jax.ShapeDtypeStruct((half, lanes), BF16),
        ],
        compiler_params=VMEM_LIMIT,
        cost_estimate=pl.CostEstimate(
            flops=40 * n_query * half * half * LANES,
            bytes_accessed=half * lanes * 16,
            transcendentals=4 * n_query * half * half,
        ),
        name="attend_back",
    )(own, sib, *out_grads, lse, *tables)


def no_round(first):
    return ()


def gather_rows(block, lay, meanwhile=no_round):
    others = [lay.to_member(block, step) for step in range(1, lay.group)]
    own = after(jnp.concatenate([block] + others, 0), *meanwhile(others))
    return own, lay.to_core(own)


def scatter_rows(own, sib, lay, meanwhile=no_round):
    own = own + lay.to_core(sib.astype(BF16)).astype(F32)
    rows = own.shape[0] // lay.group
    parts = own.reshape(lay.group, rows, -1)
    others = [lay.to_member(parts[step].astype(BF16), step) for step in range(1, lay.group)]
    total = parts[0]
    for block in others:
        total = total + block.astype(F32)
    return after(total, *meanwhile(others))


def norm_forward(inputs, gain_vec):
    inverse_rms = lax.rsqrt(jnp.mean(inputs * inputs, -1, keepdims=True) + NORM_EPS)
    return (inputs * inverse_rms * gain_vec).astype(BF16), inverse_rms


def norm_backward(inputs, inverse_rms, gain_vec, upstream):
    scaled = upstream * gain_vec
    input_grad = inverse_rms * scaled - inputs * inverse_rms**3 * jnp.mean(
        scaled * inputs, -1, keepdims=True
    )
    gain_grad = jnp.sum(upstream * inputs * inverse_rms, 0)
    return input_grad, gain_grad


def out_order(block, lay, n_query):
    if head_copies(lay) > 1:
        share = (lay.core * lay.group + lay.member) % head_copies(lay) == 0
        return jnp.where(share, block, jnp.zeros_like(block))
    if n_query != 2 or lay.cores * lay.group != KV_HEADS:
        return block
    swapped = jnp.concatenate([block[:, LANES:], block[:, :LANES]], 1)
    return jnp.where(lay.shard == 0, block, swapped)


class Layer:
    def __init__(self, lay, tables, n_query, n_key, gain_one, gain_two, qkv_w, out_w):
        self.lay, self.tables, self.n_query, self.n_key = lay, tables, n_query, n_key
        self.gain_one, self.gain_two = gain_one, gain_two
        self.qkv_w, self.out_w = qkv_w, out_w

    def start(self, inputs, meanwhile=no_round):
        self.inputs = inputs
        normed, self.inverse_first = norm_forward(inputs, self.gain_one)
        self.normed = gather_rows(relative(normed, self.lay), self.lay, meanwhile)

    def attention(self, during_out=no_round, during_rows=no_round):
        lay = self.lay
        cos_own, sin_own, cos_sib, sin_sib, pos_q, pos_k = self.tables
        heads = self.n_query, self.n_key
        own = project(self.normed[0], self.qkv_w, cos_own, sin_own, *heads)
        sib = project(self.normed[1], self.qkv_w, cos_sib, sin_sib, *heads)
        out_own, out_sib, lse = attend(own, sib, pos_q, pos_k, *heads)
        self.attn_kept = own, sib, lse
        self.attn_out = [out_order(block, lay, self.n_query) for block in (out_own, out_sib)]
        partial = [mm(block, self.out_w) for block in self.attn_out]
        self.mid_stream = self.inputs + scatter_rows(*partial, lay, during_out)
        normed, self.inverse_second = norm_forward(self.mid_stream, self.gain_two)
        self.normed_mid = gather_rows(relative(normed, lay), lay, during_rows)

    def hide(self):
        lay = self.lay
        self.gate_up, self.hidden = [], []
        for block in self.normed_mid:
            pre = mm(block, self.gate_up_w)
            ff = pre.shape[1] // 2
            gate_pre, up_pre = pre[:, :ff], pre[:, ff:]
            self.gate_up.append((gate_pre, up_pre))
            self.hidden.append(relative((jax.nn.silu(gate_pre) * up_pre).astype(BF16), lay))

    def feed_forward(self, meanwhile=no_round):
        lay = self.lay
        partial = [mm(block, self.down_w) for block in self.hidden]
        return self.mid_stream + scatter_rows(*partial, lay, meanwhile)

    def start_back(self, out_grad, meanwhile=no_round):
        self.out_grad = out_grad
        self.down_in = gather_rows(out_grad.astype(BF16), self.lay, meanwhile)

    def feed_forward_back(self):
        self.gate_up_grad, partial = [], []
        for block, (gate_pre, up_pre) in zip(self.down_in, self.gate_up):
            hidden_grad = relative(mm_nt(block, self.down_w), self.lay)
            sigmoid_gate = jax.nn.sigmoid(gate_pre)
            gate_grad_in = (
                hidden_grad * up_pre * sigmoid_gate * (1.0 + gate_pre * (1.0 - sigmoid_gate))
            ).astype(BF16)
            up_grad_in = (hidden_grad * gate_pre * sigmoid_gate).astype(BF16)
            both = jnp.concatenate([gate_grad_in, up_grad_in], 1)
            self.gate_up_grad.append(both)
            partial.append(mm_nt(both, self.gate_up_w))
        return partial

    def middle_back(self, partial, during_sum=no_round, during_rows=no_round):
        lay = self.lay
        normed_mid_grad = relative(scatter_rows(*partial, lay, during_sum), lay)
        mid_part, self.gain_two_grad = norm_backward(
            self.mid_stream, self.inverse_second, self.gain_two, normed_mid_grad
        )
        self.mid_grad = self.out_grad + mid_part
        self.mid_low = gather_rows(self.mid_grad.astype(BF16), lay, during_rows)

    def attention_back(self):
        cos_own, sin_own, cos_sib, sin_sib, pos_q, pos_k = self.tables
        grads = [
            out_order(mm_nt(block, self.out_w).astype(BF16), self.lay, self.n_query)
            for block in self.mid_low
        ]
        cos_t, sin_t = jnp.concatenate([cos_own, cos_sib]), jnp.concatenate([sin_own, sin_sib])
        tables = cos_t, sin_t, pos_q, pos_k
        self.lows = attend_back(self.attn_kept, grads, tables, self.n_query, self.n_key)
        return [mm_nt(block, self.qkv_w) for block in self.lows]

    def finish_back(self, partial, meanwhile=no_round):
        lay = self.lay
        normed_grad = relative(scatter_rows(*partial, lay, meanwhile), lay)
        input_part, gain_one_grad = norm_backward(
            self.inputs, self.inverse_first, self.gain_one, normed_grad
        )
        self.gain_grads = jnp.stack([gain_one_grad, self.gain_two_grad])
        return self.mid_grad + input_part


def joined(pair):
    return jnp.concatenate(pair, 0)


def gain_sums(gains, lay):
    own = pick(gains, lay.core) + lay.to_core(pick(gains, 1 - lay.core))
    parts = own.reshape(2, lay.shards, lay.halves, lay.group, -1).transpose(1, 2, 3, 0, 4)
    parts = pick(parts, lay.shard) + lay.to_shard(pick(parts, 1 - lay.shard))
    parts = pick(parts, lay.half) + lay.to_half(pick(parts, 1 - lay.half))
    total = pick(parts, lay.member)
    for step in range(1, lay.group):
        total = total + lay.to_member(pick(parts, lay.member ^ step), step)
    return total


def row_tables(pair_table, block_rows, lay):
    cores = []
    for core in (lay.core, 1 - lay.core):
        ctx_ids = jnp.stack([core * lay.group + (lay.member ^ step) for step in range(lay.group)])
        owned = jnp.sum(
            jnp.where(ctx_ids[:, None] == jnp.arange(lay.ctx)[None, :], pair_table[None, :], 0), 1
        )
        blocks = jnp.stack([owned, 2 * lay.ctx - 1 - owned], 1)
        rows = blocks[:, :, None] * block_rows + jnp.arange(block_rows)[None, None, :]
        cores.append(rows.reshape(-1))
    positions = jnp.concatenate(cores)
    freq_idx = jnp.arange(HALF, dtype=F32)
    inverse = ROPE_BASE ** (-2.0 * freq_idx / HEAD_DIM)
    angles = positions.astype(F32)[:, None] * inverse[None, :]
    pad = ((0, 0), (0, HALF_LANES - HALF))
    cos_h, sin_h = jnp.pad(jnp.cos(angles), pad), jnp.pad(jnp.sin(angles), pad)
    cos_t = jnp.concatenate([cos_h, cos_h], 1)
    sin_t = jnp.concatenate([-sin_h, sin_h], 1)
    count = cores[0].shape[0]
    return (
        cos_t[:count],
        sin_t[:count],
        cos_t[count:],
        sin_t[count:],
        positions[:, None],
        positions[None, :],
    )


def deal_rows(local, lay):
    turn = lay.half ^ lay.core
    straight = lay.move(
        pick(local, turn), lambda core, half, member, shard: (half, half ^ core, member, shard)
    )
    crossed = lay.move(
        pick(local, 1 - turn),
        lambda core, half, member, shard: (half, 1 - (half ^ core), member, shard),
    )
    return jnp.where(turn == 0, straight, crossed), jnp.where(turn == 0, crossed, straight)


def return_rows(input_grad, outputs, lay):
    turn = lay.half ^ lay.core
    straight = lay.move(
        jnp.where(turn == 0, input_grad, outputs),
        lambda core, half, member, shard: (core ^ half, core, member, shard),
    )
    crossed = lay.move(
        jnp.where(turn == 0, outputs, input_grad),
        lambda core, half, member, shard: (1 - (core ^ half), core, member, shard),
    )
    return two_way(turn, straight, crossed, 0)


def body(
    ends_in, pair_table, norm_attn, w_query, w_key, w_value, w_out, norm_mlp, w_gate, w_up, w_down
):
    lay = Layout()
    rows = ends_in.shape[3]
    width = ends_in.shape[4]
    row_block = w_query.shape[1]
    pairs = lay.cores * lay.group
    n_query = max(1, HEADS // pairs)
    n_key = max(1, KV_HEADS // pairs)
    ff_unit = w_down.shape[1] // lay.cores
    q_cols, k_cols = n_query * HEAD_DIM, n_key * HEAD_DIM
    spread_lanes = lane_matrix(n_query + 2 * n_key)
    spread_out = lane_matrix(n_query)
    over_half, over_shard = Wire(lay.to_half), Wire(lay.to_shard)
    cols = q_cols + 2 * k_cols
    ff = ff_unit * 4

    gains = jnp.stack([norm_attn[0], norm_mlp[0]])
    gain_parts = [lay.to_member(gains, step) for step in range(1, lay.group)]
    heads = pack_heads(w_query[0], w_key[0], w_value[0], lay)
    qkv_layers = split_cores(heads, lay)
    qkv_first, begun = swap_columns(qkv_layers[0], lay, gain_parts)
    gains = place(gains, gain_parts, lay.member)
    gains = two_way(lay.half, gains, lay.to_half(after(gains, begun)), 0)
    qkv_0 = Spread(qkv_first)
    sent = qkv_0.over_half(over_half, (gains,))
    gains = two_way(lay.shard, gains, lay.to_shard(after(gains, sent)), 0)
    local = to_inner(after(ends_in, begun)[0, :, 0], lay)
    own_in, own_cot = deal_rows(after(local, sent), lay)
    gains = two_way(lay.core, gains, lay.to_core(gains), 0)
    gains = gains.transpose(0, 4, 1, 2, 3, 5).reshape(2, 2, -1).astype(F32)
    w_gate, w_up, w_out, w_down = (after(block, begun) for block in (w_gate, w_up, w_out, w_down))
    gate_up_layers = split_cores(pack_ff(w_gate[0], w_up[0], lay, ff_unit), lay, (sent,))
    rest = jnp.concatenate([gate_up_layers[0], qkv_layers[1], gate_up_layers[1]], -1)
    rest, rest_sent = swap_columns(rest, lay, (own_in, own_cot))
    out = SpreadOut(to_inner(w_out[0], lay), lay, (rest_sent,))
    down_layers = split_cores(
        to_inner(w_down[0], lay).reshape(lay.cores, ff_unit, width), lay, (rest_sent,)
    )
    tables = row_tables(after(pair_table, begun), rows // 2, lay)
    gate_0, up_0 = Spread(rest[:, :ff]), Spread(rest[:, ff : 2 * ff])
    qkv_1 = Spread(rest[:, 2 * ff : 2 * ff + cols])
    gate_1 = Spread(rest[:, 2 * ff + cols : 3 * ff + cols])
    up_1 = Spread(rest[:, 3 * ff + cols :])
    down_0, down_1 = Spread(down_layers[0]), Spread(down_layers[1])
    out.over_half(over_half)
    qkv_0.over_shard(over_shard)
    gate_0.over_half(over_half)
    out.over_shard(over_shard)

    def round_of(halves, shards):
        def run(arrived):
            sent = [item.over_half(over_half, arrived) for item in halves]
            return sent + [item.over_shard(over_shard, arrived) for item in shards]

        return run

    def layer(index, qkv, out_w):
        return Layer(
            lay,
            tables,
            n_query,
            n_key,
            gains[index, 0],
            gains[index, 1],
            mm(qkv.full(), spread_lanes).astype(BF16),
            mm_tn(spread_out, out_w).astype(BF16),
        )

    out_w = out.full()
    first = layer(0, qkv_0, out_w[0])
    first.start(own_in.astype(F32))
    first.attention(round_of([up_0], [gate_0]), round_of([down_0], [up_0]))
    first.gate_up_w = jnp.concatenate([gate_0.full(), up_0.full()], 1)
    down_0.over_shard(over_shard)
    qkv_1.over_half(over_half, (up_0.got,))
    first.down_w = down_0.full()
    first.hide()
    first_out = first.feed_forward(round_of([gate_1], [qkv_1]))
    second = layer(1, qkv_1, out_w[1])
    second.start(first_out.astype(BF16).astype(F32), round_of([up_1], [gate_1]))
    second.start_back(own_cot.astype(F32))
    second.attention(round_of([down_1], [up_1]), round_of([], [down_1]))
    second.gate_up_w = jnp.concatenate([gate_1.full(), up_1.full()], 1)
    second.down_w = down_1.full()

    def gate_up_collects(which):
        left, right = joined(which.normed_mid), joined(which.gate_up_grad)
        return Collect(left, right[:, :ff]), Collect(left, right[:, ff:])

    def out_collect(which):
        left = mm_nt(joined(which.attn_out), spread_out).astype(BF16)
        return CollectOut(left, joined(which.mid_low), lay, row_block)

    def qkv_collect(which):
        low = mm_nt(joined(which.lows), spread_lanes).astype(BF16)
        return Collect(joined(which.normed), low)

    second.hide()
    down_1 = Collect(joined(second.hidden), joined(second.down_in))
    second_out = second.feed_forward(round_of([], [down_1]))
    partial = second.feed_forward_back()
    partial[0] = after(partial[0], second_out)
    gate_1, up_1 = gate_up_collects(second)
    second.middle_back(partial, round_of([down_1], [gate_1]), round_of([gate_1], [up_1]))
    out_1 = out_collect(second)
    partial = second.attention_back()
    qkv_1 = qkv_collect(second)

    def last_of_second(arrived):
        sent = [qkv_1.over_shard(over_shard, arrived)]
        sent.append(out_1.over_shard(over_shard, arrived, beside=True))
        return sent + [up_1.over_half(over_half, arrived)]

    second_grad = second.finish_back(partial, last_of_second)

    first.start_back(second_grad.astype(BF16).astype(F32), round_of([qkv_1], []))
    down_0 = Collect(joined(first.hidden), joined(first.down_in))
    partial = first.feed_forward_back()
    partial[0] = after(partial[0], down_0.over_shard(over_shard))
    gate_0, up_0 = gate_up_collects(first)
    first.middle_back(partial, round_of([out_1, down_0], [gate_0]), round_of([gate_0], [up_0]))
    out_0 = out_collect(first)
    parts = [gate_1.total(), up_1.total(), qkv_1.total()]
    parts = jnp.concatenate(parts, 1).reshape(lay.group, row_block, -1)
    back_1, sent = return_columns(parts, lay, (first.mid_low[1],))
    partial = first.attention_back()
    qkv_0 = qkv_collect(first)
    partial[1] = after(partial[1], qkv_0.over_shard(over_shard), *sent)
    first_grad = first.finish_back(partial, round_of([up_0], [out_0]))
    last = qkv_0.over_half(over_half)
    out_0.over_half(over_half, beside=True)

    def member_parts(blocks, deps):
        parts = jnp.concatenate([block.total(deps) for block in blocks], 1)
        return parts.reshape(lay.group, row_block, -1)

    back_0, sent = return_columns(member_parts([gate_0, up_0], sent), lay, ())
    back_q, sent = return_columns(member_parts([qkv_0], sent), lay, ())
    first_w = back_q, out_0.total(sent), back_0, down_0.total(sent)
    second_w = back_1[..., 2 * ff :], out_1.total(sent), back_1[..., : 2 * ff], down_1.total(sent)
    first_gains, second_gains = first.gain_grads, second.gain_grads
    gain_g = gain_sums(jnp.stack([first_gains, second_gains]), lay)
    ends = to_outer(return_rows(first_grad.astype(BF16), second_out.astype(BF16), lay), lay)

    qkv_g = unpack_heads(join_cores(first_w[0], second_w[0], lay), lay)
    out_g = to_outer(join_out(first_w[1], second_w[1], lay, row_block), lay)
    gate_up_g = unpack_ff(join_cores(first_w[2], second_w[2], lay), lay, ff_unit)
    down_g = to_outer(join_cores(first_w[3], second_w[3], lay).reshape(-1, width), lay)
    return (
        ends[None, :, None],
        gain_g[0][None],
        qkv_g[0][None],
        qkv_g[1][None],
        qkv_g[2][None],
        out_g[None],
        gain_g[1][None],
        gate_up_g[0][None],
        gate_up_g[1][None],
        down_g[None],
    )


def solution(mesh):
    rows = P("section", None, "shard", "ctx", None)
    vector = P("section", ("ctx", "shard"))
    matrix = P("section", ("ctx", "shard"), None)
    return jax.shard_map(
        body,
        mesh=mesh,
        in_specs=(rows, P(), vector, matrix, matrix, matrix, matrix, vector, matrix, matrix, matrix),
        out_specs=(rows, vector, matrix, matrix, matrix, matrix, vector, matrix, matrix, matrix),
        check_vma=False,
    )
```

time: 966 us -> 698 us (0.72)
  starting transfers between devices: 251 us -> 162 us
  waiting for transfers between devices: 384 us -> 299 us
  local copies, waits for them, and re-layouts: 122 us -> 37.1 us
  matrix products: 86.1 us -> 49.2 us
  Pallas kernels: 29.7 us -> 53.5 us
    ppermute x121 -> x138, starting transfers between devices: 249 us -> 158 us  [move(): return lax.ppermute(block, MESH_AXES, pairs)]
    ppermute x2 -> x3, waiting for transfers between devices: 71.1 us -> 10.5 us  [move_some(): return lax.ppermute(block, MESH_AXES, pairs)]
    dot_general x16 -> x20, matrix products: 50.3 us -> 16.9 us  [mm_nt(): lax.dot_general(a, b, (((1,), (1,)), ((), ())), preferred_element_type=F32)]
    concatenate x4 -> x32, other arithmetic: 1.85 us -> 28 us  [the longest x1 9.71 us: body(): first.gate_up_w = jnp.concatenate([gate_0.full(), up_0.full()], 1)]
    convert_element_type x21 -> x4, local copies, waits for them, and re-layouts: 27 us -> 1.14 us  [the longest x3 1.04 us: return_columns(): pick(parts, lay.member ^ step).astype(BF16)]
    ppermute x121 -> x138, waiting for transfers between devices: 313 us -> 288 us  [move(): return lax.ppermute(block, MESH_AXES, pairs)]
    pallas_call x4 -> x18, Pallas kernels: 29.7 us -> 53.5 us  [the longest x10 24.9 us: rearrange(): pl.pallas_call(lambda *refs: rearrange_kernel(plans, len(sources), *refs)...]
    select_n x13 -> x0, local copies, waits for them, and re-layouts: 21 us -> none  [body(): jnp.where(is_first, a, b)[None]]
  transfers between devices with their start and end apart: 123 -> 141, of which waited for: 30 -> 64; matrix products, arithmetic and copies ran while one was open for 23% -> 20% of each run, Pallas kernels for 3% -> 6%
where the time goes in v2:
time: 698 us; the launch traced here: 687 us
  waiting for transfers between devices  299 us (43%)
  starting transfers between devices  162 us (23%)
  other arithmetic  82.3 us (12%)
  Pallas kernels  53.5 us (8%)
  matrix products  49.2 us (7%)
  local copies, waits for them, and re-layouts  37.1 us (5%)
    ppermute x138, waiting for transfers between devices, move(): return lax.ppermute(block, MESH_AXES, pairs)  288 us
    ppermute x138, starting transfers between devices, move(): return lax.ppermute(block, MESH_AXES, pairs)  158 us
    pallas_call x10, Pallas kernels, rearrange(): pl.pallas_call(lambda *refs: rearrange_kernel(plans, len(sources), *refs)...  24.9 us
    dot_general x22, matrix products, mm_tn(): lax.dot_general(a, b, (((0,), (0,)), ((), ())), preferred_element_type=F32)  19.2 us
    dot_general x20, matrix products, mm_nt(): lax.dot_general(a, b, (((1,), (1,)), ((), ())), preferred_element_type=F32)  16.9 us
    unnamed x283, local copies, waits for them, and re-layouts  15.7 us
  transfers between devices with their start and end apart: 141, of which 64 were waited for; matrix products, arithmetic and copies ran while one was open for 20% of the time, Pallas kernels for 6%

profile of v2, /device:TPU:0, one launch (start us, length us, event | category | flops | bytes accessed | tf_op | source)
XLA Modules:
  0.0 687.0 jit_solution(14558899510703195384)
XLA Ops:
  48.7 13.5 %collective-permute-start.59 = (bf16[64,1536]{1,0:T(8,128)(2,1)S(1)}, bf16[64,1536]{1,0:T(8,128)(2,1)S(1)}, u32[]{:S(2)}, u32[]{:S(2)}) collective-permute-start(bf16[64,1536]{1,0:T(8,128)(2,1)S(1)} %get-tuple-element.288), channel_id=1, source_target_pairs={{0,6},{1,7},{2,4},{3,5},{4,2},{5,3},{6,0},{7,1},{8,14},{9,15},{10,... | collective-permute-start | bytes 589832 | tf_op jit(solution)/shard_map/ppermute | solution.py:46
  115.5 13.3 %collective-permute-done.21 = bf16[2,96,1536]{2,1,0:T(8,128)(2,1)S(1)} collective-permute-done((bf16[2,96,1536]{2,1,0:T(8,128)(2,1)S(1)}, bf16[2,96,1536]{2,1,0:T(8,128)(2,1)S(1)}, u32[]{:S(2)}, u32[]{:S(2)}) %collective-permute-start.21) | collective-permute-done | bytes 589856 | tf_op jit(solution)/shard_map/ppermute | solution.py:46
  137.4 15.2 %collective-permute-done.29 = bf16[384,512]{1,0:T(8,128)(2,1)S(1)} collective-permute-done((bf16[384,512]{1,0:T(8,128)(2,1)S(1)}, bf16[384,512]{1,0:T(8,128)(2,1)S(1)}, u32[]{:S(2)}, u32[]{:S(2)}) %collective-permute-start.29) | collective-permute-done | bytes 393248 | tf_op jit(solution)/shard_map/ppermute | solution.py:46
  160.3 6.3 collective-permute-done.32
  168.4 5.0 collective-permute-done.31
  180.3 16.3 %collective-permute-done.37 = bf16[128,1536]{1,0:T(8,128)(2,1)S(1)} collective-permute-done((bf16[128,1536]{1,0:T(8,128)(2,1)S(1)}, bf16[128,1536]{1,0:T(8,128)(2,1)S(1)}, u32[]{:S(2)}, u32[]{:S(2)}) %collective-permute-start.37) | collective-permute-done | bytes 393248 | tf_op jit(solution)/shard_map/ppermute | solution.py:46
  197.3 9.7 %maximum_maximum_fusion = bf16[1536,1024]{1,0:T(8,128)(2,1)S(1)} fusion(bf16[768,512]{1,0:T(8,128)(2,1)S(1)} %collective-permute-done.36, bf16[384,512]{1,0:T(8,128)(2,1)S(1)} %collective-permute-done.34, bf16[384,512]{1,0:T(8,128)(2,1)S(1)} %get-tuple-element.142, bf16[768,512]{1,0:T(8,128)(2,1)S(1)} %collective-permute-done.35, ...), kind=kLoop, calls=%fused_computation | loop fusion | flops 18874368 | bytes 6291456 | tf_op jit(solution)/shard_map/concatenate | solution.py:869
  209.2 7.0 %collective-permute-done.38 = bf16[256,1536]{1,0:T(8,128)(2,1)S(1)} collective-permute-done((bf16[256,1536]{1,0:T(8,128)(2,1)S(1)}, bf16[256,1536]{1,0:T(8,128)(2,1)S(1)}, u32[]{:S(2)}, u32[]{:S(2)}) %collective-permute-start.38) | collective-permute-done | bytes 786464 | tf_op jit(solution)/shard_map/ppermute | solution.py:46
  224.4 7.0 %collective-permute-done.41 = bf16[64,1536]{1,0:T(8,128)(2,1)S(1)} collective-permute-done((bf16[64,1536]{1,0:T(8,128)(2,1)S(1)}, bf16[64,1536]{1,0:T(8,128)(2,1)S(1)}, u32[]{:S(2)}, u32[]{:S(2)}) %collective-permute-start.41) | collective-permute-done | bytes 196640 | tf_op jit(solution)/shard_map/ppermute | solution.py:46
  241.4 11.9 %collective-permute-done.47 = bf16[64,1536]{1,0:T(8,128)(2,1)S(1)} collective-permute-done((bf16[64,1536]{1,0:T(8,128)(2,1)S(1)}, bf16[64,1536]{1,0:T(8,128)(2,1)S(1)}, u32[]{:S(2)}, u32[]{:S(2)}) %collective-permute-start.47) | collective-permute-done | bytes 196640 | tf_op jit(solution)/shard_map/ppermute | solution.py:46
  279.0 13.5 %collective-permute-done.55 = bf16[384,512]{1,0:T(8,128)(2,1)S(1)} collective-permute-done((bf16[384,512]{1,0:T(8,128)(2,1)S(1)}, bf16[384,512]{1,0:T(8,128)(2,1)S(1)}, u32[]{:S(2)}, u32[]{:S(2)}) %collective-permute-start.55) | collective-permute-done | bytes 393248 | tf_op jit(solution)/shard_map/ppermute | solution.py:46
  301.3 7.8 %collective-permute-done.63 = bf16[64,1536]{1,0:T(8,128)(2,1)S(1)} collective-permute-done((bf16[64,1536]{1,0:T(8,128)(2,1)S(1)}, bf16[64,1536]{1,0:T(8,128)(2,1)S(1)}, u32[]{:S(2)}, u32[]{:S(2)}) %collective-permute-start.63) | collective-permute-done | bytes 196640 | tf_op jit(solution)/shard_map/ppermute | solution.py:46
  309.1 6.6 collective-permute-done.62
  317.7 9.5 %maximum_maximum_fusion.1 = bf16[1536,1024]{1,0:T(8,128)(2,1)S(1)} fusion(bf16[768,512]{1,0:T(8,128)(2,1)S(1)} %collective-permute-done.64, bf16[384,512]{1,0:T(8,128)(2,1)S(1)} %collective-permute-done.55, bf16[384,512]{1,0:T(8,128)(2,1)S(1)} %get-tuple-element.158, bf16[768,512]{1,0:T(8,128)(2,1)S(1)} %collective-permute-done.56, ...), kind=kLoop, calls=%fused_computation.1 | loop fusion | flops 18874368 | bytes 6291456 | tf_op jit(solution)/shard_map/concatenate | solution.py:879
  328.2 5.3 collective-permute-done.65
  349.6 7.1 %collective-permute-done.68 = bf16[64,1536]{1,0:T(8,128)(2,1)S(1)} collective-permute-done((bf16[64,1536]{1,0:T(8,128)(2,1)S(1)}, bf16[64,1536]{1,0:T(8,128)(2,1)S(1)}, u32[]{:S(2)}, u32[]{:S(2)}) %collective-permute-start.68) | collective-permute-done | bytes 196640 | tf_op jit(solution)/shard_map/ppermute | solution.py:46
  364.8 5.7 collective-permute-done.73
  384.3 4.7 collective-permute-done.79
  396.3 13.3 %collective-permute-done.81 = bf16[128,1536]{1,0:T(8,128)(2,1)S(1)} collective-permute-done((bf16[128,1536]{1,0:T(8,128)(2,1)S(1)}, bf16[128,1536]{1,0:T(8,128)(2,1)S(1)}, u32[]{:S(2)}, u32[]{:S(2)}) %collective-permute-start.81) | collective-permute-done | bytes 393248 | tf_op jit(solution)/shard_map/ppermute | solution.py:46
  411.1 7.2 %collective-permute-done.88 = bf16[384,512]{1,0:T(8,128)(2,1)S(1)} collective-permute-done((bf16[384,512]{1,0:T(8,128)(2,1)S(1)}, bf16[384,512]{1,0:T(8,128)(2,1)S(1)}, u32[]{:S(2)}, u32[]{:S(2)}) %collective-permute-start.88) | collective-permute-done | bytes 393248 | tf_op jit(solution)/shard_map/ppermute | solution.py:46
  421.0 4.8 attend_back.2
  435.2 7.4 %collective-permute-done.84 = bf16[64,1536]{1,0:T(8,128)(2,1)S(1)} collective-permute-done((bf16[64,1536]{1,0:T(8,128)(2,1)S(1)}, bf16[64,1536]{1,0:T(8,128)(2,1)S(1)}, u32[]{:S(2)}, u32[]{:S(2)}) %collective-permute-start.84) | collective-permute-done | bytes 196640 | tf_op jit(solution)/shard_map/ppermute | solution.py:46
  451.8 8.7 %collective-permute-done.91 = bf16[64,1536]{1,0:T(8,128)(2,1)S(1)} collective-permute-done((bf16[64,1536]{1,0:T(8,128)(2,1)S(1)}, bf16[64,1536]{1,0:T(8,128)(2,1)S(1)}, u32[]{:S(2)}, u32[]{:S(2)}) %collective-permute-start.91) | collective-permute-done | bytes 196640 | tf_op jit(solution)/shard_map/ppermute | solution.py:46
  471.4 9.7 %collective-permute-done.100 = bf16[384,384]{1,0:T(8,128)(2,1)S(1)} collective-permute-done((bf16[384,384]{1,0:T(8,128)(2,1)S(1)}, bf16[384,384]{1,0:T(8,128)(2,1)S(1)}, u32[]{:S(2)}, u32[]{:S(2)}) %collective-permute-start.100) | collective-permute-done | bytes 294944 | tf_op jit(solution)/shard_map/ppermute | solution.py:46
  496.9 6.7 collective-permute-done.97
  509.0 9.0 %collective-permute-done.102 = bf16[96,1536]{1,0:T(8,128)(2,1)S(1)} collective-permute-done((bf16[96,1536]{1,0:T(8,128)(2,1)S(1)}, bf16[96,1536]{1,0:T(8,128)(2,1)S(1)}, u32[]{:S(2)}, u32[]{:S(2)}) %collective-permute-start.102) | collective-permute-done | bytes 294944 | tf_op jit(solution)/shard_map/ppermute | solution.py:57
  524.1 5.2 collective-permute-done.105
  532.9 6.4 collective-permute-done.107
  577.8 5.8 collective-permute-done.114
  604.0 6.4 collective-permute-done.123
  618.3 6.3 collective-permute-done.120
  639.6 11.5 %collective-permute-done.130 = bf16[96,1024]{1,0:T(8,128)(2,1)S(1)} collective-permute-done((bf16[96,1024]{1,0:T(8,128)(2,1)S(1)}, bf16[96,1024]{1,0:T(8,128)(2,1)S(1)}, u32[]{:S(2)}, u32[]{:S(2)}) %collective-permute-start.130) | collective-permute-done | bytes 196640 | tf_op jit(solution)/shard_map/ppermute | solution.py:46
  (863 shorter events, 409.2 us)
Async XLA Ops:
  39.1 25.3 %collective-permute-start.15 = (bf16[384,384]{1,0:T(8,128)(2,1)S(1)}, bf16[384,384]{1,0:T(8,128)(2,1)}, u32[]{:S(2)}, u32[]{:S(2)}) collective-permute-start(bf16[384,384]{1,0:T(8,128)(2,1)S(1)} %bitcast.275), channel_id=1, source_target_pairs={{0,8},{1,9},{2,10},{3,11},{4,12},{5,13},{6,14},{7,15},{8,0},{9,1},... | collective-permute-start | bytes 884744 | tf_op jit(solution)/shard_map/ppermute | solution.py:46
  45.8 36.5 %collective-permute-start.18 = (bf16[4,96,1024]{2,1,0:T(8,128)(2,1)S(1)}, bf16[4,96,1024]{2,1,0:T(8,128)(2,1)}, u32[]{:S(2)}, u32[]{:S(2)}) collective-permute-start(bf16[4,96,1024]{2,1,0:T(8,128)(2,1)S(1)} %dynamic-slice_bitcast_fusion), channel_id=1, source_target_pairs={{0,16},{1,17},{2,18},{3,19},{4,20},{5,21},{6,22},{7,23},{8,24},{9,... | collective-permute-start | bytes 2359304 | tf_op jit(solution)/shard_map/ppermute | solution.py:46
  48.7 19.6 %collective-permute-start.59 = (bf16[64,1536]{1,0:T(8,128)(2,1)S(1)}, bf16[64,1536]{1,0:T(8,128)(2,1)S(1)}, u32[]{:S(2)}, u32[]{:S(2)}) collective-permute-start(bf16[64,1536]{1,0:T(8,128)(2,1)S(1)} %get-tuple-element.288), channel_id=1, source_target_pairs={{0,6},{1,7},{2,4},{3,5},{4,2},{5,3},{6,0},{7,1},{8,14},{9,15},{10,... | collective-permute-start | bytes 589832 | tf_op jit(solution)/shard_map/ppermute | solution.py:46
  76.0 102.5 %collective-permute-start.71 = (bf16[256,1536]{1,0:T(8,128)(2,1)}, bf16[256,1536]{1,0:T(8,128)(2,1)}, u32[]{:S(2)}, u32[]{:S(2)}) collective-permute-start(bf16[256,1536]{1,0:T(8,128)(2,1)} %pad_maximum_fusion.16), channel_id=1, source_target_pairs={{0,16},{1,17},{2,18},{3,19},{4,20},{5,21},{6,22},{7,23},{8,24},{9,... | collective-permute-start | bytes 2359304 | tf_op jit(solution)/shard_map/ppermute | solution.py:46
  84.2 46.7 %collective-permute-start.28 = (bf16[96,2432]{1,0:T(8,128)(2,1)S(1)}, bf16[96,2432]{1,0:T(8,128)(2,1)}, u32[]{:S(2)}, u32[]{:S(2)}) collective-permute-start(bf16[96,2432]{1,0:T(8,128)(2,1)S(1)} %get-tuple-element.134), channel_id=1, source_target_pairs={{0,6},{1,7},{2,4},{3,5},{4,2},{5,3},{6,0},{7,1},{8,14},{9,15},{10,... | collective-permute-start | bytes 1400840 | tf_op jit(solution)/shard_map/ppermute | solution.py:46
  86.7 24.5 %collective-permute-start.26 = (bf16[96,2432]{1,0:T(8,128)(2,1)S(1)}, bf16[96,2432]{1,0:T(8,128)(2,1)}, u32[]{:S(2)}, u32[]{:S(2)}) collective-permute-start(bf16[96,2432]{1,0:T(8,128)(2,1)S(1)} %get-tuple-element.139), channel_id=1, source_target_pairs={{0,2},{1,3},{2,0},{3,1},{4,6},{5,7},{6,4},{7,5},{8,10},{9,11},{10,... | collective-permute-start | bytes 1400840 | tf_op jit(solution)/shard_map/ppermute | solution.py:46
  132.1 20.5 %collective-permute-start.29 = (bf16[384,512]{1,0:T(8,128)(2,1)S(1)}, bf16[384,512]{1,0:T(8,128)(2,1)S(1)}, u32[]{:S(2)}, u32[]{:S(2)}) collective-permute-start(bf16[384,512]{1,0:T(8,128)(2,1)S(1)} %get-tuple-element.141), channel_id=1, source_target_pairs={{0,8},{1,9},{2,10},{3,11},{4,12},{5,13},{6,14},{7,15},{8,0},{9,1},... | collective-permute-start | bytes 1179656 | tf_op jit(solution)/shard_map/ppermute | solution.py:46
  154.6 22.1 %collective-permute-start.35 = (bf16[768,512]{1,0:T(8,128)(2,1)S(1)}, bf16[768,512]{1,0:T(8,128)(2,1)S(1)}, u32[]{:S(2)}, u32[]{:S(2)}) collective-permute-start(bf16[768,512]{1,0:T(8,128)(2,1)S(1)} %pad_maximum_fusion.9), channel_id=1, source_target_pairs={{0,1},{1,0},{2,3},{3,2},{4,5},{5,4},{6,7},{7,6},{8,9},{9,8},{10,11... | collective-permute-start | bytes 2359304 | tf_op jit(solution)/shard_map/ppermute | solution.py:46
  176.7 19.9 %collective-permute-start.36 = (bf16[768,512]{1,0:T(8,128)(2,1)S(1)}, bf16[768,512]{1,0:T(8,128)(2,1)S(1)}, u32[]{:S(2)}, u32[]{:S(2)}) collective-permute-start(bf16[768,512]{1,0:T(8,128)(2,1)S(1)} %pad_maximum_fusion.11), channel_id=1, source_target_pairs={{0,1},{1,0},{2,3},{3,2},{4,5},{5,4},{6,7},{7,6},{8,9},{9,8},{10,11... | collective-permute-start | bytes 2359304 | tf_op jit(solution)/shard_map/ppermute | solution.py:46
  180.3 26.8 %collective-permute-start.39 = (bf16[256,1536]{1,0:T(8,128)(2,1)S(1)}, bf16[256,1536]{1,0:T(8,128)(2,1)S(1)}, u32[]{:S(2)}, u32[]{:S(2)}) collective-permute-start(bf16[256,1536]{1,0:T(8,128)(2,1)S(1)} %pad_maximum_fusion.10), channel_id=1, source_target_pairs={{0,16},{1,17},{2,18},{3,19},{4,20},{5,21},{6,22},{7,23},{8,24},{9,... | collective-permute-start | bytes 2359304 | tf_op jit(solution)/shard_map/ppermute | solution.py:46
  196.6 27.8 %collective-permute-start.44 = (bf16[384,384]{1,0:T(8,128)(2,1)S(1)}, bf16[384,384]{1,0:T(8,128)(2,1)S(1)}, u32[]{:S(2)}, u32[]{:S(2)}) collective-permute-start(bf16[384,384]{1,0:T(8,128)(2,1)S(1)} %slice.869), channel_id=1, source_target_pairs={{0,8},{1,9},{2,10},{3,11},{4,12},{5,13},{6,14},{7,15},{8,0},{9,1},... | collective-permute-start | bytes 884744 | tf_op jit(solution)/shard_map/ppermute | solution.py:46
  232.7 21.8 %collective-permute-start.48 = (bf16[384,512]{1,0:T(8,128)(2,1)S(1)}, bf16[384,512]{1,0:T(8,128)(2,1)S(1)}, u32[]{:S(2)}, u32[]{:S(2)}) collective-permute-start(bf16[384,512]{1,0:T(8,128)(2,1)S(1)} %get-tuple-element.154), channel_id=1, source_target_pairs={{0,8},{1,9},{2,10},{3,11},{4,12},{5,13},{6,14},{7,15},{8,0},{9,1},... | collective-permute-start | bytes 1179656 | tf_op jit(solution)/shard_map/ppermute | solution.py:46
  272.8 19.7 %collective-permute-start.55 = (bf16[384,512]{1,0:T(8,128)(2,1)S(1)}, bf16[384,512]{1,0:T(8,128)(2,1)S(1)}, u32[]{:S(2)}, u32[]{:S(2)}) collective-permute-start(bf16[384,512]{1,0:T(8,128)(2,1)S(1)} %get-tuple-element.158), channel_id=1, source_target_pairs={{0,8},{1,9},{2,10},{3,11},{4,12},{5,13},{6,14},{7,15},{8,0},{9,1},... | collective-permute-start | bytes 1179656 | tf_op jit(solution)/shard_map/ppermute | solution.py:46
  272.8 22.5 %collective-permute-start.56 = (bf16[768,512]{1,0:T(8,128)(2,1)S(1)}, bf16[768,512]{1,0:T(8,128)(2,1)S(1)}, u32[]{:S(2)}, u32[]{:S(2)}) collective-permute-start(bf16[768,512]{1,0:T(8,128)(2,1)S(1)} %copy-done.70), channel_id=1, source_target_pairs={{0,1},{1,0},{2,3},{3,2},{4,5},{5,4},{6,7},{7,6},{8,9},{9,8},{10,11... | collective-permute-start | bytes 2359304 | tf_op jit(solution)/shard_map/ppermute | solution.py:46
  295.2 20.5 %collective-permute-start.60 = (bf16[128,1536]{1,0:T(8,128)(2,1)S(1)}, bf16[128,1536]{1,0:T(8,128)(2,1)S(1)}, u32[]{:S(2)}, u32[]{:S(2)}) collective-permute-start(bf16[128,1536]{1,0:T(8,128)(2,1)S(1)} %copy-done.51), channel_id=1, source_target_pairs={{0,8},{1,9},{2,10},{3,11},{4,12},{5,13},{6,14},{7,15},{8,0},{9,1},... | collective-permute-start | bytes 1179656 | tf_op jit(solution)/shard_map/ppermute | solution.py:46
  295.3 20.5 %collective-permute-start.64 = (bf16[768,512]{1,0:T(8,128)(2,1)S(1)}, bf16[768,512]{1,0:T(8,128)(2,1)S(1)}, u32[]{:S(2)}, u32[]{:S(2)}) collective-permute-start(bf16[768,512]{1,0:T(8,128)(2,1)S(1)} %pad_maximum_fusion.15), channel_id=1, source_target_pairs={{0,1},{1,0},{2,3},{3,2},{4,5},{5,4},{6,7},{7,6},{8,9},{9,8},{10,11... | collective-permute-start | bytes 2359304 | tf_op jit(solution)/shard_map/ppermute | solution.py:46
  383.8 25.9 %collective-permute-start.81 = (bf16[128,1536]{1,0:T(8,128)(2,1)S(1)}, bf16[128,1536]{1,0:T(8,128)(2,1)S(1)}, u32[]{:S(2)}, u32[]{:S(2)}) collective-permute-start(bf16[128,1536]{1,0:T(8,128)(2,1)S(1)} %fusion.31), channel_id=1, source_target_pairs={{0,8},{1,9},{2,10},{3,11},{4,12},{5,13},{6,14},{7,15},{8,0},{9,1},... | collective-permute-start | bytes 1179656 | tf_op jit(solution)/shard_map/ppermute | solution.py:46
  394.5 40.7 %collective-permute-start.87 = (bf16[768,512]{1,0:T(8,128)(2,1)}, bf16[768,512]{1,0:T(8,128)(2,1)}, u32[]{:S(2)}, u32[]{:S(2)}) collective-permute-start(bf16[768,512]{1,0:T(8,128)(2,1)} %convolution_convert_fusion.17), channel_id=1, source_target_pairs={{0,1},{1,0},{2,3},{3,2},{4,5},{5,4},{6,7},{7,6},{8,9},{9,8},{10,11... | collective-permute-start | bytes 2359304 | tf_op jit(solution)/shard_map/ppermute | solution.py:46
  443.8 23.0 %collective-permute-start.92 = (bf16[768,384]{1,0:T(8,128)(2,1)S(1)}, bf16[768,384]{1,0:T(8,128)(2,1)S(1)}, u32[]{:S(2)}, u32[]{:S(2)}) collective-permute-start(bf16[768,384]{1,0:T(8,128)(2,1)S(1)} %convolution_convert_fusion.20), channel_id=1, source_target_pairs={{0,1},{1,0},{2,3},{3,2},{4,5},{5,4},{6,7},{7,6},{8,9},{9,8},{10,11... | collective-permute-start | bytes 1769480 | tf_op jit(solution)/shard_map/ppermute | solution.py:46
  446.3 20.2 %collective-permute-start.93 = (bf16[384,512]{1,0:T(8,128)(2,1)S(1)}, bf16[384,512]{1,0:T(8,128)(2,1)S(1)}, u32[]{:S(2)}, u32[]{:S(2)}) collective-permute-start(bf16[384,512]{1,0:T(8,128)(2,1)S(1)} %fusion.28), channel_id=1, source_target_pairs={{0,8},{1,9},{2,10},{3,11},{4,12},{5,13},{6,14},{7,15},{8,0},{9,1},... | collective-permute-start | bytes 1179656 | tf_op jit(solution)/shard_map/ppermute | solution.py:46
  460.4 26.9 %collective-permute-start.95 = (bf16[96,1536]{1,0:T(8,128)(2,1)S(1)}, bf16[96,1536]{1,0:T(8,128)(2,1)S(1)}, u32[]{:S(2)}, u32[]{:S(2)}) collective-permute-start(bf16[96,1536]{1,0:T(8,128)(2,1)S(1)} %convolution_convert_fusion.14), channel_id=1, source_target_pairs={{0,1},{1,0},{2,3},{3,2},{4,5},{5,4},{6,7},{7,6},{8,9},{9,8},{10,11... | collective-permute-start | bytes 884744 | tf_op jit(solution)/shard_map/ppermute | solution.py:46
  487.3 20.0 %collective-permute-start.101 = (bf16[256,1536]{1,0:T(8,128)(2,1)S(1)}, bf16[256,1536]{1,0:T(8,128)(2,1)S(1)}, u32[]{:S(2)}, u32[]{:S(2)}) collective-permute-start(bf16[256,1536]{1,0:T(8,128)(2,1)S(1)} %convolution_convert_fusion.5), channel_id=1, source_target_pairs={{0,1},{1,0},{2,3},{3,2},{4,5},{5,4},{6,7},{7,6},{8,9},{9,8},{10,11... | collective-permute-start | bytes 2359304 | tf_op jit(solution)/shard_map/ppermute | solution.py:46
  507.5 24.3 %collective-permute-start.106 = (bf16[768,512]{1,0:T(8,128)(2,1)S(1)}, bf16[768,512]{1,0:T(8,128)(2,1)S(1)}, u32[]{:S(2)}, u32[]{:S(2)}) collective-permute-start(bf16[768,512]{1,0:T(8,128)(2,1)S(1)} %convolution_convert_fusion.16), channel_id=1, source_target_pairs={{0,1},{1,0},{2,3},{3,2},{4,5},{5,4},{6,7},{7,6},{8,9},{9,8},{10,11... | collective-permute-start | bytes 2359304 | tf_op jit(solution)/shard_map/ppermute | solution.py:46
  540.5 22.7 %collective-permute-start.117 = (bf16[384,512]{1,0:T(8,128)(2,1)}, bf16[384,512]{1,0:T(8,128)(2,1)}, u32[]{:S(2)}, u32[]{:S(2)}) collective-permute-start(bf16[384,512]{1,0:T(8,128)(2,1)} %fusion.24), channel_id=1, source_target_pairs={{0,8},{1,9},{2,10},{3,11},{4,12},{5,13},{6,14},{7,15},{8,0},{9,1},... | collective-permute-start | bytes 1179656 | tf_op jit(solution)/shard_map/ppermute | solution.py:46
  540.6 20.3 %collective-permute-start.109 = (bf16[768,512]{1,0:T(8,128)(2,1)}, bf16[768,512]{1,0:T(8,128)(2,1)}, u32[]{:S(2)}, u32[]{:S(2)}) collective-permute-start(bf16[768,512]{1,0:T(8,128)(2,1)} %convolution_convert_fusion.15), channel_id=1, source_target_pairs={{0,1},{1,0},{2,3},{3,2},{4,5},{5,4},{6,7},{7,6},{8,9},{9,8},{10,11... | collective-permute-start | bytes 2359304 | tf_op jit(solution)/shard_map/ppermute | solution.py:46
  542.8 20.4 %collective-permute-start.110 = (bf16[96,1408]{1,0:T(8,128)(2,1)}, bf16[96,1408]{1,0:T(8,128)(2,1)S(1)}, u32[]{:S(2)}, u32[]{:S(2)}) collective-permute-start(bf16[96,1408]{1,0:T(8,128)(2,1)} %get-tuple-element.209), channel_id=1, source_target_pairs={{0,2},{1,3},{2,0},{3,1},{4,6},{5,7},{6,4},{7,5},{8,10},{9,11},{10,... | collective-permute-start | bytes 811016 | tf_op jit(solution)/shard_map/ppermute | solution.py:46
  547.9 20.4 %collective-permute-start.112 = (bf16[96,1408]{1,0:T(8,128)(2,1)}, bf16[96,1408]{1,0:T(8,128)(2,1)}, u32[]{:S(2)}, u32[]{:S(2)}) collective-permute-start(bf16[96,1408]{1,0:T(8,128)(2,1)} %get-tuple-element.211), channel_id=1, source_target_pairs={{0,6},{1,7},{2,4},{3,5},{4,2},{5,3},{6,0},{7,1},{8,14},{9,15},{10,... | collective-permute-start | bytes 811016 | tf_op jit(solution)/shard_map/ppermute | solution.py:46
  589.5 37.9 %collective-permute-start.127 = (bf16[384,512]{1,0:T(8,128)(2,1)}, bf16[384,512]{1,0:T(8,128)(2,1)}, u32[]{:S(2)}, u32[]{:S(2)}) collective-permute-start(bf16[384,512]{1,0:T(8,128)(2,1)} %fusion.20), channel_id=1, source_target_pairs={{0,8},{1,9},{2,10},{3,11},{4,12},{5,13},{6,14},{7,15},{8,0},{9,1},... | collective-permute-start | bytes 1179656 | tf_op jit(solution)/shard_map/ppermute | solution.py:46
  590.3 39.9 %collective-permute-start.136 = (bf16[96,1536]{1,0:T(8,128)(2,1)}, bf16[96,1536]{1,0:T(8,128)(2,1)}, u32[]{:S(2)}, u32[]{:S(2)}) collective-permute-start(bf16[96,1536]{1,0:T(8,128)(2,1)} %convolution_convert_fusion.13), channel_id=1, source_target_pairs={{0,1},{1,0},{2,3},{3,2},{4,5},{5,4},{6,7},{7,6},{8,9},{9,8},{10,11... | collective-permute-start | bytes 884744 | tf_op jit(solution)/shard_map/ppermute | solution.py:46
  631.7 33.8 %collective-permute-start.137 = (bf16[96,1536]{1,0:T(8,128)(2,1)S(1)}, bf16[96,1536]{1,0:T(8,128)(2,1)S(1)}, u32[]{:S(2)}, u32[]{:S(2)}) collective-permute-start(bf16[96,1536]{1,0:T(8,128)(2,1)S(1)} %get-tuple-element.494), channel_id=1, source_target_pairs={{8,0},{9,1},{10,2},{11,3},{12,4},{13,5},{14,6},{15,7},{16,24},{17,... | collective-permute-start | bytes 884744 | tf_op jit(solution)/shard_map/ppermute | solution.py:57
  635.5 21.4 %collective-permute-start.128 = (bf16[384,384]{1,0:T(8,128)(2,1)S(1)}, bf16[384,384]{1,0:T(8,128)(2,1)S(1)}, u32[]{:S(2)}, u32[]{:S(2)}) collective-permute-start(bf16[384,384]{1,0:T(8,128)(2,1)S(1)} %copy-done.84), channel_id=1, source_target_pairs={{0,8},{1,9},{2,10},{3,11},{4,12},{5,13},{6,14},{7,15},{8,0},{9,1},... | collective-permute-start | bytes 884744 | tf_op jit(solution)/shard_map/ppermute | solution.py:46
  652.3 27.1 %collective-permute-start.139 = (bf16[4,96,1024]{2,1,0:T(8,128)(2,1)}, bf16[4,96,1024]{2,1,0:T(8,128)(2,1)}, u32[]{:S(2)}, u32[]{:S(2)}) collective-permute-start(bf16[4,96,1024]{2,1,0:T(8,128)(2,1)} %select_convert_fusion), channel_id=1, source_target_pairs={{0,16},{1,17},{2,18},{3,19},{4,20},{5,21},{6,22},{7,23},{8,24},{9,... | collective-permute-start | bytes 2359304 | tf_op jit(solution)/shard_map/ppermute | solution.py:46
  (244 other events, 2272.2 us)

commit v3 on v2

--- a/solution.py
+++ b/solution.py
@@ -78,6 +78,20 @@
 
 def after(block, *earlier):
     return lax.optimization_barrier((block,) + earlier)[0] if earlier else block
+
+
+class Order:
+    def __init__(self):
+        self.last = ()
+
+    def __call__(self, *blocks):
+        if self.last:
+            blocks = lax.optimization_barrier(tuple(blocks) + self.last)[: len(blocks)]
+        self.last = (blocks[0],)
+        return blocks[0] if len(blocks) == 1 else blocks
+
+    def sent(self, transfer, wire):
+        self.last = (transfer(wire, self.last),)
 
 
 class Wire:
@@ -269,30 +283,40 @@
     return stacked
 
 
-def split_cores(parts, lay, deps=()):
+def split_cores(parts, lay, order):
+    return lay.to_core(order(pick(parts, 1 - lay.core)))
+
+
+def core_layers(parts, other, lay):
     kept = pick(parts, lay.core)
-    other = lay.to_core(after(pick(parts, 1 - lay.core), *deps))
     return jnp.where(lay.core == 0, kept, other), jnp.where(lay.core == 0, other, kept)
 
 
-def swap_columns(parts, lay, deps=()):
-    sent = [after(pick(parts, lay.member ^ step), *deps) for step in range(1, lay.group)]
-    others = [lay.to_member(block, step) for step, block in enumerate(sent, 1)]
-    placed = place(pick(parts, lay.member), others, lay.member)
-    return placed.reshape(-1, parts.shape[-1]), sent[-1]
+def to_members(parts, lay, order):
+    sent = order(*[pick(parts, lay.member ^ step) for step in range(1, lay.group)])
+    sent = sent if isinstance(sent, (tuple, list)) else (sent,)
+    return [lay.to_member(block, step) for step, block in enumerate(sent, 1)]
+
+
+def listed(blocks):
+    return list(blocks) if isinstance(blocks, (tuple, list)) else [blocks]
+
+
+def member_rows(parts, others, lay):
+    return place(pick(parts, lay.member), others, lay.member).reshape(-1, parts.shape[-1])
 
 
 class Spread:
     def __init__(self, block):
         self.block = block
 
-    def over_half(self, wire, deps=()):
-        self.got, sent = wire.send(self.block, deps)
+    def over_half(self, wire, deps=(), **how):
+        self.got, sent = wire.send(self.block, deps, **how)
         return sent
 
-    def over_shard(self, wire, deps=()):
+    def over_shard(self, wire, deps=(), **how):
         self.pair = jnp.concatenate([self.block, after(self.got, *deps)], 0)
-        self.got, sent = wire.send(self.pair)
+        self.got, sent = wire.send(self.pair, **how)
         return sent
 
     def full(self):
@@ -321,19 +345,13 @@
         return self.kept + after(self.arrived, *deps).astype(F32)
 
 
-def return_columns(parts, lay, deps):
-    others = [
-        lay.to_member(after(pick(parts, lay.member ^ step).astype(BF16), *deps), step)
-        for step in range(1, lay.group)
-    ]
-    placed = place(pick(parts, lay.member), [block.astype(F32) for block in others], lay.member)
-    return placed, others
-
-
-def join_cores(first, second, lay):
-    kept = jnp.where(lay.core == 0, first, second)
-    sent = jnp.where(lay.core == 0, second, first).astype(BF16)
-    return two_way(lay.core, kept, lay.to_core(sent).astype(F32), 0)
+def join_cores(first, second, lay, order):
+    sent = order(jnp.where(lay.core == 0, second, first).astype(BF16))
+    return jnp.where(lay.core == 0, first, second), lay.to_core(sent)
+
+
+def joined_cores(pair, lay, order):
+    return two_way(lay.core, pair[0], order(pair[1]).astype(F32), 0)
 
 
 def out_aligned(lay, block_rows):
@@ -341,15 +359,19 @@
 
 
 class SpreadOut:
-    def __init__(self, w_out, lay, deps):
+    def __init__(self, w_out, lay, order):
         self.lay, self.width = lay, w_out.shape[-1]
         self.aligned = out_aligned(lay, w_out.shape[0])
         if not self.aligned:
             w_out = lax.all_gather(w_out, ("ctx", "shard"), axis=0, tiled=True)
-        w_out = after(w_out, *deps)
-        other = lay.to_core(w_out)
-        layers = [jnp.where(lay.core == 0, w_out, other), jnp.where(lay.core == 0, other, w_out)]
-        self.block = jnp.stack(layers)
+        self.own = w_out
+        self.got = lay.to_core(order(w_out))
+
+    def stack(self, order):
+        lay, other = self.lay, order(self.got)
+        self.block = jnp.stack(
+            [jnp.where(lay.core == 0, self.own, other), jnp.where(lay.core == 0, other, self.own)]
+        )
 
     def over_half(self, wire, deps=()):
         lay = self.lay
@@ -379,25 +401,30 @@
         return lax.dynamic_slice_in_dim(self.block, head * count, count, 1)
 
 
+def out_pair(which, spread_out):
+    return mm_nt(joined(which.attn_out), spread_out).astype(BF16), joined(which.mid_low)
+
+
 class CollectOut:
-    def __init__(self, left, right, lay, block_rows):
-        self.left, self.right, self.lay = left, right, lay
+    def __init__(self, pairs, lay, block_rows):
+        self.pairs, self.lay = pairs, lay
         self.aligned = out_aligned(lay, block_rows)
-        self.rows = left.shape[1] // 2
+        self.rows = pairs[0][0].shape[1] // 2
 
     def over_shard(self, wire, deps=(), **how):
         if not self.aligned:
-            self.kept = mm_tn(self.left, self.right)
+            self.kept = jnp.stack([mm_tn(left, right) for left, right in self.pairs])
             return self.kept
-        block = mm_tn(self.left[:, self.rows :], self.right).astype(BF16)
-        self.got, sent = wire.send(block, deps, **how)
+        blocks = [mm_tn(left[:, self.rows :], right).astype(BF16) for left, right in self.pairs]
+        self.got, sent = wire.send(jnp.concatenate(blocks, 0), deps, **how)
         return sent
 
     def over_half(self, wire, deps=(), **how):
         lay = self.lay
         if not self.aligned:
             return self.kept
-        self.kept = mm_tn(self.left[:, : self.rows], self.right) + after(self.got, *deps).astype(F32)
+        blocks = [mm_tn(left[:, : self.rows], right) for left, right in self.pairs]
+        self.kept = jnp.concatenate(blocks, 0) + after(self.got, *deps).astype(F32)
         move = lambda block: lay.move_some(
             block,
             lambda core, half, member, shard: half != core,
@@ -407,7 +434,10 @@
         return sent
 
     def total(self, deps=()):
-        return self.kept + after(self.arrived, *deps).astype(F32) if self.aligned else self.kept
+        if not self.aligned:
+            return self.kept[0], self.kept[1]
+        total = self.kept + after(self.arrived, *deps).astype(F32)
+        return total[: self.rows], total[self.rows :]
 
 
 def join_out(first, second, lay, block_rows):
@@ -458,53 +488,32 @@
     return jnp.concatenate([block[:, i * LANES : (i + 1) * LANES] for i in range(count)], 0)
 
 
-def project_kernel(n_query, n_key, x, w, cos_t, sin_t, out):
-    cos_v, sin_v = cos_t[...], sin_t[...]
-    xv = x[...]
-    step = 2 * LANES
-    for first in range(0, out.shape[1], step):
-        raw = mm(xv, w[:, first : first + step])
-        for lane in range(first, first + step, LANES):
-            block = raw[:, lane - first : lane - first + LANES]
-            if lane < (n_query + n_key) * LANES:
-                block = rot(block, cos_v, sin_v)
-            out[:, lane : lane + LANES] = block.astype(BF16)
-
-
-def project(normed, qkv_w, cos_t, sin_t, n_query, n_key):
-    rows = normed.shape[0]
-    if (n_query + 2 * n_key) % 2:
-        qkv_w = jnp.pad(qkv_w, ((0, 0), (0, LANES)))
-    out = pl.pallas_call(
-        lambda *refs: project_kernel(n_query, n_key, *refs),
-        out_shape=jax.ShapeDtypeStruct((rows, qkv_w.shape[1]), BF16),
-        compiler_params=VMEM_LIMIT,
-        cost_estimate=pl.CostEstimate(
-            flops=2 * rows * qkv_w.shape[0] * qkv_w.shape[1],
-            bytes_accessed=2 * qkv_w.shape[0] * qkv_w.shape[1],
-            transcendentals=0,
-        ),
-        name="project",
-    )(normed, qkv_w, cos_t, sin_t)
-    return out[:, : (n_query + 2 * n_key) * LANES]
-
-
 def lanes_of(index, count=1):
     return slice(index * LANES, (index + count) * LANES)
 
 
-def attend_kernel(n_query, n_key, own, sib, pos_q, pos_k, out_own, out_sib, lse_out):
+def attend_kernel(
+    n_query, n_key, raw_own, raw_sib, cos_t, sin_t, pos_q, pos_k, out_own, out_sib, lse_out, own, sib
+):
     scale = HEAD_DIM ** (-0.5)
     per_key = n_query // n_key
-    half = own.shape[0]
+    half = raw_own.shape[0]
     rows = 2 * half
+    cos_v, sin_v = cos_t[...], sin_t[...]
     mask = pos_q[...] >= pos_k[...]
     mask = jnp.concatenate([mask] * per_key, 0)
+
+    def both(index, turned):
+        block = jnp.concatenate([raw_own[:, lanes_of(index)], raw_sib[:, lanes_of(index)]], 0)
+        block = (rot(block, cos_v, sin_v) if turned else block).astype(BF16)
+        own[:, lanes_of(index)] = block[:half]
+        sib[:, lanes_of(index)] = block[half:]
+        return block
+
     for kv_head in range(n_key):
-        both = lambda index: jnp.concatenate([own[:, lanes_of(index)], sib[:, lanes_of(index)]], 0)
-        key, value = both(n_query + kv_head), both(n_query + n_key + kv_head)
+        key, value = both(n_query + kv_head, True), both(n_query + n_key + kv_head, False)
         q_first = kv_head * per_key
-        query = jnp.concatenate([both(q_first + i) for i in range(per_key)], 0)
+        query = jnp.concatenate([both(q_first + i, True) for i in range(per_key)], 0)
         scores = jnp.where(mask, mm_nt(query, key) * scale, MASK_FILL)
         row_max = jnp.max(scores, -1, keepdims=True)
         weights = jnp.exp(scores - row_max)
@@ -517,23 +526,25 @@
         lse_out[kv_head] = row_max + jnp.log(total)
 
 
-def attend(own, sib, pos_q, pos_k, n_query, n_key):
-    half = own.shape[0]
+def attend(raw_own, raw_sib, tables, n_query, n_key):
+    half, lanes = raw_own.shape
     return pl.pallas_call(
         lambda *refs: attend_kernel(n_query, n_key, *refs),
         out_shape=[
             jax.ShapeDtypeStruct((half, n_query * LANES), BF16),
             jax.ShapeDtypeStruct((half, n_query * LANES), BF16),
             jax.ShapeDtypeStruct((n_key, n_query // n_key * 2 * half, 1), F32),
+            jax.ShapeDtypeStruct((half, lanes), BF16),
+            jax.ShapeDtypeStruct((half, lanes), BF16),
         ],
         compiler_params=VMEM_LIMIT,
         cost_estimate=pl.CostEstimate(
             flops=16 * n_query * half * half * LANES,
-            bytes_accessed=half * n_query * LANES * 8,
+            bytes_accessed=half * n_query * LANES * 24,
             transcendentals=4 * n_query * half * half,
         ),
         name="attend",
-    )(own, sib, pos_q, pos_k)
+    )(raw_own, raw_sib, *tables)
 
 
 def attend_back_kernel(
@@ -636,37 +647,38 @@
 
 
 class Layer:
-    def __init__(self, lay, tables, n_query, n_key, gain_one, gain_two, qkv_w, out_w):
+    def __init__(self, lay, tables, n_query, n_key, gain_one, gain_two, order):
+        self.order = order
         self.lay, self.tables, self.n_query, self.n_key = lay, tables, n_query, n_key
         self.gain_one, self.gain_two = gain_one, gain_two
-        self.qkv_w, self.out_w = qkv_w, out_w
-
-    def start(self, inputs, meanwhile=no_round):
+
+    def normed_rows(self, inputs):
         self.inputs = inputs
         normed, self.inverse_first = norm_forward(inputs, self.gain_one)
-        self.normed = gather_rows(relative(normed, self.lay), self.lay, meanwhile)
+        return self.order(normed, self.lay)
+
+    def start(self, inputs, meanwhile=no_round):
+        self.normed = gather_rows(self.normed_rows(inputs), self.lay, meanwhile)
+
+    def attend(self):
+        lay = self.lay
+        raw = [mm(block, self.qkv_w) for block in self.normed]
+        out_own, out_sib, lse, own, sib = attend(*raw, self.tables, self.n_query, self.n_key)
+        self.attn_kept = own, sib, lse
+        self.attn_out = [out_order(block, lay, self.n_query) for block in (out_own, out_sib)]
 
     def attention(self, during_out=no_round, during_rows=no_round):
         lay = self.lay
-        cos_own, sin_own, cos_sib, sin_sib, pos_q, pos_k = self.tables
-        heads = self.n_query, self.n_key
-        own = project(self.normed[0], self.qkv_w, cos_own, sin_own, *heads)
-        sib = project(self.normed[1], self.qkv_w, cos_sib, sin_sib, *heads)
-        out_own, out_sib, lse = attend(own, sib, pos_q, pos_k, *heads)
-        self.attn_kept = own, sib, lse
-        self.attn_out = [out_order(block, lay, self.n_query) for block in (out_own, out_sib)]
         partial = [mm(block, self.out_w) for block in self.attn_out]
         self.mid_stream = self.inputs + scatter_rows(*partial, lay, during_out)
         normed, self.inverse_second = norm_forward(self.mid_stream, self.gain_two)
-        self.normed_mid = gather_rows(relative(normed, lay), lay, during_rows)
+        self.normed_mid = gather_rows(self.order(normed, lay), lay, during_rows)
 
     def hide(self):
         lay = self.lay
         self.gate_up, self.hidden = [], []
         for block in self.normed_mid:
-            pre = mm(block, self.gate_up_w)
-            ff = pre.shape[1] // 2
-            gate_pre, up_pre = pre[:, :ff], pre[:, ff:]
+            gate_pre, up_pre = mm(block, self.gate_w), mm(block, self.up_w)
             self.gate_up.append((gate_pre, up_pre))
             self.hidden.append(relative((jax.nn.silu(gate_pre) * up_pre).astype(BF16), lay))
 
@@ -680,7 +692,7 @@
         self.down_in = gather_rows(out_grad.astype(BF16), self.lay, meanwhile)
 
     def feed_forward_back(self):
-        self.gate_up_grad, partial = [], []
+        self.gate_grad, self.up_grad, partial = [], [], []
         for block, (gate_pre, up_pre) in zip(self.down_in, self.gate_up):
             hidden_grad = relative(mm_nt(block, self.down_w), self.lay)
             sigmoid_gate = jax.nn.sigmoid(gate_pre)
@@ -688,9 +700,9 @@
                 hidden_grad * up_pre * sigmoid_gate * (1.0 + gate_pre * (1.0 - sigmoid_gate))
             ).astype(BF16)
             up_grad_in = (hidden_grad * gate_pre * sigmoid_gate).astype(BF16)
-            both = jnp.concatenate([gate_grad_in, up_grad_in], 1)
-            self.gate_up_grad.append(both)
-            partial.append(mm_nt(both, self.gate_up_w))
+            self.gate_grad.append(gate_grad_in)
+            self.up_grad.append(up_grad_in)
+            partial.append(mm_nt(gate_grad_in, self.gate_w) + mm_nt(up_grad_in, self.up_w))
         return partial
 
     def middle_back(self, partial, during_sum=no_round, during_rows=no_round):
@@ -703,14 +715,11 @@
         self.mid_low = gather_rows(self.mid_grad.astype(BF16), lay, during_rows)
 
     def attention_back(self):
-        cos_own, sin_own, cos_sib, sin_sib, pos_q, pos_k = self.tables
         grads = [
             out_order(mm_nt(block, self.out_w).astype(BF16), self.lay, self.n_query)
             for block in self.mid_low
         ]
-        cos_t, sin_t = jnp.concatenate([cos_own, cos_sib]), jnp.concatenate([sin_own, sin_sib])
-        tables = cos_t, sin_t, pos_q, pos_k
-        self.lows = attend_back(self.attn_kept, grads, tables, self.n_query, self.n_key)
+        self.lows = attend_back(self.attn_kept, grads, self.tables, self.n_query, self.n_key)
         return [mm_nt(block, self.qkv_w) for block in self.lows]
 
     def finish_back(self, partial, meanwhile=no_round):
@@ -725,17 +734,6 @@
 
 def joined(pair):
     return jnp.concatenate(pair, 0)
-
-
-def gain_sums(gains, lay):
-    own = pick(gains, lay.core) + lay.to_core(pick(gains, 1 - lay.core))
-    parts = own.reshape(2, lay.shards, lay.halves, lay.group, -1).transpose(1, 2, 3, 0, 4)
-    parts = pick(parts, lay.shard) + lay.to_shard(pick(parts, 1 - lay.shard))
-    parts = pick(parts, lay.half) + lay.to_half(pick(parts, 1 - lay.half))
-    total = pick(parts, lay.member)
-    for step in range(1, lay.group):
-        total = total + lay.to_member(pick(parts, lay.member ^ step), step)
-    return total
 
 
 def row_tables(pair_table, block_rows, lay):
@@ -756,40 +754,38 @@
     cos_h, sin_h = jnp.pad(jnp.cos(angles), pad), jnp.pad(jnp.sin(angles), pad)
     cos_t = jnp.concatenate([cos_h, cos_h], 1)
     sin_t = jnp.concatenate([-sin_h, sin_h], 1)
-    count = cores[0].shape[0]
-    return (
-        cos_t[:count],
-        sin_t[:count],
-        cos_t[count:],
-        sin_t[count:],
-        positions[:, None],
-        positions[None, :],
-    )
-
-
-def deal_rows(local, lay):
+    return cos_t, sin_t, positions[:, None], positions[None, :]
+
+
+def deal_rows(local, lay, order):
     turn = lay.half ^ lay.core
+    sent = order(pick(local, turn), pick(local, 1 - turn))
     straight = lay.move(
-        pick(local, turn), lambda core, half, member, shard: (half, half ^ core, member, shard)
+        sent[0], lambda core, half, member, shard: (half, half ^ core, member, shard)
     )
     crossed = lay.move(
-        pick(local, 1 - turn),
-        lambda core, half, member, shard: (half, 1 - (half ^ core), member, shard),
+        sent[1], lambda core, half, member, shard: (half, 1 - (half ^ core), member, shard)
     )
+    return straight, crossed
+
+
+def dealt(straight, crossed, lay):
+    turn = lay.half ^ lay.core
     return jnp.where(turn == 0, straight, crossed), jnp.where(turn == 0, crossed, straight)
 
 
-def return_rows(input_grad, outputs, lay):
+def return_rows(input_grad, outputs, lay, order):
     turn = lay.half ^ lay.core
+    sent = order(
+        jnp.where(turn == 0, input_grad, outputs), jnp.where(turn == 0, outputs, input_grad)
+    )
     straight = lay.move(
-        jnp.where(turn == 0, input_grad, outputs),
-        lambda core, half, member, shard: (core ^ half, core, member, shard),
+        sent[0], lambda core, half, member, shard: (core ^ half, core, member, shard)
     )
     crossed = lay.move(
-        jnp.where(turn == 0, outputs, input_grad),
-        lambda core, half, member, shard: (1 - (core ^ half), core, member, shard),
+        sent[1], lambda core, half, member, shard: (1 - (core ^ half), core, member, shard)
     )
-    return two_way(turn, straight, crossed, 0)
+    return straight, crossed
 
 
 def body(
@@ -810,82 +806,107 @@
     cols = q_cols + 2 * k_cols
     ff = ff_unit * 4
 
+    order = Order()
     gains = jnp.stack([norm_attn[0], norm_mlp[0]])
     gain_parts = [lay.to_member(gains, step) for step in range(1, lay.group)]
     heads = pack_heads(w_query[0], w_key[0], w_value[0], lay)
-    qkv_layers = split_cores(heads, lay)
-    qkv_first, begun = swap_columns(qkv_layers[0], lay, gain_parts)
-    gains = place(gains, gain_parts, lay.member)
-    gains = two_way(lay.half, gains, lay.to_half(after(gains, begun)), 0)
-    qkv_0 = Spread(qkv_first)
-    sent = qkv_0.over_half(over_half, (gains,))
-    gains = two_way(lay.shard, gains, lay.to_shard(after(gains, sent)), 0)
-    local = to_inner(after(ends_in, begun)[0, :, 0], lay)
-    own_in, own_cot = deal_rows(after(local, sent), lay)
-    gains = two_way(lay.core, gains, lay.to_core(gains), 0)
+    heads_other = split_cores(heads, lay, order)
+    heads_other, *gain_parts = order(heads_other, *gain_parts)
+    qkv_layers = core_layers(heads, heads_other, lay)
+    qkv_others = to_members(qkv_layers[0], lay, order)
+    gains = order(place(gains, gain_parts, lay.member))
+    gains_other = lay.to_half(gains)
+    w_gate, w_up = order(w_gate, w_up)
+    gate_up_own = pack_ff(w_gate[0], w_up[0], lay, ff_unit)
+    gate_up_other = split_cores(gate_up_own, lay, order)
+    qkv_0 = Spread(member_rows(qkv_layers[0], listed(order(*qkv_others)), lay))
+    order.sent(qkv_0.over_half, over_half)
+    gains = order(two_way(lay.half, gains, order(gains_other), 0))
+    gains_other = lay.to_shard(gains)
+    arrived = deal_rows(to_inner(order(ends_in)[0, :, 0], lay), lay, order)
+    gains = order(two_way(lay.shard, gains, order(gains_other), 0))
+    gains_other = lay.to_core(gains)
+    out = SpreadOut(to_inner(order(w_out)[0], lay), lay, order)
+    tables = row_tables(order(pair_table), rows // 2, lay)
+    gains = two_way(lay.core, gains, order(gains_other), 0)
     gains = gains.transpose(0, 4, 1, 2, 3, 5).reshape(2, 2, -1).astype(F32)
-    w_gate, w_up, w_out, w_down = (after(block, begun) for block in (w_gate, w_up, w_out, w_down))
-    gate_up_layers = split_cores(pack_ff(w_gate[0], w_up[0], lay, ff_unit), lay, (sent,))
-    rest = jnp.concatenate([gate_up_layers[0], qkv_layers[1], gate_up_layers[1]], -1)
-    rest, rest_sent = swap_columns(rest, lay, (own_in, own_cot))
-    out = SpreadOut(to_inner(w_out[0], lay), lay, (rest_sent,))
-    down_layers = split_cores(
-        to_inner(w_down[0], lay).reshape(lay.cores, ff_unit, width), lay, (rest_sent,)
-    )
-    tables = row_tables(after(pair_table, begun), rows // 2, lay)
-    gate_0, up_0 = Spread(rest[:, :ff]), Spread(rest[:, ff : 2 * ff])
-    qkv_1 = Spread(rest[:, 2 * ff : 2 * ff + cols])
-    gate_1 = Spread(rest[:, 2 * ff + cols : 3 * ff + cols])
-    up_1 = Spread(rest[:, 3 * ff + cols :])
-    down_0, down_1 = Spread(down_layers[0]), Spread(down_layers[1])
-    out.over_half(over_half)
-    qkv_0.over_shard(over_shard)
-    gate_0.over_half(over_half)
-    out.over_shard(over_shard)
+
+    def layer(index, which):
+        heads = n_query, n_key, gains[index, 0], gains[index, 1]
+        return Layer(lay, tables, *heads, which)
+
+    first, second = layer(0, relative), layer(1, relative)
+    out.stack(order)
+    own_in, own_cot = dealt(*order(*arrived), lay)
+    block = order(first.normed_rows(own_in.astype(F32)))
+    others = [lay.to_member(block, step) for step in range(1, lay.group)]
+    qkv_0.got = order(qkv_0.got)
+    order.sent(qkv_0.over_shard, over_shard)
+    order.sent(out.over_half, over_half)
+    down_own = to_inner(order(w_down)[0], lay).reshape(lay.cores, ff_unit, width)
+    down_other = split_cores(down_own, lay, order)
+    own = order(jnp.concatenate([block] + listed(order(*others)), 0))
+    first.normed = own, lay.to_core(own)
+    gate_up_layers = core_layers(gate_up_own, order(gate_up_other), lay)
+    gate_up_others = to_members(gate_up_layers[0], lay, order)
+    if out.aligned:
+        out.got = order(out.got)
+    order.sent(out.over_shard, over_shard)
+    qkv_0.got = order(qkv_0.got)
 
     def round_of(halves, shards):
         def run(arrived):
-            sent = [item.over_half(over_half, arrived) for item in halves]
-            return sent + [item.over_shard(over_shard, arrived) for item in shards]
+            sent = []
+            for order, item in enumerate(halves):
+                sent.append(item.over_half(over_half, arrived, beside=order > 0))
+            for order, item in enumerate(shards):
+                sent.append(item.over_shard(over_shard, arrived, beside=order > 0))
+            return sent
 
         return run
 
-    def layer(index, qkv, out_w):
-        return Layer(
-            lay,
-            tables,
-            n_query,
-            n_key,
-            gains[index, 0],
-            gains[index, 1],
-            mm(qkv.full(), spread_lanes).astype(BF16),
-            mm_tn(spread_out, out_w).astype(BF16),
-        )
-
+    def attention_weights(which, qkv, out_w):
+        which.qkv_w = mm(qkv.full(), spread_lanes).astype(BF16)
+        which.out_w = mm_tn(spread_out, out_w).astype(BF16)
+
+    first.qkv_w = mm(qkv_0.full(), spread_lanes).astype(BF16)
+    first.attend()
+    gate_up_others = listed(order(*gate_up_others))
+    gate_up = member_rows(gate_up_layers[0], gate_up_others, lay)
+    gate_0, up_0 = Spread(gate_up[:, :ff]), Spread(gate_up[:, ff:])
+    order.sent(gate_0.over_half, over_half)
+    down_layers = core_layers(down_own, order(down_other), lay)
+    down_0, down_1 = Spread(down_layers[0]), Spread(down_layers[1])
+    order.last = (first.attn_out[0],)
+    rest = jnp.concatenate([qkv_layers[1], gate_up_layers[1]], -1)
+    rest_others = to_members(rest, lay, order)
+    if out.aligned:
+        out.got = order(out.got)
     out_w = out.full()
-    first = layer(0, qkv_0, out_w[0])
-    first.start(own_in.astype(F32))
+    first.out_w = mm_tn(spread_out, out_w[0]).astype(BF16)
+    rest = member_rows(rest, listed(order(*rest_others)), lay)
+    qkv_1, gate_up_1 = Spread(rest[:, :cols]), Spread(rest[:, cols:])
+    first.attn_out = [after(block, *order.last) for block in first.attn_out]
     first.attention(round_of([up_0], [gate_0]), round_of([down_0], [up_0]))
-    first.gate_up_w = jnp.concatenate([gate_0.full(), up_0.full()], 1)
+    first.gate_w, first.up_w = gate_0.full(), up_0.full()
     down_0.over_shard(over_shard)
     qkv_1.over_half(over_half, (up_0.got,))
+    gate_up_1.over_half(over_half, (up_0.got,), beside=True)
     first.down_w = down_0.full()
     first.hide()
-    first_out = first.feed_forward(round_of([gate_1], [qkv_1]))
-    second = layer(1, qkv_1, out_w[1])
-    second.start(first_out.astype(BF16).astype(F32), round_of([up_1], [gate_1]))
-    second.start_back(own_cot.astype(F32))
-    second.attention(round_of([down_1], [up_1]), round_of([], [down_1]))
-    second.gate_up_w = jnp.concatenate([gate_1.full(), up_1.full()], 1)
+    first_out = first.feed_forward(round_of([], [qkv_1]))
+    second.start(first_out.astype(BF16).astype(F32), round_of([down_1], [gate_up_1]))
+    second.start_back(after(own_cot, second.normed[0]).astype(F32))
+    attention_weights(second, qkv_1, out_w[1])
+    second.attend()
+    second.attention(round_of([], [down_1]))
+    both = gate_up_1.full()
+    second.gate_w, second.up_w = both[:, :ff], both[:, ff:]
     second.down_w = down_1.full()
 
     def gate_up_collects(which):
-        left, right = joined(which.normed_mid), joined(which.gate_up_grad)
-        return Collect(left, right[:, :ff]), Collect(left, right[:, ff:])
-
-    def out_collect(which):
-        left = mm_nt(joined(which.attn_out), spread_out).astype(BF16)
-        return CollectOut(left, joined(which.mid_low), lay, row_block)
+        left = joined(which.normed_mid)
+        return Collect(left, joined(which.gate_grad)), Collect(left, joined(which.up_grad))
 
     def qkv_collect(which):
         low = mm_nt(joined(which.lows), spread_lanes).astype(BF16)
@@ -896,52 +917,72 @@
     second_out = second.feed_forward(round_of([], [down_1]))
     partial = second.feed_forward_back()
     partial[0] = after(partial[0], second_out)
-    gate_1, up_1 = gate_up_collects(second)
-    second.middle_back(partial, round_of([down_1], [gate_1]), round_of([gate_1], [up_1]))
-    out_1 = out_collect(second)
+    grads = [jnp.concatenate(pair, 1) for pair in zip(second.gate_grad, second.up_grad)]
+    gate_up_1 = Collect(joined(second.normed_mid), joined(grads))
+    second.middle_back(partial, round_of([down_1], [gate_up_1]))
     partial = second.attention_back()
     qkv_1 = qkv_collect(second)
-
-    def last_of_second(arrived):
-        sent = [qkv_1.over_shard(over_shard, arrived)]
-        sent.append(out_1.over_shard(over_shard, arrived, beside=True))
-        return sent + [up_1.over_half(over_half, arrived)]
-
-    second_grad = second.finish_back(partial, last_of_second)
-
-    first.start_back(second_grad.astype(BF16).astype(F32), round_of([qkv_1], []))
+    second_grad = second.finish_back(partial, round_of([gate_up_1], [qkv_1]))
+
+    first.start_back(second_grad.astype(BF16).astype(F32))
     down_0 = Collect(joined(first.hidden), joined(first.down_in))
     partial = first.feed_forward_back()
     partial[0] = after(partial[0], down_0.over_shard(over_shard))
     gate_0, up_0 = gate_up_collects(first)
-    first.middle_back(partial, round_of([out_1, down_0], [gate_0]), round_of([gate_0], [up_0]))
-    out_0 = out_collect(first)
-    parts = [gate_1.total(), up_1.total(), qkv_1.total()]
-    parts = jnp.concatenate(parts, 1).reshape(lay.group, row_block, -1)
-    back_1, sent = return_columns(parts, lay, (first.mid_low[1],))
+    first.middle_back(partial, round_of([qkv_1], [gate_0]), round_of([down_0], [up_0]))
     partial = first.attention_back()
     qkv_0 = qkv_collect(first)
-    partial[1] = after(partial[1], qkv_0.over_shard(over_shard), *sent)
-    first_grad = first.finish_back(partial, round_of([up_0], [out_0]))
-    last = qkv_0.over_half(over_half)
-    out_0.over_half(over_half, beside=True)
-
-    def member_parts(blocks, deps):
-        parts = jnp.concatenate([block.total(deps) for block in blocks], 1)
-        return parts.reshape(lay.group, row_block, -1)
-
-    back_0, sent = return_columns(member_parts([gate_0, up_0], sent), lay, ())
-    back_q, sent = return_columns(member_parts([qkv_0], sent), lay, ())
-    first_w = back_q, out_0.total(sent), back_0, down_0.total(sent)
-    second_w = back_1[..., 2 * ff :], out_1.total(sent), back_1[..., : 2 * ff], down_1.total(sent)
-    first_gains, second_gains = first.gain_grads, second.gain_grads
-    gain_g = gain_sums(jnp.stack([first_gains, second_gains]), lay)
-    ends = to_outer(return_rows(first_grad.astype(BF16), second_out.astype(BF16), lay), lay)
-
-    qkv_g = unpack_heads(join_cores(first_w[0], second_w[0], lay), lay)
-    out_g = to_outer(join_out(first_w[1], second_w[1], lay, row_block), lay)
-    gate_up_g = unpack_ff(join_cores(first_w[2], second_w[2], lay), lay, ff_unit)
-    down_g = to_outer(join_cores(first_w[3], second_w[3], lay).reshape(-1, width), lay)
+    last = [gate_0.over_half(over_half, (first.lows[0],))]
+    last.append(up_0.over_half(over_half, (first.lows[0],), beside=True))
+    partial[1] = after(partial[1], *last)
+    first_grad = first.finish_back(partial)
+
+    def by_member(*blocks):
+        return jnp.concatenate(blocks, 1).reshape(lay.group, row_block, -1)
+
+    out_both = CollectOut([out_pair(which, spread_out) for which in (first, second)], lay, row_block)
+    order = Order()
+    order.last = (first_grad,)
+    gains, gains_other = jnp.stack([first.gain_grads, second.gain_grads]), None
+    gains_other = lay.to_core(order(pick(gains, 1 - lay.core)))
+    arrived = return_rows(first_grad.astype(BF16), second_out.astype(BF16), lay, order)
+    gains = pick(gains, lay.core) + order(gains_other)
+    gains = gains.reshape(2, lay.shards, lay.halves, lay.group, -1).transpose(1, 2, 3, 0, 4)
+    gains_other = lay.to_shard(order(pick(gains, 1 - lay.shard)))
+    order.sent(qkv_0.over_shard, over_shard)
+    down_join = join_cores(down_0.total(order.last), down_1.total(order.last), lay, order)
+    straight, crossed = order(*arrived)
+    ends = two_way(lay.half ^ lay.core, straight, crossed, 0)
+    mlp = [block.total(order.last) for block in (gate_up_1, qkv_1, gate_0, up_0)]
+    mlp = by_member(*mlp)
+    others = to_members(mlp.astype(BF16), lay, order)
+    gains = pick(gains, lay.shard) + order(gains_other)
+    gains_other = lay.to_half(order(pick(gains, 1 - lay.half)))
+    qkv_0.got = order(qkv_0.got)
+    order.sent(qkv_0.over_half, over_half)
+    order.sent(out_both.over_shard, over_shard)
+    down_join = joined_cores(down_join, lay, order)
+    others = listed(order(*others))
+    back = place(pick(mlp, lay.member), [block.astype(F32) for block in others], lay.member)
+    ff_join = join_cores(back[..., cols + 2 * ff :], back[..., : 2 * ff], lay, order)
+    gains = pick(gains, lay.half) + order(gains_other)
+    mlp = by_member(qkv_0.total(order.last))
+    others = to_members(mlp.astype(BF16), lay, order)
+    gain_g = pick(gains, lay.member)
+    gain_others = to_members(gains, lay, order)
+    if out_both.aligned:
+        out_both.got = order(out_both.got)
+    order.sent(out_both.over_half, over_half)
+    gate_up_g = unpack_ff(joined_cores(ff_join, lay, order), lay, ff_unit)
+    others = listed(order(*others))
+    back_0 = place(pick(mlp, lay.member), [block.astype(F32) for block in others], lay.member)
+    qkv_join = join_cores(back_0, back[..., 2 * ff : 2 * ff + cols], lay, order)
+    for block in listed(order(*gain_others)):
+        gain_g = gain_g + block
+    qkv_g = unpack_heads(joined_cores(qkv_join, lay, order), lay)
+    out_g = to_outer(join_out(*out_both.total(order.last), lay, row_block), lay)
+    down_g = to_outer(down_join.reshape(-1, width), lay)
+    ends = to_outer(ends, lay)
     return (
         ends[None, :, None],
         gain_g[0][None],

time: 698 us -> 647 us (0.927)
  waiting for transfers between devices: 299 us -> 278 us
  other arithmetic: 82.3 us -> 63.5 us
  matrix products: 49.2 us -> 67 us
  Pallas kernels: 53.5 us -> 42 us
  starting transfers between devices: 162 us -> 155 us
    ppermute x138 -> x133, waiting for transfers between devices: 288 us -> 266 us  [move(): return lax.ppermute(block, MESH_AXES, pairs)]
    concatenate x5 -> x4, other arithmetic: 19.6 us -> 2.88 us  [the longest x1 1.72 us: full(): return jnp.concatenate([self.pair, self.got], 0)]
    pallas_call x4 -> x0, Pallas kernels: 12.2 us -> none  [project(): pl.pallas_call(lambda *refs: project_kernel(n_query, n_key, *refs), out_s...]
    ppermute x138 -> x133, starting transfers between devices: 158 us -> 148 us  [move(): return lax.ppermute(block, MESH_AXES, pairs)]
    dot_general x14 -> x22, matrix products: 13.1 us -> 22.4 us  [mm(): lax.dot_general(a, b, (((1,), (0,)), ((), ())), preferred_element_type=F32)]
    dot_general x22 -> x20, matrix products: 19.2 us -> 24.2 us  [mm_tn(): lax.dot_general(a, b, (((0,), (0,)), ((), ())), preferred_element_type=F32)]
    dot_general x20 -> x24, matrix products: 16.9 us -> 20.4 us  [mm_nt(): lax.dot_general(a, b, (((1,), (1,)), ((), ())), preferred_element_type=F32)]
    unnamed x283 -> x239, local copies, waits for them, and re-layouts: 15.7 us -> 14.8 us
  transfers between devices with their start and end apart: 141 -> 135, of which waited for: 64 -> 58; matrix products, arithmetic and copies ran while one was open for 20% -> 22% of each run, Pallas kernels for 6% -> 6%
where the time goes in v3:
time: 647 us; the launch traced here: 640 us
  waiting for transfers between devices  278 us (43%)
  starting transfers between devices  155 us (24%)
  matrix products  67 us (10%)
  other arithmetic  63.5 us (10%)
  Pallas kernels  42 us (6%)
  local copies, waits for them, and re-layouts  31.7 us (5%)
    ppermute x133, waiting for transfers between devices, move(): return lax.ppermute(block, MESH_AXES, pairs)  266 us
    ppermute x133, starting transfers between devices, move(): return lax.ppermute(block, MESH_AXES, pairs)  148 us
    pallas_call x10, Pallas kernels, rearrange(): pl.pallas_call(lambda *refs: rearrange_kernel(plans, len(sources), *refs)...  24.9 us
    dot_general x20, matrix products, mm_tn(): lax.dot_general(a, b, (((0,), (0,)), ((), ())), preferred_element_type=F32)  24.2 us
    dot_general x22, matrix products, mm(): lax.dot_general(a, b, (((1,), (0,)), ((), ())), preferred_element_type=F32)  22.4 us
    dot_general x24, matrix products, mm_nt(): lax.dot_general(a, b, (((1,), (1,)), ((), ())), preferred_element_type=F32)  20.4 us
    unnamed x239, local copies, waits for them, and re-layouts  14.8 us
  transfers between devices with their start and end apart: 135, of which 58 were waited for; matrix products, arithmetic and copies ran while one was open for 22% of the time, Pallas kernels for 6%

profile of v3, /device:TPU:0, one launch (start us, length us, event | category | flops | bytes accessed | tf_op | source)
XLA Modules:
  0.0 640.4 jit_solution(6871551230223113064)
XLA Ops:
  28.5 4.5 collective-permute-start.9
  44.0 5.0 collective-permute-start.15
  50.5 5.8 collective-permute-start.18
  68.1 5.5 collective-permute-done.17
  98.1 8.8 %collective-permute-done.22 = bf16[96,1408]{1,0:T(8,128)(2,1)S(1)} collective-permute-done((bf16[96,1408]{1,0:T(8,128)(2,1)}, bf16[96,1408]{1,0:T(8,128)(2,1)S(1)}, u32[]{:S(2)}, u32[]{:S(2)}) %collective-permute-start.22) | collective-permute-done | bytes 270368 | tf_op jit(solution)/shard_map/ppermute | solution.py:46
  106.9 7.0 %collective-permute-done.23 = bf16[96,1408]{1,0:T(8,128)(2,1)S(1)} collective-permute-done((bf16[96,1408]{1,0:T(8,128)(2,1)}, bf16[96,1408]{1,0:T(8,128)(2,1)S(1)}, u32[]{:S(2)}, u32[]{:S(2)}) %collective-permute-start.23) | collective-permute-done | bytes 270368 | tf_op jit(solution)/shard_map/ppermute | solution.py:46
  121.0 8.0 %collective-permute-done.26 = bf16[64,1536]{1,0:T(8,128)(2,1)S(1)} collective-permute-done((bf16[64,1536]{1,0:T(8,128)(2,1)S(1)}, bf16[64,1536]{1,0:T(8,128)(2,1)S(1)}, u32[]{:S(2)}, u32[]{:S(2)}) %collective-permute-start.26) | collective-permute-done | bytes 196640 | tf_op jit(solution)/shard_map/ppermute | solution.py:46
  137.1 7.0 %collective-permute-done.35 = bf16[64,1536]{1,0:T(8,128)(2,1)S(1)} collective-permute-done((bf16[64,1536]{1,0:T(8,128)(2,1)S(1)}, bf16[64,1536]{1,0:T(8,128)(2,1)S(1)}, u32[]{:S(2)}, u32[]{:S(2)}) %collective-permute-start.35) | collective-permute-done | bytes 196640 | tf_op jit(solution)/shard_map/ppermute | solution.py:46
  144.0 7.7 %collective-permute-done.34 = bf16[64,1536]{1,0:T(8,128)(2,1)S(1)} collective-permute-done((bf16[64,1536]{1,0:T(8,128)(2,1)S(1)}, bf16[64,1536]{1,0:T(8,128)(2,1)S(1)}, u32[]{:S(2)}, u32[]{:S(2)}) %collective-permute-start.34) | collective-permute-done | bytes 196640 | tf_op jit(solution)/shard_map/ppermute | solution.py:46
  156.1 13.9 %collective-permute-done.40 = bf16[128,1536]{1,0:T(8,128)(2,1)S(1)} collective-permute-done((bf16[128,1536]{1,0:T(8,128)(2,1)S(1)}, bf16[128,1536]{1,0:T(8,128)(2,1)S(1)}, u32[]{:S(2)}, u32[]{:S(2)}) %collective-permute-start.40) | collective-permute-done | bytes 393248 | tf_op jit(solution)/shard_map/ppermute | solution.py:46
  175.1 14.6 %collective-permute-done.41 = bf16[256,1536]{1,0:T(8,128)(2,1)S(1)} collective-permute-done((bf16[256,1536]{1,0:T(8,128)(2,1)S(1)}, bf16[256,1536]{1,0:T(8,128)(2,1)S(1)}, u32[]{:S(2)}, u32[]{:S(2)}) %collective-permute-start.41) | collective-permute-done | bytes 786464 | tf_op jit(solution)/shard_map/ppermute | solution.py:46
  200.7 7.6 %collective-permute-done.47 = bf16[384,384]{1,0:T(8,128)(2,1)S(1)} collective-permute-done((bf16[384,384]{1,0:T(8,128)(2,1)S(1)}, bf16[384,384]{1,0:T(8,128)(2,1)S(1)}, u32[]{:S(2)}, u32[]{:S(2)}) %collective-permute-start.47) | collective-permute-done | bytes 294944 | tf_op jit(solution)/shard_map/ppermute | solution.py:46
  208.3 5.0 collective-permute-done.46
  223.1 18.9 %collective-permute-done.51 = bf16[384,1024]{1,0:T(8,128)(2,1)S(1)} collective-permute-done((bf16[384,1024]{1,0:T(8,128)(2,1)S(1)}, bf16[384,1024]{1,0:T(8,128)(2,1)S(1)}, u32[]{:S(2)}, u32[]{:S(2)}) %collective-permute-start.51) | collective-permute-done | bytes 786464 | tf_op jit(solution)/shard_map/ppermute | solution.py:46
  257.4 6.6 %collective-permute-done.61 = bf16[64,1536]{1,0:T(8,128)(2,1)S(1)} collective-permute-done((bf16[64,1536]{1,0:T(8,128)(2,1)}, bf16[64,1536]{1,0:T(8,128)(2,1)S(1)}, u32[]{:S(2)}, u32[]{:S(2)}) %collective-permute-start.61) | collective-permute-done | bytes 196640 | tf_op jit(solution)/shard_map/ppermute | solution.py:46
  281.7 6.7 %collective-permute-done.55 = bf16[64,1536]{1,0:T(8,128)(2,1)S(1)} collective-permute-done((bf16[64,1536]{1,0:T(8,128)(2,1)S(1)}, bf16[64,1536]{1,0:T(8,128)(2,1)S(1)}, u32[]{:S(2)}, u32[]{:S(2)}) %collective-permute-start.55) | collective-permute-done | bytes 196640 | tf_op jit(solution)/shard_map/ppermute | solution.py:46
  304.8 11.2 %collective-permute-done.63 = bf16[256,1536]{1,0:T(8,128)(2,1)S(1)} collective-permute-done((bf16[256,1536]{1,0:T(8,128)(2,1)S(1)}, bf16[256,1536]{1,0:T(8,128)(2,1)S(1)}, u32[]{:S(2)}, u32[]{:S(2)}) %collective-permute-start.63) | collective-permute-done | bytes 786464 | tf_op jit(solution)/shard_map/ppermute | solution.py:46
  335.7 7.0 %collective-permute-done.69 = bf16[64,1536]{1,0:T(8,128)(2,1)S(1)} collective-permute-done((bf16[64,1536]{1,0:T(8,128)(2,1)S(1)}, bf16[64,1536]{1,0:T(8,128)(2,1)S(1)}, u32[]{:S(2)}, u32[]{:S(2)}) %collective-permute-start.69) | collective-permute-done | bytes 196640 | tf_op jit(solution)/shard_map/ppermute | solution.py:46
  349.7 5.6 collective-permute-done.74
  356.6 5.7 collective-permute-done.77
  381.7 4.6 attend_back.2
  396.6 9.4 %collective-permute-done.86 = bf16[768,1024]{1,0:T(8,128)(2,1)} collective-permute-done((bf16[768,1024]{1,0:T(8,128)(2,1)}, bf16[768,1024]{1,0:T(8,128)(2,1)}, u32[]{:S(2)}, u32[]{:S(2)}) %collective-permute-start.86) | collective-permute-done | bytes 1572896 | tf_op jit(solution)/shard_map/ppermute | solution.py:46
  416.6 7.1 %collective-permute-done.90 = bf16[64,1536]{1,0:T(8,128)(2,1)S(1)} collective-permute-done((bf16[64,1536]{1,0:T(8,128)(2,1)S(1)}, bf16[64,1536]{1,0:T(8,128)(2,1)S(1)}, u32[]{:S(2)}, u32[]{:S(2)}) %collective-permute-start.90) | collective-permute-done | bytes 196640 | tf_op jit(solution)/shard_map/ppermute | solution.py:46
  446.1 5.9 collective-permute-done.98
  473.9 7.0 %collective-permute-done.102 = bf16[384,384]{1,0:T(8,128)(2,1)S(1)} collective-permute-done((bf16[384,384]{1,0:T(8,128)(2,1)S(1)}, bf16[384,384]{1,0:T(8,128)(2,1)S(1)}, u32[]{:S(2)}, u32[]{:S(2)}) %collective-permute-start.102) | collective-permute-done | bytes 294944 | tf_op jit(solution)/shard_map/ppermute | solution.py:46
  482.1 9.2 %collective-permute-start.106 = (bf16[768,512]{1,0:T(8,128)(2,1)}, bf16[768,512]{1,0:T(8,128)(2,1)}, u32[]{:S(2)}, u32[]{:S(2)}) collective-permute-start(bf16[768,512]{1,0:T(8,128)(2,1)} %convolution_convert_fusion.14), channel_id=1, source_target_pairs={{0,1},{1,0},{2,3},{3,2},{4,5},{5,4},{6,7},{7,6},{8,9},{9,8},{10,11... | collective-permute-start | bytes 2359304 | tf_op jit(solution)/shard_map/ppermute | solution.py:46
  493.6 4.6 attend_back.3
  504.8 5.0 collective-permute-done.106
  527.8 12.0 %collective-permute-done.110 = bf16[64,1536]{1,0:T(8,128)(2,1)S(1)} collective-permute-done((bf16[64,1536]{1,0:T(8,128)(2,1)S(1)}, bf16[64,1536]{1,0:T(8,128)(2,1)S(1)}, u32[]{:S(2)}, u32[]{:S(2)}) %collective-permute-start.110) | collective-permute-done | bytes 196640 | tf_op jit(solution)/shard_map/ppermute | solution.py:46
  582.8 8.6 %collective-permute-done.119 = bf16[96,2432]{1,0:T(8,128)(2,1)} collective-permute-done((bf16[96,2432]{1,0:T(8,128)(2,1)}, bf16[96,2432]{1,0:T(8,128)(2,1)}, u32[]{:S(2)}, u32[]{:S(2)}) %collective-permute-start.119) | collective-permute-done | bytes 466976 | tf_op jit(solution)/shard_map/ppermute | solution.py:46
  591.9 8.7 %collective-permute-done.120 = bf16[96,2432]{1,0:T(8,128)(2,1)S(1)} collective-permute-done((bf16[96,2432]{1,0:T(8,128)(2,1)}, bf16[96,2432]{1,0:T(8,128)(2,1)S(1)}, u32[]{:S(2)}, u32[]{:S(2)}) %collective-permute-start.120) | collective-permute-done | bytes 466976 | tf_op jit(solution)/shard_map/ppermute | solution.py:46
  621.6 11.4 %collective-permute-done.133 = bf16[192,1536]{1,0:T(8,128)(2,1)S(1)} collective-permute-done((bf16[192,1536]{1,0:T(8,128)(2,1)S(1)}, bf16[192,1536]{1,0:T(8,128)(2,1)S(1)}, u32[]{:S(2)}, u32[]{:S(2)}) %collective-permute-start.133) | collective-permute-done | bytes 589856 | tf_op jit(solution)/shard_map/ppermute | solution.py:57
  (803 shorter events, 381.5 us)
Async XLA Ops:
  23.4 38.7 %collective-permute-start.19 = (bf16[4,96,1024]{2,1,0:T(8,128)(2,1)}, bf16[4,96,1024]{2,1,0:T(8,128)(2,1)}, u32[]{:S(2)}, u32[]{:S(2)}) collective-permute-start(bf16[4,96,1024]{2,1,0:T(8,128)(2,1)} %dynamic-slice_bitcast_fusion), channel_id=1, source_target_pairs={{0,16},{1,17},{2,18},{3,19},{4,20},{5,21},{6,22},{7,23},{8,24},{9,... | collective-permute-start | bytes 2359304 | tf_op jit(solution)/shard_map/ppermute | solution.py:46
  23.5 26.9 %collective-permute-start.16 = (bf16[384,384]{1,0:T(8,128)(2,1)S(1)}, bf16[384,384]{1,0:T(8,128)(2,1)S(1)}, u32[]{:S(2)}, u32[]{:S(2)}) collective-permute-start(bf16[384,384]{1,0:T(8,128)(2,1)S(1)} %bitcast.280), channel_id=1, source_target_pairs={{0,8},{1,9},{2,10},{3,11},{4,12},{5,13},{6,14},{7,15},{8,0},{9,1},... | collective-permute-start | bytes 884744 | tf_op jit(solution)/shard_map/ppermute | solution.py:46
  61.4 22.5 %collective-permute-start.36 = (bf16[128,1536]{1,0:T(8,128)(2,1)S(1)}, bf16[128,1536]{1,0:T(8,128)(2,1)S(1)}, u32[]{:S(2)}, u32[]{:S(2)}) collective-permute-start(bf16[128,1536]{1,0:T(8,128)(2,1)S(1)} %dynamic-slice_bitcast_fusion.4), channel_id=1, source_target_pairs={{0,16},{1,17},{2,18},{3,19},{4,20},{5,21},{6,22},{7,23},{8,24},{9,... | collective-permute-start | bytes 1179656 | tf_op jit(solution)/shard_map/ppermute | solution.py:46
  61.4 22.5 %collective-permute-start.20 = (bf16[256,1536]{1,0:T(8,128)(2,1)S(1)}, bf16[256,1536]{1,0:T(8,128)(2,1)S(1)}, u32[]{:S(2)}, u32[]{:S(2)}) collective-permute-start(bf16[256,1536]{1,0:T(8,128)(2,1)S(1)} %pad_maximum_fusion.10), channel_id=1, source_target_pairs={{0,16},{1,17},{2,18},{3,19},{4,20},{5,21},{6,22},{7,23},{8,24},{9,... | collective-permute-start | bytes 2359304 | tf_op jit(solution)/shard_map/ppermute | solution.py:46
  77.2 19.3 %collective-permute-start.24 = (bf16[2,96,1536]{2,1,0:T(8,128)(2,1)S(1)}, bf16[2,96,1536]{2,1,0:T(8,128)(2,1)}, u32[]{:S(2)}, u32[]{:S(2)}) collective-permute-start(bf16[2,96,1536]{2,1,0:T(8,128)(2,1)S(1)} %broadcast_select_fusion), channel_id=1, source_target_pairs={{0,1},{1,0},{2,3},{3,2},{4,5},{5,4},{6,7},{7,6},{8,9},{9,8},{10,11... | collective-permute-start | bytes 1769480 | tf_op jit(solution)/shard_map/ppermute | solution.py:46
  81.1 39.9 %collective-permute-start.32 = (bf16[384,512]{1,0:T(8,128)(2,1)S(1)}, bf16[384,512]{1,0:T(8,128)(2,1)}, u32[]{:S(2)}, u32[]{:S(2)}) collective-permute-start(bf16[384,512]{1,0:T(8,128)(2,1)S(1)} %get-tuple-element.240), channel_id=1, source_target_pairs={{0,8},{1,9},{2,10},{3,11},{4,12},{5,13},{6,14},{7,15},{8,0},{9,1},... | collective-permute-start | bytes 1179656 | tf_op jit(solution)/shard_map/ppermute | solution.py:46
  93.1 20.8 %collective-permute-start.23 = (bf16[96,1408]{1,0:T(8,128)(2,1)}, bf16[96,1408]{1,0:T(8,128)(2,1)S(1)}, u32[]{:S(2)}, u32[]{:S(2)}) collective-permute-start(bf16[96,1408]{1,0:T(8,128)(2,1)} %get-tuple-element.229), channel_id=1, source_target_pairs={{0,6},{1,7},{2,4},{3,5},{4,2},{5,3},{6,0},{7,1},{8,14},{9,15},{10,... | collective-permute-start | bytes 811016 | tf_op jit(solution)/shard_map/ppermute | solution.py:46
  93.9 20.0 %collective-permute-start.21 = (bf16[96,1408]{1,0:T(8,128)(2,1)}, bf16[96,1408]{1,0:T(8,128)(2,1)S(1)}, u32[]{:S(2)}, u32[]{:S(2)}) collective-permute-start(bf16[96,1408]{1,0:T(8,128)(2,1)} %get-tuple-element.227), channel_id=1, source_target_pairs={{0,2},{1,3},{2,0},{3,1},{4,6},{5,7},{6,4},{7,5},{8,10},{9,11},{10,... | collective-permute-start | bytes 811016 | tf_op jit(solution)/shard_map/ppermute | solution.py:46
  130.2 21.6 %collective-permute-start.37 = (bf16[384,512]{1,0:T(8,128)(2,1)S(1)}, bf16[384,512]{1,0:T(8,128)(2,1)S(1)}, u32[]{:S(2)}, u32[]{:S(2)}) collective-permute-start(bf16[384,512]{1,0:T(8,128)(2,1)S(1)} %copy-done.47), channel_id=1, source_target_pairs={{0,8},{1,9},{2,10},{3,11},{4,12},{5,13},{6,14},{7,15},{8,0},{9,1},... | collective-permute-start | bytes 1179656 | tf_op jit(solution)/shard_map/ppermute | solution.py:46
  198.7 43.2 %collective-permute-start.51 = (bf16[384,1024]{1,0:T(8,128)(2,1)S(1)}, bf16[384,1024]{1,0:T(8,128)(2,1)S(1)}, u32[]{:S(2)}, u32[]{:S(2)}) collective-permute-start(bf16[384,1024]{1,0:T(8,128)(2,1)S(1)} %slice.794), channel_id=1, source_target_pairs={{0,8},{1,9},{2,10},{3,11},{4,12},{5,13},{6,14},{7,15},{8,0},{9,1},... | collective-permute-start | bytes 2359304 | tf_op jit(solution)/shard_map/ppermute | solution.py:46
  217.8 24.1 %collective-permute-start.50 = (bf16[64,1536]{1,0:T(8,128)(2,1)S(1)}, bf16[64,1536]{1,0:T(8,128)(2,1)S(1)}, u32[]{:S(2)}, u32[]{:S(2)}) collective-permute-start(bf16[64,1536]{1,0:T(8,128)(2,1)S(1)} %pad_maximum_fusion.45), channel_id=1, source_target_pairs={{0,6},{1,7},{2,4},{3,5},{4,2},{5,3},{6,0},{7,1},{8,14},{9,15},{10,... | collective-permute-start | bytes 589832 | tf_op jit(solution)/shard_map/ppermute | solution.py:46
  217.9 25.1 %collective-permute-start.49 = (bf16[64,1536]{1,0:T(8,128)(2,1)S(1)}, bf16[64,1536]{1,0:T(8,128)(2,1)S(1)}, u32[]{:S(2)}, u32[]{:S(2)}) collective-permute-start(bf16[64,1536]{1,0:T(8,128)(2,1)S(1)} %pad_maximum_fusion.45), channel_id=1, source_target_pairs={{0,4},{1,5},{2,6},{3,7},{4,0},{5,1},{6,2},{7,3},{8,12},{9,13},{10,... | collective-permute-start | bytes 589832 | tf_op jit(solution)/shard_map/ppermute | solution.py:46
  220.3 22.7 %collective-permute-start.48 = (bf16[64,1536]{1,0:T(8,128)(2,1)S(1)}, bf16[64,1536]{1,0:T(8,128)(2,1)S(1)}, u32[]{:S(2)}, u32[]{:S(2)}) collective-permute-start(bf16[64,1536]{1,0:T(8,128)(2,1)S(1)} %pad_maximum_fusion.45), channel_id=1, source_target_pairs={{0,2},{1,3},{2,0},{3,1},{4,6},{5,7},{6,4},{7,5},{8,10},{9,11},{10,... | collective-permute-start | bytes 589832 | tf_op jit(solution)/shard_map/ppermute | solution.py:46
  221.4 22.9 %collective-permute-start.52 = (bf16[768,384]{1,0:T(8,128)(2,1)S(1)}, bf16[768,384]{1,0:T(8,128)(2,1)S(1)}, u32[]{:S(2)}, u32[]{:S(2)}) collective-permute-start(bf16[768,384]{1,0:T(8,128)(2,1)S(1)} %pad_maximum_fusion.24), channel_id=1, source_target_pairs={{0,1},{1,0},{2,3},{3,2},{4,5},{5,4},{6,7},{7,6},{8,9},{9,8},{10,11... | collective-permute-start | bytes 1769480 | tf_op jit(solution)/shard_map/ppermute | solution.py:46
  243.0 38.7 %collective-permute-start.58 = (bf16[128,1536]{1,0:T(8,128)(2,1)}, bf16[128,1536]{1,0:T(8,128)(2,1)}, u32[]{:S(2)}, u32[]{:S(2)}) collective-permute-start(bf16[128,1536]{1,0:T(8,128)(2,1)} %get-tuple-element.258), channel_id=1, source_target_pairs={{0,8},{1,9},{2,10},{3,11},{4,12},{5,13},{6,14},{7,15},{8,0},{9,1},... | collective-permute-start | bytes 1179656 | tf_op jit(solution)/shard_map/ppermute | solution.py:46
  244.4 20.4 %collective-permute-start.62 = (bf16[64,1536]{1,0:T(8,128)(2,1)}, bf16[64,1536]{1,0:T(8,128)(2,1)S(1)}, u32[]{:S(2)}, u32[]{:S(2)}) collective-permute-start(bf16[64,1536]{1,0:T(8,128)(2,1)} %broadcast_select_fusion.5), channel_id=1, source_target_pairs={{0,6},{1,7},{2,4},{3,5},{4,2},{5,3},{6,0},{7,1},{8,14},{9,15},{10,... | collective-permute-start | bytes 589832 | tf_op jit(solution)/shard_map/ppermute | solution.py:46
  256.0 36.5 %collective-permute-start.59 = (bf16[768,1024]{1,0:T(8,128)(2,1)}, bf16[768,1024]{1,0:T(8,128)(2,1)}, u32[]{:S(2)}, u32[]{:S(2)}) collective-permute-start(bf16[768,1024]{1,0:T(8,128)(2,1)} %pad_maximum_fusion.6), channel_id=1, source_target_pairs={{0,1},{1,0},{2,3},{3,2},{4,5},{5,4},{6,7},{7,6},{8,9},{9,8},{10,11... | collective-permute-start | bytes 4718600 | tf_op jit(solution)/shard_map/ppermute | solution.py:46
  371.9 37.5 %collective-permute-start.87 = (bf16[128,1536]{1,0:T(8,128)(2,1)}, bf16[128,1536]{1,0:T(8,128)(2,1)}, u32[]{:S(2)}, u32[]{:S(2)}) collective-permute-start(bf16[128,1536]{1,0:T(8,128)(2,1)} %fusion.48), channel_id=1, source_target_pairs={{0,8},{1,9},{2,10},{3,11},{4,12},{5,13},{6,14},{7,15},{8,0},{9,1},... | collective-permute-start | bytes 1179656 | tf_op jit(solution)/shard_map/ppermute | solution.py:46
  372.5 33.5 %collective-permute-start.86 = (bf16[768,1024]{1,0:T(8,128)(2,1)}, bf16[768,1024]{1,0:T(8,128)(2,1)}, u32[]{:S(2)}, u32[]{:S(2)}) collective-permute-start(bf16[768,1024]{1,0:T(8,128)(2,1)} %convolution_convert_fusion.13), channel_id=1, source_target_pairs={{0,1},{1,0},{2,3},{3,2},{4,5},{5,4},{6,7},{7,6},{8,9},{9,8},{10,11... | collective-permute-start | bytes 4718600 | tf_op jit(solution)/shard_map/ppermute | solution.py:46
  406.0 27.0 %collective-permute-start.92 = (bf16[768,384]{1,0:T(8,128)(2,1)S(1)}, bf16[768,384]{1,0:T(8,128)(2,1)S(1)}, u32[]{:S(2)}, u32[]{:S(2)}) collective-permute-start(bf16[768,384]{1,0:T(8,128)(2,1)S(1)} %convolution_convert_fusion.17), channel_id=1, source_target_pairs={{0,1},{1,0},{2,3},{3,2},{4,5},{5,4},{6,7},{7,6},{8,9},{9,8},{10,11... | collective-permute-start | bytes 1769480 | tf_op jit(solution)/shard_map/ppermute | solution.py:46
  414.2 43.3 %collective-permute-start.97 = (bf16[384,1024]{1,0:T(8,128)(2,1)S(1)}, bf16[384,1024]{1,0:T(8,128)(2,1)S(1)}, u32[]{:S(2)}, u32[]{:S(2)}) collective-permute-start(bf16[384,1024]{1,0:T(8,128)(2,1)S(1)} %fusion.5), channel_id=1, source_target_pairs={{0,8},{1,9},{2,10},{3,11},{4,12},{5,13},{6,14},{7,15},{8,0},{9,1},... | collective-permute-start | bytes 2359304 | tf_op jit(solution)/shard_map/ppermute | solution.py:46
  480.9 19.9 %collective-permute-start.105 = (bf16[128,1536]{1,0:T(8,128)(2,1)}, bf16[128,1536]{1,0:T(8,128)(2,1)S(1)}, u32[]{:S(2)}, u32[]{:S(2)}) collective-permute-start(bf16[128,1536]{1,0:T(8,128)(2,1)} %fusion.41), channel_id=1, source_target_pairs={{0,8},{1,9},{2,10},{3,11},{4,12},{5,13},{6,14},{7,15},{8,0},{9,1},... | collective-permute-start | bytes 1179656 | tf_op jit(solution)/shard_map/ppermute | solution.py:46
  482.1 27.7 %collective-permute-start.106 = (bf16[768,512]{1,0:T(8,128)(2,1)}, bf16[768,512]{1,0:T(8,128)(2,1)}, u32[]{:S(2)}, u32[]{:S(2)}) collective-permute-start(bf16[768,512]{1,0:T(8,128)(2,1)} %convolution_convert_fusion.14), channel_id=1, source_target_pairs={{0,1},{1,0},{2,3},{3,2},{4,5},{5,4},{6,7},{7,6},{8,9},{9,8},{10,11... | collective-permute-start | bytes 2359304 | tf_op jit(solution)/shard_map/ppermute | solution.py:46
  500.7 60.4 %collective-permute-start.115 = (bf16[384,512]{1,0:T(8,128)(2,1)}, bf16[384,512]{1,0:T(8,128)(2,1)}, u32[]{:S(2)}, u32[]{:S(2)}) collective-permute-start(bf16[384,512]{1,0:T(8,128)(2,1)} %fusion.40), channel_id=1, source_target_pairs={{0,8},{1,9},{2,10},{3,11},{4,12},{5,13},{6,14},{7,15},{8,0},{9,1},... | collective-permute-start | bytes 1179656 | tf_op jit(solution)/shard_map/ppermute | solution.py:46
  512.1 47.6 %collective-permute-start.116 = (bf16[384,512]{1,0:T(8,128)(2,1)}, bf16[384,512]{1,0:T(8,128)(2,1)}, u32[]{:S(2)}, u32[]{:S(2)}) collective-permute-start(bf16[384,512]{1,0:T(8,128)(2,1)} %fusion.39), channel_id=1, source_target_pairs={{0,8},{1,9},{2,10},{3,11},{4,12},{5,13},{6,14},{7,15},{8,0},{9,1},... | collective-permute-start | bytes 1179656 | tf_op jit(solution)/shard_map/ppermute | solution.py:46
  520.5 19.4 %collective-permute-start.110 = (bf16[64,1536]{1,0:T(8,128)(2,1)S(1)}, bf16[64,1536]{1,0:T(8,128)(2,1)S(1)}, u32[]{:S(2)}, u32[]{:S(2)}) collective-permute-start(bf16[64,1536]{1,0:T(8,128)(2,1)S(1)} %get-tuple-element.462), channel_id=1, source_target_pairs={{0,6},{1,7},{2,4},{3,5},{4,2},{5,3},{6,0},{7,1},{8,14},{9,15},{10,... | collective-permute-start | bytes 589832 | tf_op jit(solution)/shard_map/ppermute | solution.py:46
  520.6 23.1 %collective-permute-start.109 = (bf16[64,1536]{1,0:T(8,128)(2,1)S(1)}, bf16[64,1536]{1,0:T(8,128)(2,1)S(1)}, u32[]{:S(2)}, u32[]{:S(2)}) collective-permute-start(bf16[64,1536]{1,0:T(8,128)(2,1)S(1)} %get-tuple-element.463), channel_id=1, source_target_pairs={{0,4},{1,5},{2,6},{3,7},{4,0},{5,1},{6,2},{7,3},{8,12},{9,13},{10,... | collective-permute-start | bytes 589832 | tf_op jit(solution)/shard_map/ppermute | solution.py:46
  567.1 33.5 %collective-permute-start.118 = (bf16[96,2432]{1,0:T(8,128)(2,1)}, bf16[96,2432]{1,0:T(8,128)(2,1)}, u32[]{:S(2)}, u32[]{:S(2)}) collective-permute-start(bf16[96,2432]{1,0:T(8,128)(2,1)} %get-tuple-element.318), channel_id=1, source_target_pairs={{0,2},{1,3},{2,0},{3,1},{4,6},{5,7},{6,4},{7,5},{8,10},{9,11},{10,... | collective-permute-start | bytes 1400840 | tf_op jit(solution)/shard_map/ppermute | solution.py:46
  571.0 32.1 %collective-permute-start.117 = (f32[4,2,96]{2,0,1:T(4,128)S(1)}, f32[4,2,96]{2,0,1:T(4,128)S(1)}, u32[]{:S(2)}, u32[]{:S(2)}) collective-permute-start(f32[4,2,96]{2,0,1:T(4,128)S(1)} %fusion.181), channel_id=1, source_target_pairs={{0,8},{1,9},{2,10},{3,11},{4,12},{5,13},{6,14},{7,15},{8,0},{9,1},... | collective-permute-start | bytes 9224 | tf_op jit(solution)/shard_map/ppermute | solution.py:46
  571.0 20.4 %collective-permute-start.119 = (bf16[96,2432]{1,0:T(8,128)(2,1)}, bf16[96,2432]{1,0:T(8,128)(2,1)}, u32[]{:S(2)}, u32[]{:S(2)}) collective-permute-start(bf16[96,2432]{1,0:T(8,128)(2,1)} %get-tuple-element.321), channel_id=1, source_target_pairs={{0,4},{1,5},{2,6},{3,7},{4,0},{5,1},{6,2},{7,3},{8,12},{9,13},{10,... | collective-permute-start | bytes 1400840 | tf_op jit(solution)/shard_map/ppermute | solution.py:46
  573.6 27.0 %collective-permute-start.120 = (bf16[96,2432]{1,0:T(8,128)(2,1)}, bf16[96,2432]{1,0:T(8,128)(2,1)S(1)}, u32[]{:S(2)}, u32[]{:S(2)}) collective-permute-start(bf16[96,2432]{1,0:T(8,128)(2,1)} %get-tuple-element.322), channel_id=1, source_target_pairs={{0,6},{1,7},{2,4},{3,5},{4,2},{5,3},{6,0},{7,1},{8,14},{9,15},{10,... | collective-permute-start | bytes 1400840 | tf_op jit(solution)/shard_map/ppermute | solution.py:46
  575.3 27.8 %collective-permute-start.123 = (bf16[384,384]{1,0:T(8,128)(2,1)S(1)}, bf16[384,384]{1,0:T(8,128)(2,1)S(1)}, u32[]{:S(2)}, u32[]{:S(2)}) collective-permute-start(bf16[384,384]{1,0:T(8,128)(2,1)S(1)} %fusion.62), channel_id=1, source_target_pairs={{0,8},{1,9},{2,10},{3,11},{4,12},{5,13},{6,14},{7,15},{8,0},{9,1},... | collective-permute-start | bytes 884744 | tf_op jit(solution)/shard_map/ppermute | solution.py:46
  (214 other events, 2375.1 us)

commit v4 on v3

--- a/solution.py
+++ b/solution.py
@@ -76,10 +76,6 @@
     return lax.dynamic_index_in_dim(parts, index, 0, False)
 
 
-def after(block, *earlier):
-    return lax.optimization_barrier((block,) + earlier)[0] if earlier else block
-
-
 class Order:
     def __init__(self):
         self.last = ()
@@ -90,20 +86,9 @@
         self.last = (blocks[0],)
         return blocks[0] if len(blocks) == 1 else blocks
 
-    def sent(self, transfer, wire):
-        self.last = (transfer(wire, self.last),)
-
-
-class Wire:
-    def __init__(self, move):
-        self.move = move
-        self.last = ()
-
-    def send(self, block, deps=(), move=None, beside=False):
-        block = after(block, *(() if beside else self.last), *deps)
-        got = (move or self.move)(block)
-        self.last = self.last + (got,) if beside else (got,)
-        return got, block
+    def each(self, blocks):
+        blocks = self(*blocks)
+        return list(blocks) if isinstance(blocks, (tuple, list)) else [blocks]
 
 
 def two_way(index, own, other, axis):
@@ -130,7 +115,7 @@
         lambda *refs: rearrange_kernel(plans, len(sources), *refs),
         out_shape=[jax.ShapeDtypeStruct(shape, dtype) for shape in shapes],
         compiler_params=VMEM_LIMIT,
-        cost_estimate=pl.CostEstimate(flops=0, bytes_accessed=2 * moved, transcendentals=0),
+        cost_estimate=pl.CostEstimate(flops=0, bytes_accessed=0, transcendentals=0),
         name="rearrange",
     )(*sources)
 
@@ -293,13 +278,8 @@
 
 
 def to_members(parts, lay, order):
-    sent = order(*[pick(parts, lay.member ^ step) for step in range(1, lay.group)])
-    sent = sent if isinstance(sent, (tuple, list)) else (sent,)
+    sent = order.each([pick(parts, lay.member ^ step) for step in range(1, lay.group)])
     return [lay.to_member(block, step) for step, block in enumerate(sent, 1)]
-
-
-def listed(blocks):
-    return list(blocks) if isinstance(blocks, (tuple, list)) else [blocks]
 
 
 def member_rows(parts, others, lay):
@@ -307,42 +287,42 @@
 
 
 class Spread:
-    def __init__(self, block):
-        self.block = block
-
-    def over_half(self, wire, deps=(), **how):
-        self.got, sent = wire.send(self.block, deps, **how)
-        return sent
-
-    def over_shard(self, wire, deps=(), **how):
-        self.pair = jnp.concatenate([self.block, after(self.got, *deps)], 0)
-        self.got, sent = wire.send(self.pair, **how)
-        return sent
-
-    def full(self):
-        return jnp.concatenate([self.pair, self.got], 0)
+    def __init__(self, block, lay, order):
+        self.block, self.lay, self.order = block, lay, order
+
+    def half(self):
+        self.got = self.lay.to_half(self.order(self.block))
+
+    def half_done(self):
+        self.pair = jnp.concatenate([self.block, self.order(self.got)], 0)
+
+    def shard(self):
+        self.got = self.lay.to_shard(self.order(self.pair))
+
+    def shard_done(self):
+        self.full = jnp.concatenate([self.pair, self.order(self.got)], 0)
 
 
 class Collect:
-    def __init__(self, left, right):
-        self.left, self.right = left, right
+    def __init__(self, left, right, lay, order):
+        self.left, self.right, self.lay, self.order = left, right, lay, order
         self.rows = left.shape[1] // 4
 
-    def over_shard(self, wire, deps=(), **how):
+    def shard(self):
         block = mm_tn(self.left[:, 2 * self.rows :], self.right).astype(BF16)
-        self.got, sent = wire.send(block, deps, **how)
-        return sent
-
-    def over_half(self, wire, deps=(), **how):
-        rows = self.rows
+        self.got = self.lay.to_shard(self.order(block))
+
+    def shard_done(self):
+        self.got, self.left = self.order(self.got, self.left)
+
+    def half(self):
+        rows, got = self.rows, self.got.astype(F32)
         kept = mm_tn(self.left[:, : 2 * rows], self.right)
-        got = after(self.got, *deps).astype(F32)
         self.kept = kept[:rows] + got[:rows]
-        self.arrived, sent = wire.send((kept[rows:] + got[rows:]).astype(BF16), **how)
-        return sent
-
-    def total(self, deps=()):
-        return self.kept + after(self.arrived, *deps).astype(F32)
+        self.got = self.lay.to_half(self.order((kept[rows:] + got[rows:]).astype(BF16)))
+
+    def half_done(self):
+        self.total = self.kept + self.order(self.got).astype(F32)
 
 
 def join_cores(first, second, lay, order):
@@ -360,45 +340,46 @@
 
 class SpreadOut:
     def __init__(self, w_out, lay, order):
-        self.lay, self.width = lay, w_out.shape[-1]
+        self.lay, self.order, self.width = lay, order, w_out.shape[-1]
         self.aligned = out_aligned(lay, w_out.shape[0])
         if not self.aligned:
-            w_out = lax.all_gather(w_out, ("ctx", "shard"), axis=0, tiled=True)
+            w_out = lax.all_gather(w_out, MESH_AXES[1:], axis=0, tiled=True)
         self.own = w_out
-        self.got = lay.to_core(order(w_out))
-
-    def stack(self, order):
-        lay, other = self.lay, order(self.got)
+
+    def core(self):
+        self.got = self.lay.to_core(self.order(self.own))
+
+    def core_done(self):
+        lay, other = self.lay, self.order(self.got)
         self.block = jnp.stack(
             [jnp.where(lay.core == 0, self.own, other), jnp.where(lay.core == 0, other, self.own)]
         )
 
-    def over_half(self, wire, deps=()):
+    def half(self):
+        if self.aligned:
+            self.got = self.lay.move_some(
+                self.order(self.block),
+                lambda core, half, member, shard: half == core,
+                lambda core, half, member, shard: (core, 1 - half, member, shard),
+            )
+
+    def half_done(self):
+        if self.aligned:
+            lay = self.lay
+            self.block = jnp.where(lay.half == lay.core, self.block, self.order(self.got))
+
+    def shard(self):
+        if self.aligned:
+            self.got = self.lay.to_shard(self.order(self.block))
+
+    def shard_done(self):
+        if self.aligned:
+            self.full = jnp.concatenate([self.block, self.order(self.got)], 1)
+            return
         lay = self.lay
-        if not self.aligned:
-            return self.block
-        move = lambda block: lay.move_some(
-            block,
-            lambda core, half, member, shard: half == core,
-            lambda core, half, member, shard: (core, 1 - half, member, shard),
-        )
-        self.got, sent = wire.send(self.block, deps, move)
-        return sent
-
-    def over_shard(self, wire, deps=()):
-        lay = self.lay
-        if not self.aligned:
-            return self.block
-        self.block = jnp.where(lay.half == lay.core, self.block, after(self.got, *deps))
-        self.got, sent = wire.send(self.block)
-        return sent
-
-    def full(self):
-        if self.aligned:
-            return jnp.concatenate([self.block, self.got], 1)
-        head = (self.lay.core * self.lay.group + self.lay.member) // head_copies(self.lay)
-        count = max(1, HEADS // (self.lay.cores * self.lay.group)) * HEAD_DIM
-        return lax.dynamic_slice_in_dim(self.block, head * count, count, 1)
+        head = (lay.core * lay.group + lay.member) // head_copies(lay)
+        count = max(1, HEADS // (lay.cores * lay.group)) * HEAD_DIM
+        self.full = lax.dynamic_slice_in_dim(self.block, head * count, count, 1)
 
 
 def out_pair(which, spread_out):
@@ -406,41 +387,40 @@
 
 
 class CollectOut:
-    def __init__(self, pairs, lay, block_rows):
-        self.pairs, self.lay = pairs, lay
+    def __init__(self, pairs, lay, order, block_rows):
+        self.pairs, self.lay, self.order = pairs, lay, order
         self.aligned = out_aligned(lay, block_rows)
         self.rows = pairs[0][0].shape[1] // 2
 
-    def over_shard(self, wire, deps=(), **how):
+    def shard(self):
         if not self.aligned:
-            self.kept = jnp.stack([mm_tn(left, right) for left, right in self.pairs])
-            return self.kept
+            self.total = [mm_tn(left, right) for left, right in self.pairs]
+            return
         blocks = [mm_tn(left[:, self.rows :], right).astype(BF16) for left, right in self.pairs]
-        self.got, sent = wire.send(jnp.concatenate(blocks, 0), deps, **how)
-        return sent
-
-    def over_half(self, wire, deps=(), **how):
-        lay = self.lay
+        self.got = self.lay.to_shard(self.order(jnp.concatenate(blocks, 0)))
+
+    def shard_done(self):
+        if self.aligned:
+            self.got = self.order(self.got)
+
+    def half(self):
         if not self.aligned:
-            return self.kept
+            return
         blocks = [mm_tn(left[:, : self.rows], right) for left, right in self.pairs]
-        self.kept = jnp.concatenate(blocks, 0) + after(self.got, *deps).astype(F32)
-        move = lambda block: lay.move_some(
-            block,
+        self.kept = jnp.concatenate(blocks, 0) + self.got.astype(F32)
+        self.got = self.lay.move_some(
+            self.order(self.kept.astype(BF16)),
             lambda core, half, member, shard: half != core,
             lambda core, half, member, shard: (core, 1 - half, member, shard),
         )
-        self.arrived, sent = wire.send(self.kept.astype(BF16), (), move, **how)
-        return sent
-
-    def total(self, deps=()):
-        if not self.aligned:
-            return self.kept[0], self.kept[1]
-        total = self.kept + after(self.arrived, *deps).astype(F32)
-        return total[: self.rows], total[self.rows :]
-
-
-def join_out(first, second, lay, block_rows):
+
+    def half_done(self):
+        if self.aligned:
+            total = self.kept + self.order(self.got).astype(F32)
+            self.total = total[: self.rows], total[self.rows :]
+
+
+def join_out_start(first, second, lay, order, block_rows):
     if not out_aligned(lay, block_rows):
         width = first.shape[1]
         head = (lay.core * lay.group + lay.member) // head_copies(lay)
@@ -450,11 +430,15 @@
         )
         full = pick(lax.psum(full, MESH_AXES), lay.core)
         block = (lay.half * lay.group + lay.member) * lay.shards + lay.shard
-        return lax.dynamic_slice_in_dim(full, block * block_rows, block_rows, 0)
-    kept = jnp.where(lay.core == 0, first, second)
-    sent = jnp.where(lay.core == 0, second, first).astype(BF16)
-    other = lay.to_core(sent).astype(F32)
-    return jnp.where(lay.half == lay.core, kept, other)
+        return lax.dynamic_slice_in_dim(full, block * block_rows, block_rows, 0), None
+    return join_cores(first, second, lay, order)
+
+
+def join_out(pair, lay, order):
+    kept, other = pair
+    if other is None:
+        return kept
+    return jnp.where(lay.half == lay.core, kept, order(other).astype(F32))
 
 
 def lane_matrix(heads):
@@ -538,11 +522,7 @@
             jax.ShapeDtypeStruct((half, lanes), BF16),
         ],
         compiler_params=VMEM_LIMIT,
-        cost_estimate=pl.CostEstimate(
-            flops=16 * n_query * half * half * LANES,
-            bytes_accessed=half * n_query * LANES * 24,
-            transcendentals=4 * n_query * half * half,
-        ),
+        cost_estimate=pl.CostEstimate(flops=0, bytes_accessed=0, transcendentals=0),
         name="attend",
     )(raw_own, raw_sib, *tables)
 
@@ -592,34 +572,45 @@
             jax.ShapeDtypeStruct((half, lanes), BF16),
         ],
         compiler_params=VMEM_LIMIT,
-        cost_estimate=pl.CostEstimate(
-            flops=40 * n_query * half * half * LANES,
-            bytes_accessed=half * lanes * 16,
-            transcendentals=4 * n_query * half * half,
-        ),
+        cost_estimate=pl.CostEstimate(flops=0, bytes_accessed=0, transcendentals=0),
         name="attend_back",
     )(own, sib, *out_grads, lse, *tables)
 
 
-def no_round(first):
-    return ()
-
-
-def gather_rows(block, lay, meanwhile=no_round):
-    others = [lay.to_member(block, step) for step in range(1, lay.group)]
-    own = after(jnp.concatenate([block] + others, 0), *meanwhile(others))
-    return own, lay.to_core(own)
-
-
-def scatter_rows(own, sib, lay, meanwhile=no_round):
-    own = own + lay.to_core(sib.astype(BF16)).astype(F32)
+def rows_start(block, lay, order):
+    block = order(block)
+    return block, [lay.to_member(block, step) for step in range(1, lay.group)]
+
+
+def rows_middle(begun, lay, order):
+    block, others = begun
+    own = order(jnp.concatenate([block] + order.each(others), 0))
+    return [own, lay.to_core(own)]
+
+
+def rows_done(rows, order):
+    rows[1] = order(rows[1])
+    return rows
+
+
+def sums_start(own, sib, lay, order):
+    return own, lay.to_core(order(sib.astype(BF16)))
+
+
+def sums_middle(begun, lay, order):
+    own, got = begun
+    own = own + order(got).astype(F32)
     rows = own.shape[0] // lay.group
     parts = own.reshape(lay.group, rows, -1)
-    others = [lay.to_member(parts[step].astype(BF16), step) for step in range(1, lay.group)]
-    total = parts[0]
-    for block in others:
+    sent = order.each([parts[step].astype(BF16) for step in range(1, lay.group)])
+    return parts[0], [lay.to_member(block, step) for step, block in enumerate(sent, 1)]
+
+
+def sums_done(begun, order):
+    total, others = begun
+    for block in order.each(others):
         total = total + block.astype(F32)
-    return after(total, *meanwhile(others))
+    return total
 
 
 def norm_forward(inputs, gain_vec):
@@ -647,49 +638,39 @@
 
 
 class Layer:
-    def __init__(self, lay, tables, n_query, n_key, gain_one, gain_two, order):
-        self.order = order
+    def __init__(self, lay, tables, n_query, n_key, gain_one, gain_two):
         self.lay, self.tables, self.n_query, self.n_key = lay, tables, n_query, n_key
         self.gain_one, self.gain_two = gain_one, gain_two
 
-    def normed_rows(self, inputs):
+    def first_norm(self, inputs):
         self.inputs = inputs
         normed, self.inverse_first = norm_forward(inputs, self.gain_one)
-        return self.order(normed, self.lay)
-
-    def start(self, inputs, meanwhile=no_round):
-        self.normed = gather_rows(self.normed_rows(inputs), self.lay, meanwhile)
+        return relative(normed, self.lay)
 
     def attend(self):
-        lay = self.lay
         raw = [mm(block, self.qkv_w) for block in self.normed]
         out_own, out_sib, lse, own, sib = attend(*raw, self.tables, self.n_query, self.n_key)
         self.attn_kept = own, sib, lse
-        self.attn_out = [out_order(block, lay, self.n_query) for block in (out_own, out_sib)]
-
-    def attention(self, during_out=no_round, during_rows=no_round):
-        lay = self.lay
-        partial = [mm(block, self.out_w) for block in self.attn_out]
-        self.mid_stream = self.inputs + scatter_rows(*partial, lay, during_out)
+        self.attn_out = [out_order(block, self.lay, self.n_query) for block in (out_own, out_sib)]
+
+    def out_partial(self):
+        return [mm(block, self.out_w) for block in self.attn_out]
+
+    def second_norm(self, attended):
+        self.mid_stream = self.inputs + attended
         normed, self.inverse_second = norm_forward(self.mid_stream, self.gain_two)
-        self.normed_mid = gather_rows(self.order(normed, lay), lay, during_rows)
+        return relative(normed, self.lay)
 
     def hide(self):
-        lay = self.lay
         self.gate_up, self.hidden = [], []
         for block in self.normed_mid:
             gate_pre, up_pre = mm(block, self.gate_w), mm(block, self.up_w)
             self.gate_up.append((gate_pre, up_pre))
-            self.hidden.append(relative((jax.nn.silu(gate_pre) * up_pre).astype(BF16), lay))
-
-    def feed_forward(self, meanwhile=no_round):
-        lay = self.lay
-        partial = [mm(block, self.down_w) for block in self.hidden]
-        return self.mid_stream + scatter_rows(*partial, lay, meanwhile)
-
-    def start_back(self, out_grad, meanwhile=no_round):
-        self.out_grad = out_grad
-        self.down_in = gather_rows(out_grad.astype(BF16), self.lay, meanwhile)
+            hidden = (jax.nn.silu(gate_pre) * up_pre).astype(BF16)
+            self.hidden.append(relative(hidden, self.lay))
+
+    def down_partial(self):
+        return [mm(block, self.down_w) for block in self.hidden]
 
     def feed_forward_back(self):
         self.gate_grad, self.up_grad, partial = [], [], []
@@ -705,14 +686,12 @@
             partial.append(mm_nt(gate_grad_in, self.gate_w) + mm_nt(up_grad_in, self.up_w))
         return partial
 
-    def middle_back(self, partial, during_sum=no_round, during_rows=no_round):
-        lay = self.lay
-        normed_mid_grad = relative(scatter_rows(*partial, lay, during_sum), lay)
-        mid_part, self.gain_two_grad = norm_backward(
-            self.mid_stream, self.inverse_second, self.gain_two, normed_mid_grad
+    def second_norm_back(self, out_grad, upstream):
+        part, self.gain_two_grad = norm_backward(
+            self.mid_stream, self.inverse_second, self.gain_two, relative(upstream, self.lay)
         )
-        self.mid_grad = self.out_grad + mid_part
-        self.mid_low = gather_rows(self.mid_grad.astype(BF16), lay, during_rows)
+        self.mid_grad = out_grad + part
+        return self.mid_grad.astype(BF16)
 
     def attention_back(self):
         grads = [
@@ -722,14 +701,12 @@
         self.lows = attend_back(self.attn_kept, grads, self.tables, self.n_query, self.n_key)
         return [mm_nt(block, self.qkv_w) for block in self.lows]
 
-    def finish_back(self, partial, meanwhile=no_round):
-        lay = self.lay
-        normed_grad = relative(scatter_rows(*partial, lay, meanwhile), lay)
-        input_part, gain_one_grad = norm_backward(
-            self.inputs, self.inverse_first, self.gain_one, normed_grad
+    def first_norm_back(self, upstream):
+        part, gain_one_grad = norm_backward(
+            self.inputs, self.inverse_first, self.gain_one, relative(upstream, self.lay)
         )
         self.gain_grads = jnp.stack([gain_one_grad, self.gain_two_grad])
-        return self.mid_grad + input_part
+        return self.mid_grad + part
 
 
 def joined(pair):
@@ -802,11 +779,14 @@
     q_cols, k_cols = n_query * HEAD_DIM, n_key * HEAD_DIM
     spread_lanes = lane_matrix(n_query + 2 * n_key)
     spread_out = lane_matrix(n_query)
-    over_half, over_shard = Wire(lay.to_half), Wire(lay.to_shard)
     cols = q_cols + 2 * k_cols
     ff = ff_unit * 4
-
     order = Order()
+
+    def by_member(*blocks):
+        return jnp.concatenate(blocks, 1).reshape(lay.group, row_block, -1)
+
+    tables = row_tables(pair_table, rows // 2, lay)
     gains = jnp.stack([norm_attn[0], norm_mlp[0]])
     gain_parts = [lay.to_member(gains, step) for step in range(1, lay.group)]
     heads = pack_heads(w_query[0], w_key[0], w_value[0], lay)
@@ -816,172 +796,223 @@
     qkv_others = to_members(qkv_layers[0], lay, order)
     gains = order(place(gains, gain_parts, lay.member))
     gains_other = lay.to_half(gains)
-    w_gate, w_up = order(w_gate, w_up)
+    w_gate, w_up, ends_in = order(w_gate, w_up, ends_in)
+    own_rows = to_inner(ends_in[0, :, 0], lay)
     gate_up_own = pack_ff(w_gate[0], w_up[0], lay, ff_unit)
     gate_up_other = split_cores(gate_up_own, lay, order)
-    qkv_0 = Spread(member_rows(qkv_layers[0], listed(order(*qkv_others)), lay))
-    order.sent(qkv_0.over_half, over_half)
+    rows_other = deal_rows(own_rows, lay, order)
+    qkv_0 = Spread(member_rows(qkv_layers[0], order.each(qkv_others), lay), lay, order)
+    qkv_0.half()
     gains = order(two_way(lay.half, gains, order(gains_other), 0))
     gains_other = lay.to_shard(gains)
-    arrived = deal_rows(to_inner(order(ends_in)[0, :, 0], lay), lay, order)
     gains = order(two_way(lay.shard, gains, order(gains_other), 0))
     gains_other = lay.to_core(gains)
     out = SpreadOut(to_inner(order(w_out)[0], lay), lay, order)
-    tables = row_tables(order(pair_table), rows // 2, lay)
+    out.core()
     gains = two_way(lay.core, gains, order(gains_other), 0)
     gains = gains.transpose(0, 4, 1, 2, 3, 5).reshape(2, 2, -1).astype(F32)
-
-    def layer(index, which):
-        heads = n_query, n_key, gains[index, 0], gains[index, 1]
-        return Layer(lay, tables, *heads, which)
-
-    first, second = layer(0, relative), layer(1, relative)
-    out.stack(order)
-    own_in, own_cot = dealt(*order(*arrived), lay)
-    block = order(first.normed_rows(own_in.astype(F32)))
-    others = [lay.to_member(block, step) for step in range(1, lay.group)]
-    qkv_0.got = order(qkv_0.got)
-    order.sent(qkv_0.over_shard, over_shard)
-    order.sent(out.over_half, over_half)
+    gate_up_layers = core_layers(gate_up_own, order(gate_up_other), lay)
+    out.core_done()
+    own_in, own_cot = dealt(*order(*rows_other), lay)
+    first = Layer(lay, tables, n_query, n_key, gains[0, 0], gains[0, 1])
+    second = Layer(lay, tables, n_query, n_key, gains[1, 0], gains[1, 1])
+    normed = rows_start(first.first_norm(own_in.astype(F32)), lay, order)
+    qkv_0.half_done()
+    qkv_0.shard()
+    out.half()
+    normed = rows_middle(normed, lay, order)
+    gate_up_others = to_members(gate_up_layers[0], lay, order)
+    qkv_0.shard_done()
+    out.half_done()
+    out.shard()
+    first.qkv_w = mm(qkv_0.full, spread_lanes).astype(BF16)
+    first.normed = rows_done(normed, order)
+    first.attend()
+    first.attn_out = order.each(first.attn_out)
+    gate_up = member_rows(gate_up_layers[0], order.each(gate_up_others), lay)
+    gate_0 = Spread(gate_up[:, :ff], lay, order)
+    up_0 = Spread(gate_up[:, ff:], lay, order)
+    gate_0.half()
     down_own = to_inner(order(w_down)[0], lay).reshape(lay.cores, ff_unit, width)
     down_other = split_cores(down_own, lay, order)
-    own = order(jnp.concatenate([block] + listed(order(*others)), 0))
-    first.normed = own, lay.to_core(own)
-    gate_up_layers = core_layers(gate_up_own, order(gate_up_other), lay)
-    gate_up_others = to_members(gate_up_layers[0], lay, order)
-    if out.aligned:
-        out.got = order(out.got)
-    order.sent(out.over_shard, over_shard)
-    qkv_0.got = order(qkv_0.got)
-
-    def round_of(halves, shards):
-        def run(arrived):
-            sent = []
-            for order, item in enumerate(halves):
-                sent.append(item.over_half(over_half, arrived, beside=order > 0))
-            for order, item in enumerate(shards):
-                sent.append(item.over_shard(over_shard, arrived, beside=order > 0))
-            return sent
-
-        return run
-
-    def attention_weights(which, qkv, out_w):
-        which.qkv_w = mm(qkv.full(), spread_lanes).astype(BF16)
-        which.out_w = mm_tn(spread_out, out_w).astype(BF16)
-
-    first.qkv_w = mm(qkv_0.full(), spread_lanes).astype(BF16)
-    first.attend()
-    gate_up_others = listed(order(*gate_up_others))
-    gate_up = member_rows(gate_up_layers[0], gate_up_others, lay)
-    gate_0, up_0 = Spread(gate_up[:, :ff]), Spread(gate_up[:, ff:])
-    order.sent(gate_0.over_half, over_half)
+    out.shard_done()
+    first.out_w = mm_tn(spread_out, out.full[0]).astype(BF16)
+    second.out_w = mm_tn(spread_out, out.full[1]).astype(BF16)
+    sums = sums_middle(sums_start(*first.out_partial(), lay, order), lay, order)
     down_layers = core_layers(down_own, order(down_other), lay)
-    down_0, down_1 = Spread(down_layers[0]), Spread(down_layers[1])
-    order.last = (first.attn_out[0],)
+    down_0, down_1 = Spread(down_layers[0], lay, order), Spread(down_layers[1], lay, order)
+    attended = sums_done(sums, order)
+    gate_0.half_done()
+    gate_0.shard()
+    up_0.half()
+    normed = rows_start(first.second_norm(attended), lay, order)
+    normed = rows_middle(normed, lay, order)
     rest = jnp.concatenate([qkv_layers[1], gate_up_layers[1]], -1)
     rest_others = to_members(rest, lay, order)
-    if out.aligned:
-        out.got = order(out.got)
-    out_w = out.full()
-    first.out_w = mm_tn(spread_out, out_w[0]).astype(BF16)
-    rest = member_rows(rest, listed(order(*rest_others)), lay)
-    qkv_1, gate_up_1 = Spread(rest[:, :cols]), Spread(rest[:, cols:])
-    first.attn_out = [after(block, *order.last) for block in first.attn_out]
-    first.attention(round_of([up_0], [gate_0]), round_of([down_0], [up_0]))
-    first.gate_w, first.up_w = gate_0.full(), up_0.full()
-    down_0.over_shard(over_shard)
-    qkv_1.over_half(over_half, (up_0.got,))
-    gate_up_1.over_half(over_half, (up_0.got,), beside=True)
-    first.down_w = down_0.full()
+    up_0.half_done()
+    gate_0.shard_done()
+    up_0.shard()
+    down_0.half()
+    first.normed_mid = rows_done(normed, order)
+    rest = member_rows(rest, order.each(rest_others), lay)
+    qkv_1 = Spread(rest[:, :cols], lay, order)
+    gate_up_1 = Spread(rest[:, cols:], lay, order)
+    up_0.shard_done()
+    down_0.half_done()
+    down_0.shard()
+    qkv_1.half()
+    own_cot = own_cot.astype(F32)
+    cot = rows_start(own_cot.astype(BF16), lay, order)
+    first.gate_w, first.up_w = gate_0.full, up_0.full
     first.hide()
-    first_out = first.feed_forward(round_of([], [qkv_1]))
-    second.start(first_out.astype(BF16).astype(F32), round_of([down_1], [gate_up_1]))
-    second.start_back(after(own_cot, second.normed[0]).astype(F32))
-    attention_weights(second, qkv_1, out_w[1])
+    second.down_in = rows_middle(cot, lay, order)
+    qkv_1.half_done()
+    gate_up_1.half()
+    down_0.shard_done()
+    qkv_1.shard()
+    first.down_w = down_0.full
+    sums = sums_middle(sums_start(*first.down_partial(), lay, order), lay, order)
+    first_out = first.mid_stream + sums_done(sums, order)
+    normed = rows_start(second.first_norm(first_out.astype(BF16).astype(F32)), lay, order)
+    normed = rows_middle(normed, lay, order)
+    gate_up_1.half_done()
+    gate_up_1.shard()
+    down_1.half()
+    qkv_1.shard_done()
+    second.qkv_w = mm(qkv_1.full, spread_lanes).astype(BF16)
+    second.normed = rows_done(normed, order)
     second.attend()
-    second.attention(round_of([], [down_1]))
-    both = gate_up_1.full()
-    second.gate_w, second.up_w = both[:, :ff], both[:, ff:]
-    second.down_w = down_1.full()
-
-    def gate_up_collects(which):
-        left = joined(which.normed_mid)
-        return Collect(left, joined(which.gate_grad)), Collect(left, joined(which.up_grad))
-
-    def qkv_collect(which):
-        low = mm_nt(joined(which.lows), spread_lanes).astype(BF16)
-        return Collect(joined(which.normed), low)
-
+    sums = sums_start(*second.out_partial(), lay, order)
+    sums = sums_middle(sums, lay, order)
+    attended = sums_done(sums, order)
+    gate_up_1.shard_done()
+    down_1.half_done()
+    down_1.shard()
+    normed = rows_start(second.second_norm(attended), lay, order)
+    normed = rows_middle(normed, lay, order)
+    second.gate_w, second.up_w = gate_up_1.full[:, :ff], gate_up_1.full[:, ff:]
+    second.normed_mid = rows_done(normed, order)
+    second.down_in = rows_done(second.down_in, order)
     second.hide()
-    down_1 = Collect(joined(second.hidden), joined(second.down_in))
-    second_out = second.feed_forward(round_of([], [down_1]))
+
+    down_g1 = Collect(joined(second.hidden), joined(second.down_in), lay, order)
+    down_g1.shard()
+    down_1.shard_done()
+    second.down_w = down_1.full
     partial = second.feed_forward_back()
-    partial[0] = after(partial[0], second_out)
+    sums = sums_start(*partial, lay, order)
     grads = [jnp.concatenate(pair, 1) for pair in zip(second.gate_grad, second.up_grad)]
-    gate_up_1 = Collect(joined(second.normed_mid), joined(grads))
-    second.middle_back(partial, round_of([down_1], [gate_up_1]))
+    gate_up_g1 = Collect(joined(second.normed_mid), joined(grads), lay, order)
+    sums = sums_middle(sums, lay, order)
+    gate_up_g1.shard()
+    upstream = sums_done(sums, order)
+    low = second.second_norm_back(own_cot, upstream)
+    down_g1.shard_done()
+    low = rows_start(low, lay, order)
+    low = rows_middle(low, lay, order)
+    down_g1.half()
+    outputs = sums_start(*second.down_partial(), lay, order)
+    second.mid_low = rows_done(low, order)
+    outputs = sums_middle(outputs, lay, order)
     partial = second.attention_back()
-    qkv_1 = qkv_collect(second)
-    second_grad = second.finish_back(partial, round_of([gate_up_1], [qkv_1]))
-
-    first.start_back(second_grad.astype(BF16).astype(F32))
-    down_0 = Collect(joined(first.hidden), joined(first.down_in))
+    sums = sums_start(*partial, lay, order)
+    second_out = second.mid_stream + sums_done(outputs, order)
+    low = mm_nt(joined(second.lows), spread_lanes).astype(BF16)
+    qkv_g1 = Collect(joined(second.normed), low, lay, order)
+    gate_up_g1.shard_done()
+    qkv_g1.shard()
+    sums = sums_middle(sums, lay, order)
+    upstream = sums_done(sums, order)
+    down_g1.half_done()
+    gate_up_g1.half()
+    second_grad = second.first_norm_back(upstream)
+
+    first_cot = second_grad.astype(BF16)
+    down_in = rows_start(first_cot, lay, order)
+    down_in = rows_middle(down_in, lay, order)
+    first.down_in = rows_done(down_in, order)
+    down_g0 = Collect(joined(first.hidden), joined(first.down_in), lay, order)
+    qkv_g1.shard_done()
+    down_g0.shard()
     partial = first.feed_forward_back()
-    partial[0] = after(partial[0], down_0.over_shard(over_shard))
-    gate_0, up_0 = gate_up_collects(first)
-    first.middle_back(partial, round_of([qkv_1], [gate_0]), round_of([down_0], [up_0]))
+    sums = sums_start(*partial, lay, order)
+    left = joined(first.normed_mid)
+    gate_g0 = Collect(left, joined(first.gate_grad), lay, order)
+    up_g0 = Collect(left, joined(first.up_grad), lay, order)
+    gate_up_g1.half_done()
+    qkv_g1.half()
+    sums = sums_middle(sums, lay, order)
+    upstream = sums_done(sums, order)
+    low = rows_start(first.second_norm_back(first_cot.astype(F32), upstream), lay, order)
+    down_g0.shard_done()
+    gate_g0.shard()
+    qkv_g1.half_done()
+    down_g0.half()
+    low = rows_middle(low, lay, order)
+    first.mid_low = rows_done(low, order)
+    mlp_1 = by_member(gate_up_g1.total)
+    others_1 = to_members(mlp_1.astype(BF16), lay, order)
     partial = first.attention_back()
-    qkv_0 = qkv_collect(first)
-    last = [gate_0.over_half(over_half, (first.lows[0],))]
-    last.append(up_0.over_half(over_half, (first.lows[0],), beside=True))
-    partial[1] = after(partial[1], *last)
-    first_grad = first.finish_back(partial)
-
-    def by_member(*blocks):
-        return jnp.concatenate(blocks, 1).reshape(lay.group, row_block, -1)
-
-    out_both = CollectOut([out_pair(which, spread_out) for which in (first, second)], lay, row_block)
-    order = Order()
-    order.last = (first_grad,)
-    gains, gains_other = jnp.stack([first.gain_grads, second.gain_grads]), None
+    first.lows = order.each(first.lows)
+    others_1 = order.each(others_1)
+    gate_g0.shard_done()
+    up_g0.shard()
+    down_g0.half_done()
+    gate_g0.half()
+    sums = sums_start(*partial, lay, order)
+    low = mm_nt(joined(first.lows), spread_lanes).astype(BF16)
+    qkv_g0 = Collect(joined(first.normed), low, lay, order)
+    sums = sums_middle(sums, lay, order)
+    upstream = sums_done(sums, order)
+    first_grad = first.first_norm_back(upstream)
+
+    out_both = CollectOut(
+        [out_pair(which, spread_out) for which in (first, second)], lay, order, row_block
+    )
+    up_g0.shard_done()
+    up_g0.half()
+    qkv_g0.shard()
+    out_both.shard()
+    gains = jnp.stack([first.gain_grads, second.gain_grads])
     gains_other = lay.to_core(order(pick(gains, 1 - lay.core)))
-    arrived = return_rows(first_grad.astype(BF16), second_out.astype(BF16), lay, order)
+    gate_g0.half_done()
+    down_join = join_cores(down_g0.total, down_g1.total, lay, order)
     gains = pick(gains, lay.core) + order(gains_other)
     gains = gains.reshape(2, lay.shards, lay.halves, lay.group, -1).transpose(1, 2, 3, 0, 4)
     gains_other = lay.to_shard(order(pick(gains, 1 - lay.shard)))
-    order.sent(qkv_0.over_shard, over_shard)
-    down_join = join_cores(down_0.total(order.last), down_1.total(order.last), lay, order)
-    straight, crossed = order(*arrived)
-    ends = two_way(lay.half ^ lay.core, straight, crossed, 0)
-    mlp = [block.total(order.last) for block in (gate_up_1, qkv_1, gate_0, up_0)]
-    mlp = by_member(*mlp)
-    others = to_members(mlp.astype(BF16), lay, order)
+    down_g = to_outer(joined_cores(down_join, lay, order).reshape(-1, width), lay)
+    back_1 = place(pick(mlp_1, lay.member), [block.astype(F32) for block in others_1], lay.member)
+    qkv_g0.shard_done()
+    up_g0.half_done()
+    qkv_g0.half()
+    mlp_0 = by_member(gate_g0.total, up_g0.total)
+    others_0 = to_members(mlp_0.astype(BF16), lay, order)
+    rows_other = return_rows(first_grad.astype(BF16), second_out.astype(BF16), lay, order)
+    others_0 = order.each(others_0)
+    back_0 = place(pick(mlp_0, lay.member), [block.astype(F32) for block in others_0], lay.member)
+    ff_join = join_cores(back_0, back_1, lay, order)
+    out_both.shard_done()
+    out_both.half()
     gains = pick(gains, lay.shard) + order(gains_other)
     gains_other = lay.to_half(order(pick(gains, 1 - lay.half)))
-    qkv_0.got = order(qkv_0.got)
-    order.sent(qkv_0.over_half, over_half)
-    order.sent(out_both.over_shard, over_shard)
-    down_join = joined_cores(down_join, lay, order)
-    others = listed(order(*others))
-    back = place(pick(mlp, lay.member), [block.astype(F32) for block in others], lay.member)
-    ff_join = join_cores(back[..., cols + 2 * ff :], back[..., : 2 * ff], lay, order)
+    gate_up_g = order.each(unpack_ff(joined_cores(ff_join, lay, order), lay, ff_unit))
+    qkv_g0.half_done()
+    attn = by_member(qkv_g0.total, qkv_g1.total)
+    others_q = to_members(attn.astype(BF16), lay, order)
+    straight, crossed = order(*rows_other)
+    ends = two_way(lay.half ^ lay.core, straight, crossed, 0)
+    others_q = order.each(others_q)
+    back_q = place(pick(attn, lay.member), [block.astype(F32) for block in others_q], lay.member)
+    qkv_join = join_cores(back_q[..., :cols], back_q[..., cols:], lay, order)
     gains = pick(gains, lay.half) + order(gains_other)
-    mlp = by_member(qkv_0.total(order.last))
-    others = to_members(mlp.astype(BF16), lay, order)
     gain_g = pick(gains, lay.member)
     gain_others = to_members(gains, lay, order)
-    if out_both.aligned:
-        out_both.got = order(out_both.got)
-    order.sent(out_both.over_half, over_half)
-    gate_up_g = unpack_ff(joined_cores(ff_join, lay, order), lay, ff_unit)
-    others = listed(order(*others))
-    back_0 = place(pick(mlp, lay.member), [block.astype(F32) for block in others], lay.member)
-    qkv_join = join_cores(back_0, back[..., 2 * ff : 2 * ff + cols], lay, order)
-    for block in listed(order(*gain_others)):
+    qkv_g = unpack_heads(joined_cores(qkv_join, lay, order), lay)
+    out_both.half_done()
+    out_join = join_out_start(*out_both.total, lay, order, row_block)
+    for block in order.each(gain_others):
         gain_g = gain_g + block
-    qkv_g = unpack_heads(joined_cores(qkv_join, lay, order), lay)
-    out_g = to_outer(join_out(*out_both.total(order.last), lay, row_block), lay)
-    down_g = to_outer(down_join.reshape(-1, width), lay)
+    out_g = to_outer(join_out(out_join, lay, order), lay)
     ends = to_outer(ends, lay)
     return (
         ends[None, :, None],

time: 647 us -> 604 us (0.934)
  waiting for transfers between devices: 278 us -> 251 us
  local copies, waits for them, and re-layouts: 31.7 us -> 23.3 us
  matrix products: 67 us -> 59.9 us
    ppermute x133 -> x136, waiting for transfers between devices: 266 us -> 251 us  [move(): return lax.ppermute(block, MESH_AXES, pairs)]
    ppermute x2, waiting for transfers between devices: 11.4 us -> 0.01 us  [move_some(): return lax.ppermute(block, MESH_AXES, pairs)]
    ppermute x133 -> x136, starting transfers between devices: 148 us -> 157 us  [move(): return lax.ppermute(block, MESH_AXES, pairs)]
    unnamed x239 -> x265, local copies, waits for them, and re-layouts: 14.8 us -> 10.5 us
    convert_element_type x21 -> x25, other arithmetic: 13 us -> 13.1 us  [the longest x7 4.97 us: half(): rows, got = (self.rows, self.got.astype(F32))]
  transfers between devices with their start and end apart: 135 -> 138, of which waited for: 58 -> 72; matrix products, arithmetic and copies ran while one was open for 22% -> 20% of each run, Pallas kernels for 6% -> 7%
where the time goes in v4:
time: 604 us; the launch traced here: 598 us
  waiting for transfers between devices  251 us (42%)
  starting transfers between devices  160 us (26%)
  matrix products  59.9 us (10%)
  other arithmetic  57.4 us (10%)
  Pallas kernels  42.3 us (7%)
  local copies, waits for them, and re-layouts  23.3 us (4%)
    ppermute x136, waiting for transfers between devices, move(): return lax.ppermute(block, MESH_AXES, pairs)  251 us
    ppermute x136, starting transfers between devices, move(): return lax.ppermute(block, MESH_AXES, pairs)  157 us
    pallas_call x10, Pallas kernels, rearrange(): pl.pallas_call(lambda *refs: rearrange_kernel(plans, len(sources), *refs)...  25.2 us
    dot_general x22, matrix products, mm(): lax.dot_general(a, b, (((1,), (0,)), ((), ())), preferred_element_type=F32)  21.1 us
    dot_general x20, matrix products, mm_tn(): lax.dot_general(a, b, (((0,), (0,)), ((), ())), preferred_element_type=F32)  19.8 us
    dot_general x24, matrix products, mm_nt(): lax.dot_general(a, b, (((1,), (1,)), ((), ())), preferred_element_type=F32)  19 us
  transfers between devices with their start and end apart: 138, of which 72 were waited for; matrix products, arithmetic and copies ran while one was open for 20% of the time, Pallas kernels for 7%

profile of v4, /device:TPU:0, one launch (start us, length us, event | category | flops | bytes accessed | tf_op | source)
XLA Modules:
  0.0 597.8 jit_solution(2385941899037961809)
XLA Ops:
  45.3 9.7 %collective-permute-start.15 = (bf16[64,1536]{1,0:T(8,128)(2,1)S(1)}, bf16[64,1536]{1,0:T(8,128)(2,1)S(1)}, u32[]{:S(2)}, u32[]{:S(2)}) collective-permute-start(bf16[64,1536]{1,0:T(8,128)(2,1)S(1)} %pad_maximum_fusion.45), channel_id=1, source_target_pairs={{0,4},{1,5},{2,6},{3,7},{4,0},{5,1},{6,2},{7,3},{8,12},{9,13},{10,... | collective-permute-start | bytes 589832 | tf_op jit(solution)/shard_map/ppermute | solution.py:46
  55.0 4.5 collective-permute-done.17
  63.5 5.2 collective-permute-done.16
  69.5 4.2 collective-permute-done.18
  79.8 4.0 attend.2
  98.8 4.8 collective-permute-start.27
  105.0 6.1 %collective-permute-done.27 = bf16[64,1536]{1,0:T(8,128)(2,1)S(1)} collective-permute-done((bf16[64,1536]{1,0:T(8,128)(2,1)S(1)}, bf16[64,1536]{1,0:T(8,128)(2,1)S(1)}, u32[]{:S(2)}, u32[]{:S(2)}) %collective-permute-start.27) | collective-permute-done | bytes 196640 | tf_op jit(solution)/shard_map/ppermute | solution.py:46
  111.1 8.0 %collective-permute-done.28 = bf16[64,1536]{1,0:T(8,128)(2,1)S(1)} collective-permute-done((bf16[64,1536]{1,0:T(8,128)(2,1)S(1)}, bf16[64,1536]{1,0:T(8,128)(2,1)S(1)}, u32[]{:S(2)}, u32[]{:S(2)}) %collective-permute-start.28) | collective-permute-done | bytes 196640 | tf_op jit(solution)/shard_map/ppermute | solution.py:46
  127.2 9.0 %collective-permute-done.32 = bf16[64,1536]{1,0:T(8,128)(2,1)S(1)} collective-permute-done((bf16[64,1536]{1,0:T(8,128)(2,1)S(1)}, bf16[64,1536]{1,0:T(8,128)(2,1)S(1)}, u32[]{:S(2)}, u32[]{:S(2)}) %collective-permute-start.32) | collective-permute-done | bytes 196640 | tf_op jit(solution)/shard_map/ppermute | solution.py:46
  149.5 7.1 %collective-permute-done.38 = bf16[96,1408]{1,0:T(8,128)(2,1)S(1)} collective-permute-done((bf16[96,1408]{1,0:T(8,128)(2,1)S(1)}, bf16[96,1408]{1,0:T(8,128)(2,1)S(1)}, u32[]{:S(2)}, u32[]{:S(2)}) %collective-permute-start.38) | collective-permute-done | bytes 270368 | tf_op jit(solution)/shard_map/ppermute | solution.py:46
  156.6 4.4 collective-permute-done.39
  172.7 6.6 %collective-permute-done.45 = bf16[64,1536]{1,0:T(8,128)(2,1)S(1)} collective-permute-done((bf16[64,1536]{1,0:T(8,128)(2,1)S(1)}, bf16[64,1536]{1,0:T(8,128)(2,1)S(1)}, u32[]{:S(2)}, u32[]{:S(2)}) %collective-permute-start.45) | collective-permute-done | bytes 196640 | tf_op jit(solution)/shard_map/ppermute | solution.py:46
  181.3 8.3 %collective-permute-done.42 = bf16[256,1536]{1,0:T(8,128)(2,1)S(1)} collective-permute-done((bf16[256,1536]{1,0:T(8,128)(2,1)S(1)}, bf16[256,1536]{1,0:T(8,128)(2,1)S(1)}, u32[]{:S(2)}, u32[]{:S(2)}) %collective-permute-start.42) | collective-permute-done | bytes 786464 | tf_op jit(solution)/shard_map/ppermute | solution.py:46
  200.4 7.3 %collective-permute-done.49 = bf16[64,1536]{1,0:T(8,128)(2,1)S(1)} collective-permute-done((bf16[64,1536]{1,0:T(8,128)(2,1)S(1)}, bf16[64,1536]{1,0:T(8,128)(2,1)S(1)}, u32[]{:S(2)}, u32[]{:S(2)}) %collective-permute-start.49) | collective-permute-done | bytes 196640 | tf_op jit(solution)/shard_map/ppermute | solution.py:46
  217.8 9.3 %collective-permute-done.52 = bf16[64,1536]{1,0:T(8,128)(2,1)S(1)} collective-permute-done((bf16[64,1536]{1,0:T(8,128)(2,1)S(1)}, bf16[64,1536]{1,0:T(8,128)(2,1)S(1)}, u32[]{:S(2)}, u32[]{:S(2)}) %collective-permute-start.52) | collective-permute-done | bytes 196640 | tf_op jit(solution)/shard_map/ppermute | solution.py:46
  227.1 8.1 %collective-permute-done.53 = bf16[64,1536]{1,0:T(8,128)(2,1)S(1)} collective-permute-done((bf16[64,1536]{1,0:T(8,128)(2,1)S(1)}, bf16[64,1536]{1,0:T(8,128)(2,1)S(1)}, u32[]{:S(2)}, u32[]{:S(2)}) %collective-permute-start.53) | collective-permute-done | bytes 196640 | tf_op jit(solution)/shard_map/ppermute | solution.py:46
  242.0 4.0 attend.3
  261.4 3.9 collective-permute-done.60
  265.3 8.6 %collective-permute-done.62 = bf16[768,1024]{1,0:T(8,128)(2,1)} collective-permute-done((bf16[768,1024]{1,0:T(8,128)(2,1)}, bf16[768,1024]{1,0:T(8,128)(2,1)}, u32[]{:S(2)}, u32[]{:S(2)}) %collective-permute-start.62) | collective-permute-done | bytes 1572896 | tf_op jit(solution)/shard_map/ppermute | solution.py:46
  291.7 5.5 collective-permute-done.63
  339.4 4.6 attend_back.2
  353.7 4.5 collective-permute-done.83
  369.0 8.7 %collective-permute-done.85 = bf16[64,1536]{1,0:T(8,128)(2,1)S(1)} collective-permute-done((bf16[64,1536]{1,0:T(8,128)(2,1)S(1)}, bf16[64,1536]{1,0:T(8,128)(2,1)S(1)}, u32[]{:S(2)}, u32[]{:S(2)}) %collective-permute-start.85) | collective-permute-done | bytes 196640 | tf_op jit(solution)/shard_map/ppermute | solution.py:46
  388.1 7.4 %collective-permute-done.89 = bf16[64,1536]{1,0:T(8,128)(2,1)S(1)} collective-permute-done((bf16[64,1536]{1,0:T(8,128)(2,1)S(1)}, bf16[64,1536]{1,0:T(8,128)(2,1)S(1)}, u32[]{:S(2)}, u32[]{:S(2)}) %collective-permute-start.89) | collective-permute-done | bytes 196640 | tf_op jit(solution)/shard_map/ppermute | solution.py:46
  405.6 17.9 %collective-permute-done.94 = bf16[384,1024]{1,0:T(8,128)(2,1)S(1)} collective-permute-done((bf16[384,1024]{1,0:T(8,128)(2,1)S(1)}, bf16[384,1024]{1,0:T(8,128)(2,1)S(1)}, u32[]{:S(2)}, u32[]{:S(2)}) %collective-permute-start.94) | collective-permute-done | bytes 786464 | tf_op jit(solution)/shard_map/ppermute | solution.py:46
  428.7 6.0 %collective-permute-start.95 = (bf16[64,1536]{1,0:T(8,128)(2,1)S(1)}, bf16[64,1536]{1,0:T(8,128)(2,1)S(1)}, u32[]{:S(2)}, u32[]{:S(2)}) collective-permute-start(bf16[64,1536]{1,0:T(8,128)(2,1)S(1)} %get-tuple-element.494), channel_id=1, source_target_pairs={{0,2},{1,3},{2,0},{3,1},{4,6},{5,7},{6,4},{7,5},{8,10},{9,11},{10,... | collective-permute-start | bytes 589832 | tf_op jit(solution)/shard_map/ppermute | solution.py:46
  449.4 6.3 %collective-permute-start.108 = (bf16[128,1536]{1,0:T(8,128)(2,1)}, bf16[128,1536]{1,0:T(8,128)(2,1)}, u32[]{:S(2)}, u32[]{:S(2)}) collective-permute-start(bf16[128,1536]{1,0:T(8,128)(2,1)} %fusion.41), channel_id=1, source_target_pairs={{0,8},{1,9},{2,10},{3,11},{4,12},{5,13},{6,14},{7,15},{8,0},{9,1},... | collective-permute-start | bytes 1179656 | tf_op jit(solution)/shard_map/ppermute | solution.py:46
  461.6 4.6 attend_back.3
  476.1 4.1 collective-permute-done.107
  496.1 9.3 %collective-permute-done.111 = bf16[64,1536]{1,0:T(8,128)(2,1)S(1)} collective-permute-done((bf16[64,1536]{1,0:T(8,128)(2,1)S(1)}, bf16[64,1536]{1,0:T(8,128)(2,1)S(1)}, u32[]{:S(2)}, u32[]{:S(2)}) %collective-permute-start.111) | collective-permute-done | bytes 196640 | tf_op jit(solution)/shard_map/ppermute | solution.py:46
  521.2 8.5 %collective-permute-done.116 = bf16[768,384]{1,0:T(8,128)(2,1)} collective-permute-done((bf16[768,384]{1,0:T(8,128)(2,1)}, bf16[768,384]{1,0:T(8,128)(2,1)}, u32[]{:S(2)}, u32[]{:S(2)}) %collective-permute-start.116) | collective-permute-done | bytes 589856 | tf_op jit(solution)/shard_map/ppermute | solution.py:46
  575.3 5.5 collective-permute-done.130
  (838 shorter events, 377.8 us)
Async XLA Ops:
  36.9 22.6 %collective-permute-start.17 = (bf16[384,384]{1,0:T(8,128)(2,1)S(1)}, bf16[384,384]{1,0:T(8,128)(2,1)S(1)}, u32[]{:S(2)}, u32[]{:S(2)}) collective-permute-start(bf16[384,384]{1,0:T(8,128)(2,1)S(1)} %bitcast.302), channel_id=1, source_target_pairs={{0,8},{1,9},{2,10},{3,11},{4,12},{5,13},{6,14},{7,15},{8,0},{9,1},... | collective-permute-start | bytes 884744 | tf_op jit(solution)/shard_map/ppermute | solution.py:46
  43.8 19.5 %collective-permute-start.14 = (bf16[64,1536]{1,0:T(8,128)(2,1)S(1)}, bf16[64,1536]{1,0:T(8,128)(2,1)S(1)}, u32[]{:S(2)}, u32[]{:S(2)}) collective-permute-start(bf16[64,1536]{1,0:T(8,128)(2,1)S(1)} %pad_maximum_fusion.45), channel_id=1, source_target_pairs={{0,2},{1,3},{2,0},{3,1},{4,6},{5,7},{6,4},{7,5},{8,10},{9,11},{10,... | collective-permute-start | bytes 589832 | tf_op jit(solution)/shard_map/ppermute | solution.py:46
  96.6 22.4 %collective-permute-start.30 = (bf16[384,512]{1,0:T(8,128)(2,1)S(1)}, bf16[384,512]{1,0:T(8,128)(2,1)S(1)}, u32[]{:S(2)}, u32[]{:S(2)}) collective-permute-start(bf16[384,512]{1,0:T(8,128)(2,1)S(1)} %get-tuple-element.353), channel_id=1, source_target_pairs={{0,8},{1,9},{2,10},{3,11},{4,12},{5,13},{6,14},{7,15},{8,0},{9,1},... | collective-permute-start | bytes 1179656 | tf_op jit(solution)/shard_map/ppermute | solution.py:46
  124.6 18.7 %collective-permute-start.35 = (bf16[384,512]{1,0:T(8,128)(2,1)S(1)}, bf16[384,512]{1,0:T(8,128)(2,1)S(1)}, u32[]{:S(2)}, u32[]{:S(2)}) collective-permute-start(bf16[384,512]{1,0:T(8,128)(2,1)S(1)} %get-tuple-element.369), channel_id=1, source_target_pairs={{0,8},{1,9},{2,10},{3,11},{4,12},{5,13},{6,14},{7,15},{8,0},{9,1},... | collective-permute-start | bytes 1179656 | tf_op jit(solution)/shard_map/ppermute | solution.py:46
  127.1 18.7 %collective-permute-start.34 = (bf16[768,512]{1,0:T(8,128)(2,1)S(1)}, bf16[768,512]{1,0:T(8,128)(2,1)S(1)}, u32[]{:S(2)}, u32[]{:S(2)}) collective-permute-start(bf16[768,512]{1,0:T(8,128)(2,1)S(1)} %pad_maximum_fusion.12), channel_id=1, source_target_pairs={{0,1},{1,0},{2,3},{3,2},{4,5},{5,4},{6,7},{7,6},{8,9},{9,8},{10,11... | collective-permute-start | bytes 2359304 | tf_op jit(solution)/shard_map/ppermute | solution.py:46
  146.0 19.3 %collective-permute-start.41 = (bf16[128,1536]{1,0:T(8,128)(2,1)S(1)}, bf16[128,1536]{1,0:T(8,128)(2,1)S(1)}, u32[]{:S(2)}, u32[]{:S(2)}) collective-permute-start(bf16[128,1536]{1,0:T(8,128)(2,1)S(1)} %get-tuple-element.381), channel_id=1, source_target_pairs={{0,8},{1,9},{2,10},{3,11},{4,12},{5,13},{6,14},{7,15},{8,0},{9,1},... | collective-permute-start | bytes 1179656 | tf_op jit(solution)/shard_map/ppermute | solution.py:46
  196.8 38.6 %collective-permute-start.55 = (bf16[384,1024]{1,0:T(8,128)(2,1)S(1)}, bf16[384,1024]{1,0:T(8,128)(2,1)S(1)}, u32[]{:S(2)}, u32[]{:S(2)}) collective-permute-start(bf16[384,1024]{1,0:T(8,128)(2,1)S(1)} %slice.779), channel_id=1, source_target_pairs={{0,8},{1,9},{2,10},{3,11},{4,12},{5,13},{6,14},{7,15},{8,0},{9,1},... | collective-permute-start | bytes 2359304 | tf_op jit(solution)/shard_map/ppermute | solution.py:46
  212.9 22.2 %collective-permute-start.53 = (bf16[64,1536]{1,0:T(8,128)(2,1)S(1)}, bf16[64,1536]{1,0:T(8,128)(2,1)S(1)}, u32[]{:S(2)}, u32[]{:S(2)}) collective-permute-start(bf16[64,1536]{1,0:T(8,128)(2,1)S(1)} %pad_maximum_fusion.47), channel_id=1, source_target_pairs={{0,6},{1,7},{2,4},{3,5},{4,2},{5,3},{6,0},{7,1},{8,14},{9,15},{10,... | collective-permute-start | bytes 589832 | tf_op jit(solution)/shard_map/ppermute | solution.py:46
  215.5 21.7 %collective-permute-start.54 = (bf16[768,384]{1,0:T(8,128)(2,1)S(1)}, bf16[768,384]{1,0:T(8,128)(2,1)S(1)}, u32[]{:S(2)}, u32[]{:S(2)}) collective-permute-start(bf16[768,384]{1,0:T(8,128)(2,1)S(1)} %pad_maximum_fusion.26), channel_id=1, source_target_pairs={{0,1},{1,0},{2,3},{3,2},{4,5},{5,4},{6,7},{7,6},{8,9},{9,8},{10,11... | collective-permute-start | bytes 1769480 | tf_op jit(solution)/shard_map/ppermute | solution.py:46
  236.9 37.0 %collective-permute-start.62 = (bf16[768,1024]{1,0:T(8,128)(2,1)}, bf16[768,1024]{1,0:T(8,128)(2,1)}, u32[]{:S(2)}, u32[]{:S(2)}) collective-permute-start(bf16[768,1024]{1,0:T(8,128)(2,1)} %pad_maximum_fusion.5), channel_id=1, source_target_pairs={{0,1},{1,0},{2,3},{3,2},{4,5},{5,4},{6,7},{7,6},{8,9},{9,8},{10,11... | collective-permute-start | bytes 4718600 | tf_op jit(solution)/shard_map/ppermute | solution.py:46
  237.2 36.7 %collective-permute-start.61 = (bf16[128,1536]{1,0:T(8,128)(2,1)}, bf16[128,1536]{1,0:T(8,128)(2,1)}, u32[]{:S(2)}, u32[]{:S(2)}) collective-permute-start(bf16[128,1536]{1,0:T(8,128)(2,1)} %get-tuple-element.414), channel_id=1, source_target_pairs={{0,8},{1,9},{2,10},{3,11},{4,12},{5,13},{6,14},{7,15},{8,0},{9,1},... | collective-permute-start | bytes 1179656 | tf_op jit(solution)/shard_map/ppermute | solution.py:46
  258.1 32.9 %collective-permute-start.68 = (bf16[256,1536]{1,0:T(8,128)(2,1)S(1)}, bf16[256,1536]{1,0:T(8,128)(2,1)S(1)}, u32[]{:S(2)}, u32[]{:S(2)}) collective-permute-start(bf16[256,1536]{1,0:T(8,128)(2,1)S(1)} %copy-done.16), channel_id=1, source_target_pairs={{0,16},{1,17},{2,18},{3,19},{4,20},{5,21},{6,22},{7,23},{8,24},{9,... | collective-permute-start | bytes 2359304 | tf_op jit(solution)/shard_map/ppermute | solution.py:46
  300.7 19.8 %collective-permute-start.73 = (bf16[256,1536]{1,0:T(8,128)(2,1)S(1)}, bf16[256,1536]{1,0:T(8,128)(2,1)S(1)}, u32[]{:S(2)}, u32[]{:S(2)}) collective-permute-start(bf16[256,1536]{1,0:T(8,128)(2,1)S(1)} %convolution_convert_fusion.8), channel_id=1, source_target_pairs={{0,1},{1,0},{2,3},{3,2},{4,5},{5,4},{6,7},{7,6},{8,9},{9,8},{10,11... | collective-permute-start | bytes 2359304 | tf_op jit(solution)/shard_map/ppermute | solution.py:46
  313.3 44.9 %collective-permute-start.80 = (bf16[768,1024]{1,0:T(8,128)(2,1)}, bf16[768,1024]{1,0:T(8,128)(2,1)}, u32[]{:S(2)}, u32[]{:S(2)}) collective-permute-start(bf16[768,1024]{1,0:T(8,128)(2,1)} %convolution_convert_fusion.14), channel_id=1, source_target_pairs={{0,1},{1,0},{2,3},{3,2},{4,5},{5,4},{6,7},{7,6},{8,9},{9,8},{10,11... | collective-permute-start | bytes 4718600 | tf_op jit(solution)/shard_map/ppermute | solution.py:46
  352.5 28.2 %collective-permute-start.87 = (bf16[128,1536]{1,0:T(8,128)(2,1)S(1)}, bf16[128,1536]{1,0:T(8,128)(2,1)S(1)}, u32[]{:S(2)}, u32[]{:S(2)}) collective-permute-start(bf16[128,1536]{1,0:T(8,128)(2,1)S(1)} %copy-done.84), channel_id=1, source_target_pairs={{0,8},{1,9},{2,10},{3,11},{4,12},{5,13},{6,14},{7,15},{8,0},{9,1},... | collective-permute-start | bytes 1179656 | tf_op jit(solution)/shard_map/ppermute | solution.py:46
  360.1 40.5 %collective-permute-start.92 = (bf16[768,384]{1,0:T(8,128)(2,1)S(1)}, bf16[768,384]{1,0:T(8,128)(2,1)S(1)}, u32[]{:S(2)}, u32[]{:S(2)}) collective-permute-start(bf16[768,384]{1,0:T(8,128)(2,1)S(1)} %convolution_convert_fusion.18), channel_id=1, source_target_pairs={{0,1},{1,0},{2,3},{3,2},{4,5},{5,4},{6,7},{7,6},{8,9},{9,8},{10,11... | collective-permute-start | bytes 1769480 | tf_op jit(solution)/shard_map/ppermute | solution.py:46
  385.0 38.5 %collective-permute-start.94 = (bf16[384,1024]{1,0:T(8,128)(2,1)S(1)}, bf16[384,1024]{1,0:T(8,128)(2,1)S(1)}, u32[]{:S(2)}, u32[]{:S(2)}) collective-permute-start(bf16[384,1024]{1,0:T(8,128)(2,1)S(1)} %fusion.5), channel_id=1, source_target_pairs={{0,8},{1,9},{2,10},{3,11},{4,12},{5,13},{6,14},{7,15},{8,0},{9,1},... | collective-permute-start | bytes 2359304 | tf_op jit(solution)/shard_map/ppermute | solution.py:46
  402.3 45.2 %collective-permute-start.101 = (bf16[256,1536]{1,0:T(8,128)(2,1)S(1)}, bf16[256,1536]{1,0:T(8,128)(2,1)S(1)}, u32[]{:S(2)}, u32[]{:S(2)}) collective-permute-start(bf16[256,1536]{1,0:T(8,128)(2,1)S(1)} %convolution_convert_fusion.5), channel_id=1, source_target_pairs={{0,1},{1,0},{2,3},{3,2},{4,5},{5,4},{6,7},{7,6},{8,9},{9,8},{10,11... | collective-permute-start | bytes 2359304 | tf_op jit(solution)/shard_map/ppermute | solution.py:46
  405.4 22.6 %collective-permute-start.93 = (bf16[256,1536]{1,0:T(8,128)(2,1)S(1)}, bf16[256,1536]{1,0:T(8,128)(2,1)S(1)}, u32[]{:S(2)}, u32[]{:S(2)}) collective-permute-start(bf16[256,1536]{1,0:T(8,128)(2,1)S(1)} %fusion.1), channel_id=1, source_target_pairs={{0,16},{1,17},{2,18},{3,19},{4,20},{5,21},{6,22},{7,23},{8,24},{9,... | collective-permute-start | bytes 2359304 | tf_op jit(solution)/shard_map/ppermute | solution.py:46
  424.1 23.7 %collective-permute-start.102 = (bf16[384,384]{1,0:T(8,128)(2,1)S(1)}, bf16[384,384]{1,0:T(8,128)(2,1)S(1)}, u32[]{:S(2)}, u32[]{:S(2)}) collective-permute-start(bf16[384,384]{1,0:T(8,128)(2,1)S(1)} %fusion.66), channel_id=1, source_target_pairs={{0,8},{1,9},{2,10},{3,11},{4,12},{5,13},{6,14},{7,15},{8,0},{9,1},... | collective-permute-start | bytes 884744 | tf_op jit(solution)/shard_map/ppermute | solution.py:46
  447.7 32.4 %collective-permute-start.104 = (bf16[768,512]{1,0:T(8,128)(2,1)}, bf16[768,512]{1,0:T(8,128)(2,1)}, u32[]{:S(2)}, u32[]{:S(2)}) collective-permute-start(bf16[768,512]{1,0:T(8,128)(2,1)} %convolution_convert_fusion.16), channel_id=1, source_target_pairs={{0,1},{1,0},{2,3},{3,2},{4,5},{5,4},{6,7},{7,6},{8,9},{9,8},{10,11... | collective-permute-start | bytes 2359304 | tf_op jit(solution)/shard_map/ppermute | solution.py:46
  449.4 33.5 %collective-permute-start.108 = (bf16[128,1536]{1,0:T(8,128)(2,1)}, bf16[128,1536]{1,0:T(8,128)(2,1)}, u32[]{:S(2)}, u32[]{:S(2)}) collective-permute-start(bf16[128,1536]{1,0:T(8,128)(2,1)} %fusion.41), channel_id=1, source_target_pairs={{0,8},{1,9},{2,10},{3,11},{4,12},{5,13},{6,14},{7,15},{8,0},{9,1},... | collective-permute-start | bytes 1179656 | tf_op jit(solution)/shard_map/ppermute | solution.py:46
  481.5 27.5 %collective-permute-start.114 = (bf16[768,512]{1,0:T(8,128)(2,1)S(1)}, bf16[768,512]{1,0:T(8,128)(2,1)S(1)}, u32[]{:S(2)}, u32[]{:S(2)}) collective-permute-start(bf16[768,512]{1,0:T(8,128)(2,1)S(1)} %copy-done.125), channel_id=1, source_target_pairs={{0,1},{1,0},{2,3},{3,2},{4,5},{5,4},{6,7},{7,6},{8,9},{9,8},{10,11... | collective-permute-start | bytes 2359304 | tf_op jit(solution)/shard_map/ppermute | solution.py:46
  483.7 32.1 %collective-permute-start.113 = (bf16[384,512]{1,0:T(8,128)(2,1)S(1)}, bf16[384,512]{1,0:T(8,128)(2,1)S(1)}, u32[]{:S(2)}, u32[]{:S(2)}) collective-permute-start(bf16[384,512]{1,0:T(8,128)(2,1)S(1)} %fusion.40), channel_id=1, source_target_pairs={{0,8},{1,9},{2,10},{3,11},{4,12},{5,13},{6,14},{7,15},{8,0},{9,1},... | collective-permute-start | bytes 1179656 | tf_op jit(solution)/shard_map/ppermute | solution.py:46
  510.9 20.6 %collective-permute-start.115 = (bf16[384,512]{1,0:T(8,128)(2,1)}, bf16[384,512]{1,0:T(8,128)(2,1)}, u32[]{:S(2)}, u32[]{:S(2)}) collective-permute-start(bf16[384,512]{1,0:T(8,128)(2,1)} %fusion.37), channel_id=1, source_target_pairs={{0,8},{1,9},{2,10},{3,11},{4,12},{5,13},{6,14},{7,15},{8,0},{9,1},... | collective-permute-start | bytes 1179656 | tf_op jit(solution)/shard_map/ppermute | solution.py:46
  513.8 35.6 %collective-permute-start.127 = (bf16[192,1536]{1,0:T(8,128)(2,1)}, bf16[192,1536]{1,0:T(8,128)(2,1)}, u32[]{:S(2)}, u32[]{:S(2)}) collective-permute-start(bf16[192,1536]{1,0:T(8,128)(2,1)} %pad_maximum_fusion.27), channel_id=1, source_target_pairs={{0,1},{1,0},{2,3},{3,2},{4,5},{5,4},{6,7},{7,6},{8,9},{9,8},{10,11... | collective-permute-start | bytes 1769480 | tf_op jit(solution)/shard_map/ppermute | solution.py:46
  519.5 32.8 %collective-permute-start.126 = (f32[2,4,2,96]{3,1,0,2:T(4,128)S(1)}, f32[2,4,2,96]{3,1,0,2:T(4,128)S(1)}, u32[]{:S(2)}, u32[]{:S(2)}) collective-permute-start(f32[2,4,2,96]{3,1,0,2:T(4,128)S(1)} %fusion.189), channel_id=1, source_target_pairs={{0,1},{1,0},{2,3},{3,2},{4,5},{5,4},{6,7},{7,6},{8,9},{9,8},{10,11... | collective-permute-start | bytes 18440 | tf_op jit(solution)/shard_map/ppermute | solution.py:46
  542.8 24.3 %collective-permute-start.121 = (bf16[384,384]{1,0:T(8,128)(2,1)S(1)}, bf16[384,384]{1,0:T(8,128)(2,1)S(1)}, u32[]{:S(2)}, u32[]{:S(2)}) collective-permute-start(bf16[384,384]{1,0:T(8,128)(2,1)S(1)} %fusion.65), channel_id=1, source_target_pairs={{0,8},{1,9},{2,10},{3,11},{4,12},{5,13},{6,14},{7,15},{8,0},{9,1},... | collective-permute-start | bytes 884744 | tf_op jit(solution)/shard_map/ppermute | solution.py:46
  543.4 25.2 %collective-permute-start.119 = (bf16[64,1536]{1,0:T(8,128)(2,1)S(1)}, bf16[64,1536]{1,0:T(8,128)(2,1)}, u32[]{:S(2)}, u32[]{:S(2)}) collective-permute-start(bf16[64,1536]{1,0:T(8,128)(2,1)S(1)} %broadcast_select_fusion.4), channel_id=1, source_target_pairs={{0,0},{1,1},{2,2},{3,3},{4,4},{5,5},{6,6},{7,7},{8,16},{9,17},{10,... | collective-permute-start | bytes 589832 | tf_op jit(solution)/shard_map/ppermute | solution.py:46
  547.0 24.4 %collective-permute-start.120 = (bf16[64,1536]{1,0:T(8,128)(2,1)S(1)}, bf16[64,1536]{1,0:T(8,128)(2,1)}, u32[]{:S(2)}, u32[]{:S(2)}) collective-permute-start(bf16[64,1536]{1,0:T(8,128)(2,1)S(1)} %copy-done.106), channel_id=1, source_target_pairs={{0,16},{1,17},{2,18},{3,19},{4,20},{5,21},{6,22},{7,23},{8,0},{9,1... | collective-permute-start | bytes 589832 | tf_op jit(solution)/shard_map/ppermute | solution.py:46
  552.3 36.2 %collective-permute-start.135 = (bf16[192,1536]{1,0:T(8,128)(2,1)S(1)}, bf16[192,1536]{1,0:T(8,128)(2,1)S(1)}, u32[]{:S(2)}, u32[]{:S(2)}) collective-permute-start(bf16[192,1536]{1,0:T(8,128)(2,1)S(1)} %fusion.57), channel_id=1, source_target_pairs={{8,0},{9,1},{10,2},{11,3},{12,4},{13,5},{14,6},{15,7},{16,24},{17,... | collective-permute-start | bytes 1769480 | tf_op jit(solution)/shard_map/ppermute | solution.py:57
  553.8 31.1 %collective-permute-start.128 = (f32[4,2,96]{2,0,1:T(4,128)S(1)}, f32[4,2,96]{2,0,1:T(4,128)S(1)}, u32[]{:S(2)}, u32[]{:S(2)}) collective-permute-start(f32[4,2,96]{2,0,1:T(4,128)S(1)} %fusion.192), channel_id=1, source_target_pairs={{0,8},{1,9},{2,10},{3,11},{4,12},{5,13},{6,14},{7,15},{8,0},{9,1},... | collective-permute-start | bytes 9224 | tf_op jit(solution)/shard_map/ppermute | solution.py:46
  (234 other events, 2996.0 us)

commit v5 on v4

--- a/solution.py
+++ b/solution.py
@@ -693,12 +693,13 @@
         self.mid_grad = out_grad + part
         return self.mid_grad.astype(BF16)
 
-    def attention_back(self):
+    def attention_back(self, order):
         grads = [
             out_order(mm_nt(block, self.out_w).astype(BF16), self.lay, self.n_query)
             for block in self.mid_low
         ]
         self.lows = attend_back(self.attn_kept, grads, self.tables, self.n_query, self.n_key)
+        self.lows = order.each(self.lows)
         return [mm_nt(block, self.qkv_w) for block in self.lows]
 
     def first_norm_back(self, upstream):
@@ -911,12 +912,9 @@
     low = rows_start(low, lay, order)
     low = rows_middle(low, lay, order)
     down_g1.half()
-    outputs = sums_start(*second.down_partial(), lay, order)
     second.mid_low = rows_done(low, order)
-    outputs = sums_middle(outputs, lay, order)
-    partial = second.attention_back()
+    partial = second.attention_back(order)
     sums = sums_start(*partial, lay, order)
-    second_out = second.mid_stream + sums_done(outputs, order)
     low = mm_nt(joined(second.lows), spread_lanes).astype(BF16)
     qkv_g1 = Collect(joined(second.normed), low, lay, order)
     gate_up_g1.shard_done()
@@ -939,22 +937,18 @@
     left = joined(first.normed_mid)
     gate_g0 = Collect(left, joined(first.gate_grad), lay, order)
     up_g0 = Collect(left, joined(first.up_grad), lay, order)
+    sums = sums_middle(sums, lay, order)
+    upstream = sums_done(sums, order)
     gate_up_g1.half_done()
     qkv_g1.half()
-    sums = sums_middle(sums, lay, order)
-    upstream = sums_done(sums, order)
     low = rows_start(first.second_norm_back(first_cot.astype(F32), upstream), lay, order)
     down_g0.shard_done()
     gate_g0.shard()
+    low = rows_middle(low, lay, order)
     qkv_g1.half_done()
     down_g0.half()
-    low = rows_middle(low, lay, order)
     first.mid_low = rows_done(low, order)
-    mlp_1 = by_member(gate_up_g1.total)
-    others_1 = to_members(mlp_1.astype(BF16), lay, order)
-    partial = first.attention_back()
-    first.lows = order.each(first.lows)
-    others_1 = order.each(others_1)
+    partial = first.attention_back(order)
     gate_g0.shard_done()
     up_g0.shard()
     down_g0.half_done()
@@ -972,47 +966,53 @@
     up_g0.shard_done()
     up_g0.half()
     qkv_g0.shard()
-    out_both.shard()
+    mlp_1 = by_member(gate_up_g1.total)
+    others_1 = to_members(mlp_1.astype(BF16), lay, order)
+    gate_g0.half_done()
+    up_g0.half_done()
+    others_1 = order.each(others_1)
     gains = jnp.stack([first.gain_grads, second.gain_grads])
     gains_other = lay.to_core(order(pick(gains, 1 - lay.core)))
-    gate_g0.half_done()
+    mlp_0 = by_member(gate_g0.total, up_g0.total)
+    others_0 = to_members(mlp_0.astype(BF16), lay, order)
+    qkv_g0.shard_done()
+    qkv_g0.half()
+    out_both.shard()
+    outputs = sums_start(*second.down_partial(), lay, order)
     down_join = join_cores(down_g0.total, down_g1.total, lay, order)
+    back_1 = place(pick(mlp_1, lay.member), [block.astype(F32) for block in others_1], lay.member)
+    others_0 = order.each(others_0)
     gains = pick(gains, lay.core) + order(gains_other)
     gains = gains.reshape(2, lay.shards, lay.halves, lay.group, -1).transpose(1, 2, 3, 0, 4)
-    gains_other = lay.to_shard(order(pick(gains, 1 - lay.shard)))
-    down_g = to_outer(joined_cores(down_join, lay, order).reshape(-1, width), lay)
-    back_1 = place(pick(mlp_1, lay.member), [block.astype(F32) for block in others_1], lay.member)
-    qkv_g0.shard_done()
-    up_g0.half_done()
-    qkv_g0.half()
-    mlp_0 = by_member(gate_g0.total, up_g0.total)
-    others_0 = to_members(mlp_0.astype(BF16), lay, order)
-    rows_other = return_rows(first_grad.astype(BF16), second_out.astype(BF16), lay, order)
-    others_0 = order.each(others_0)
+    outputs = sums_middle(outputs, lay, order)
     back_0 = place(pick(mlp_0, lay.member), [block.astype(F32) for block in others_0], lay.member)
     ff_join = join_cores(back_0, back_1, lay, order)
     out_both.shard_done()
     out_both.half()
+    gains_other = lay.to_shard(order(pick(gains, 1 - lay.shard)))
+    qkv_g0.half_done()
+    second_out = second.mid_stream + sums_done(outputs, order)
+    attn = by_member(qkv_g0.total, qkv_g1.total)
+    others_q = to_members(attn.astype(BF16), lay, order)
+    rows_other = return_rows(first_grad.astype(BF16), second_out.astype(BF16), lay, order)
     gains = pick(gains, lay.shard) + order(gains_other)
     gains_other = lay.to_half(order(pick(gains, 1 - lay.half)))
     gate_up_g = order.each(unpack_ff(joined_cores(ff_join, lay, order), lay, ff_unit))
-    qkv_g0.half_done()
-    attn = by_member(qkv_g0.total, qkv_g1.total)
-    others_q = to_members(attn.astype(BF16), lay, order)
-    straight, crossed = order(*rows_other)
-    ends = two_way(lay.half ^ lay.core, straight, crossed, 0)
     others_q = order.each(others_q)
     back_q = place(pick(attn, lay.member), [block.astype(F32) for block in others_q], lay.member)
     qkv_join = join_cores(back_q[..., :cols], back_q[..., cols:], lay, order)
+    out_both.half_done()
+    out_join = join_out_start(*out_both.total, lay, order, row_block)
     gains = pick(gains, lay.half) + order(gains_other)
     gain_g = pick(gains, lay.member)
     gain_others = to_members(gains, lay, order)
+    down_g = to_outer(joined_cores(down_join, lay, order).reshape(-1, width), lay)
     qkv_g = unpack_heads(joined_cores(qkv_join, lay, order), lay)
-    out_both.half_done()
-    out_join = join_out_start(*out_both.total, lay, order, row_block)
+    straight, crossed = order(*rows_other)
+    ends = two_way(lay.half ^ lay.core, straight, crossed, 0)
+    out_g = to_outer(join_out(out_join, lay, order), lay)
     for block in order.each(gain_others):
         gain_g = gain_g + block
-    out_g = to_outer(join_out(out_join, lay, order), lay)
     ends = to_outer(ends, lay)
     return (
         ends[None, :, None],

time: 604 us -> 595 us (0.985)
  starting transfers between devices: 160 us -> 141 us
  local copies, waits for them, and re-layouts: 23.3 us -> 33.1 us
    ppermute x136, starting transfers between devices: 157 us -> 138 us  [move(): return lax.ppermute(block, MESH_AXES, pairs)]
    unnamed x265 -> x319, local copies, waits for them, and re-layouts: 10.5 us -> 15.9 us
  transfers between devices with their start and end apart: 138 -> 138, of which waited for: 72 -> 65; matrix products, arithmetic and copies ran while one was open for 20% -> 21% of each run, Pallas kernels for 7% -> 7%
where the time goes in v5:
time: 595 us; the launch traced here: 589 us
  waiting for transfers between devices  252 us (42%)
  starting transfers between devices  141 us (24%)
  matrix products  58.8 us (10%)
  other arithmetic  57.2 us (10%)
  Pallas kernels  42.4 us (7%)
  local copies, waits for them, and re-layouts  33.1 us (6%)
    ppermute x136, waiting for transfers between devices, move(): return lax.ppermute(block, MESH_AXES, pairs)  252 us
    ppermute x136, starting transfers between devices, move(): return lax.ppermute(block, MESH_AXES, pairs)  138 us
    pallas_call x10, Pallas kernels, rearrange(): pl.pallas_call(lambda *refs: rearrange_kernel(plans, len(sources), *refs)...  25.2 us
    dot_general x22, matrix products, mm(): lax.dot_general(a, b, (((1,), (0,)), ((), ())), preferred_element_type=F32)  22 us
    dot_general x20, matrix products, mm_tn(): lax.dot_general(a, b, (((0,), (0,)), ((), ())), preferred_element_type=F32)  18.9 us
    dot_general x24, matrix products, mm_nt(): lax.dot_general(a, b, (((1,), (1,)), ((), ())), preferred_element_type=F32)  17.9 us
    unnamed x319, local copies, waits for them, and re-layouts  15.9 us
  transfers between devices with their start and end apart: 138, of which 65 were waited for; matrix products, arithmetic and copies ran while one was open for 21% of the time, Pallas kernels for 7%

profile of v5, /device:TPU:0, one launch (start us, length us, event | category | flops | bytes accessed | tf_op | source)
XLA Modules:
  0.0 588.6 jit_solution(3107610119176425634)
XLA Ops:
  45.2 9.4 %collective-permute-start.15 = (bf16[64,1536]{1,0:T(8,128)(2,1)S(1)}, bf16[64,1536]{1,0:T(8,128)(2,1)S(1)}, u32[]{:S(2)}, u32[]{:S(2)}) collective-permute-start(bf16[64,1536]{1,0:T(8,128)(2,1)S(1)} %pad_maximum_fusion.45), channel_id=1, source_target_pairs={{0,4},{1,5},{2,6},{3,7},{4,0},{5,1},{6,2},{7,3},{8,12},{9,13},{10,... | collective-permute-start | bytes 589832 | tf_op jit(solution)/shard_map/ppermute | solution.py:46
  54.6 4.9 collective-permute-done.17
  69.5 5.4 collective-permute-done.18
  103.2 4.1 collective-permute-start.27
  109.1 6.6 %collective-permute-done.27 = bf16[64,1536]{1,0:T(8,128)(2,1)S(1)} collective-permute-done((bf16[64,1536]{1,0:T(8,128)(2,1)S(1)}, bf16[64,1536]{1,0:T(8,128)(2,1)S(1)}, u32[]{:S(2)}, u32[]{:S(2)}) %collective-permute-start.27) | collective-permute-done | bytes 196640 | tf_op jit(solution)/shard_map/ppermute | solution.py:46
  115.7 7.7 %collective-permute-done.28 = bf16[64,1536]{1,0:T(8,128)(2,1)S(1)} collective-permute-done((bf16[64,1536]{1,0:T(8,128)(2,1)S(1)}, bf16[64,1536]{1,0:T(8,128)(2,1)S(1)}, u32[]{:S(2)}, u32[]{:S(2)}) %collective-permute-start.28) | collective-permute-done | bytes 196640 | tf_op jit(solution)/shard_map/ppermute | solution.py:46
  131.2 7.9 %collective-permute-done.32 = bf16[64,1536]{1,0:T(8,128)(2,1)S(1)} collective-permute-done((bf16[64,1536]{1,0:T(8,128)(2,1)S(1)}, bf16[64,1536]{1,0:T(8,128)(2,1)S(1)}, u32[]{:S(2)}, u32[]{:S(2)}) %collective-permute-start.32) | collective-permute-done | bytes 196640 | tf_op jit(solution)/shard_map/ppermute | solution.py:46
  153.3 5.9 collective-permute-done.38
  159.1 6.7 %collective-permute-done.39 = bf16[96,1408]{1,0:T(8,128)(2,1)S(1)} collective-permute-done((bf16[96,1408]{1,0:T(8,128)(2,1)S(1)}, bf16[96,1408]{1,0:T(8,128)(2,1)S(1)}, u32[]{:S(2)}, u32[]{:S(2)}) %collective-permute-start.39) | collective-permute-done | bytes 270368 | tf_op jit(solution)/shard_map/ppermute | solution.py:46
  176.3 6.3 %collective-permute-done.45 = bf16[64,1536]{1,0:T(8,128)(2,1)S(1)} collective-permute-done((bf16[64,1536]{1,0:T(8,128)(2,1)S(1)}, bf16[64,1536]{1,0:T(8,128)(2,1)S(1)}, u32[]{:S(2)}, u32[]{:S(2)}) %collective-permute-start.45) | collective-permute-done | bytes 196640 | tf_op jit(solution)/shard_map/ppermute | solution.py:46
  184.9 8.4 %collective-permute-done.42 = bf16[256,1536]{1,0:T(8,128)(2,1)S(1)} collective-permute-done((bf16[256,1536]{1,0:T(8,128)(2,1)S(1)}, bf16[256,1536]{1,0:T(8,128)(2,1)S(1)}, u32[]{:S(2)}, u32[]{:S(2)}) %collective-permute-start.42) | collective-permute-done | bytes 786464 | tf_op jit(solution)/shard_map/ppermute | solution.py:46
  204.0 5.5 collective-permute-done.49
  209.5 5.1 collective-permute-done.50
  222.6 7.0 %collective-permute-done.52 = bf16[64,1536]{1,0:T(8,128)(2,1)S(1)} collective-permute-done((bf16[64,1536]{1,0:T(8,128)(2,1)S(1)}, bf16[64,1536]{1,0:T(8,128)(2,1)S(1)}, u32[]{:S(2)}, u32[]{:S(2)}) %collective-permute-start.52) | collective-permute-done | bytes 196640 | tf_op jit(solution)/shard_map/ppermute | solution.py:46
  229.6 9.1 %collective-permute-done.53 = bf16[64,1536]{1,0:T(8,128)(2,1)S(1)} collective-permute-done((bf16[64,1536]{1,0:T(8,128)(2,1)S(1)}, bf16[64,1536]{1,0:T(8,128)(2,1)S(1)}, u32[]{:S(2)}, u32[]{:S(2)}) %collective-permute-start.53) | collective-permute-done | bytes 196640 | tf_op jit(solution)/shard_map/ppermute | solution.py:46
  264.6 5.2 collective-permute-done.60
  269.8 7.7 %collective-permute-done.62 = bf16[768,1024]{1,0:T(8,128)(2,1)} collective-permute-done((bf16[768,1024]{1,0:T(8,128)(2,1)}, bf16[768,1024]{1,0:T(8,128)(2,1)}, u32[]{:S(2)}, u32[]{:S(2)}) %collective-permute-start.62) | collective-permute-done | bytes 1572896 | tf_op jit(solution)/shard_map/ppermute | solution.py:46
  295.5 5.5 collective-permute-done.63
  339.7 4.6 attend_back.2
  350.0 6.0 %collective-permute-done.79 = bf16[768,1024]{1,0:T(8,128)(2,1)} collective-permute-done((bf16[768,1024]{1,0:T(8,128)(2,1)}, bf16[768,1024]{1,0:T(8,128)(2,1)}, u32[]{:S(2)}, u32[]{:S(2)}) %collective-permute-start.79) | collective-permute-done | bytes 1572896 | tf_op jit(solution)/shard_map/ppermute | solution.py:46
  378.5 7.2 %collective-permute-done.85 = bf16[64,1536]{1,0:T(8,128)(2,1)S(1)} collective-permute-done((bf16[64,1536]{1,0:T(8,128)(2,1)S(1)}, bf16[64,1536]{1,0:T(8,128)(2,1)S(1)}, u32[]{:S(2)}, u32[]{:S(2)}) %collective-permute-start.85) | collective-permute-done | bytes 196640 | tf_op jit(solution)/shard_map/ppermute | solution.py:46
  408.5 4.4 collective-permute-done.91
  413.0 5.2 collective-permute-done.92
  426.6 5.4 collective-permute-done.95
  432.0 5.4 collective-permute-done.96
  440.9 4.6 attend_back.3
  450.6 8.3 %collective-permute-done.101 = bf16[128,1536]{1,0:T(8,128)(2,1)S(1)} collective-permute-done((bf16[128,1536]{1,0:T(8,128)(2,1)}, bf16[128,1536]{1,0:T(8,128)(2,1)S(1)}, u32[]{:S(2)}, u32[]{:S(2)}) %collective-permute-start.101) | collective-permute-done | bytes 393248 | tf_op jit(solution)/shard_map/ppermute | solution.py:46
  472.2 9.3 %collective-permute-done.104 = bf16[64,1536]{1,0:T(8,128)(2,1)S(1)} collective-permute-done((bf16[64,1536]{1,0:T(8,128)(2,1)S(1)}, bf16[64,1536]{1,0:T(8,128)(2,1)S(1)}, u32[]{:S(2)}, u32[]{:S(2)}) %collective-permute-start.104) | collective-permute-done | bytes 196640 | tf_op jit(solution)/shard_map/ppermute | solution.py:46
  481.5 4.2 collective-permute-done.105
  492.3 13.9 %collective-permute-done.109 = bf16[384,512]{1,0:T(8,128)(2,1)S(1)} collective-permute-done((bf16[384,512]{1,0:T(8,128)(2,1)S(1)}, bf16[384,512]{1,0:T(8,128)(2,1)S(1)}, u32[]{:S(2)}, u32[]{:S(2)}) %collective-permute-start.109) | collective-permute-done | bytes 393248 | tf_op jit(solution)/shard_map/ppermute | solution.py:46
  517.1 4.8 collective-permute-done.117
  539.4 4.5 collective-permute-done.119
  (892 shorter events, 378.1 us)
Async XLA Ops:
  36.8 22.7 %collective-permute-start.17 = (bf16[384,384]{1,0:T(8,128)(2,1)S(1)}, bf16[384,384]{1,0:T(8,128)(2,1)}, u32[]{:S(2)}, u32[]{:S(2)}) collective-permute-start(bf16[384,384]{1,0:T(8,128)(2,1)S(1)} %bitcast.302), channel_id=1, source_target_pairs={{0,8},{1,9},{2,10},{3,11},{4,12},{5,13},{6,14},{7,15},{8,0},{9,1},... | collective-permute-start | bytes 884744 | tf_op jit(solution)/shard_map/ppermute | solution.py:46
  43.7 21.2 %collective-permute-start.14 = (bf16[64,1536]{1,0:T(8,128)(2,1)S(1)}, bf16[64,1536]{1,0:T(8,128)(2,1)S(1)}, u32[]{:S(2)}, u32[]{:S(2)}) collective-permute-start(bf16[64,1536]{1,0:T(8,128)(2,1)S(1)} %pad_maximum_fusion.45), channel_id=1, source_target_pairs={{0,2},{1,3},{2,0},{3,1},{4,6},{5,7},{6,4},{7,5},{8,10},{9,11},{10,... | collective-permute-start | bytes 589832 | tf_op jit(solution)/shard_map/ppermute | solution.py:46
  45.2 19.7 %collective-permute-start.15 = (bf16[64,1536]{1,0:T(8,128)(2,1)S(1)}, bf16[64,1536]{1,0:T(8,128)(2,1)S(1)}, u32[]{:S(2)}, u32[]{:S(2)}) collective-permute-start(bf16[64,1536]{1,0:T(8,128)(2,1)S(1)} %pad_maximum_fusion.45), channel_id=1, source_target_pairs={{0,4},{1,5},{2,6},{3,7},{4,0},{5,1},{6,2},{7,3},{8,12},{9,13},{10,... | collective-permute-start | bytes 589832 | tf_op jit(solution)/shard_map/ppermute | solution.py:46
  68.8 21.3 %collective-permute-start.22 = (bf16[96,1024]{1,0:T(8,128)(2,1)}, bf16[96,1024]{1,0:T(8,128)(2,1)S(1)}, u32[]{:S(2)}, u32[]{:S(2)}) collective-permute-start(bf16[96,1024]{1,0:T(8,128)(2,1)} %get-tuple-element.342), channel_id=1, source_target_pairs={{0,2},{1,3},{2,0},{3,1},{4,6},{5,7},{6,4},{7,5},{8,10},{9,11},{10,... | collective-permute-start | bytes 589832 | tf_op jit(solution)/shard_map/ppermute | solution.py:46
  69.5 20.6 %collective-permute-start.23 = (bf16[96,1024]{1,0:T(8,128)(2,1)}, bf16[96,1024]{1,0:T(8,128)(2,1)}, u32[]{:S(2)}, u32[]{:S(2)}) collective-permute-start(bf16[96,1024]{1,0:T(8,128)(2,1)} %get-tuple-element.350), channel_id=1, source_target_pairs={{0,4},{1,5},{2,6},{3,7},{4,0},{5,1},{6,2},{7,3},{8,12},{9,13},{10,... | collective-permute-start | bytes 589832 | tf_op jit(solution)/shard_map/ppermute | solution.py:46
  75.2 20.6 %collective-permute-start.21 = (bf16[2,96,1536]{2,1,0:T(8,128)(2,1)S(1)}, bf16[2,96,1536]{2,1,0:T(8,128)(2,1)}, u32[]{:S(2)}, u32[]{:S(2)}) collective-permute-start(bf16[2,96,1536]{2,1,0:T(8,128)(2,1)S(1)} %broadcast_select_fusion.1), channel_id=1, source_target_pairs={{0,1},{1,0},{2,3},{3,2},{4,5},{5,4},{6,7},{7,6},{8,9},{9,8},{10,11... | collective-permute-start | bytes 1769480 | tf_op jit(solution)/shard_map/ppermute | solution.py:46
  100.2 23.2 %collective-permute-start.30 = (bf16[384,512]{1,0:T(8,128)(2,1)S(1)}, bf16[384,512]{1,0:T(8,128)(2,1)S(1)}, u32[]{:S(2)}, u32[]{:S(2)}) collective-permute-start(bf16[384,512]{1,0:T(8,128)(2,1)S(1)} %get-tuple-element.355), channel_id=1, source_target_pairs={{0,8},{1,9},{2,10},{3,11},{4,12},{5,13},{6,14},{7,15},{8,0},{9,1},... | collective-permute-start | bytes 1179656 | tf_op jit(solution)/shard_map/ppermute | solution.py:46
  131.2 18.5 %collective-permute-start.34 = (bf16[768,512]{1,0:T(8,128)(2,1)S(1)}, bf16[768,512]{1,0:T(8,128)(2,1)S(1)}, u32[]{:S(2)}, u32[]{:S(2)}) collective-permute-start(bf16[768,512]{1,0:T(8,128)(2,1)S(1)} %pad_maximum_fusion.12), channel_id=1, source_target_pairs={{0,1},{1,0},{2,3},{3,2},{4,5},{5,4},{6,7},{7,6},{8,9},{9,8},{10,11... | collective-permute-start | bytes 2359304 | tf_op jit(solution)/shard_map/ppermute | solution.py:46
  149.7 19.1 %collective-permute-start.41 = (bf16[128,1536]{1,0:T(8,128)(2,1)S(1)}, bf16[128,1536]{1,0:T(8,128)(2,1)S(1)}, u32[]{:S(2)}, u32[]{:S(2)}) collective-permute-start(bf16[128,1536]{1,0:T(8,128)(2,1)S(1)} %get-tuple-element.383), channel_id=1, source_target_pairs={{0,8},{1,9},{2,10},{3,11},{4,12},{5,13},{6,14},{7,15},{8,0},{9,1},... | collective-permute-start | bytes 1179656 | tf_op jit(solution)/shard_map/ppermute | solution.py:46
  174.6 18.7 %collective-permute-start.42 = (bf16[256,1536]{1,0:T(8,128)(2,1)S(1)}, bf16[256,1536]{1,0:T(8,128)(2,1)S(1)}, u32[]{:S(2)}, u32[]{:S(2)}) collective-permute-start(bf16[256,1536]{1,0:T(8,128)(2,1)S(1)} %pad_maximum_fusion.15), channel_id=1, source_target_pairs={{0,1},{1,0},{2,3},{3,2},{4,5},{5,4},{6,7},{7,6},{8,9},{9,8},{10,11... | collective-permute-start | bytes 2359304 | tf_op jit(solution)/shard_map/ppermute | solution.py:46
  200.4 38.5 %collective-permute-start.55 = (bf16[384,1024]{1,0:T(8,128)(2,1)S(1)}, bf16[384,1024]{1,0:T(8,128)(2,1)S(1)}, u32[]{:S(2)}, u32[]{:S(2)}) collective-permute-start(bf16[384,1024]{1,0:T(8,128)(2,1)S(1)} %slice.779), channel_id=1, source_target_pairs={{0,8},{1,9},{2,10},{3,11},{4,12},{5,13},{6,14},{7,15},{8,0},{9,1},... | collective-permute-start | bytes 2359304 | tf_op jit(solution)/shard_map/ppermute | solution.py:46
  215.8 22.9 %collective-permute-start.53 = (bf16[64,1536]{1,0:T(8,128)(2,1)S(1)}, bf16[64,1536]{1,0:T(8,128)(2,1)S(1)}, u32[]{:S(2)}, u32[]{:S(2)}) collective-permute-start(bf16[64,1536]{1,0:T(8,128)(2,1)S(1)} %pad_maximum_fusion.47), channel_id=1, source_target_pairs={{0,6},{1,7},{2,4},{3,5},{4,2},{5,3},{6,0},{7,1},{8,14},{9,15},{10,... | collective-permute-start | bytes 589832 | tf_op jit(solution)/shard_map/ppermute | solution.py:46
  220.2 20.5 %collective-permute-start.54 = (bf16[768,384]{1,0:T(8,128)(2,1)S(1)}, bf16[768,384]{1,0:T(8,128)(2,1)S(1)}, u32[]{:S(2)}, u32[]{:S(2)}) collective-permute-start(bf16[768,384]{1,0:T(8,128)(2,1)S(1)} %pad_maximum_fusion.26), channel_id=1, source_target_pairs={{0,1},{1,0},{2,3},{3,2},{4,5},{5,4},{6,7},{7,6},{8,9},{9,8},{10,11... | collective-permute-start | bytes 1769480 | tf_op jit(solution)/shard_map/ppermute | solution.py:46
  240.4 37.1 %collective-permute-start.62 = (bf16[768,1024]{1,0:T(8,128)(2,1)}, bf16[768,1024]{1,0:T(8,128)(2,1)}, u32[]{:S(2)}, u32[]{:S(2)}) collective-permute-start(bf16[768,1024]{1,0:T(8,128)(2,1)} %pad_maximum_fusion.5), channel_id=1, source_target_pairs={{0,1},{1,0},{2,3},{3,2},{4,5},{5,4},{6,7},{7,6},{8,9},{9,8},{10,11... | collective-permute-start | bytes 4718600 | tf_op jit(solution)/shard_map/ppermute | solution.py:46
  240.7 36.8 %collective-permute-start.61 = (bf16[128,1536]{1,0:T(8,128)(2,1)}, bf16[128,1536]{1,0:T(8,128)(2,1)}, u32[]{:S(2)}, u32[]{:S(2)}) collective-permute-start(bf16[128,1536]{1,0:T(8,128)(2,1)} %get-tuple-element.416), channel_id=1, source_target_pairs={{0,8},{1,9},{2,10},{3,11},{4,12},{5,13},{6,14},{7,15},{8,0},{9,1},... | collective-permute-start | bytes 1179656 | tf_op jit(solution)/shard_map/ppermute | solution.py:46
  261.6 33.1 %collective-permute-start.68 = (bf16[256,1536]{1,0:T(8,128)(2,1)S(1)}, bf16[256,1536]{1,0:T(8,128)(2,1)S(1)}, u32[]{:S(2)}, u32[]{:S(2)}) collective-permute-start(bf16[256,1536]{1,0:T(8,128)(2,1)S(1)} %copy-done.24), channel_id=1, source_target_pairs={{0,16},{1,17},{2,18},{3,19},{4,20},{5,21},{6,22},{7,23},{8,24},{9,... | collective-permute-start | bytes 2359304 | tf_op jit(solution)/shard_map/ppermute | solution.py:46
  304.7 19.4 %collective-permute-start.73 = (bf16[256,1536]{1,0:T(8,128)(2,1)S(1)}, bf16[256,1536]{1,0:T(8,128)(2,1)S(1)}, u32[]{:S(2)}, u32[]{:S(2)}) collective-permute-start(bf16[256,1536]{1,0:T(8,128)(2,1)S(1)} %convolution_convert_fusion.8), channel_id=1, source_target_pairs={{0,1},{1,0},{2,3},{3,2},{4,5},{5,4},{6,7},{7,6},{8,9},{9,8},{10,11... | collective-permute-start | bytes 2359304 | tf_op jit(solution)/shard_map/ppermute | solution.py:46
  318.1 37.9 %collective-permute-start.79 = (bf16[768,1024]{1,0:T(8,128)(2,1)}, bf16[768,1024]{1,0:T(8,128)(2,1)}, u32[]{:S(2)}, u32[]{:S(2)}) collective-permute-start(bf16[768,1024]{1,0:T(8,128)(2,1)} %convolution_convert_fusion.14), channel_id=1, source_target_pairs={{0,1},{1,0},{2,3},{3,2},{4,5},{5,4},{6,7},{7,6},{8,9},{9,8},{10,11... | collective-permute-start | bytes 4718600 | tf_op jit(solution)/shard_map/ppermute | solution.py:46
  336.2 34.6 %collective-permute-start.83 = (bf16[128,1536]{1,0:T(8,128)(2,1)}, bf16[128,1536]{1,0:T(8,128)(2,1)}, u32[]{:S(2)}, u32[]{:S(2)}) collective-permute-start(bf16[128,1536]{1,0:T(8,128)(2,1)} %fusion.43), channel_id=1, source_target_pairs={{0,8},{1,9},{2,10},{3,11},{4,12},{5,13},{6,14},{7,15},{8,0},{9,1},... | collective-permute-start | bytes 1179656 | tf_op jit(solution)/shard_map/ppermute | solution.py:46
  357.8 33.0 %collective-permute-start.88 = (bf16[768,384]{1,0:T(8,128)(2,1)S(1)}, bf16[768,384]{1,0:T(8,128)(2,1)S(1)}, u32[]{:S(2)}, u32[]{:S(2)}) collective-permute-start(bf16[768,384]{1,0:T(8,128)(2,1)S(1)} %convolution_convert_fusion.18), channel_id=1, source_target_pairs={{0,1},{1,0},{2,3},{3,2},{4,5},{5,4},{6,7},{7,6},{8,9},{9,8},{10,11... | collective-permute-start | bytes 1769480 | tf_op jit(solution)/shard_map/ppermute | solution.py:46
  374.9 43.3 %collective-permute-start.93 = (bf16[384,1024]{1,0:T(8,128)(2,1)S(1)}, bf16[384,1024]{1,0:T(8,128)(2,1)S(1)}, u32[]{:S(2)}, u32[]{:S(2)}) collective-permute-start(bf16[384,1024]{1,0:T(8,128)(2,1)S(1)} %fusion.5), channel_id=1, source_target_pairs={{0,8},{1,9},{2,10},{3,11},{4,12},{5,13},{6,14},{7,15},{8,0},{9,1},... | collective-permute-start | bytes 2359304 | tf_op jit(solution)/shard_map/ppermute | solution.py:46
  393.9 29.4 %collective-permute-start.97 = (bf16[256,1536]{1,0:T(8,128)(2,1)S(1)}, bf16[256,1536]{1,0:T(8,128)(2,1)S(1)}, u32[]{:S(2)}, u32[]{:S(2)}) collective-permute-start(bf16[256,1536]{1,0:T(8,128)(2,1)S(1)} %convolution_convert_fusion.6), channel_id=1, source_target_pairs={{0,1},{1,0},{2,3},{3,2},{4,5},{5,4},{6,7},{7,6},{8,9},{9,8},{10,11... | collective-permute-start | bytes 2359304 | tf_op jit(solution)/shard_map/ppermute | solution.py:46
  424.1 23.2 %collective-permute-start.100 = (bf16[768,512]{1,0:T(8,128)(2,1)}, bf16[768,512]{1,0:T(8,128)(2,1)}, u32[]{:S(2)}, u32[]{:S(2)}) collective-permute-start(bf16[768,512]{1,0:T(8,128)(2,1)} %convolution_convert_fusion.16), channel_id=1, source_target_pairs={{0,1},{1,0},{2,3},{3,2},{4,5},{5,4},{6,7},{7,6},{8,9},{9,8},{10,11... | collective-permute-start | bytes 2359304 | tf_op jit(solution)/shard_map/ppermute | solution.py:46
  438.7 20.2 %collective-permute-start.101 = (bf16[128,1536]{1,0:T(8,128)(2,1)}, bf16[128,1536]{1,0:T(8,128)(2,1)S(1)}, u32[]{:S(2)}, u32[]{:S(2)}) collective-permute-start(bf16[128,1536]{1,0:T(8,128)(2,1)} %fusion.41), channel_id=1, source_target_pairs={{0,8},{1,9},{2,10},{3,11},{4,12},{5,13},{6,14},{7,15},{8,0},{9,1},... | collective-permute-start | bytes 1179656 | tf_op jit(solution)/shard_map/ppermute | solution.py:46
  447.3 38.4 %collective-permute-start.106 = (bf16[768,512]{1,0:T(8,128)(2,1)S(1)}, bf16[768,512]{1,0:T(8,128)(2,1)S(1)}, u32[]{:S(2)}, u32[]{:S(2)}) collective-permute-start(bf16[768,512]{1,0:T(8,128)(2,1)S(1)} %copy-done.152), channel_id=1, source_target_pairs={{0,1},{1,0},{2,3},{3,2},{4,5},{5,4},{6,7},{7,6},{8,9},{9,8},{10,11... | collective-permute-start | bytes 2359304 | tf_op jit(solution)/shard_map/ppermute | solution.py:46
  459.9 31.0 %collective-permute-start.108 = (bf16[384,512]{1,0:T(8,128)(2,1)S(1)}, bf16[384,512]{1,0:T(8,128)(2,1)S(1)}, u32[]{:S(2)}, u32[]{:S(2)}) collective-permute-start(bf16[384,512]{1,0:T(8,128)(2,1)S(1)} %fusion.40), channel_id=1, source_target_pairs={{0,8},{1,9},{2,10},{3,11},{4,12},{5,13},{6,14},{7,15},{8,0},{9,1},... | collective-permute-start | bytes 1179656 | tf_op jit(solution)/shard_map/ppermute | solution.py:46
  466.6 19.1 %collective-permute-start.105 = (bf16[64,1536]{1,0:T(8,128)(2,1)S(1)}, bf16[64,1536]{1,0:T(8,128)(2,1)S(1)}, u32[]{:S(2)}, u32[]{:S(2)}) collective-permute-start(bf16[64,1536]{1,0:T(8,128)(2,1)S(1)} %get-tuple-element.525), channel_id=1, source_target_pairs={{0,6},{1,7},{2,4},{3,5},{4,2},{5,3},{6,0},{7,1},{8,14},{9,15},{10,... | collective-permute-start | bytes 589832 | tf_op jit(solution)/shard_map/ppermute | solution.py:46
  486.8 19.4 %collective-permute-start.109 = (bf16[384,512]{1,0:T(8,128)(2,1)S(1)}, bf16[384,512]{1,0:T(8,128)(2,1)S(1)}, u32[]{:S(2)}, u32[]{:S(2)}) collective-permute-start(bf16[384,512]{1,0:T(8,128)(2,1)S(1)} %fusion.38), channel_id=1, source_target_pairs={{0,8},{1,9},{2,10},{3,11},{4,12},{5,13},{6,14},{7,15},{8,0},{9,1},... | collective-permute-start | bytes 1179656 | tf_op jit(solution)/shard_map/ppermute | solution.py:46
  486.9 25.1 %collective-permute-start.107 = (bf16[768,384]{1,0:T(8,128)(2,1)S(1)}, bf16[768,384]{1,0:T(8,128)(2,1)S(1)}, u32[]{:S(2)}, u32[]{:S(2)}) collective-permute-start(bf16[768,384]{1,0:T(8,128)(2,1)S(1)} %convolution_convert_fusion.17), channel_id=1, source_target_pairs={{0,1},{1,0},{2,3},{3,2},{4,5},{5,4},{6,7},{7,6},{8,9},{9,8},{10,11... | collective-permute-start | bytes 1769480 | tf_op jit(solution)/shard_map/ppermute | solution.py:46
  487.6 18.8 %collective-permute-start.110 = (bf16[96,1024]{1,0:T(8,128)(2,1)S(1)}, bf16[96,1024]{1,0:T(8,128)(2,1)S(1)}, u32[]{:S(2)}, u32[]{:S(2)}) collective-permute-start(bf16[96,1024]{1,0:T(8,128)(2,1)S(1)} %copy-done.121), channel_id=1, source_target_pairs={{0,2},{1,3},{2,0},{3,1},{4,6},{5,7},{6,4},{7,5},{8,10},{9,11},{10,... | collective-permute-start | bytes 589832 | tf_op jit(solution)/shard_map/ppermute | solution.py:46
  521.9 46.2 %collective-permute-start.131 = (bf16[128,1536]{1,0:T(8,128)(2,1)}, bf16[128,1536]{1,0:T(8,128)(2,1)}, u32[]{:S(2)}, u32[]{:S(2)}) collective-permute-start(bf16[128,1536]{1,0:T(8,128)(2,1)} %get-tuple-element.548), channel_id=1, source_target_pairs={{0,16},{1,17},{2,18},{3,19},{4,20},{5,21},{6,22},{7,23},{8,24},{9,... | collective-permute-start | bytes 1179656 | tf_op jit(solution)/shard_map/ppermute | solution.py:46
  543.9 21.6 %collective-permute-start.133 = (bf16[192,1536]{1,0:T(8,128)(2,1)S(1)}, bf16[192,1536]{1,0:T(8,128)(2,1)}, u32[]{:S(2)}, u32[]{:S(2)}) collective-permute-start(bf16[192,1536]{1,0:T(8,128)(2,1)S(1)} %fusion.57), channel_id=1, source_target_pairs={{8,0},{9,1},{10,2},{11,3},{12,4},{13,5},{14,6},{15,7},{16,24},{17,... | collective-permute-start | bytes 1769480 | tf_op jit(solution)/shard_map/ppermute | solution.py:57
  (261 other events, 3029.5 us)

commit v6 on v5

--- a/solution.py
+++ b/solution.py
@@ -861,9 +861,9 @@
     up_0.shard_done()
     down_0.half_done()
     down_0.shard()
-    qkv_1.half()
     own_cot = own_cot.astype(F32)
     cot = rows_start(own_cot.astype(BF16), lay, order)
+    qkv_1.half()
     first.gate_w, first.up_w = gate_0.full, up_0.full
     first.hide()
     second.down_in = rows_middle(cot, lay, order)
@@ -990,8 +990,8 @@
     out_both.shard_done()
     out_both.half()
     gains_other = lay.to_shard(order(pick(gains, 1 - lay.shard)))
+    second_out = second.mid_stream + sums_done(outputs, order)
     qkv_g0.half_done()
-    second_out = second.mid_stream + sums_done(outputs, order)
     attn = by_member(qkv_g0.total, qkv_g1.total)
     others_q = to_members(attn.astype(BF16), lay, order)
     rows_other = return_rows(first_grad.astype(BF16), second_out.astype(BF16), lay, order)

time: 595 us -> 592 us (level)
  waiting for transfers between devices: 252 us -> 227 us
  starting transfers between devices: 141 us -> 162 us
    ppermute x136, waiting for transfers between devices: 252 us -> 227 us  [move(): return lax.ppermute(block, MESH_AXES, pairs)]
    ppermute x136, starting transfers between devices: 138 us -> 159 us  [move(): return lax.ppermute(block, MESH_AXES, pairs)]
  transfers between devices with their start and end apart: 138 -> 138, of which waited for: 65 -> 66; matrix products, arithmetic and copies ran while one was open for 21% -> 21% of each run, Pallas kernels for 7% -> 7%
where the time goes in v6:
time: 592 us; the launch traced here: 586 us
  waiting for transfers between devices  227 us (38%)
  starting transfers between devices  162 us (27%)
  matrix products  58.8 us (10%)
  other arithmetic  58.2 us (10%)
  Pallas kernels  42.4 us (7%)
  local copies, waits for them, and re-layouts  32.3 us (5%)
    ppermute x136, waiting for transfers between devices, move(): return lax.ppermute(block, MESH_AXES, pairs)  227 us
    ppermute x136, starting transfers between devices, move(): return lax.ppermute(block, MESH_AXES, pairs)  159 us
    pallas_call x10, Pallas kernels, rearrange(): pl.pallas_call(lambda *refs: rearrange_kernel(plans, len(sources), *refs)...  25.2 us
    dot_general x22, matrix products, mm(): lax.dot_general(a, b, (((1,), (0,)), ((), ())), preferred_element_type=F32)  22 us
    dot_general x20, matrix products, mm_tn(): lax.dot_general(a, b, (((0,), (0,)), ((), ())), preferred_element_type=F32)  18.9 us
    dot_general x24, matrix products, mm_nt(): lax.dot_general(a, b, (((1,), (1,)), ((), ())), preferred_element_type=F32)  17.9 us
    unnamed x319, local copies, waits for them, and re-layouts  15.2 us
  transfers between devices with their start and end apart: 138, of which 66 were waited for; matrix products, arithmetic and copies ran while one was open for 21% of the time, Pallas kernels for 7%

profile of v6, /device:TPU:0, one launch (start us, length us, event | category | flops | bytes accessed | tf_op | source)
XLA Modules:
  0.0 585.7 jit_solution(2421461103709128106)
XLA Ops:
  45.2 9.4 %collective-permute-start.15 = (bf16[64,1536]{1,0:T(8,128)(2,1)S(1)}, bf16[64,1536]{1,0:T(8,128)(2,1)S(1)}, u32[]{:S(2)}, u32[]{:S(2)}) collective-permute-start(bf16[64,1536]{1,0:T(8,128)(2,1)S(1)} %pad_maximum_fusion.45), channel_id=1, source_target_pairs={{0,4},{1,5},{2,6},{3,7},{4,0},{5,1},{6,2},{7,3},{8,12},{9,13},{10,... | collective-permute-start | bytes 589832 | tf_op jit(solution)/shard_map/ppermute | solution.py:46
  54.6 4.9 collective-permute-done.17
  69.5 5.4 collective-permute-done.18
  81.6 4.0 attend.2
  103.2 4.1 collective-permute-start.27
  109.1 6.6 %collective-permute-done.27 = bf16[64,1536]{1,0:T(8,128)(2,1)S(1)} collective-permute-done((bf16[64,1536]{1,0:T(8,128)(2,1)S(1)}, bf16[64,1536]{1,0:T(8,128)(2,1)S(1)}, u32[]{:S(2)}, u32[]{:S(2)}) %collective-permute-start.27) | collective-permute-done | bytes 196640 | tf_op jit(solution)/shard_map/ppermute | solution.py:46
  115.7 7.7 %collective-permute-done.28 = bf16[64,1536]{1,0:T(8,128)(2,1)S(1)} collective-permute-done((bf16[64,1536]{1,0:T(8,128)(2,1)S(1)}, bf16[64,1536]{1,0:T(8,128)(2,1)S(1)}, u32[]{:S(2)}, u32[]{:S(2)}) %collective-permute-start.28) | collective-permute-done | bytes 196640 | tf_op jit(solution)/shard_map/ppermute | solution.py:46
  131.2 7.9 %collective-permute-done.32 = bf16[64,1536]{1,0:T(8,128)(2,1)S(1)} collective-permute-done((bf16[64,1536]{1,0:T(8,128)(2,1)S(1)}, bf16[64,1536]{1,0:T(8,128)(2,1)S(1)}, u32[]{:S(2)}, u32[]{:S(2)}) %collective-permute-start.32) | collective-permute-done | bytes 196640 | tf_op jit(solution)/shard_map/ppermute | solution.py:46
  153.3 5.9 %collective-permute-done.38 = bf16[96,1408]{1,0:T(8,128)(2,1)S(1)} collective-permute-done((bf16[96,1408]{1,0:T(8,128)(2,1)S(1)}, bf16[96,1408]{1,0:T(8,128)(2,1)S(1)}, u32[]{:S(2)}, u32[]{:S(2)}) %collective-permute-start.38) | collective-permute-done | bytes 270368 | tf_op jit(solution)/shard_map/ppermute | solution.py:46
  159.1 6.7 %collective-permute-done.39 = bf16[96,1408]{1,0:T(8,128)(2,1)S(1)} collective-permute-done((bf16[96,1408]{1,0:T(8,128)(2,1)S(1)}, bf16[96,1408]{1,0:T(8,128)(2,1)S(1)}, u32[]{:S(2)}, u32[]{:S(2)}) %collective-permute-start.39) | collective-permute-done | bytes 270368 | tf_op jit(solution)/shard_map/ppermute | solution.py:46
  176.3 6.1 %collective-permute-done.45 = bf16[64,1536]{1,0:T(8,128)(2,1)S(1)} collective-permute-done((bf16[64,1536]{1,0:T(8,128)(2,1)S(1)}, bf16[64,1536]{1,0:T(8,128)(2,1)S(1)}, u32[]{:S(2)}, u32[]{:S(2)}) %collective-permute-start.45) | collective-permute-done | bytes 196640 | tf_op jit(solution)/shard_map/ppermute | solution.py:46
  195.6 5.7 collective-permute-start.55
  201.5 10.6 %collective-permute-done.50 = bf16[64,1536]{1,0:T(8,128)(2,1)S(1)} collective-permute-done((bf16[64,1536]{1,0:T(8,128)(2,1)S(1)}, bf16[64,1536]{1,0:T(8,128)(2,1)S(1)}, u32[]{:S(2)}, u32[]{:S(2)}) %collective-permute-start.50) | collective-permute-done | bytes 196640 | tf_op jit(solution)/shard_map/ppermute | solution.py:46
  220.2 4.7 collective-permute-done.52
  228.3 7.0 %collective-permute-done.55 = bf16[384,1024]{1,0:T(8,128)(2,1)S(1)} collective-permute-done((bf16[384,1024]{1,0:T(8,128)(2,1)S(1)}, bf16[384,1024]{1,0:T(8,128)(2,1)S(1)}, u32[]{:S(2)}, u32[]{:S(2)}) %collective-permute-start.55) | collective-permute-done | bytes 786464 | tf_op jit(solution)/shard_map/ppermute | solution.py:46
  242.0 4.0 attend.3
  262.4 4.8 collective-permute-done.60
  267.2 5.2 collective-permute-done.62
  290.5 5.6 collective-permute-done.63
  332.8 4.2 collective-permute-start.83
  339.4 4.6 attend_back.2
  360.7 3.9 collective-permute-done.80
  371.2 4.4 collective-permute-start.93
  376.3 4.3 collective-permute-done.85
  380.6 5.6 collective-permute-done.86
  407.2 3.9 collective-permute-done.91
  411.1 4.1 collective-permute-done.92
  425.8 6.2 %collective-permute-done.95 = bf16[64,1536]{1,0:T(8,128)(2,1)S(1)} collective-permute-done((bf16[64,1536]{1,0:T(8,128)(2,1)S(1)}, bf16[64,1536]{1,0:T(8,128)(2,1)S(1)}, u32[]{:S(2)}, u32[]{:S(2)}) %collective-permute-start.95) | collective-permute-done | bytes 196640 | tf_op jit(solution)/shard_map/ppermute | solution.py:46
  438.6 4.6 attend_back.3
  448.0 8.4 %collective-permute-done.101 = bf16[128,1536]{1,0:T(8,128)(2,1)S(1)} collective-permute-done((bf16[128,1536]{1,0:T(8,128)(2,1)}, bf16[128,1536]{1,0:T(8,128)(2,1)S(1)}, u32[]{:S(2)}, u32[]{:S(2)}) %collective-permute-start.101) | collective-permute-done | bytes 393248 | tf_op jit(solution)/shard_map/ppermute | solution.py:46
  469.8 10.2 %collective-permute-done.104 = bf16[64,1536]{1,0:T(8,128)(2,1)S(1)} collective-permute-done((bf16[64,1536]{1,0:T(8,128)(2,1)S(1)}, bf16[64,1536]{1,0:T(8,128)(2,1)S(1)}, u32[]{:S(2)}, u32[]{:S(2)}) %collective-permute-start.104) | collective-permute-done | bytes 196640 | tf_op jit(solution)/shard_map/ppermute | solution.py:46
  489.7 13.7 %collective-permute-done.109 = bf16[384,512]{1,0:T(8,128)(2,1)S(1)} collective-permute-done((bf16[384,512]{1,0:T(8,128)(2,1)S(1)}, bf16[384,512]{1,0:T(8,128)(2,1)S(1)}, u32[]{:S(2)}, u32[]{:S(2)}) %collective-permute-start.109) | collective-permute-done | bytes 393248 | tf_op jit(solution)/shard_map/ppermute | solution.py:46
  (892 shorter events, 386.7 us)
Async XLA Ops:
  36.8 22.7 %collective-permute-start.17 = (bf16[384,384]{1,0:T(8,128)(2,1)S(1)}, bf16[384,384]{1,0:T(8,128)(2,1)}, u32[]{:S(2)}, u32[]{:S(2)}) collective-permute-start(bf16[384,384]{1,0:T(8,128)(2,1)S(1)} %bitcast.302), channel_id=1, source_target_pairs={{0,8},{1,9},{2,10},{3,11},{4,12},{5,13},{6,14},{7,15},{8,0},{9,1},... | collective-permute-start | bytes 884744 | tf_op jit(solution)/shard_map/ppermute | solution.py:46
  43.7 21.2 %collective-permute-start.14 = (bf16[64,1536]{1,0:T(8,128)(2,1)S(1)}, bf16[64,1536]{1,0:T(8,128)(2,1)S(1)}, u32[]{:S(2)}, u32[]{:S(2)}) collective-permute-start(bf16[64,1536]{1,0:T(8,128)(2,1)S(1)} %pad_maximum_fusion.45), channel_id=1, source_target_pairs={{0,2},{1,3},{2,0},{3,1},{4,6},{5,7},{6,4},{7,5},{8,10},{9,11},{10,... | collective-permute-start | bytes 589832 | tf_op jit(solution)/shard_map/ppermute | solution.py:46
  45.2 19.7 %collective-permute-start.15 = (bf16[64,1536]{1,0:T(8,128)(2,1)S(1)}, bf16[64,1536]{1,0:T(8,128)(2,1)S(1)}, u32[]{:S(2)}, u32[]{:S(2)}) collective-permute-start(bf16[64,1536]{1,0:T(8,128)(2,1)S(1)} %pad_maximum_fusion.45), channel_id=1, source_target_pairs={{0,4},{1,5},{2,6},{3,7},{4,0},{5,1},{6,2},{7,3},{8,12},{9,13},{10,... | collective-permute-start | bytes 589832 | tf_op jit(solution)/shard_map/ppermute | solution.py:46
  68.8 21.3 %collective-permute-start.22 = (bf16[96,1024]{1,0:T(8,128)(2,1)}, bf16[96,1024]{1,0:T(8,128)(2,1)S(1)}, u32[]{:S(2)}, u32[]{:S(2)}) collective-permute-start(bf16[96,1024]{1,0:T(8,128)(2,1)} %get-tuple-element.342), channel_id=1, source_target_pairs={{0,2},{1,3},{2,0},{3,1},{4,6},{5,7},{6,4},{7,5},{8,10},{9,11},{10,... | collective-permute-start | bytes 589832 | tf_op jit(solution)/shard_map/ppermute | solution.py:46
  69.5 20.6 %collective-permute-start.23 = (bf16[96,1024]{1,0:T(8,128)(2,1)}, bf16[96,1024]{1,0:T(8,128)(2,1)}, u32[]{:S(2)}, u32[]{:S(2)}) collective-permute-start(bf16[96,1024]{1,0:T(8,128)(2,1)} %get-tuple-element.350), channel_id=1, source_target_pairs={{0,4},{1,5},{2,6},{3,7},{4,0},{5,1},{6,2},{7,3},{8,12},{9,13},{10,... | collective-permute-start | bytes 589832 | tf_op jit(solution)/shard_map/ppermute | solution.py:46
  75.2 20.6 %collective-permute-start.21 = (bf16[2,96,1536]{2,1,0:T(8,128)(2,1)S(1)}, bf16[2,96,1536]{2,1,0:T(8,128)(2,1)}, u32[]{:S(2)}, u32[]{:S(2)}) collective-permute-start(bf16[2,96,1536]{2,1,0:T(8,128)(2,1)S(1)} %broadcast_select_fusion.1), channel_id=1, source_target_pairs={{0,1},{1,0},{2,3},{3,2},{4,5},{5,4},{6,7},{7,6},{8,9},{9,8},{10,11... | collective-permute-start | bytes 1769480 | tf_op jit(solution)/shard_map/ppermute | solution.py:46
  100.2 23.2 %collective-permute-start.30 = (bf16[384,512]{1,0:T(8,128)(2,1)S(1)}, bf16[384,512]{1,0:T(8,128)(2,1)S(1)}, u32[]{:S(2)}, u32[]{:S(2)}) collective-permute-start(bf16[384,512]{1,0:T(8,128)(2,1)S(1)} %get-tuple-element.355), channel_id=1, source_target_pairs={{0,8},{1,9},{2,10},{3,11},{4,12},{5,13},{6,14},{7,15},{8,0},{9,1},... | collective-permute-start | bytes 1179656 | tf_op jit(solution)/shard_map/ppermute | solution.py:46
  128.9 18.5 %collective-permute-start.35 = (bf16[384,512]{1,0:T(8,128)(2,1)S(1)}, bf16[384,512]{1,0:T(8,128)(2,1)S(1)}, u32[]{:S(2)}, u32[]{:S(2)}) collective-permute-start(bf16[384,512]{1,0:T(8,128)(2,1)S(1)} %get-tuple-element.371), channel_id=1, source_target_pairs={{0,8},{1,9},{2,10},{3,11},{4,12},{5,13},{6,14},{7,15},{8,0},{9,1},... | collective-permute-start | bytes 1179656 | tf_op jit(solution)/shard_map/ppermute | solution.py:46
  131.2 18.5 %collective-permute-start.34 = (bf16[768,512]{1,0:T(8,128)(2,1)S(1)}, bf16[768,512]{1,0:T(8,128)(2,1)S(1)}, u32[]{:S(2)}, u32[]{:S(2)}) collective-permute-start(bf16[768,512]{1,0:T(8,128)(2,1)S(1)} %pad_maximum_fusion.12), channel_id=1, source_target_pairs={{0,1},{1,0},{2,3},{3,2},{4,5},{5,4},{6,7},{7,6},{8,9},{9,8},{10,11... | collective-permute-start | bytes 2359304 | tf_op jit(solution)/shard_map/ppermute | solution.py:46
  149.7 19.1 %collective-permute-start.41 = (bf16[128,1536]{1,0:T(8,128)(2,1)S(1)}, bf16[128,1536]{1,0:T(8,128)(2,1)S(1)}, u32[]{:S(2)}, u32[]{:S(2)}) collective-permute-start(bf16[128,1536]{1,0:T(8,128)(2,1)S(1)} %get-tuple-element.383), channel_id=1, source_target_pairs={{0,8},{1,9},{2,10},{3,11},{4,12},{5,13},{6,14},{7,15},{8,0},{9,1},... | collective-permute-start | bytes 1179656 | tf_op jit(solution)/shard_map/ppermute | solution.py:46
  195.6 39.7 %collective-permute-start.55 = (bf16[384,1024]{1,0:T(8,128)(2,1)S(1)}, bf16[384,1024]{1,0:T(8,128)(2,1)S(1)}, u32[]{:S(2)}, u32[]{:S(2)}) collective-permute-start(bf16[384,1024]{1,0:T(8,128)(2,1)S(1)} %slice.779), channel_id=1, source_target_pairs={{0,8},{1,9},{2,10},{3,11},{4,12},{5,13},{6,14},{7,15},{8,0},{9,1},... | collective-permute-start | bytes 2359304 | tf_op jit(solution)/shard_map/ppermute | solution.py:46
  217.7 19.5 %collective-permute-start.54 = (bf16[768,384]{1,0:T(8,128)(2,1)S(1)}, bf16[768,384]{1,0:T(8,128)(2,1)S(1)}, u32[]{:S(2)}, u32[]{:S(2)}) collective-permute-start(bf16[768,384]{1,0:T(8,128)(2,1)S(1)} %pad_maximum_fusion.26), channel_id=1, source_target_pairs={{0,1},{1,0},{2,3},{3,2},{4,5},{5,4},{6,7},{7,6},{8,9},{9,8},{10,11... | collective-permute-start | bytes 1769480 | tf_op jit(solution)/shard_map/ppermute | solution.py:46
  236.8 35.5 %collective-permute-start.62 = (bf16[768,1024]{1,0:T(8,128)(2,1)}, bf16[768,1024]{1,0:T(8,128)(2,1)}, u32[]{:S(2)}, u32[]{:S(2)}) collective-permute-start(bf16[768,1024]{1,0:T(8,128)(2,1)} %pad_maximum_fusion.5), channel_id=1, source_target_pairs={{0,1},{1,0},{2,3},{3,2},{4,5},{5,4},{6,7},{7,6},{8,9},{9,8},{10,11... | collective-permute-start | bytes 4718600 | tf_op jit(solution)/shard_map/ppermute | solution.py:46
  237.2 35.1 %collective-permute-start.61 = (bf16[128,1536]{1,0:T(8,128)(2,1)}, bf16[128,1536]{1,0:T(8,128)(2,1)}, u32[]{:S(2)}, u32[]{:S(2)}) collective-permute-start(bf16[128,1536]{1,0:T(8,128)(2,1)} %get-tuple-element.416), channel_id=1, source_target_pairs={{0,8},{1,9},{2,10},{3,11},{4,12},{5,13},{6,14},{7,15},{8,0},{9,1},... | collective-permute-start | bytes 1179656 | tf_op jit(solution)/shard_map/ppermute | solution.py:46
  259.9 29.9 %collective-permute-start.68 = (bf16[256,1536]{1,0:T(8,128)(2,1)S(1)}, bf16[256,1536]{1,0:T(8,128)(2,1)S(1)}, u32[]{:S(2)}, u32[]{:S(2)}) collective-permute-start(bf16[256,1536]{1,0:T(8,128)(2,1)S(1)} %copy-done.24), channel_id=1, source_target_pairs={{0,16},{1,17},{2,18},{3,19},{4,20},{5,21},{6,22},{7,23},{8,24},{9,... | collective-permute-start | bytes 2359304 | tf_op jit(solution)/shard_map/ppermute | solution.py:46
  277.6 18.6 %collective-permute-start.63 = (bf16[256,1536]{1,0:T(8,128)(2,1)S(1)}, bf16[256,1536]{1,0:T(8,128)(2,1)S(1)}, u32[]{:S(2)}, u32[]{:S(2)}) collective-permute-start(bf16[256,1536]{1,0:T(8,128)(2,1)S(1)} %pad_maximum_fusion.18), channel_id=1, source_target_pairs={{0,1},{1,0},{2,3},{3,2},{4,5},{5,4},{6,7},{7,6},{8,9},{9,8},{10,11... | collective-permute-start | bytes 2359304 | tf_op jit(solution)/shard_map/ppermute | solution.py:46
  299.9 19.2 %collective-permute-start.73 = (bf16[256,1536]{1,0:T(8,128)(2,1)S(1)}, bf16[256,1536]{1,0:T(8,128)(2,1)S(1)}, u32[]{:S(2)}, u32[]{:S(2)}) collective-permute-start(bf16[256,1536]{1,0:T(8,128)(2,1)S(1)} %convolution_convert_fusion.8), channel_id=1, source_target_pairs={{0,1},{1,0},{2,3},{3,2},{4,5},{5,4},{6,7},{7,6},{8,9},{9,8},{10,11... | collective-permute-start | bytes 2359304 | tf_op jit(solution)/shard_map/ppermute | solution.py:46
  314.7 36.7 %collective-permute-start.79 = (bf16[768,1024]{1,0:T(8,128)(2,1)}, bf16[768,1024]{1,0:T(8,128)(2,1)}, u32[]{:S(2)}, u32[]{:S(2)}) collective-permute-start(bf16[768,1024]{1,0:T(8,128)(2,1)} %convolution_convert_fusion.14), channel_id=1, source_target_pairs={{0,1},{1,0},{2,3},{3,2},{4,5},{5,4},{6,7},{7,6},{8,9},{9,8},{10,11... | collective-permute-start | bytes 4718600 | tf_op jit(solution)/shard_map/ppermute | solution.py:46
  332.8 34.3 %collective-permute-start.83 = (bf16[128,1536]{1,0:T(8,128)(2,1)}, bf16[128,1536]{1,0:T(8,128)(2,1)}, u32[]{:S(2)}, u32[]{:S(2)}) collective-permute-start(bf16[128,1536]{1,0:T(8,128)(2,1)} %fusion.43), channel_id=1, source_target_pairs={{0,8},{1,9},{2,10},{3,11},{4,12},{5,13},{6,14},{7,15},{8,0},{9,1},... | collective-permute-start | bytes 1179656 | tf_op jit(solution)/shard_map/ppermute | solution.py:46
  353.3 37.3 %collective-permute-start.88 = (bf16[768,384]{1,0:T(8,128)(2,1)S(1)}, bf16[768,384]{1,0:T(8,128)(2,1)S(1)}, u32[]{:S(2)}, u32[]{:S(2)}) collective-permute-start(bf16[768,384]{1,0:T(8,128)(2,1)S(1)} %convolution_convert_fusion.18), channel_id=1, source_target_pairs={{0,1},{1,0},{2,3},{3,2},{4,5},{5,4},{6,7},{7,6},{8,9},{9,8},{10,11... | collective-permute-start | bytes 1769480 | tf_op jit(solution)/shard_map/ppermute | solution.py:46
  371.2 44.0 %collective-permute-start.93 = (bf16[384,1024]{1,0:T(8,128)(2,1)S(1)}, bf16[384,1024]{1,0:T(8,128)(2,1)S(1)}, u32[]{:S(2)}, u32[]{:S(2)}) collective-permute-start(bf16[384,1024]{1,0:T(8,128)(2,1)S(1)} %fusion.5), channel_id=1, source_target_pairs={{0,8},{1,9},{2,10},{3,11},{4,12},{5,13},{6,14},{7,15},{8,0},{9,1},... | collective-permute-start | bytes 2359304 | tf_op jit(solution)/shard_map/ppermute | solution.py:46
  393.7 28.9 %collective-permute-start.97 = (bf16[256,1536]{1,0:T(8,128)(2,1)S(1)}, bf16[256,1536]{1,0:T(8,128)(2,1)S(1)}, u32[]{:S(2)}, u32[]{:S(2)}) collective-permute-start(bf16[256,1536]{1,0:T(8,128)(2,1)S(1)} %convolution_convert_fusion.6), channel_id=1, source_target_pairs={{0,1},{1,0},{2,3},{3,2},{4,5},{5,4},{6,7},{7,6},{8,9},{9,8},{10,11... | collective-permute-start | bytes 2359304 | tf_op jit(solution)/shard_map/ppermute | solution.py:46
  423.4 21.5 %collective-permute-start.100 = (bf16[768,512]{1,0:T(8,128)(2,1)}, bf16[768,512]{1,0:T(8,128)(2,1)}, u32[]{:S(2)}, u32[]{:S(2)}) collective-permute-start(bf16[768,512]{1,0:T(8,128)(2,1)} %convolution_convert_fusion.16), channel_id=1, source_target_pairs={{0,1},{1,0},{2,3},{3,2},{4,5},{5,4},{6,7},{7,6},{8,9},{9,8},{10,11... | collective-permute-start | bytes 2359304 | tf_op jit(solution)/shard_map/ppermute | solution.py:46
  436.3 20.1 %collective-permute-start.101 = (bf16[128,1536]{1,0:T(8,128)(2,1)}, bf16[128,1536]{1,0:T(8,128)(2,1)S(1)}, u32[]{:S(2)}, u32[]{:S(2)}) collective-permute-start(bf16[128,1536]{1,0:T(8,128)(2,1)} %fusion.41), channel_id=1, source_target_pairs={{0,8},{1,9},{2,10},{3,11},{4,12},{5,13},{6,14},{7,15},{8,0},{9,1},... | collective-permute-start | bytes 1179656 | tf_op jit(solution)/shard_map/ppermute | solution.py:46
  444.9 38.6 %collective-permute-start.106 = (bf16[768,512]{1,0:T(8,128)(2,1)S(1)}, bf16[768,512]{1,0:T(8,128)(2,1)S(1)}, u32[]{:S(2)}, u32[]{:S(2)}) collective-permute-start(bf16[768,512]{1,0:T(8,128)(2,1)S(1)} %copy-done.152), channel_id=1, source_target_pairs={{0,1},{1,0},{2,3},{3,2},{4,5},{5,4},{6,7},{7,6},{8,9},{9,8},{10,11... | collective-permute-start | bytes 2359304 | tf_op jit(solution)/shard_map/ppermute | solution.py:46
  457.4 31.9 %collective-permute-start.108 = (bf16[384,512]{1,0:T(8,128)(2,1)S(1)}, bf16[384,512]{1,0:T(8,128)(2,1)S(1)}, u32[]{:S(2)}, u32[]{:S(2)}) collective-permute-start(bf16[384,512]{1,0:T(8,128)(2,1)S(1)} %fusion.40), channel_id=1, source_target_pairs={{0,8},{1,9},{2,10},{3,11},{4,12},{5,13},{6,14},{7,15},{8,0},{9,1},... | collective-permute-start | bytes 1179656 | tf_op jit(solution)/shard_map/ppermute | solution.py:46
  484.6 18.9 %collective-permute-start.109 = (bf16[384,512]{1,0:T(8,128)(2,1)S(1)}, bf16[384,512]{1,0:T(8,128)(2,1)S(1)}, u32[]{:S(2)}, u32[]{:S(2)}) collective-permute-start(bf16[384,512]{1,0:T(8,128)(2,1)S(1)} %fusion.38), channel_id=1, source_target_pairs={{0,8},{1,9},{2,10},{3,11},{4,12},{5,13},{6,14},{7,15},{8,0},{9,1},... | collective-permute-start | bytes 1179656 | tf_op jit(solution)/shard_map/ppermute | solution.py:46
  484.9 24.4 %collective-permute-start.107 = (bf16[768,384]{1,0:T(8,128)(2,1)S(1)}, bf16[768,384]{1,0:T(8,128)(2,1)S(1)}, u32[]{:S(2)}, u32[]{:S(2)}) collective-permute-start(bf16[768,384]{1,0:T(8,128)(2,1)S(1)} %convolution_convert_fusion.17), channel_id=1, source_target_pairs={{0,1},{1,0},{2,3},{3,2},{4,5},{5,4},{6,7},{7,6},{8,9},{9,8},{10,11... | collective-permute-start | bytes 1769480 | tf_op jit(solution)/shard_map/ppermute | solution.py:46
  485.3 18.4 %collective-permute-start.110 = (bf16[96,1024]{1,0:T(8,128)(2,1)S(1)}, bf16[96,1024]{1,0:T(8,128)(2,1)S(1)}, u32[]{:S(2)}, u32[]{:S(2)}) collective-permute-start(bf16[96,1024]{1,0:T(8,128)(2,1)S(1)} %copy-done.121), channel_id=1, source_target_pairs={{0,2},{1,3},{2,0},{3,1},{4,6},{5,7},{6,4},{7,5},{8,10},{9,11},{10,... | collective-permute-start | bytes 589832 | tf_op jit(solution)/shard_map/ppermute | solution.py:46
  514.8 27.5 %collective-permute-start.122 = (bf16[384,384]{1,0:T(8,128)(2,1)}, bf16[384,384]{1,0:T(8,128)(2,1)}, u32[]{:S(2)}, u32[]{:S(2)}) collective-permute-start(bf16[384,384]{1,0:T(8,128)(2,1)} %fusion.65), channel_id=1, source_target_pairs={{0,8},{1,9},{2,10},{3,11},{4,12},{5,13},{6,14},{7,15},{8,0},{9,1},... | collective-permute-start | bytes 884744 | tf_op jit(solution)/shard_map/ppermute | solution.py:46
  518.1 47.7 %collective-permute-start.131 = (bf16[128,1536]{1,0:T(8,128)(2,1)}, bf16[128,1536]{1,0:T(8,128)(2,1)}, u32[]{:S(2)}, u32[]{:S(2)}) collective-permute-start(bf16[128,1536]{1,0:T(8,128)(2,1)} %get-tuple-element.548), channel_id=1, source_target_pairs={{0,16},{1,17},{2,18},{3,19},{4,20},{5,21},{6,22},{7,23},{8,24},{9,... | collective-permute-start | bytes 1179656 | tf_op jit(solution)/shard_map/ppermute | solution.py:46
  536.4 27.3 %collective-permute-start.133 = (bf16[192,1536]{1,0:T(8,128)(2,1)S(1)}, bf16[192,1536]{1,0:T(8,128)(2,1)}, u32[]{:S(2)}, u32[]{:S(2)}) collective-permute-start(bf16[192,1536]{1,0:T(8,128)(2,1)S(1)} %fusion.57), channel_id=1, source_target_pairs={{8,0},{9,1},{10,2},{11,3},{12,4},{13,5},{14,6},{15,7},{16,24},{17,... | collective-permute-start | bytes 1769480 | tf_op jit(solution)/shard_map/ppermute | solution.py:57
  (261 other events, 2897.5 us)

commit v7 on v6

--- a/solution.py
+++ b/solution.py
@@ -213,14 +213,15 @@
     k_cols = max(1, KV_HEADS // pairs) * HEAD_DIM
     if pairs != KV_HEADS:
         sides = [(0, q_cols, HEADS), (q_cols, k_cols, KV_HEADS), (q_cols + k_cols, k_cols, KV_HEADS)]
+        parts = jnp.stack(parts)
         return [merge_heads(parts[..., at : at + cols], lay, heads) for at, cols, heads in sides]
-    rows = parts.shape[2]
+    rows = parts[0].shape[1]
     plans, shapes = [], []
     for first, cols in ((0, q_cols), (q_cols, k_cols), (q_cols + k_cols, k_cols)):
-        pieces = [(0, (pair // lay.group, pair % lay.group), first, cols) for pair in range(pairs)]
+        pieces = [(pair // lay.group, (pair % lay.group,), first, cols) for pair in range(pairs)]
         plans.append([((slice(None), slice(None)), pieces)])
         shapes.append((rows, pairs * cols))
-    return rearrange([parts], shapes, plans)
+    return rearrange(parts, shapes, plans)
 
 
 def ff_columns(lay, core, member, unit):
@@ -246,18 +247,19 @@
 def unpack_ff(parts, lay, unit):
     ff = 4 * unit
     if not kernel_width(unit):
+        parts = jnp.stack(parts)
         return [merge_ff(parts[..., :ff], lay, unit), merge_ff(parts[..., ff:], lay, unit)]
-    rows = parts.shape[2]
+    rows = parts[0].shape[1]
     plans = []
     for side in (0, 1):
         found = {}
         for core in range(lay.cores):
             for member in range(lay.group):
                 for column, place in ff_columns(lay, core, member, unit):
-                    found[column] = (0, (core, member), side * ff + place * unit, unit)
+                    found[column] = (core, (member,), side * ff + place * unit, unit)
         pieces = [found[column] for column in sorted(found)]
         plans.append([((slice(None), slice(None)), pieces)])
-    return rearrange([parts], [(rows, len(found) * unit)] * 2, plans)
+    return rearrange(parts, [(rows, len(found) * unit)] * 2, plans)
 
 
 def place(own, others, member):
@@ -331,7 +333,8 @@
 
 
 def joined_cores(pair, lay, order):
-    return two_way(lay.core, pair[0], order(pair[1]).astype(F32), 0)
+    kept, other = pair[0], order(pair[1]).astype(F32)
+    return [jnp.where(lay.core == 0, kept, other), jnp.where(lay.core == 0, other, kept)]
 
 
 def out_aligned(lay, block_rows):
@@ -1006,7 +1009,7 @@
     gains = pick(gains, lay.half) + order(gains_other)
     gain_g = pick(gains, lay.member)
     gain_others = to_members(gains, lay, order)
-    down_g = to_outer(joined_cores(down_join, lay, order).reshape(-1, width), lay)
+    down_g = to_outer(jnp.concatenate(joined_cores(down_join, lay, order), 0).reshape(-1, width), lay)
     qkv_g = unpack_heads(joined_cores(qkv_join, lay, order), lay)
     straight, crossed = order(*rows_other)
     ends = two_way(lay.half ^ lay.core, straight, crossed, 0)

time: 592 us -> 592 us (level)
    another operation x13 -> x7, other arithmetic: 7.03 us -> 0.87 us  [two_way(): return jnp.stack([first, second], axis)]
    unnamed x319 -> x317, local copies, waits for them, and re-layouts: 15.2 us -> 15.2 us
  transfers between devices with their start and end apart: 138 -> 138, of which waited for: 66 -> 67; matrix products, arithmetic and copies ran while one was open for 21% -> 21% of each run, Pallas kernels for 7% -> 6%
where the time goes in v7:
time: 592 us; the launch traced here: 586 us
  waiting for transfers between devices  228 us (39%)
  starting transfers between devices  162 us (27%)
  matrix products  58.8 us (10%)
  other arithmetic  58 us (10%)
  Pallas kernels  42.4 us (7%)
  local copies, waits for them, and re-layouts  32.4 us (5%)
    ppermute x136, waiting for transfers between devices, move(): return lax.ppermute(block, MESH_AXES, pairs)  228 us
    ppermute x136, starting transfers between devices, move(): return lax.ppermute(block, MESH_AXES, pairs)  159 us
    pallas_call x10, Pallas kernels, rearrange(): pl.pallas_call(lambda *refs: rearrange_kernel(plans, len(sources), *refs)...  25.1 us
    dot_general x22, matrix products, mm(): lax.dot_general(a, b, (((1,), (0,)), ((), ())), preferred_element_type=F32)  22 us
    dot_general x20, matrix products, mm_tn(): lax.dot_general(a, b, (((0,), (0,)), ((), ())), preferred_element_type=F32)  18.9 us
    dot_general x24, matrix products, mm_nt(): lax.dot_general(a, b, (((1,), (1,)), ((), ())), preferred_element_type=F32)  17.9 us
    unnamed x317, local copies, waits for them, and re-layouts  15.2 us
  transfers between devices with their start and end apart: 138, of which 67 were waited for; matrix products, arithmetic and copies ran while one was open for 21% of the time, Pallas kernels for 6%

profile of v7, /device:TPU:0, one launch (start us, length us, event | category | flops | bytes accessed | tf_op | source)
XLA Modules:
  0.0 585.8 jit_solution(16966964809547433363)
XLA Ops:
  45.2 9.4 %collective-permute-start.15 = (bf16[64,1536]{1,0:T(8,128)(2,1)S(1)}, bf16[64,1536]{1,0:T(8,128)(2,1)S(1)}, u32[]{:S(2)}, u32[]{:S(2)}) collective-permute-start(bf16[64,1536]{1,0:T(8,128)(2,1)S(1)} %pad_maximum_fusion.43), channel_id=1, source_target_pairs={{0,4},{1,5},{2,6},{3,7},{4,0},{5,1},{6,2},{7,3},{8,12},{9,13},{10,... | collective-permute-start | bytes 589832 | tf_op jit(solution)/shard_map/ppermute | solution.py:46
  54.6 4.9 collective-permute-done.17
  69.5 5.4 collective-permute-done.18
  81.7 4.0 attend.2
  103.3 4.1 collective-permute-start.27
  109.1 6.6 %collective-permute-done.27 = bf16[64,1536]{1,0:T(8,128)(2,1)S(1)} collective-permute-done((bf16[64,1536]{1,0:T(8,128)(2,1)S(1)}, bf16[64,1536]{1,0:T(8,128)(2,1)S(1)}, u32[]{:S(2)}, u32[]{:S(2)}) %collective-permute-start.27) | collective-permute-done | bytes 196640 | tf_op jit(solution)/shard_map/ppermute | solution.py:46
  115.8 7.7 %collective-permute-done.28 = bf16[64,1536]{1,0:T(8,128)(2,1)S(1)} collective-permute-done((bf16[64,1536]{1,0:T(8,128)(2,1)S(1)}, bf16[64,1536]{1,0:T(8,128)(2,1)S(1)}, u32[]{:S(2)}, u32[]{:S(2)}) %collective-permute-start.28) | collective-permute-done | bytes 196640 | tf_op jit(solution)/shard_map/ppermute | solution.py:46
  131.3 7.8 %collective-permute-done.32 = bf16[64,1536]{1,0:T(8,128)(2,1)S(1)} collective-permute-done((bf16[64,1536]{1,0:T(8,128)(2,1)S(1)}, bf16[64,1536]{1,0:T(8,128)(2,1)S(1)}, u32[]{:S(2)}, u32[]{:S(2)}) %collective-permute-start.32) | collective-permute-done | bytes 196640 | tf_op jit(solution)/shard_map/ppermute | solution.py:46
  153.3 5.9 collective-permute-done.38
  159.2 6.7 %collective-permute-done.39 = bf16[96,1408]{1,0:T(8,128)(2,1)S(1)} collective-permute-done((bf16[96,1408]{1,0:T(8,128)(2,1)S(1)}, bf16[96,1408]{1,0:T(8,128)(2,1)S(1)}, u32[]{:S(2)}, u32[]{:S(2)}) %collective-permute-start.39) | collective-permute-done | bytes 270368 | tf_op jit(solution)/shard_map/ppermute | solution.py:46
  176.4 6.1 %collective-permute-done.45 = bf16[64,1536]{1,0:T(8,128)(2,1)S(1)} collective-permute-done((bf16[64,1536]{1,0:T(8,128)(2,1)S(1)}, bf16[64,1536]{1,0:T(8,128)(2,1)S(1)}, u32[]{:S(2)}, u32[]{:S(2)}) %collective-permute-start.45) | collective-permute-done | bytes 196640 | tf_op jit(solution)/shard_map/ppermute | solution.py:46
  195.7 5.7 collective-permute-start.55
  201.6 10.6 %collective-permute-done.50 = bf16[64,1536]{1,0:T(8,128)(2,1)S(1)} collective-permute-done((bf16[64,1536]{1,0:T(8,128)(2,1)S(1)}, bf16[64,1536]{1,0:T(8,128)(2,1)S(1)}, u32[]{:S(2)}, u32[]{:S(2)}) %collective-permute-start.50) | collective-permute-done | bytes 196640 | tf_op jit(solution)/shard_map/ppermute | solution.py:46
  220.2 4.7 collective-permute-done.52
  228.4 7.0 %collective-permute-done.55 = bf16[384,1024]{1,0:T(8,128)(2,1)S(1)} collective-permute-done((bf16[384,1024]{1,0:T(8,128)(2,1)S(1)}, bf16[384,1024]{1,0:T(8,128)(2,1)S(1)}, u32[]{:S(2)}, u32[]{:S(2)}) %collective-permute-start.55) | collective-permute-done | bytes 786464 | tf_op jit(solution)/shard_map/ppermute | solution.py:46
  242.1 4.0 attend.3
  262.5 4.8 collective-permute-done.60
  267.2 5.2 collective-permute-done.62
  290.6 5.7 collective-permute-done.63
  332.9 4.2 collective-permute-start.83
  339.5 4.6 attend_back.2
  360.8 3.9 collective-permute-done.80
  371.4 4.4 collective-permute-start.93
  376.4 4.3 collective-permute-done.85
  380.7 5.7 collective-permute-done.86
  407.4 3.8 collective-permute-done.91
  411.2 4.1 collective-permute-done.92
  425.9 6.3 %collective-permute-done.95 = bf16[64,1536]{1,0:T(8,128)(2,1)S(1)} collective-permute-done((bf16[64,1536]{1,0:T(8,128)(2,1)S(1)}, bf16[64,1536]{1,0:T(8,128)(2,1)S(1)}, u32[]{:S(2)}, u32[]{:S(2)}) %collective-permute-start.95) | collective-permute-done | bytes 196640 | tf_op jit(solution)/shard_map/ppermute | solution.py:46
  438.6 4.7 attend_back.3
  448.2 8.4 %collective-permute-done.101 = bf16[128,1536]{1,0:T(8,128)(2,1)S(1)} collective-permute-done((bf16[128,1536]{1,0:T(8,128)(2,1)}, bf16[128,1536]{1,0:T(8,128)(2,1)S(1)}, u32[]{:S(2)}, u32[]{:S(2)}) %collective-permute-start.101) | collective-permute-done | bytes 393248 | tf_op jit(solution)/shard_map/ppermute | solution.py:46
  470.0 10.3 %collective-permute-done.104 = bf16[64,1536]{1,0:T(8,128)(2,1)S(1)} collective-permute-done((bf16[64,1536]{1,0:T(8,128)(2,1)S(1)}, bf16[64,1536]{1,0:T(8,128)(2,1)S(1)}, u32[]{:S(2)}, u32[]{:S(2)}) %collective-permute-start.104) | collective-permute-done | bytes 196640 | tf_op jit(solution)/shard_map/ppermute | solution.py:46
  489.9 13.7 %collective-permute-done.109 = bf16[384,512]{1,0:T(8,128)(2,1)S(1)} collective-permute-done((bf16[384,512]{1,0:T(8,128)(2,1)S(1)}, bf16[384,512]{1,0:T(8,128)(2,1)S(1)}, u32[]{:S(2)}, u32[]{:S(2)}) %collective-permute-start.109) | collective-permute-done | bytes 393248 | tf_op jit(solution)/shard_map/ppermute | solution.py:46
  (888 shorter events, 386.7 us)
Async XLA Ops:
  36.9 22.7 %collective-permute-start.17 = (bf16[384,384]{1,0:T(8,128)(2,1)S(1)}, bf16[384,384]{1,0:T(8,128)(2,1)}, u32[]{:S(2)}, u32[]{:S(2)}) collective-permute-start(bf16[384,384]{1,0:T(8,128)(2,1)S(1)} %bitcast.288), channel_id=1, source_target_pairs={{0,8},{1,9},{2,10},{3,11},{4,12},{5,13},{6,14},{7,15},{8,0},{9,1},... | collective-permute-start | bytes 884744 | tf_op jit(solution)/shard_map/ppermute | solution.py:46
  43.8 21.2 %collective-permute-start.14 = (bf16[64,1536]{1,0:T(8,128)(2,1)S(1)}, bf16[64,1536]{1,0:T(8,128)(2,1)S(1)}, u32[]{:S(2)}, u32[]{:S(2)}) collective-permute-start(bf16[64,1536]{1,0:T(8,128)(2,1)S(1)} %pad_maximum_fusion.43), channel_id=1, source_target_pairs={{0,2},{1,3},{2,0},{3,1},{4,6},{5,7},{6,4},{7,5},{8,10},{9,11},{10,... | collective-permute-start | bytes 589832 | tf_op jit(solution)/shard_map/ppermute | solution.py:46
  45.2 19.7 %collective-permute-start.15 = (bf16[64,1536]{1,0:T(8,128)(2,1)S(1)}, bf16[64,1536]{1,0:T(8,128)(2,1)S(1)}, u32[]{:S(2)}, u32[]{:S(2)}) collective-permute-start(bf16[64,1536]{1,0:T(8,128)(2,1)S(1)} %pad_maximum_fusion.43), channel_id=1, source_target_pairs={{0,4},{1,5},{2,6},{3,7},{4,0},{5,1},{6,2},{7,3},{8,12},{9,13},{10,... | collective-permute-start | bytes 589832 | tf_op jit(solution)/shard_map/ppermute | solution.py:46
  68.8 21.3 %collective-permute-start.22 = (bf16[96,1024]{1,0:T(8,128)(2,1)}, bf16[96,1024]{1,0:T(8,128)(2,1)S(1)}, u32[]{:S(2)}, u32[]{:S(2)}) collective-permute-start(bf16[96,1024]{1,0:T(8,128)(2,1)} %get-tuple-element.342), channel_id=1, source_target_pairs={{0,2},{1,3},{2,0},{3,1},{4,6},{5,7},{6,4},{7,5},{8,10},{9,11},{10,... | collective-permute-start | bytes 589832 | tf_op jit(solution)/shard_map/ppermute | solution.py:46
  69.5 20.6 %collective-permute-start.23 = (bf16[96,1024]{1,0:T(8,128)(2,1)}, bf16[96,1024]{1,0:T(8,128)(2,1)}, u32[]{:S(2)}, u32[]{:S(2)}) collective-permute-start(bf16[96,1024]{1,0:T(8,128)(2,1)} %get-tuple-element.350), channel_id=1, source_target_pairs={{0,4},{1,5},{2,6},{3,7},{4,0},{5,1},{6,2},{7,3},{8,12},{9,13},{10,... | collective-permute-start | bytes 589832 | tf_op jit(solution)/shard_map/ppermute | solution.py:46
  75.3 20.6 %collective-permute-start.21 = (bf16[2,96,1536]{2,1,0:T(8,128)(2,1)S(1)}, bf16[2,96,1536]{2,1,0:T(8,128)(2,1)}, u32[]{:S(2)}, u32[]{:S(2)}) collective-permute-start(bf16[2,96,1536]{2,1,0:T(8,128)(2,1)S(1)} %broadcast_select_fusion.1), channel_id=1, source_target_pairs={{0,1},{1,0},{2,3},{3,2},{4,5},{5,4},{6,7},{7,6},{8,9},{9,8},{10,11... | collective-permute-start | bytes 1769480 | tf_op jit(solution)/shard_map/ppermute | solution.py:46
  100.3 23.2 %collective-permute-start.30 = (bf16[384,512]{1,0:T(8,128)(2,1)S(1)}, bf16[384,512]{1,0:T(8,128)(2,1)S(1)}, u32[]{:S(2)}, u32[]{:S(2)}) collective-permute-start(bf16[384,512]{1,0:T(8,128)(2,1)S(1)} %get-tuple-element.355), channel_id=1, source_target_pairs={{0,8},{1,9},{2,10},{3,11},{4,12},{5,13},{6,14},{7,15},{8,0},{9,1},... | collective-permute-start | bytes 1179656 | tf_op jit(solution)/shard_map/ppermute | solution.py:46
  129.0 18.5 %collective-permute-start.35 = (bf16[384,512]{1,0:T(8,128)(2,1)S(1)}, bf16[384,512]{1,0:T(8,128)(2,1)S(1)}, u32[]{:S(2)}, u32[]{:S(2)}) collective-permute-start(bf16[384,512]{1,0:T(8,128)(2,1)S(1)} %get-tuple-element.371), channel_id=1, source_target_pairs={{0,8},{1,9},{2,10},{3,11},{4,12},{5,13},{6,14},{7,15},{8,0},{9,1},... | collective-permute-start | bytes 1179656 | tf_op jit(solution)/shard_map/ppermute | solution.py:46
  131.2 18.5 %collective-permute-start.34 = (bf16[768,512]{1,0:T(8,128)(2,1)S(1)}, bf16[768,512]{1,0:T(8,128)(2,1)S(1)}, u32[]{:S(2)}, u32[]{:S(2)}) collective-permute-start(bf16[768,512]{1,0:T(8,128)(2,1)S(1)} %pad_maximum_fusion.10), channel_id=1, source_target_pairs={{0,1},{1,0},{2,3},{3,2},{4,5},{5,4},{6,7},{7,6},{8,9},{9,8},{10,11... | collective-permute-start | bytes 2359304 | tf_op jit(solution)/shard_map/ppermute | solution.py:46
  149.8 19.1 %collective-permute-start.41 = (bf16[128,1536]{1,0:T(8,128)(2,1)S(1)}, bf16[128,1536]{1,0:T(8,128)(2,1)S(1)}, u32[]{:S(2)}, u32[]{:S(2)}) collective-permute-start(bf16[128,1536]{1,0:T(8,128)(2,1)S(1)} %get-tuple-element.383), channel_id=1, source_target_pairs={{0,8},{1,9},{2,10},{3,11},{4,12},{5,13},{6,14},{7,15},{8,0},{9,1},... | collective-permute-start | bytes 1179656 | tf_op jit(solution)/shard_map/ppermute | solution.py:46
  195.7 39.8 %collective-permute-start.55 = (bf16[384,1024]{1,0:T(8,128)(2,1)S(1)}, bf16[384,1024]{1,0:T(8,128)(2,1)S(1)}, u32[]{:S(2)}, u32[]{:S(2)}) collective-permute-start(bf16[384,1024]{1,0:T(8,128)(2,1)S(1)} %slice.779), channel_id=1, source_target_pairs={{0,8},{1,9},{2,10},{3,11},{4,12},{5,13},{6,14},{7,15},{8,0},{9,1},... | collective-permute-start | bytes 2359304 | tf_op jit(solution)/shard_map/ppermute | solution.py:46
  217.8 19.5 %collective-permute-start.54 = (bf16[768,384]{1,0:T(8,128)(2,1)S(1)}, bf16[768,384]{1,0:T(8,128)(2,1)S(1)}, u32[]{:S(2)}, u32[]{:S(2)}) collective-permute-start(bf16[768,384]{1,0:T(8,128)(2,1)S(1)} %pad_maximum_fusion.24), channel_id=1, source_target_pairs={{0,1},{1,0},{2,3},{3,2},{4,5},{5,4},{6,7},{7,6},{8,9},{9,8},{10,11... | collective-permute-start | bytes 1769480 | tf_op jit(solution)/shard_map/ppermute | solution.py:46
  236.9 35.5 %collective-permute-start.62 = (bf16[768,1024]{1,0:T(8,128)(2,1)}, bf16[768,1024]{1,0:T(8,128)(2,1)}, u32[]{:S(2)}, u32[]{:S(2)}) collective-permute-start(bf16[768,1024]{1,0:T(8,128)(2,1)} %pad_maximum_fusion.4), channel_id=1, source_target_pairs={{0,1},{1,0},{2,3},{3,2},{4,5},{5,4},{6,7},{7,6},{8,9},{9,8},{10,11... | collective-permute-start | bytes 4718600 | tf_op jit(solution)/shard_map/ppermute | solution.py:46
  237.3 35.1 %collective-permute-start.61 = (bf16[128,1536]{1,0:T(8,128)(2,1)}, bf16[128,1536]{1,0:T(8,128)(2,1)}, u32[]{:S(2)}, u32[]{:S(2)}) collective-permute-start(bf16[128,1536]{1,0:T(8,128)(2,1)} %get-tuple-element.416), channel_id=1, source_target_pairs={{0,8},{1,9},{2,10},{3,11},{4,12},{5,13},{6,14},{7,15},{8,0},{9,1},... | collective-permute-start | bytes 1179656 | tf_op jit(solution)/shard_map/ppermute | solution.py:46
  259.9 29.8 %collective-permute-start.68 = (bf16[256,1536]{1,0:T(8,128)(2,1)S(1)}, bf16[256,1536]{1,0:T(8,128)(2,1)S(1)}, u32[]{:S(2)}, u32[]{:S(2)}) collective-permute-start(bf16[256,1536]{1,0:T(8,128)(2,1)S(1)} %copy-done.23), channel_id=1, source_target_pairs={{0,16},{1,17},{2,18},{3,19},{4,20},{5,21},{6,22},{7,23},{8,24},{9,... | collective-permute-start | bytes 2359304 | tf_op jit(solution)/shard_map/ppermute | solution.py:46
  277.7 18.6 %collective-permute-start.63 = (bf16[256,1536]{1,0:T(8,128)(2,1)S(1)}, bf16[256,1536]{1,0:T(8,128)(2,1)S(1)}, u32[]{:S(2)}, u32[]{:S(2)}) collective-permute-start(bf16[256,1536]{1,0:T(8,128)(2,1)S(1)} %pad_maximum_fusion.16), channel_id=1, source_target_pairs={{0,1},{1,0},{2,3},{3,2},{4,5},{5,4},{6,7},{7,6},{8,9},{9,8},{10,11... | collective-permute-start | bytes 2359304 | tf_op jit(solution)/shard_map/ppermute | solution.py:46
  300.0 19.2 %collective-permute-start.73 = (bf16[256,1536]{1,0:T(8,128)(2,1)S(1)}, bf16[256,1536]{1,0:T(8,128)(2,1)S(1)}, u32[]{:S(2)}, u32[]{:S(2)}) collective-permute-start(bf16[256,1536]{1,0:T(8,128)(2,1)S(1)} %convolution_convert_fusion.8), channel_id=1, source_target_pairs={{0,1},{1,0},{2,3},{3,2},{4,5},{5,4},{6,7},{7,6},{8,9},{9,8},{10,11... | collective-permute-start | bytes 2359304 | tf_op jit(solution)/shard_map/ppermute | solution.py:46
  314.8 36.7 %collective-permute-start.79 = (bf16[768,1024]{1,0:T(8,128)(2,1)}, bf16[768,1024]{1,0:T(8,128)(2,1)}, u32[]{:S(2)}, u32[]{:S(2)}) collective-permute-start(bf16[768,1024]{1,0:T(8,128)(2,1)} %convolution_convert_fusion.14), channel_id=1, source_target_pairs={{0,1},{1,0},{2,3},{3,2},{4,5},{5,4},{6,7},{7,6},{8,9},{9,8},{10,11... | collective-permute-start | bytes 4718600 | tf_op jit(solution)/shard_map/ppermute | solution.py:46
  332.9 34.3 %collective-permute-start.83 = (bf16[128,1536]{1,0:T(8,128)(2,1)}, bf16[128,1536]{1,0:T(8,128)(2,1)}, u32[]{:S(2)}, u32[]{:S(2)}) collective-permute-start(bf16[128,1536]{1,0:T(8,128)(2,1)} %fusion.39), channel_id=1, source_target_pairs={{0,8},{1,9},{2,10},{3,11},{4,12},{5,13},{6,14},{7,15},{8,0},{9,1},... | collective-permute-start | bytes 1179656 | tf_op jit(solution)/shard_map/ppermute | solution.py:46
  353.3 37.4 %collective-permute-start.88 = (bf16[768,384]{1,0:T(8,128)(2,1)S(1)}, bf16[768,384]{1,0:T(8,128)(2,1)S(1)}, u32[]{:S(2)}, u32[]{:S(2)}) collective-permute-start(bf16[768,384]{1,0:T(8,128)(2,1)S(1)} %convolution_convert_fusion.18), channel_id=1, source_target_pairs={{0,1},{1,0},{2,3},{3,2},{4,5},{5,4},{6,7},{7,6},{8,9},{9,8},{10,11... | collective-permute-start | bytes 1769480 | tf_op jit(solution)/shard_map/ppermute | solution.py:46
  371.4 44.0 %collective-permute-start.93 = (bf16[384,1024]{1,0:T(8,128)(2,1)S(1)}, bf16[384,1024]{1,0:T(8,128)(2,1)S(1)}, u32[]{:S(2)}, u32[]{:S(2)}) collective-permute-start(bf16[384,1024]{1,0:T(8,128)(2,1)S(1)} %fusion.3), channel_id=1, source_target_pairs={{0,8},{1,9},{2,10},{3,11},{4,12},{5,13},{6,14},{7,15},{8,0},{9,1},... | collective-permute-start | bytes 2359304 | tf_op jit(solution)/shard_map/ppermute | solution.py:46
  393.9 28.8 %collective-permute-start.97 = (bf16[256,1536]{1,0:T(8,128)(2,1)S(1)}, bf16[256,1536]{1,0:T(8,128)(2,1)S(1)}, u32[]{:S(2)}, u32[]{:S(2)}) collective-permute-start(bf16[256,1536]{1,0:T(8,128)(2,1)S(1)} %convolution_convert_fusion.6), channel_id=1, source_target_pairs={{0,1},{1,0},{2,3},{3,2},{4,5},{5,4},{6,7},{7,6},{8,9},{9,8},{10,11... | collective-permute-start | bytes 2359304 | tf_op jit(solution)/shard_map/ppermute | solution.py:46
  423.4 21.6 %collective-permute-start.100 = (bf16[768,512]{1,0:T(8,128)(2,1)}, bf16[768,512]{1,0:T(8,128)(2,1)}, u32[]{:S(2)}, u32[]{:S(2)}) collective-permute-start(bf16[768,512]{1,0:T(8,128)(2,1)} %convolution_convert_fusion.16), channel_id=1, source_target_pairs={{0,1},{1,0},{2,3},{3,2},{4,5},{5,4},{6,7},{7,6},{8,9},{9,8},{10,11... | collective-permute-start | bytes 2359304 | tf_op jit(solution)/shard_map/ppermute | solution.py:46
  436.4 20.1 %collective-permute-start.101 = (bf16[128,1536]{1,0:T(8,128)(2,1)}, bf16[128,1536]{1,0:T(8,128)(2,1)S(1)}, u32[]{:S(2)}, u32[]{:S(2)}) collective-permute-start(bf16[128,1536]{1,0:T(8,128)(2,1)} %fusion.37), channel_id=1, source_target_pairs={{0,8},{1,9},{2,10},{3,11},{4,12},{5,13},{6,14},{7,15},{8,0},{9,1},... | collective-permute-start | bytes 1179656 | tf_op jit(solution)/shard_map/ppermute | solution.py:46
  445.0 38.6 %collective-permute-start.106 = (bf16[768,512]{1,0:T(8,128)(2,1)S(1)}, bf16[768,512]{1,0:T(8,128)(2,1)S(1)}, u32[]{:S(2)}, u32[]{:S(2)}) collective-permute-start(bf16[768,512]{1,0:T(8,128)(2,1)S(1)} %copy-done.151), channel_id=1, source_target_pairs={{0,1},{1,0},{2,3},{3,2},{4,5},{5,4},{6,7},{7,6},{8,9},{9,8},{10,11... | collective-permute-start | bytes 2359304 | tf_op jit(solution)/shard_map/ppermute | solution.py:46
  457.6 31.9 %collective-permute-start.108 = (bf16[384,512]{1,0:T(8,128)(2,1)S(1)}, bf16[384,512]{1,0:T(8,128)(2,1)S(1)}, u32[]{:S(2)}, u32[]{:S(2)}) collective-permute-start(bf16[384,512]{1,0:T(8,128)(2,1)S(1)} %fusion.36), channel_id=1, source_target_pairs={{0,8},{1,9},{2,10},{3,11},{4,12},{5,13},{6,14},{7,15},{8,0},{9,1},... | collective-permute-start | bytes 1179656 | tf_op jit(solution)/shard_map/ppermute | solution.py:46
  484.8 18.8 %collective-permute-start.109 = (bf16[384,512]{1,0:T(8,128)(2,1)S(1)}, bf16[384,512]{1,0:T(8,128)(2,1)S(1)}, u32[]{:S(2)}, u32[]{:S(2)}) collective-permute-start(bf16[384,512]{1,0:T(8,128)(2,1)S(1)} %fusion.34), channel_id=1, source_target_pairs={{0,8},{1,9},{2,10},{3,11},{4,12},{5,13},{6,14},{7,15},{8,0},{9,1},... | collective-permute-start | bytes 1179656 | tf_op jit(solution)/shard_map/ppermute | solution.py:46
  485.1 24.4 %collective-permute-start.107 = (bf16[768,384]{1,0:T(8,128)(2,1)S(1)}, bf16[768,384]{1,0:T(8,128)(2,1)S(1)}, u32[]{:S(2)}, u32[]{:S(2)}) collective-permute-start(bf16[768,384]{1,0:T(8,128)(2,1)S(1)} %convolution_convert_fusion.17), channel_id=1, source_target_pairs={{0,1},{1,0},{2,3},{3,2},{4,5},{5,4},{6,7},{7,6},{8,9},{9,8},{10,11... | collective-permute-start | bytes 1769480 | tf_op jit(solution)/shard_map/ppermute | solution.py:46
  485.4 18.4 %collective-permute-start.110 = (bf16[96,1024]{1,0:T(8,128)(2,1)S(1)}, bf16[96,1024]{1,0:T(8,128)(2,1)S(1)}, u32[]{:S(2)}, u32[]{:S(2)}) collective-permute-start(bf16[96,1024]{1,0:T(8,128)(2,1)S(1)} %copy-done.120), channel_id=1, source_target_pairs={{0,2},{1,3},{2,0},{3,1},{4,6},{5,7},{6,4},{7,5},{8,10},{9,11},{10,... | collective-permute-start | bytes 589832 | tf_op jit(solution)/shard_map/ppermute | solution.py:46
  514.9 27.5 %collective-permute-start.122 = (bf16[384,384]{1,0:T(8,128)(2,1)}, bf16[384,384]{1,0:T(8,128)(2,1)}, u32[]{:S(2)}, u32[]{:S(2)}) collective-permute-start(bf16[384,384]{1,0:T(8,128)(2,1)} %fusion.59), channel_id=1, source_target_pairs={{0,8},{1,9},{2,10},{3,11},{4,12},{5,13},{6,14},{7,15},{8,0},{9,1},... | collective-permute-start | bytes 884744 | tf_op jit(solution)/shard_map/ppermute | solution.py:46
  518.3 47.8 %collective-permute-start.131 = (bf16[128,1536]{1,0:T(8,128)(2,1)}, bf16[128,1536]{1,0:T(8,128)(2,1)}, u32[]{:S(2)}, u32[]{:S(2)}) collective-permute-start(bf16[128,1536]{1,0:T(8,128)(2,1)} %get-tuple-element.548), channel_id=1, source_target_pairs={{0,16},{1,17},{2,18},{3,19},{4,20},{5,21},{6,22},{7,23},{8,24},{9,... | collective-permute-start | bytes 1179656 | tf_op jit(solution)/shard_map/ppermute | solution.py:46
  536.6 27.4 %collective-permute-start.133 = (bf16[192,1536]{1,0:T(8,128)(2,1)S(1)}, bf16[192,1536]{1,0:T(8,128)(2,1)}, u32[]{:S(2)}, u32[]{:S(2)}) collective-permute-start(bf16[192,1536]{1,0:T(8,128)(2,1)S(1)} %fusion.53), channel_id=1, source_target_pairs={{8,0},{9,1},{10,2},{11,3},{12,4},{13,5},{14,6},{15,7},{16,24},{17,... | collective-permute-start | bytes 1769480 | tf_op jit(solution)/shard_map/ppermute | solution.py:57
  (260 other events, 2880.4 us)
